TPU v7x, 32 devices: a whole 2x2x4 slice. The times are simulated.
32 devices in a mesh: groups: 2 (over x), gx: 16 (over z, y, core).
Axes of the slice: x: 2, y: 2, z: 4, core: 2. Of those that a mesh axis runs over, the one named last changes fastest.
Arguments:
- hidden_in: bfloat16 [704, 8192], P('groups', 'gx'), parts along dimension 0, may hold values from -22 to 22
- norm_gain: float32 [8192], P('gx'), may hold values from 0.4 to 1.6
- w_qkv: bfloat16 [8192, 10240], P('gx'), may hold values from -0.0625 to 0.0625
- w_out: bfloat16 [8192, 8192], P(None, 'gx'), may hold values from -0.0625 to 0.0625
- cache_keys: bfloat16 [704, 128, 1024], P(('groups', 'gx')), parts along dimension 0, may hold values from -34 to 34
- cache_values: bfloat16 [704, 128, 1024], P(('groups', 'gx')), parts along dimension 0, may hold values from -6 to 6
- lengths: int32 [704], P(('groups', 'gx')), parts along dimension 0, may hold values from 1 to 128, as said below
Outputs:
- hidden_out: bfloat16 [704, 8192], P('groups', 'gx'), parts along dimension 0
There are 2 independent parts, one for each index of `groups`. A program takes and returns all parts, laid end to end along the dimension named above; an argument that names none is the same for every part. Nothing has to cross between parts.
Inputs may be any that keep to these rules, and one draw needn't show every extreme that they name: `lengths`: each sequence's length lies between 1 and 128; the first sequence of each replica has 128.
All inputs are finite; a program needn't handle non-finite values.
Results may differ from a plain program's by a relative error of at most 0.014.
Values may be sent and summed in bfloat16 or wider, within the bound.
No kernel may reach another device: no remote copies, remote signals or barrier semaphores. Data moves between devices by JAX's collectives and lax.ppermute only.
A program may use at most 128 MiB of HBM per device.

v0:
```python
import jax
import jax.numpy as jnp
from jax import lax
from jax.sharding import PartitionSpec as P

D = 8192
HEADS = 64
KVH = 8
HD = 128


def rotate(heads, positions):
    half = heads.shape[-1] // 2
    inverse = 500000.0 ** (-(jnp.arange(half, dtype=jnp.float32) * 2.0 / heads.shape[-1]))
    angle = positions.astype(jnp.float32)[:, None] * inverse[None, :]
    cosine = jnp.cos(angle)[:, None, :]
    sine = jnp.sin(angle)[:, None, :]
    first = heads[..., :half]
    second = heads[..., half:]
    return jnp.concatenate(
        [first * cosine - second * sine, second * cosine + first * sine], axis=-1
    )


def attend(query, key_new, value_new, cache_keys, cache_values, lengths):
    count = query.shape[0]
    slots = cache_keys.shape[1]
    kv_heads = key_new.shape[1]
    size = key_new.shape[2]
    group = query.shape[1] // kv_heads
    scale = 1.0 / size**0.5
    grouped = query.reshape(count, kv_heads, group, size)
    keys = cache_keys.reshape(count, slots, kv_heads, size)
    values = cache_values.reshape(count, slots, kv_heads, size)
    scores = (
        jnp.einsum("skgd,slkd->skgl", grouped, keys, preferred_element_type=jnp.float32) * scale
    )
    valid = (jnp.arange(slots, dtype=jnp.int32)[None, :] < lengths[:, None])[:, None, None, :]
    scores = jnp.where(valid, scores, -1e30)
    own = jnp.einsum("skgd,skd->skg", grouped, key_new, preferred_element_type=jnp.float32) * scale
    top = jnp.maximum(jnp.max(scores, axis=-1), own)
    expo = jnp.where(valid, jnp.exp(scores - top[..., None]), 0.0)
    own_expo = jnp.exp(own - top)
    total = jnp.sum(expo, axis=-1) + own_expo
    weights = (expo / total[..., None]).astype(jnp.bfloat16)
    own_weight = (own_expo / total).astype(jnp.bfloat16)
    mixed = jnp.einsum("skgl,slkd->skgd", weights, values, preferred_element_type=jnp.float32)
    mixed = (
        mixed
        + own_weight.astype(jnp.float32)[..., None] * value_new.astype(jnp.float32)[:, :, None, :]
    )
    return mixed.astype(jnp.bfloat16).reshape(count, kv_heads * group * size)


def per_device(hidden_in, norm_gain, w_qkv, w_out, cache_keys, cache_values, lengths):
    own_rows = cache_keys.shape[0]
    model_width = D
    features = hidden_in.astype(jnp.float32)
    square_part = jnp.sum(features * features, axis=1)
    square_all = lax.psum(square_part, "gx")
    square_own = lax.dynamic_slice_in_dim(square_all, lax.axis_index("gx") * own_rows, own_rows, 0)
    inverse_rms = lax.rsqrt(square_own / model_width + 1e-05)[:, None]
    scaled = (features * norm_gain[None, :]).astype(jnp.bfloat16)
    width_q = HEADS * HD
    width_k = KVH * HD
    projected = (
        lax.psum_scatter(
            jnp.dot(scaled, w_qkv, preferred_element_type=jnp.float32).astype(jnp.bfloat16),
            "gx",
            scatter_dimension=0,
            tiled=True,
        ).astype(jnp.float32)
        * inverse_rms
    )
    query_part = projected[:, :width_q]
    key_part = projected[:, width_q : width_q + width_k]
    value_part = projected[:, width_q + width_k :]
    query = rotate(query_part.reshape(own_rows, HEADS, HD), lengths).astype(jnp.bfloat16)
    key_new = rotate(key_part.reshape(own_rows, KVH, HD), lengths).astype(jnp.bfloat16)
    value_new = value_part.reshape(own_rows, KVH, HD).astype(jnp.bfloat16)
    attended = attend(query, key_new, value_new, cache_keys, cache_values, lengths)
    projected_out = jnp.dot(
        lax.all_gather(attended, "gx", axis=0, tiled=True),
        w_out,
        preferred_element_type=jnp.float32,
    )
    return (features + projected_out).astype(jnp.bfloat16)


def solution(mesh):
    in_specs = (
        P("groups", "gx"),
        P("gx"),
        P("gx", None),
        P(None, "gx"),
        P(("groups", "gx"), None, None),
        P(("groups", "gx"), None, None),
        P(("groups", "gx")),
    )
    out_specs = P("groups", "gx")
    return jax.shard_map(
        per_device, mesh=mesh, in_specs=in_specs, out_specs=out_specs, check_vma=False
    )
```

profile of v0, /device:TPU:0, one launch (start us, length us, event | category | flops | bytes accessed | tf_op | source)
XLA Modules:
  0.0 239.5 jit_solution(790541528677821959)
XLA Ops:
  6.5 0.0 all-gather.3.cloned.1.call-start
  6.5 11.0 %convolution_convert_fusion = bf16[352,10240]{1,0:T(8,128)(2,1)} fusion(bf16[512,10240]{1,0:T(8,128)(2,1)} %param.9, bf16[352,512]{1,0:T(8,128)(2,1)} %param.7, f32[512]{0:T(512)} %param.8), kind=kOutput, calls=%fused_computation | convolution fusion | flops 3695132672 | bytes 18057216 | tf_op jit(solution)/shard_map/dot_general | solution.py:68
  17.5 0.0 copy-start.2
  17.5 0.0 copy-start
  17.5 0.0 copy-start.3
  17.5 0.0 slice-start
  17.5 88.3 %fusion = bf16[24,10240]{1,0:T(8,128)(2,1)S(1)} fusion(bf16[352,10240]{1,0:T(8,128)(2,1)} %convolution_convert_fusion), kind=kCustom, calls=%all-reduce-scatter | all-reduce-scatter fusion | flops 3932161 | bytes 7700992
  105.9 3.1 %collective-permute-start = (bf16[24,10240]{1,0:T(8,128)(2,1)S(1)}, bf16[24,10240]{1,0:T(8,128)(2,1)}, u32[]{:S(2)}, u32[]{:S(2)}) collective-permute-start(bf16[24,10240]{1,0:T(8,128)(2,1)S(1)} %fusion), channel_id=1, source_target_pairs={{0,1},{1,2},{2,3},{3,4},{4,5},{5,6},{6,7},{7,8},{8,9},{9,10},{10,1... | collective-permute-start | bytes 1474568
  109.0 3.4 %collective-permute-start.1 = (bf16[6,10240]{1,0:T(8,128)(2,1)S(1)}, bf16[6,10240]{1,0:T(8,128)(2,1)S(1)}, u32[]{:S(2)}, u32[]{:S(2)}) collective-permute-start(bf16[6,10240]{1,0:T(8,128)(2,1)S(1)} %slice.36), channel_id=1, source_target_pairs={{0,2},{1,3},{2,4},{3,5},{4,6},{5,7},{6,8},{7,9},{8,10},{9,11},{10,... | collective-permute-start | bytes 368648
  112.5 0.0 copy-done.2
  112.5 0.1 iota_compare_fusion
  112.6 0.1 multiply_cosine_fusion
  112.7 0.0 copy-done
  112.7 0.2 fusion.21
  112.9 0.0 copy-done.3
  112.9 0.6 dynamic-slice.4
  114.1 30.3 %psum.7 = f32[352]{0:T(512)S(1)} all-reduce(f32[352]{0:T(512)S(1)} %fusion.21), channel_id=1, replica_groups=mesh['groups'=2,'gx'=16] {'gx'}, use_global_device_ids=true, to_apply=%region_2.0 | all-reduce | flops 352 | bytes 2816 | tf_op jit(solution)/shard_map/psum | solution.py:60
  144.4 0.1 add_rsqrt_fusion
  144.5 0.0 collective-permute-done.1
  144.5 0.0 collective-permute-done
  144.5 4.8 %concatenate.17 = bf16[54,10240]{1,0:T(8,128)(2,1)S(1)} concatenate(bf16[6,10240]{1,0:T(8,128)(2,1)S(1)} %collective-permute-done.1, bf16[24,10240]{1,0:T(8,128)(2,1)} %collective-permute-done, bf16[24,10240]{1,0:T(8,128)(2,1)S(1)} %fusion), dimensions={0} | concatenate | bytes 2211840
  149.3 0.0 slice-start.1
  149.3 0.2 convert_multiply_fusion.2
  149.5 0.1 slice.29
  149.7 0.1 copy.18
  149.8 0.1 slice.37
  149.9 0.1 subtract_convert_fusion.1
  150.0 0.0 slice-start.2
  150.0 0.3 fusion.23
  150.4 0.1 maximum_bitcast_fusion
  150.5 0.4 fusion.31
  150.9 0.0 slice-done
  150.9 0.6 slice-done.1
  151.5 0.0 slice-start.3
  151.5 3.2 %fusion.39 = (f32[22,8,8]{2,1,0:T(8,128)S(1)}, f32[22,8,8,128]{3,2,1,0:T(8,128)S(1)}) fusion(bf16[22,8,8,64]{3,2,1,0:T(8,128)(2,1)S(1)} %get-tuple-element.6, bf16[22,8,8,64]{3,2,1,0:T(8,128)(2,1)S(1)} %get-tuple-element.5, pred[22,128]{1,0:T(8,128)(4,1)S(1)} %iota_compare_fusion, bf16[22,128,1024]{2,1,0:T(8,128)(2,1)S(1)} %bitcast.50), kind=kOutput, calls=%fused_computation.51 | convolution fusion | flops 47397504 | bytes 6856960 | tf_op jit(solution)/shard_map/skgd,slkd->skgl/dot_general | solution.py:36
  154.8 0.5 fusion.22
  155.3 0.0 slice-done.2
  155.3 0.0 slice-done.3
  155.3 1.7 fusion.14
  157.1 1.0 reshape.109
  158.0 0.0 all-gather.3.cloned.1.call-update
  158.1 0.0 copy-start.1
  158.1 59.2 %all-gather.3.cloned.1.call-done = bf16[16,22,8192]{2,1,0:T(8,128)(2,1)} async-done(((bf16[1,22,8192]{2,1,0:T(8,128)(2,1)}), bf16[16,22,8192]{2,1,0:T(8,128)(2,1)}) %all-gather.3.cloned.1.call-update) | async-done | bytes 5767184 | tf_op jit(solution)/shard_map/all_gather | solution.py:83
  217.3 6.4 %reshape.110 = bf16[352,8192]{1,0:T(8,128)(2,1)} reshape(bf16[16,22,8192]{2,1,0:T(8,128)(2,1)} %all-gather.3.cloned.1.call-done) | data formatting | bytes 11534336
  223.7 0.0 copy-done.1
  223.7 8.9 %fusion.13 = bf16[352,512]{1,0:T(8,128)(2,1)} fusion(bf16[352,8192]{1,0:T(8,128)(2,1)} %reshape.110, bf16[8192,512]{1,0:T(8,128)(2,1)} %param.10, bf16[352,512]{1,0:T(8,128)(2,1)S(1)} %copy-done.1), kind=kOutput, calls=%fused_computation.10 | convolution fusion | flops 2953330688 | bytes 14876672 | tf_op jit(solution)/shard_map/dot_general | solution.py:82
  (13 shorter events, 0.2 us)
Async XLA Ops:
  6.5 210.8 %all-gather.3.cloned.1.call-start = ((), (), s32[]{:S(2)}) async-start(), calls=%async_computation | async-start | bytes 6684672 | tf_op jit(solution)/shard_map/all_gather | solution.py:83
  17.5 94.9 %copy-start.2 = (s32[22]{0:T(128)S(1)}, s32[22]{0:T(128)}, u32[]{:S(2)}) copy-start(s32[22]{0:T(128)} %param.13) | copy-start | bytes 268
  17.5 95.2 %copy-start = (bf16[352,512]{1,0:T(8,128)(2,1)S(1)}, bf16[352,512]{1,0:T(8,128)(2,1)}, u32[]{:S(2)}) copy-start(bf16[352,512]{1,0:T(8,128)(2,1)} %param.7) | copy-start | bytes 1081348
  17.5 95.3 %copy-start.3 = (u32[32]{0:T(128)S(1)}, u32[32]{0:T(128)}, u32[]{:S(2)}) copy-start(u32[32]{0:T(128)} %constant.36) | copy-start | bytes 388
  17.5 133.4 %slice-start = ((s8[5767168]{0:T(1024)(128)(4,1)}), s8[1572864]{0:T(1024)(128)(4,1)S(1)}, s32[]{:S(2)}) async-start(s8[5767168]{0:T(1024)(128)(4,1)} %bitcast.49), calls=%async_computation.1 | async-start | bytes 3145728
  105.9 38.7 %collective-permute-start = (bf16[24,10240]{1,0:T(8,128)(2,1)S(1)}, bf16[24,10240]{1,0:T(8,128)(2,1)}, u32[]{:S(2)}, u32[]{:S(2)}) collective-permute-start(bf16[24,10240]{1,0:T(8,128)(2,1)S(1)} %fusion), channel_id=1, source_target_pairs={{0,1},{1,2},{2,3},{3,4},{4,5},{5,6},{6,7},{7,8},{8,9},{9,10},{10,1... | collective-permute-start | bytes 1474568
  109.0 35.5 %collective-permute-start.1 = (bf16[6,10240]{1,0:T(8,128)(2,1)S(1)}, bf16[6,10240]{1,0:T(8,128)(2,1)S(1)}, u32[]{:S(2)}, u32[]{:S(2)}) collective-permute-start(bf16[6,10240]{1,0:T(8,128)(2,1)S(1)} %slice.36), channel_id=1, source_target_pairs={{0,2},{1,3},{2,4},{3,5},{4,6},{5,7},{6,8},{7,9},{8,10},{9,11},{10,... | collective-permute-start | bytes 368648
  149.3 2.2 slice-start.1
  150.0 5.3 %slice-start.2 = ((s8[5767168]{0:T(1024)(128)(4,1)}), s8[4194304]{0:T(1024)(128)(4,1)S(1)}, s32[]{:S(2)}) async-start(s8[5767168]{0:T(1024)(128)(4,1)} %bitcast.59), calls=%async_computation.3 | async-start | bytes 8388608
  151.5 3.8 %slice-start.3 = ((s8[5767168]{0:T(1024)(128)(4,1)}), s8[1572864]{0:T(1024)(128)(4,1)S(1)}, s32[]{:S(2)}) async-start(s8[5767168]{0:T(1024)(128)(4,1)} %bitcast.59), calls=%async_computation.4 | async-start | bytes 3145728
  158.1 65.7 %copy-start.1 = (bf16[352,512]{1,0:T(8,128)(2,1)S(1)}, bf16[352,512]{1,0:T(8,128)(2,1)}, u32[]{:S(2)}) copy-start(bf16[352,512]{1,0:T(8,128)(2,1)} %param.7) | copy-start | bytes 1081348
Sparse Core Ops, SparseCore 0:
  158.2 59.0 all-gather.2
where the time goes:
time: 240 us
  blocking collectives  119 us (50%)
  waiting for transfers between devices  59.3 us (25%)
  matrix products  25.2 us (10%)
  between operations  14.3 us (6%)
  local copies, waits for them, and re-layouts  13.8 us (6%)
  starting transfers between devices  6.55 us (3%)
    unnamed x1, blocking collectives  88.3 us
    all_gather x1, waiting for transfers between devices, per_device(): lax.all_gather(attended, 'gx', axis=0, tiled=True)  59.2 us
    psum x1, blocking collectives, per_device(): square_all = lax.psum(square_part, 'gx')  30.3 us
    unnamed x24, local copies, waits for them, and re-layouts  13.7 us
    dot_general x1, matrix products, per_device(): jnp.dot(scaled, w_qkv, preferred_element_type=jnp.float32)  11 us
    dot_general x1, matrix products, per_device(): jnp.dot(lax.all_gather(attended, 'gx', axis=0, tiled=True), w_out, prefer...  8.95 us
    unnamed x2, starting transfers between devices  6.54 us
  transfers between devices with their start and end apart: 3, of which 1 were waited for; matrix products, arithmetic and copies ran while one was open for 0% of the time, Pallas kernels for 0%

commit v1 on v0

v1 whole, which is shorter than its diff:
```python
import functools

import jax
import jax.numpy as jnp
import numpy as np
from jax import lax
from jax.experimental import pallas as pl
from jax.experimental.pallas import tpu as pltpu
from jax.sharding import PartitionSpec as P

D = 8192
HEADS = 64
KVH = 8
HD = 128
GROUP = HEADS // KVH
PARTS = 2
KV_PART = KVH // PARTS
Q_PART = HEADS * HD // PARTS
K_PART = KVH * HD // PARTS
N_PART = Q_PART + 2 * K_PART
MIB = 1 << 20
BF = jnp.bfloat16
F32 = jnp.float32


def chip_cycle(mesh):
    devices = np.moveaxis(mesh.devices, mesh.axis_names.index("gx"), -1)
    devices = devices.reshape(-1, devices.shape[-1])[0][::2]
    count = len(devices)
    places = [getattr(d, "coords", None) for d in devices]
    if any(p is None for p in places):
        return list(range(count))

    def linked(a, b):
        return sum(abs(int(u) - int(v)) for u, v in zip(places[a], places[b])) == 1

    def extend(path):
        if len(path) == count:
            return path if linked(path[-1], path[0]) else None
        for nxt in range(count):
            if nxt not in path and linked(path[-1], nxt):
                found = extend(path + [nxt])
                if found:
                    return found
        return None

    return extend([0]) or list(range(count))


def hops(part, chips):
    far = chips // 2
    near = chips - 1 - far
    return (far, near) if part % 2 == 0 else (near, far)


def offsets(part, chips):
    right, left = hops(part, chips)
    first = [right % chips, -left % chips]
    return first + [k for k in range(chips) if k not in first]


def qkv_kernel(rows, pad, chips, slots_ref, x_ref, gain_ref, w_ref, mine_ref, sib_a_ref, sib_b_ref, xs_ref):
    total = x_ref.shape[0]

    @pl.when(pl.program_id(0) == 0)
    def _():
        scaled = (x_ref[...].astype(F32) * gain_ref[...]).astype(BF)
        me = lax.axis_index("gx")
        row = lax.broadcasted_iota(jnp.int32, (pad, total), 0)
        col = lax.broadcasted_iota(jnp.int32, (pad, total), 1)
        picks = []
        for slot in range(2 * chips):
            start = slots_ref[me, slot] * rows
            picks.append(jnp.where((col == row + start) & (row < rows), 1.0, 0.0))
        pick = jnp.concatenate(picks, axis=0).astype(BF)
        xs_ref[...] = jnp.dot(pick, scaled, preferred_element_type=F32).astype(BF)

    out = jnp.dot(xs_ref[...], w_ref[...], preferred_element_type=F32)
    for slot in range(chips):
        mine_ref[slot] = out[slot * pad : (slot + 1) * pad].astype(BF)
        other = out[(chips + slot) * pad : (chips + slot + 1) * pad].astype(BF)
        if slot < 2:
            sib_a_ref[slot] = other
        else:
            sib_b_ref[slot - 2] = other


def project(part, rows, pad, chips, slots, x, gain, w):
    block = K_PART
    q_blocks = Q_PART // block
    k_first = HEADS * HD // block
    v_first = k_first + KVH * HD // block
    total, depth = x.shape

    def w_index(j, slots_ref):
        q = part * q_blocks + j
        return 0, jnp.where(j < q_blocks, q, jnp.where(j == q_blocks, k_first + part, v_first + part))

    return pl.pallas_call(
        functools.partial(qkv_kernel, rows, pad, chips),
        grid_spec=pltpu.PrefetchScalarGridSpec(
            num_scalar_prefetch=1,
            grid=(N_PART // block,),
            in_specs=[
                pl.BlockSpec((total, depth), lambda j, s: (0, 0)),
                pl.BlockSpec((1, depth), lambda j, s: (0, 0)),
                pl.BlockSpec((depth, block), w_index),
            ],
            out_specs=[
                pl.BlockSpec((chips, pad, block), lambda j, s: (0, 0, j)),
                pl.BlockSpec((2, pad, block), lambda j, s: (0, 0, j)),
                pl.BlockSpec((chips - 2, pad, block), lambda j, s: (0, 0, j)),
            ],
            scratch_shapes=[pltpu.VMEM((2 * chips * pad, depth), BF)],
        ),
        out_shape=[
            jax.ShapeDtypeStruct((chips, pad, N_PART), BF),
            jax.ShapeDtypeStruct((2, pad, N_PART), BF),
            jax.ShapeDtypeStruct((chips - 2, pad, N_PART), BF),
        ],
        compiler_params=pltpu.CompilerParams(vmem_limit_bytes=24 * MIB),
        cost_estimate=pl.CostEstimate(
            flops=2 * 2 * chips * pad * depth * N_PART, bytes_accessed=depth * N_PART * 2 + 2 * chips * pad * N_PART * 2, transcendentals=0
        ),
        name="qkv_part",
    )(slots, x, gain, w)


def attend_kernel(rows, pad, own_ref, sib_ref, left_ref, right_ref, inv_ref, cos_ref, sin_ref, len_ref, k_ref, v_ref, out_ref, s_ref, m_ref):
    live = rows * GROUP
    full = pad * GROUP
    slots = k_ref.shape[1]
    scale = 1.0 / HD**0.5
    inv = inv_ref[...]
    cos = cos_ref[...]
    sin = sin_ref[...]

    def tile(t):
        lanes = slice(t * HD, (t + 1) * HD)
        got = own_ref[0, :, lanes].astype(F32) + sib_ref[0, :, lanes].astype(F32)
        got = got + (left_ref[0, :, lanes].astype(F32) + right_ref[0, :, lanes].astype(F32))
        return got * inv

    def turned(t):
        a = tile(t)
        return (a * cos + pltpu.roll(a, HD // 2, 1) * sin).astype(BF)

    r = lax.broadcasted_iota(jnp.int32, (full, full), 0)
    c = lax.broadcasted_iota(jnp.int32, (full, full), 1)
    by_seq = jnp.where(c == (r % GROUP) * pad + r // GROUP, 1.0, 0.0).astype(BF)
    by_head = jnp.where(r == (c % GROUP) * pad + c // GROUP, 1.0, 0.0).astype(BF)
    r2 = lax.broadcasted_iota(jnp.int32, (full, pad), 0)
    c2 = lax.broadcasted_iota(jnp.int32, (full, pad), 1)
    spread = jnp.where(c2 == r2 // GROUP, 1.0, 0.0).astype(BF)
    valid = lax.broadcasted_iota(jnp.int32, (live, slots), 1) < len_ref[...]

    for kk in range(KV_PART):
        q = jnp.concatenate([turned(kk * GROUP + g).astype(F32) for g in range(GROUP)], axis=0).astype(BF)
        q = jnp.dot(by_seq, q, preferred_element_type=F32)
        k_new = jnp.dot(spread, turned(KV_PART * GROUP + kk), preferred_element_type=F32)
        v_new = jnp.dot(spread, tile(KV_PART * GROUP + KV_PART + kk).astype(BF), preferred_element_type=F32)
        own = (jnp.sum(q * k_new, axis=1, keepdims=True) * scale)[:live]
        lanes = slice(kk * HD, (kk + 1) * HD)
        for s in range(rows):
            s_ref[s * GROUP : (s + 1) * GROUP] = lax.dot_general(
                q[s * GROUP : (s + 1) * GROUP].astype(BF),
                k_ref[s, :, lanes],
                (((1,), (1,)), ((), ())),
                preferred_element_type=F32,
            )
        scores = jnp.where(valid, s_ref[...] * scale, -1e30)
        top = jnp.maximum(jnp.max(scores, axis=1, keepdims=True), own)
        expo = jnp.where(valid, jnp.exp(scores - top), 0.0)
        own_expo = jnp.exp(own - top)
        total = jnp.sum(expo, axis=1, keepdims=True) + own_expo
        s_ref[...] = expo / total
        own_weight = (own_expo / total).astype(BF).astype(F32)
        for s in range(rows):
            m_ref[s * GROUP : (s + 1) * GROUP] = jnp.dot(
                s_ref[s * GROUP : (s + 1) * GROUP].astype(BF), v_ref[s, :, lanes], preferred_element_type=F32
            )
        mixed = m_ref[...] + own_weight * v_new[:live]
        mixed = jnp.concatenate([mixed, jnp.zeros((full - live, HD), F32)], axis=0).astype(BF)
        mixed = jnp.dot(by_head, mixed, preferred_element_type=F32)
        for g in range(GROUP):
            out_ref[:, (kk * GROUP + g) * HD : (kk * GROUP + g + 1) * HD] = mixed[g * pad : (g + 1) * pad].astype(BF)


def attend(part, rows, pad, mine, sib, at, from_left, from_right, inv, cos, sin, lens, keys, values):
    slots = keys.shape[1]
    at_mine, at_sib = at
    return pl.pallas_call(
        functools.partial(attend_kernel, rows, pad),
        grid=(1,),
        in_specs=[
            pl.BlockSpec((1, pad, N_PART), lambda i: (at_mine, 0, 0)),
            pl.BlockSpec((1, pad, N_PART), lambda i: (at_sib, 0, 0)),
            pl.BlockSpec((1, pad, N_PART), lambda i: (0, 0, 0)),
            pl.BlockSpec((1, pad, N_PART), lambda i: (0, 0, 0)),
            pl.BlockSpec((pad, HD), lambda i: (0, 0)),
            pl.BlockSpec((pad, HD), lambda i: (0, 0)),
            pl.BlockSpec((pad, HD), lambda i: (0, 0)),
            pl.BlockSpec((rows * GROUP, 1), lambda i: (0, 0)),
            pl.BlockSpec((rows, slots, K_PART), lambda i: (0, 0, part)),
            pl.BlockSpec((rows, slots, K_PART), lambda i: (0, 0, part)),
        ],
        out_specs=pl.BlockSpec((pad, Q_PART), lambda i: (0, 0)),
        out_shape=jax.ShapeDtypeStruct((pad, Q_PART), BF),
        scratch_shapes=[pltpu.VMEM((rows * GROUP, slots), F32), pltpu.VMEM((rows * GROUP, HD), F32)],
        compiler_params=pltpu.CompilerParams(vmem_limit_bytes=32 * MIB),
        cost_estimate=pl.CostEstimate(
            flops=4 * rows * KV_PART * GROUP * slots * HD * 16, bytes_accessed=4 * rows * slots * K_PART * 2, transcendentals=rows * 32 * slots
        ),
        name="attend_part",
    )(mine, sib, from_left, from_right, inv, cos, sin, lens, keys, values)


def out_kernel(rows, pad, count, last, slots_ref, *refs):
    blocks = refs[:count]
    w_ref = refs[count]
    rest = refs[count + 1 :]
    if last:
        x_ref, prior_ref, out_ref, acc_ref, a_ref = rest
    else:
        out_ref, acc_ref, a_ref = rest
    step = pl.program_id(0)
    for b in range(count):
        a_ref[b * pad : (b + 1) * pad] = blocks[b][...].astype(F32)
    prod = jnp.dot(a_ref[...].astype(BF), w_ref[...], preferred_element_type=F32)

    @pl.when(step == 0)
    def _():
        acc_ref[...] = prod + prior_ref[...] if last else prod

    @pl.when(step > 0)
    def _():
        acc_ref[...] += prod

    @pl.when(step == pl.num_programs(0) - 1)
    def _():
        if not last:
            out_ref[...] = acc_ref[...]
            return
        total = x_ref.shape[0]
        me = lax.axis_index("gx")
        row = lax.broadcasted_iota(jnp.int32, (pad, total), 0)
        col = lax.broadcasted_iota(jnp.int32, (pad, total), 1)
        picks = []
        for slot in range(count):
            start = slots_ref[me, slot] * rows
            picks.append(jnp.where((col == row + start) & (row < rows), 1.0, 0.0))
        pick = jnp.concatenate(picks, axis=0).astype(BF)
        features = jnp.dot(pick, x_ref[...], preferred_element_type=F32)
        result = (features + acc_ref[...]).astype(BF)
        out_ref[...] = lax.dot_general(pick, result, (((0,), (0,)), ((), ())), preferred_element_type=F32).astype(BF)


def project_out(part, rows, pad, slots, blocks, w, x=None, prior=None):
    count = len(blocks)
    cols = w.shape[1]
    block = 1024
    steps = Q_PART // block
    last = prior is not None
    in_specs = [pl.BlockSpec((pad, block), lambda k, s: (0, k)) for _ in blocks]
    in_specs.append(pl.BlockSpec((block, cols), lambda k, s: (part * steps + k, 0)))
    args = list(blocks) + [w]
    if last:
        in_specs += [pl.BlockSpec(x.shape, lambda k, s: (0, 0)), pl.BlockSpec((count * pad, cols), lambda k, s: (0, 0))]
        args += [x, prior]
        out_shape = jax.ShapeDtypeStruct((x.shape[0], cols), BF)
    else:
        out_shape = jax.ShapeDtypeStruct((count * pad, cols), F32)
    return pl.pallas_call(
        functools.partial(out_kernel, rows, pad, count, last),
        grid_spec=pltpu.PrefetchScalarGridSpec(
            num_scalar_prefetch=1,
            grid=(steps,),
            in_specs=in_specs,
            out_specs=pl.BlockSpec(out_shape.shape, lambda k, s: (0, 0)),
            scratch_shapes=[pltpu.VMEM((count * pad, cols), F32), pltpu.VMEM((count * pad, block), F32)],
        ),
        out_shape=out_shape,
        compiler_params=pltpu.CompilerParams(vmem_limit_bytes=24 * MIB),
        cost_estimate=pl.CostEstimate(
            flops=2 * count * pad * Q_PART * cols, bytes_accessed=Q_PART * cols * 2 + count * pad * Q_PART * 2, transcendentals=0
        ),
        name="out_part",
    )(slots, *args)


def wide(a):
    return a.astype(F32)


def per_device(order, hidden_in, norm_gain, w_qkv, w_out, cache_keys, cache_values, lengths):
    rows = cache_keys.shape[0]
    pad = -(-rows // 8) * 8
    chips = len(order)
    count = 2 * chips
    place = {chip: p for p, chip in enumerate(order)}

    def shift(step):
        return [(order[p] * 2 + c, order[(p + step) % chips] * 2 + c) for p in range(chips) for c in range(2)]

    to_right, to_left, to_core = shift(1), shift(-1), [(i, i ^ 1) for i in range(count)]

    def slot_table(ks):
        table = np.zeros((count, count), np.int32)
        for dev in range(count):
            p, core = place[dev // 2], dev % 2
            for j, k in enumerate(ks):
                target = order[(p + k) % chips] * 2
                table[dev, j] = target + core
                table[dev, chips + j] = target + 1 - core
        return jnp.asarray(table)

    def move(a, pairs):
        return lax.ppermute(a, "gx", pairs)

    features = wide(hidden_in)
    square = jnp.sum(features * features, axis=1)
    bit = 1
    while bit < count:
        square = square + move(square, [(i, i ^ bit) for i in range(count)])
        bit *= 2
    square_own = lax.dynamic_slice_in_dim(square, lax.axis_index("gx") * rows, rows, 0)
    inverse_rms = jnp.pad(lax.rsqrt(square_own / D + 1e-05), (0, pad - rows))
    inv = jnp.broadcast_to(inverse_rms[:, None], (pad, HD))

    half = HD // 2
    inverse = 500000.0 ** (-(jnp.arange(half, dtype=F32) * 2.0 / HD))
    angle = jnp.pad(lengths, (0, pad - rows)).astype(F32)[:, None] * inverse[None, :]
    cos = jnp.cos(angle)
    sin = jnp.sin(angle)
    cos = jnp.concatenate([cos, cos], axis=1)
    sin = jnp.concatenate([-sin, sin], axis=1)
    lens = jnp.repeat(lengths, GROUP)[:, None]

    gain = norm_gain[None, :]
    attended = []
    for part in range(PARTS):
        ks = offsets(part, chips)
        mine, sib_a, sib_b = project(part, rows, pad, chips, slot_table(ks), hidden_in, gain, w_qkv)
        got_a = move(sib_a, to_core)
        got_b = move(sib_b, to_core)

        def terms(k):
            j = ks.index(k % chips)
            return wide(mine[j : j + 1]) + wide(got_a[j : j + 1] if j < 2 else got_b[j - 2 : j - 1])

        right, left = hops(part, chips)
        from_left = move(terms(right).astype(BF), to_right)
        from_right = move(terms(-left).astype(BF), to_left)
        for step in range(1, max(right, left)):
            if step < right:
                from_left = move((terms(right - step) + wide(from_left)).astype(BF), to_right)
            if step < left:
                from_right = move((terms(step - left) + wide(from_right)).astype(BF), to_left)
        at = ks.index(0)
        attended.append(
            attend(part, rows, pad, mine, got_b, (at, at - 2), from_left, from_right, inv, cos, sin, lens, cache_keys, cache_values)
        )

    total = None
    for part in range(PARTS):
        right, left = hops(part, chips)
        blocks = {0: attended[part]}
        for step in range(max(right, left)):
            if step < right:
                blocks[-(step + 1) % chips] = move(blocks[-step % chips], to_right)
            if step < left:
                blocks[step + 1] = move(blocks[step], to_left)
        ks = list(range(chips))
        ordered = [blocks[k] for k in ks] + [move(blocks[k], to_core) for k in ks]
        if part < PARTS - 1:
            total = project_out(part, rows, pad, slot_table(ks), ordered, w_out)
        else:
            total = project_out(part, rows, pad, slot_table(ks), ordered, w_out, hidden_in, total)
    return total


def solution(mesh):
    in_specs = (
        P("groups", "gx"),
        P("gx"),
        P("gx", None),
        P(None, "gx"),
        P(("groups", "gx"), None, None),
        P(("groups", "gx"), None, None),
        P(("groups", "gx")),
    )
    out_specs = P("groups", "gx")
    return jax.shard_map(
        functools.partial(per_device, chip_cycle(mesh)), mesh=mesh, in_specs=in_specs, out_specs=out_specs, check_vma=False
    )
```

time: 240 us -> 145 us (0.60)
  blocking collectives: 119 us -> 0 us
  starting transfers between devices: 6.55 us -> 34.7 us
  Pallas kernels: 0 us -> 27.5 us
  matrix products: 25.2 us -> 0 us
  between operations: 14.3 us -> 0.27 us
  other arithmetic: 1.73 us -> 5.38 us
  local copies, waits for them, and re-layouts: 13.8 us -> 16.5 us
    unnamed x1 -> x0, blocking collectives: 88.3 us -> none
    ppermute x0 -> x52, waiting for transfers between devices: none -> 60.7 us  [move(): return lax.ppermute(a, 'gx', pairs)]
    all_gather x1 -> x0, waiting for transfers between devices: 59.2 us -> none  [per_device(): lax.all_gather(attended, 'gx', axis=0, tiled=True)]
    ppermute x0 -> x52, starting transfers between devices: none -> 34.7 us  [move(): return lax.ppermute(a, 'gx', pairs)]
    psum x1 -> x0, blocking collectives: 30.3 us -> none  [per_device(): square_all = lax.psum(square_part, 'gx')]
    pallas_call x0 -> x6, Pallas kernels: none -> 27.5 us  [the longest x2 11 us: project(): pl.pallas_call(functools.partial(qkv_kernel, rows, pad, chips), grid_spec...]
    dot_general x5 -> x0, matrix products: 25.2 us -> none  [the longest x1 11 us: per_device(): jnp.dot(scaled, w_qkv, preferred_element_type=jnp.float32)]
    unnamed x2 -> x0, starting transfers between devices: 6.54 us -> none
  transfers between devices with their start and end apart: 3 -> 52, of which waited for: 1 -> 21; matrix products, arithmetic and copies ran while one was open for 0% -> 3% of each run, Pallas kernels for 0% -> 15%
where the time goes in v1:
time: 145 us
  waiting for transfers between devices  60.7 us (42%)
  starting transfers between devices  34.7 us (24%)
  Pallas kernels  27.5 us (19%)
  local copies, waits for them, and re-layouts  16.5 us (11%)
  other arithmetic  5.38 us (4%)
    ppermute x52, waiting for transfers between devices, move(): return lax.ppermute(a, 'gx', pairs)  60.7 us
    ppermute x52, starting transfers between devices, move(): return lax.ppermute(a, 'gx', pairs)  34.7 us
    unnamed x40, local copies, waits for them, and re-layouts  16.2 us
    pallas_call x2, Pallas kernels, project(): pl.pallas_call(functools.partial(qkv_kernel, rows, pad, chips), grid_spec...  11 us
    pallas_call x2, Pallas kernels, project_out(): pl.pallas_call(functools.partial(out_kernel, rows, pad, count, last), gri...  9.12 us
    pallas_call x2, Pallas kernels, attend(): pl.pallas_call(functools.partial(attend_kernel, rows, pad), grid=(1,), in...  7.42 us
  transfers between devices with their start and end apart: 52, of which 21 were waited for; matrix products, arithmetic and copies ran while one was open for 3% of the time, Pallas kernels for 15%

profile of v1, /device:TPU:0, one launch (start us, length us, event | category | flops | bytes accessed | tf_op | source)
XLA Modules:
  0.0 145.1 jit_solution(16006413614349263311)
XLA Ops:
  0.0 1.1 multiply_reduce_fusion
  1.7 4.0 %copy-done = bf16[512,10240]{1,0:T(8,128)(2,1)S(1)} copy-done((bf16[512,10240]{1,0:T(8,128)(2,1)S(1)}, bf16[512,10240]{1,0:T(8,128)(2,1)}, u32[]{:S(2)}) %copy-start) | copy-done | bytes 10485784
  5.6 1.0 copy-done.7
  8.0 5.5 %qkv_part.3 = (bf16[8,24,5120]{2,1,0:T(8,128)(2,1)S(1)}, bf16[2,24,5120]{2,1,0:T(8,128)(2,1)S(1)}, bf16[6,24,5120]{2,1,0:T(8,128)(2,1)S(1)}) custom-call(s32[16,16]{1,0:T(8,128)S(1)} %copy-done.15, bf16[352,512]{1,0:T(8,128)(2,1)S(1)} %copy-done.7, f32[1,512]{1,0:T(1,128)S(1)} %bitcast.3, bf16[512,10240]{1,0:T(8,128)(2,1)S(1)} %copy-done), custom_call_target="tpu_custom_call" | custom-call | flops 2013265920 | bytes 9175040 | tf_op jit(solution)/shard_map/qkv_part/pallas_call | solution.py:99
  14.1 5.5 %qkv_part.2 = (bf16[8,24,5120]{2,1,0:T(8,128)(2,1)S(1)}, bf16[2,24,5120]{2,1,0:T(8,128)(2,1)S(1)}, bf16[6,24,5120]{2,1,0:T(8,128)(2,1)S(1)}) custom-call(s32[16,16]{1,0:T(8,128)S(1)} %copy-done.14, bf16[352,512]{1,0:T(8,128)(2,1)S(1)} %copy-done.8, f32[1,512]{1,0:T(1,128)S(1)} %bitcast.4, bf16[512,10240]{1,0:T(8,128)(2,1)S(1)} %copy-done.1), custom_call_target="tpu_custom_call" | custom-call | flops 2013265920 | bytes 9175040 | tf_op jit(solution)/shard_map/qkv_part/pallas_call | solution.py:99
  20.2 2.7 %collective-permute-start.10 = (f32[352]{0:T(512)S(1)}, f32[352]{0:T(512)S(1)}, u32[]{:S(2)}, u32[]{:S(2)}) collective-permute-start(f32[352]{0:T(512)S(1)} %add.106), channel_id=1, source_target_pairs={{0,2},{1,3},{2,0},{3,1},{4,6},{5,7},{6,4},{7,5},{8,10},{9,11},{10,... | collective-permute-start | bytes 4232 | tf_op jit(solution)/shard_map/ppermute | solution.py:318
  22.9 1.6 %collective-permute-done.10 = f32[352]{0:T(512)S(1)} collective-permute-done((f32[352]{0:T(512)S(1)}, f32[352]{0:T(512)S(1)}, u32[]{:S(2)}, u32[]{:S(2)}) %collective-permute-start.10) | collective-permute-done | bytes 1440 | tf_op jit(solution)/shard_map/ppermute | solution.py:318
  24.4 2.1 %collective-permute-start.11 = (f32[352]{0:T(512)S(1)}, f32[352]{0:T(512)S(1)}, u32[]{:S(2)}, u32[]{:S(2)}) collective-permute-start(f32[352]{0:T(512)S(1)} %add.107), channel_id=1, source_target_pairs={{0,4},{1,5},{2,6},{3,7},{4,0},{5,1},{6,2},{7,3},{8,12},{9,13},{10,... | collective-permute-start | bytes 4232 | tf_op jit(solution)/shard_map/ppermute | solution.py:318
  26.6 1.4 collective-permute-done.11
  28.1 3.0 %collective-permute-start.12 = (f32[352]{0:T(512)S(1)}, f32[352]{0:T(512)S(1)}, u32[]{:S(2)}, u32[]{:S(2)}) collective-permute-start(f32[352]{0:T(512)S(1)} %add.108), channel_id=1, source_target_pairs={{0,8},{1,9},{2,10},{3,11},{4,12},{5,13},{6,14},{7,15},{8,0},{9,1},... | collective-permute-start | bytes 4232 | tf_op jit(solution)/shard_map/ppermute | solution.py:318
  31.2 1.6 %collective-permute-start.34 = (bf16[1,24,5120]{2,1,0:T(8,128)(2,1)S(1)}, bf16[1,24,5120]{2,1,0:T(8,128)(2,1)S(1)}, u32[]{:S(2)}, u32[]{:S(2)}) collective-permute-start(bf16[1,24,5120]{2,1,0:T(8,128)(2,1)S(1)} %get-tuple-element.21), channel_id=1, source_target_pairs={{0,4},{1,5},{2,0},{3,1},{6,2},{7,3},{10,6},{11,7},{14,10},{15,11},... | collective-permute-start | bytes 737288 | tf_op jit(solution)/shard_map/ppermute | solution.py:318
  33.4 4.7 %collective-permute-done.34 = bf16[1,24,5120]{2,1,0:T(8,128)(2,1)S(1)} collective-permute-done((bf16[1,24,5120]{2,1,0:T(8,128)(2,1)S(1)}, bf16[1,24,5120]{2,1,0:T(8,128)(2,1)S(1)}, u32[]{:S(2)}, u32[]{:S(2)}) %collective-permute-start.34) | collective-permute-done | bytes 245792 | tf_op jit(solution)/shard_map/ppermute | solution.py:318
  38.1 1.6 %collective-permute-start.5 = (bf16[1,24,5120]{2,1,0:T(8,128)(2,1)S(1)}, bf16[1,24,5120]{2,1,0:T(8,128)(2,1)S(1)}, u32[]{:S(2)}, u32[]{:S(2)}) collective-permute-start(bf16[1,24,5120]{2,1,0:T(8,128)(2,1)S(1)} %get-tuple-element.23), channel_id=1, source_target_pairs={{0,4},{1,5},{2,0},{3,1},{6,2},{7,3},{10,6},{11,7},{14,10},{15,11},... | collective-permute-start | bytes 737288 | tf_op jit(solution)/shard_map/ppermute | solution.py:318
  40.2 5.7 %collective-permute-done.5 = bf16[1,24,5120]{2,1,0:T(8,128)(2,1)S(1)} collective-permute-done((bf16[1,24,5120]{2,1,0:T(8,128)(2,1)S(1)}, bf16[1,24,5120]{2,1,0:T(8,128)(2,1)S(1)}, u32[]{:S(2)}, u32[]{:S(2)}) %collective-permute-start.5) | collective-permute-done | bytes 245792 | tf_op jit(solution)/shard_map/ppermute | solution.py:318
  45.9 1.7 %collective-permute-start.35 = (bf16[1,24,5120]{2,1,0:T(8,128)(2,1)S(1)}, bf16[1,24,5120]{2,1,0:T(8,128)(2,1)S(1)}, u32[]{:S(2)}, u32[]{:S(2)}) collective-permute-start(bf16[1,24,5120]{2,1,0:T(8,128)(2,1)S(1)} %add_convert_fusion.1), channel_id=1, source_target_pairs={{0,4},{1,5},{2,0},{3,1},{6,2},{7,3},{10,6},{11,7},{14,10},{15,11},... | collective-permute-start | bytes 737288 | tf_op jit(solution)/shard_map/ppermute | solution.py:318
  47.8 6.1 %collective-permute-done.35 = bf16[1,24,5120]{2,1,0:T(8,128)(2,1)S(1)} collective-permute-done((bf16[1,24,5120]{2,1,0:T(8,128)(2,1)S(1)}, bf16[1,24,5120]{2,1,0:T(8,128)(2,1)S(1)}, u32[]{:S(2)}, u32[]{:S(2)}) %collective-permute-start.35) | collective-permute-done | bytes 245792 | tf_op jit(solution)/shard_map/ppermute | solution.py:318
  54.0 0.9 add_convert_fusion
  54.9 1.7 %collective-permute-start.36 = (bf16[1,24,5120]{2,1,0:T(8,128)(2,1)}, bf16[1,24,5120]{2,1,0:T(8,128)(2,1)S(1)}, u32[]{:S(2)}, u32[]{:S(2)}) collective-permute-start(bf16[1,24,5120]{2,1,0:T(8,128)(2,1)} %get-tuple-element.17), channel_id=1, source_target_pairs={{0,4},{1,5},{2,0},{3,1},{6,2},{7,3},{10,6},{11,7},{14,10},{15,11},... | collective-permute-start | bytes 737288 | tf_op jit(solution)/shard_map/ppermute | solution.py:318
  56.9 2.4 %collective-permute-done.6 = bf16[1,24,5120]{2,1,0:T(8,128)(2,1)S(1)} collective-permute-done((bf16[1,24,5120]{2,1,0:T(8,128)(2,1)S(1)}, bf16[1,24,5120]{2,1,0:T(8,128)(2,1)S(1)}, u32[]{:S(2)}, u32[]{:S(2)}) %collective-permute-start.6) | collective-permute-done | bytes 245792 | tf_op jit(solution)/shard_map/ppermute | solution.py:318
  59.3 1.8 %collective-permute-start.7 = (bf16[1,24,5120]{2,1,0:T(8,128)(2,1)S(1)}, bf16[1,24,5120]{2,1,0:T(8,128)(2,1)S(1)}, u32[]{:S(2)}, u32[]{:S(2)}) collective-permute-start(bf16[1,24,5120]{2,1,0:T(8,128)(2,1)S(1)} %add_convert_fusion.8), channel_id=1, source_target_pairs={{0,4},{1,5},{2,0},{3,1},{6,2},{7,3},{10,6},{11,7},{14,10},{15,11},... | collective-permute-start | bytes 737288 | tf_op jit(solution)/shard_map/ppermute | solution.py:318
  61.1 1.7 %collective-permute-done.31 = bf16[1,24,5120]{2,1,0:T(8,128)(2,1)S(1)} collective-permute-done((bf16[1,24,5120]{2,1,0:T(8,128)(2,1)S(1)}, bf16[1,24,5120]{2,1,0:T(8,128)(2,1)S(1)}, u32[]{:S(2)}, u32[]{:S(2)}) %collective-permute-start.31) | collective-permute-done | bytes 245792 | tf_op jit(solution)/shard_map/ppermute | solution.py:318
  63.2 3.1 %collective-permute-done.7 = bf16[1,24,5120]{2,1,0:T(8,128)(2,1)S(1)} collective-permute-done((bf16[1,24,5120]{2,1,0:T(8,128)(2,1)S(1)}, bf16[1,24,5120]{2,1,0:T(8,128)(2,1)S(1)}, u32[]{:S(2)}, u32[]{:S(2)}) %collective-permute-start.7) | collective-permute-done | bytes 245792 | tf_op jit(solution)/shard_map/ppermute | solution.py:318
  67.2 1.9 %collective-permute-start.8 = (bf16[1,24,5120]{2,1,0:T(8,128)(2,1)}, bf16[1,24,5120]{2,1,0:T(8,128)(2,1)S(1)}, u32[]{:S(2)}, u32[]{:S(2)}) collective-permute-start(bf16[1,24,5120]{2,1,0:T(8,128)(2,1)} %get-tuple-element.19), channel_id=1, source_target_pairs={{0,4},{1,5},{2,0},{3,1},{6,2},{7,3},{10,6},{11,7},{14,10},{15,11},... | collective-permute-start | bytes 737288 | tf_op jit(solution)/shard_map/ppermute | solution.py:318
  69.3 2.4 %collective-permute-done.32 = bf16[1,24,5120]{2,1,0:T(8,128)(2,1)S(1)} collective-permute-done((bf16[1,24,5120]{2,1,0:T(8,128)(2,1)S(1)}, bf16[1,24,5120]{2,1,0:T(8,128)(2,1)S(1)}, u32[]{:S(2)}, u32[]{:S(2)}) %collective-permute-start.32) | collective-permute-done | bytes 245792 | tf_op jit(solution)/shard_map/ppermute | solution.py:318
  72.8 5.3 %collective-permute-done.3 = bf16[1,24,5120]{2,1,0:T(8,128)(2,1)S(1)} collective-permute-done((bf16[1,24,5120]{2,1,0:T(8,128)(2,1)S(1)}, bf16[1,24,5120]{2,1,0:T(8,128)(2,1)S(1)}, u32[]{:S(2)}, u32[]{:S(2)}) %collective-permute-start.3) | collective-permute-done | bytes 245792 | tf_op jit(solution)/shard_map/ppermute | solution.py:318
  79.3 2.3 %collective-permute-done.33.left_ref = bf16[1,24,5120]{2,1,0:T(8,128)(2,1)S(1)} collective-permute-done((bf16[1,24,5120]{2,1,0:T(8,128)(2,1)}, bf16[1,24,5120]{2,1,0:T(8,128)(2,1)S(1)}, u32[]{:S(2)}, u32[]{:S(2)}) %collective-permute-start.33) | collective-permute-done | bytes 245792 | tf_op jit(solution)/shard_map/ppermute | solution.py:318
  81.7 2.8 %copy-done.2 = bf16[22,128,1024]{2,1,0:T(8,128)(2,1)S(1)} copy-done((bf16[22,128,1024]{2,1,0:T(8,128)(2,1)S(1)}, bf16[22,128,1024]{2,1,0:T(8,128)(2,1)}, u32[]{:S(2)}) %copy-start.2) | copy-done | bytes 5767192
  84.5 2.8 %copy-done.4 = bf16[22,128,1024]{2,1,0:T(8,128)(2,1)S(1)} copy-done((bf16[22,128,1024]{2,1,0:T(8,128)(2,1)S(1)}, bf16[22,128,1024]{2,1,0:T(8,128)(2,1)}, u32[]{:S(2)}) %copy-start.4) | copy-done | bytes 5767192
  87.3 1.5 %copy-done.6 = bf16[8,24,5120]{2,1,0:T(8,128)(2,1)S(1)} copy-done((bf16[8,24,5120]{2,1,0:T(8,128)(2,1)S(1)}, bf16[8,24,5120]{2,1,0:T(8,128)(2,1)}, u32[]{:S(2)}) %copy-start.6) | copy-done | bytes 1966104
  88.8 1.4 copy-done.12
  90.2 3.7 %attend_part.3.refs_0_ = bf16[24,4096]{1,0:T(8,128)(2,1)S(1)} custom-call(bf16[8,24,5120]{2,1,0:T(8,128)(2,1)S(1)} %copy-done.6, bf16[6,24,5120]{2,1,0:T(8,128)(2,1)S(1)} %copy-done.12, bf16[1,24,5120]{2,1,0:T(8,128)(2,1)S(1)} %collective-permute-done.33.left_ref, bf16[1,24,5120]{2,1,0:T(8,128)(2,1)S(1)} %collective-permute-done.36.right_ref, ...), custom_call_target="tpu_custom_call" | custom-call | flops 738197504 | bytes 11534336 | tf_op jit(solution)/shard_map/attend_part/pallas_call | solution.py:192
  94.5 1.6 %collective-permute-start.37 = (bf16[24,4096]{1,0:T(8,128)(2,1)S(1)}, bf16[24,4096]{1,0:T(8,128)(2,1)S(1)}, u32[]{:S(2)}, u32[]{:S(2)}) collective-permute-start(bf16[24,4096]{1,0:T(8,128)(2,1)S(1)} %attend_part.3.refs_0_), channel_id=1, source_target_pairs={{0,4},{1,5},{2,0},{3,1},{6,2},{7,3},{10,6},{11,7},{14,10},{15,11},... | collective-permute-start | bytes 589832 | tf_op jit(solution)/shard_map/ppermute | solution.py:318
  96.1 1.4 copy-done.10
  97.4 3.7 %attend_part.2.refs_0_ = bf16[24,4096]{1,0:T(8,128)(2,1)S(1)} custom-call(bf16[8,24,5120]{2,1,0:T(8,128)(2,1)S(1)} %get-tuple-element.11.own_ref, bf16[6,24,5120]{2,1,0:T(8,128)(2,1)S(1)} %copy-done.10, bf16[1,24,5120]{2,1,0:T(8,128)(2,1)S(1)} %collective-permute-done.4.left_ref, bf16[1,24,5120]{2,1,0:T(8,128)(2,1)S(1)} %collective-permute-done.8.right_ref, ...), custom_call_target="tpu_custom_call" | custom-call | flops 738197504 | bytes 11534336 | tf_op jit(solution)/shard_map/attend_part/pallas_call | solution.py:192
  101.8 1.6 %collective-permute-start.13 = (bf16[24,4096]{1,0:T(8,128)(2,1)S(1)}, bf16[24,4096]{1,0:T(8,128)(2,1)S(1)}, u32[]{:S(2)}, u32[]{:S(2)}) collective-permute-start(bf16[24,4096]{1,0:T(8,128)(2,1)S(1)} %attend_part.2.refs_0_), channel_id=1, source_target_pairs={{0,4},{1,5},{2,0},{3,1},{6,2},{7,3},{10,6},{11,7},{14,10},{15,11},... | collective-permute-start | bytes 589832 | tf_op jit(solution)/shard_map/ppermute | solution.py:318
  104.0 5.0 %collective-permute-done.17.refs_7_ = bf16[24,4096]{1,0:T(8,128)(2,1)S(1)} collective-permute-done((bf16[24,4096]{1,0:T(8,128)(2,1)S(1)}, bf16[24,4096]{1,0:T(8,128)(2,1)S(1)}, u32[]{:S(2)}, u32[]{:S(2)}) %collective-permute-start.17) | collective-permute-done | bytes 196640 | tf_op jit(solution)/shard_map/ppermute | solution.py:318
  109.3 1.9 %collective-permute-start.18 = (bf16[24,4096]{1,0:T(8,128)(2,1)S(1)}, bf16[24,4096]{1,0:T(8,128)(2,1)S(1)}, u32[]{:S(2)}, u32[]{:S(2)}) collective-permute-start(bf16[24,4096]{1,0:T(8,128)(2,1)S(1)} %collective-permute-done.17.refs_7_), channel_id=1, source_target_pairs={{0,2},{1,3},{2,6},{3,7},{6,10},{7,11},{10,14},{11,15},{14,12},{15,... | collective-permute-start | bytes 589832 | tf_op jit(solution)/shard_map/ppermute | solution.py:318
  111.3 1.7 %collective-permute-done.41.refs_6_ = bf16[24,4096]{1,0:T(8,128)(2,1)S(1)} collective-permute-done((bf16[24,4096]{1,0:T(8,128)(2,1)S(1)}, bf16[24,4096]{1,0:T(8,128)(2,1)S(1)}, u32[]{:S(2)}, u32[]{:S(2)}) %collective-permute-start.41) | collective-permute-done | bytes 196640 | tf_op jit(solution)/shard_map/ppermute | solution.py:318
  113.1 1.9 %collective-permute-done.38.refs_2_ = bf16[24,4096]{1,0:T(8,128)(2,1)S(1)} collective-permute-done((bf16[24,4096]{1,0:T(8,128)(2,1)S(1)}, bf16[24,4096]{1,0:T(8,128)(2,1)S(1)}, u32[]{:S(2)}, u32[]{:S(2)}) %collective-permute-start.38) | collective-permute-done | bytes 196640 | tf_op jit(solution)/shard_map/ppermute | solution.py:318
  115.5 1.8 %collective-permute-done.18.refs_6_ = bf16[24,4096]{1,0:T(8,128)(2,1)S(1)} collective-permute-done((bf16[24,4096]{1,0:T(8,128)(2,1)S(1)}, bf16[24,4096]{1,0:T(8,128)(2,1)S(1)}, u32[]{:S(2)}, u32[]{:S(2)}) %collective-permute-start.18) | collective-permute-done | bytes 196640 | tf_op jit(solution)/shard_map/ppermute | solution.py:318
  118.1 2.3 %collective-permute-done.14.refs_2_ = bf16[24,4096]{1,0:T(8,128)(2,1)S(1)} collective-permute-done((bf16[24,4096]{1,0:T(8,128)(2,1)S(1)}, bf16[24,4096]{1,0:T(8,128)(2,1)S(1)}, u32[]{:S(2)}, u32[]{:S(2)}) %collective-permute-start.14) | collective-permute-done | bytes 196640 | tf_op jit(solution)/shard_map/ppermute | solution.py:318
  121.2 1.4 collective-permute-start.43
  123.3 1.7 %collective-permute-done.39.refs_3_ = bf16[24,4096]{1,0:T(8,128)(2,1)S(1)} collective-permute-done((bf16[24,4096]{1,0:T(8,128)(2,1)S(1)}, bf16[24,4096]{1,0:T(8,128)(2,1)S(1)}, u32[]{:S(2)}, u32[]{:S(2)}) %collective-permute-start.39) | collective-permute-done | bytes 196640 | tf_op jit(solution)/shard_map/ppermute | solution.py:318
  125.0 3.8 %collective-permute-done.15.refs_3_ = bf16[24,4096]{1,0:T(8,128)(2,1)S(1)} collective-permute-done((bf16[24,4096]{1,0:T(8,128)(2,1)S(1)}, bf16[24,4096]{1,0:T(8,128)(2,1)S(1)}, u32[]{:S(2)}, u32[]{:S(2)}) %collective-permute-start.15) | collective-permute-done | bytes 196640 | tf_op jit(solution)/shard_map/ppermute | solution.py:318
  129.6 1.6 %collective-permute-done.19.refs_5_ = bf16[24,4096]{1,0:T(8,128)(2,1)S(1)} collective-permute-done((bf16[24,4096]{1,0:T(8,128)(2,1)S(1)}, bf16[24,4096]{1,0:T(8,128)(2,1)S(1)}, u32[]{:S(2)}, u32[]{:S(2)}) %collective-permute-start.19) | collective-permute-done | bytes 196640 | tf_op jit(solution)/shard_map/ppermute | solution.py:318
  131.8 3.5 %collective-permute-done.16.refs_4_ = bf16[24,4096]{1,0:T(8,128)(2,1)S(1)} collective-permute-done((bf16[24,4096]{1,0:T(8,128)(2,1)S(1)}, bf16[24,4096]{1,0:T(8,128)(2,1)S(1)}, u32[]{:S(2)}, u32[]{:S(2)}) %collective-permute-start.16) | collective-permute-done | bytes 196640 | tf_op jit(solution)/shard_map/ppermute | solution.py:318
  135.9 3.9 %out_part.2.refs_18_ = f32[384,512]{1,0:T(8,128)S(1)} custom-call(s32[16,16]{1,0:T(8,128)S(1)} %copy-done.13, bf16[24,4096]{1,0:T(8,128)(2,1)S(1)} %attend_part.3.refs_0_, bf16[24,4096]{1,0:T(8,128)(2,1)S(1)} %collective-permute-done.37.refs_1_, bf16[24,4096]{1,0:T(8,128)(2,1)S(1)} %collective-permute-done.38.refs_2_, ...), custom_call_target="tpu_custom_call" | custom-call | flops 1610612736 | bytes 7340032 | tf_op jit(solution)/shard_map/out_part/pallas_call | solution.py:273
  139.8 5.3 %out_part.3 = bf16[352,512]{1,0:T(8,128)(2,1)} custom-call(s32[16,16]{1,0:T(8,128)S(1)} %copy-done.13, bf16[24,4096]{1,0:T(8,128)(2,1)S(1)} %attend_part.2.refs_0_, bf16[24,4096]{1,0:T(8,128)(2,1)S(1)} %collective-permute-done.13.refs_1_, bf16[24,4096]{1,0:T(8,128)(2,1)S(1)} %collective-permute-done.14.refs_2_, ...), custom_call_target="tpu_custom_call" | custom-call | flops 1610612736 | bytes 7340032 | tf_op jit(solution)/shard_map/out_part/pallas_call | solution.py:273
  (127 shorter events, 15.8 us)
Async XLA Ops:
  1.1 19.0 %collective-permute-start.9 = (f32[352]{0:T(512)S(1)}, f32[352]{0:T(512)S(1)}, u32[]{:S(2)}, u32[]{:S(2)}) collective-permute-start(f32[352]{0:T(512)S(1)} %multiply_reduce_fusion), channel_id=1, source_target_pairs={{0,1},{1,0},{2,3},{3,2},{4,5},{5,4},{6,7},{7,6},{8,9},{9,8},{10,11... | collective-permute-start | bytes 4232 | tf_op jit(solution)/shard_map/ppermute | solution.py:318
  13.5 17.6 %collective-permute-start.29 = (bf16[2,24,5120]{2,1,0:T(8,128)(2,1)S(1)}, bf16[2,24,5120]{2,1,0:T(8,128)(2,1)S(1)}, u32[]{:S(2)}, u32[]{:S(2)}) collective-permute-start(bf16[2,24,5120]{2,1,0:T(8,128)(2,1)S(1)} %get-tuple-element.16), channel_id=1, source_target_pairs={{0,1},{1,0},{2,3},{3,2},{4,5},{5,4},{6,7},{7,6},{8,9},{9,8},{10,11... | collective-permute-start | bytes 1474568 | tf_op jit(solution)/shard_map/ppermute | solution.py:318
  13.6 26.0 %collective-permute-start.28 = (bf16[6,24,5120]{2,1,0:T(8,128)(2,1)S(1)}, bf16[6,24,5120]{2,1,0:T(8,128)(2,1)S(1)}, u32[]{:S(2)}, u32[]{:S(2)}) collective-permute-start(bf16[6,24,5120]{2,1,0:T(8,128)(2,1)S(1)} %get-tuple-element.15), channel_id=1, source_target_pairs={{0,1},{1,0},{2,3},{3,2},{4,5},{5,4},{6,7},{7,6},{8,9},{9,8},{10,11... | collective-permute-start | bytes 4423688 | tf_op jit(solution)/shard_map/ppermute | solution.py:318
  19.6 13.3 %collective-permute-start.1 = (bf16[2,24,5120]{2,1,0:T(8,128)(2,1)S(1)}, bf16[2,24,5120]{2,1,0:T(8,128)(2,1)S(1)}, u32[]{:S(2)}, u32[]{:S(2)}) collective-permute-start(bf16[2,24,5120]{2,1,0:T(8,128)(2,1)S(1)} %get-tuple-element.13), channel_id=1, source_target_pairs={{0,1},{1,0},{2,3},{3,2},{4,5},{5,4},{6,7},{7,6},{8,9},{9,8},{10,11... | collective-permute-start | bytes 1474568 | tf_op jit(solution)/shard_map/ppermute | solution.py:318
  19.7 27.9 %collective-permute-start = (bf16[6,24,5120]{2,1,0:T(8,128)(2,1)S(1)}, bf16[6,24,5120]{2,1,0:T(8,128)(2,1)S(1)}, u32[]{:S(2)}, u32[]{:S(2)}) collective-permute-start(bf16[6,24,5120]{2,1,0:T(8,128)(2,1)S(1)} %get-tuple-element.12), channel_id=1, source_target_pairs={{0,1},{1,0},{2,3},{3,2},{4,5},{5,4},{6,7},{7,6},{8,9},{9,8},{10,11... | collective-permute-start | bytes 4423688 | tf_op jit(solution)/shard_map/ppermute | solution.py:318
  28.1 51.1 %collective-permute-start.12 = (f32[352]{0:T(512)S(1)}, f32[352]{0:T(512)S(1)}, u32[]{:S(2)}, u32[]{:S(2)}) collective-permute-start(f32[352]{0:T(512)S(1)} %add.108), channel_id=1, source_target_pairs={{0,8},{1,9},{2,10},{3,11},{4,12},{5,13},{6,14},{7,15},{8,0},{9,1},... | collective-permute-start | bytes 4232 | tf_op jit(solution)/shard_map/ppermute | solution.py:318
  31.2 6.9 %collective-permute-start.34 = (bf16[1,24,5120]{2,1,0:T(8,128)(2,1)S(1)}, bf16[1,24,5120]{2,1,0:T(8,128)(2,1)S(1)}, u32[]{:S(2)}, u32[]{:S(2)}) collective-permute-start(bf16[1,24,5120]{2,1,0:T(8,128)(2,1)S(1)} %get-tuple-element.21), channel_id=1, source_target_pairs={{0,4},{1,5},{2,0},{3,1},{6,2},{7,3},{10,6},{11,7},{14,10},{15,11},... | collective-permute-start | bytes 737288 | tf_op jit(solution)/shard_map/ppermute | solution.py:318
  32.9 15.0 %collective-permute-start.30 = (bf16[1,24,5120]{2,1,0:T(8,128)(2,1)S(1)}, bf16[1,24,5120]{2,1,0:T(8,128)(2,1)S(1)}, u32[]{:S(2)}, u32[]{:S(2)}) collective-permute-start(bf16[1,24,5120]{2,1,0:T(8,128)(2,1)S(1)} %get-tuple-element.22), channel_id=1, source_target_pairs={{0,2},{1,3},{2,6},{3,7},{6,10},{7,11},{10,14},{11,15},{14,12},{15,... | collective-permute-start | bytes 737288 | tf_op jit(solution)/shard_map/ppermute | solution.py:318
  38.1 7.8 %collective-permute-start.5 = (bf16[1,24,5120]{2,1,0:T(8,128)(2,1)S(1)}, bf16[1,24,5120]{2,1,0:T(8,128)(2,1)S(1)}, u32[]{:S(2)}, u32[]{:S(2)}) collective-permute-start(bf16[1,24,5120]{2,1,0:T(8,128)(2,1)S(1)} %get-tuple-element.23), channel_id=1, source_target_pairs={{0,4},{1,5},{2,0},{3,1},{6,2},{7,3},{10,6},{11,7},{14,10},{15,11},... | collective-permute-start | bytes 737288 | tf_op jit(solution)/shard_map/ppermute | solution.py:318
  39.7 23.5 %collective-permute-start.2 = (bf16[1,24,5120]{2,1,0:T(8,128)(2,1)S(1)}, bf16[1,24,5120]{2,1,0:T(8,128)(2,1)S(1)}, u32[]{:S(2)}, u32[]{:S(2)}) collective-permute-start(bf16[1,24,5120]{2,1,0:T(8,128)(2,1)S(1)} %get-tuple-element.24), channel_id=1, source_target_pairs={{0,2},{1,3},{2,6},{3,7},{6,10},{7,11},{10,14},{11,15},{14,12},{15,... | collective-permute-start | bytes 737288 | tf_op jit(solution)/shard_map/ppermute | solution.py:318
  45.9 8.0 %collective-permute-start.35 = (bf16[1,24,5120]{2,1,0:T(8,128)(2,1)S(1)}, bf16[1,24,5120]{2,1,0:T(8,128)(2,1)S(1)}, u32[]{:S(2)}, u32[]{:S(2)}) collective-permute-start(bf16[1,24,5120]{2,1,0:T(8,128)(2,1)S(1)} %add_convert_fusion.1), channel_id=1, source_target_pairs={{0,4},{1,5},{2,0},{3,1},{6,2},{7,3},{10,6},{11,7},{14,10},{15,11},... | collective-permute-start | bytes 737288 | tf_op jit(solution)/shard_map/ppermute | solution.py:318
  47.8 11.5 %collective-permute-start.6 = (bf16[1,24,5120]{2,1,0:T(8,128)(2,1)S(1)}, bf16[1,24,5120]{2,1,0:T(8,128)(2,1)S(1)}, u32[]{:S(2)}, u32[]{:S(2)}) collective-permute-start(bf16[1,24,5120]{2,1,0:T(8,128)(2,1)S(1)} %add_convert_fusion.9), channel_id=1, source_target_pairs={{0,4},{1,5},{2,0},{3,1},{6,2},{7,3},{10,6},{11,7},{14,10},{15,11},... | collective-permute-start | bytes 737288 | tf_op jit(solution)/shard_map/ppermute | solution.py:318
  54.9 24.5 %collective-permute-start.36 = (bf16[1,24,5120]{2,1,0:T(8,128)(2,1)}, bf16[1,24,5120]{2,1,0:T(8,128)(2,1)S(1)}, u32[]{:S(2)}, u32[]{:S(2)}) collective-permute-start(bf16[1,24,5120]{2,1,0:T(8,128)(2,1)} %get-tuple-element.17), channel_id=1, source_target_pairs={{0,4},{1,5},{2,0},{3,1},{6,2},{7,3},{10,6},{11,7},{14,10},{15,11},... | collective-permute-start | bytes 737288 | tf_op jit(solution)/shard_map/ppermute | solution.py:318
  56.6 6.2 %collective-permute-start.31 = (bf16[1,24,5120]{2,1,0:T(8,128)(2,1)S(1)}, bf16[1,24,5120]{2,1,0:T(8,128)(2,1)S(1)}, u32[]{:S(2)}, u32[]{:S(2)}) collective-permute-start(bf16[1,24,5120]{2,1,0:T(8,128)(2,1)S(1)} %get-tuple-element.18), channel_id=1, source_target_pairs={{0,2},{1,3},{2,6},{3,7},{6,10},{7,11},{10,14},{11,15},{14,12},{15,... | collective-permute-start | bytes 737288 | tf_op jit(solution)/shard_map/ppermute | solution.py:318
  59.3 7.0 %collective-permute-start.7 = (bf16[1,24,5120]{2,1,0:T(8,128)(2,1)S(1)}, bf16[1,24,5120]{2,1,0:T(8,128)(2,1)S(1)}, u32[]{:S(2)}, u32[]{:S(2)}) collective-permute-start(bf16[1,24,5120]{2,1,0:T(8,128)(2,1)S(1)} %add_convert_fusion.8), channel_id=1, source_target_pairs={{0,4},{1,5},{2,0},{3,1},{6,2},{7,3},{10,6},{11,7},{14,10},{15,11},... | collective-permute-start | bytes 737288 | tf_op jit(solution)/shard_map/ppermute | solution.py:318
  62.9 8.8 %collective-permute-start.32 = (bf16[1,24,5120]{2,1,0:T(8,128)(2,1)S(1)}, bf16[1,24,5120]{2,1,0:T(8,128)(2,1)S(1)}, u32[]{:S(2)}, u32[]{:S(2)}) collective-permute-start(bf16[1,24,5120]{2,1,0:T(8,128)(2,1)S(1)} %add_convert_fusion.4), channel_id=1, source_target_pairs={{0,2},{1,3},{2,6},{3,7},{6,10},{7,11},{10,14},{11,15},{14,12},{15,... | collective-permute-start | bytes 737288 | tf_op jit(solution)/shard_map/ppermute | solution.py:318
  67.2 28.8 %collective-permute-start.8 = (bf16[1,24,5120]{2,1,0:T(8,128)(2,1)}, bf16[1,24,5120]{2,1,0:T(8,128)(2,1)S(1)}, u32[]{:S(2)}, u32[]{:S(2)}) collective-permute-start(bf16[1,24,5120]{2,1,0:T(8,128)(2,1)} %get-tuple-element.19), channel_id=1, source_target_pairs={{0,4},{1,5},{2,0},{3,1},{6,2},{7,3},{10,6},{11,7},{14,10},{15,11},... | collective-permute-start | bytes 737288 | tf_op jit(solution)/shard_map/ppermute | solution.py:318
  69.2 8.9 %collective-permute-start.3 = (bf16[1,24,5120]{2,1,0:T(8,128)(2,1)S(1)}, bf16[1,24,5120]{2,1,0:T(8,128)(2,1)S(1)}, u32[]{:S(2)}, u32[]{:S(2)}) collective-permute-start(bf16[1,24,5120]{2,1,0:T(8,128)(2,1)S(1)} %get-tuple-element.20), channel_id=1, source_target_pairs={{0,2},{1,3},{2,6},{3,7},{6,10},{7,11},{10,14},{11,15},{14,12},{15,... | collective-permute-start | bytes 737288 | tf_op jit(solution)/shard_map/ppermute | solution.py:318
  72.5 9.1 %collective-permute-start.33 = (bf16[1,24,5120]{2,1,0:T(8,128)(2,1)}, bf16[1,24,5120]{2,1,0:T(8,128)(2,1)S(1)}, u32[]{:S(2)}, u32[]{:S(2)}) collective-permute-start(bf16[1,24,5120]{2,1,0:T(8,128)(2,1)} %add_convert_fusion.3), channel_id=1, source_target_pairs={{0,2},{1,3},{2,6},{3,7},{6,10},{7,11},{10,14},{11,15},{14,12},{15,... | collective-permute-start | bytes 737288 | tf_op jit(solution)/shard_map/ppermute | solution.py:318
  78.9 17.2 %collective-permute-start.4 = (bf16[1,24,5120]{2,1,0:T(8,128)(2,1)}, bf16[1,24,5120]{2,1,0:T(8,128)(2,1)S(1)}, u32[]{:S(2)}, u32[]{:S(2)}) collective-permute-start(bf16[1,24,5120]{2,1,0:T(8,128)(2,1)} %add_convert_fusion.11), channel_id=1, source_target_pairs={{0,2},{1,3},{2,6},{3,7},{6,10},{7,11},{10,14},{11,15},{14,12},{15,... | collective-permute-start | bytes 737288 | tf_op jit(solution)/shard_map/ppermute | solution.py:318
  93.9 7.9 %collective-permute-start.44 = (bf16[24,4096]{1,0:T(8,128)(2,1)S(1)}, bf16[24,4096]{1,0:T(8,128)(2,1)S(1)}, u32[]{:S(2)}, u32[]{:S(2)}) collective-permute-start(bf16[24,4096]{1,0:T(8,128)(2,1)S(1)} %attend_part.3.refs_0_), channel_id=1, source_target_pairs={{0,1},{1,0},{2,3},{3,2},{4,5},{5,4},{6,7},{7,6},{8,9},{9,8},{10,11... | collective-permute-start | bytes 589832 | tf_op jit(solution)/shard_map/ppermute | solution.py:318
  94.0 9.3 %collective-permute-start.40 = (bf16[24,4096]{1,0:T(8,128)(2,1)S(1)}, bf16[24,4096]{1,0:T(8,128)(2,1)S(1)}, u32[]{:S(2)}, u32[]{:S(2)}) collective-permute-start(bf16[24,4096]{1,0:T(8,128)(2,1)S(1)} %attend_part.3.refs_0_), channel_id=1, source_target_pairs={{0,2},{1,3},{2,6},{3,7},{6,10},{7,11},{10,14},{11,15},{14,12},{15,... | collective-permute-start | bytes 589832 | tf_op jit(solution)/shard_map/ppermute | solution.py:318
  94.5 8.8 %collective-permute-start.37 = (bf16[24,4096]{1,0:T(8,128)(2,1)S(1)}, bf16[24,4096]{1,0:T(8,128)(2,1)S(1)}, u32[]{:S(2)}, u32[]{:S(2)}) collective-permute-start(bf16[24,4096]{1,0:T(8,128)(2,1)S(1)} %attend_part.3.refs_0_), channel_id=1, source_target_pairs={{0,4},{1,5},{2,0},{3,1},{6,2},{7,3},{10,6},{11,7},{14,10},{15,11},... | collective-permute-start | bytes 589832 | tf_op jit(solution)/shard_map/ppermute | solution.py:318
  101.2 7.8 %collective-permute-start.17 = (bf16[24,4096]{1,0:T(8,128)(2,1)S(1)}, bf16[24,4096]{1,0:T(8,128)(2,1)S(1)}, u32[]{:S(2)}, u32[]{:S(2)}) collective-permute-start(bf16[24,4096]{1,0:T(8,128)(2,1)S(1)} %attend_part.2.refs_0_), channel_id=1, source_target_pairs={{0,2},{1,3},{2,6},{3,7},{6,10},{7,11},{10,14},{11,15},{14,12},{15,... | collective-permute-start | bytes 589832 | tf_op jit(solution)/shard_map/ppermute | solution.py:318
  101.8 7.5 %collective-permute-start.13 = (bf16[24,4096]{1,0:T(8,128)(2,1)S(1)}, bf16[24,4096]{1,0:T(8,128)(2,1)S(1)}, u32[]{:S(2)}, u32[]{:S(2)}) collective-permute-start(bf16[24,4096]{1,0:T(8,128)(2,1)S(1)} %attend_part.2.refs_0_), channel_id=1, source_target_pairs={{0,4},{1,5},{2,0},{3,1},{6,2},{7,3},{10,6},{11,7},{14,10},{15,11},... | collective-permute-start | bytes 589832 | tf_op jit(solution)/shard_map/ppermute | solution.py:318
  103.3 6.0 %collective-permute-start.51 = (bf16[24,4096]{1,0:T(8,128)(2,1)S(1)}, bf16[24,4096]{1,0:T(8,128)(2,1)S(1)}, u32[]{:S(2)}, u32[]{:S(2)}) collective-permute-start(bf16[24,4096]{1,0:T(8,128)(2,1)S(1)} %collective-permute-done.40.refs_7_), channel_id=1, source_target_pairs={{0,1},{1,0},{2,3},{3,2},{4,5},{5,4},{6,7},{7,6},{8,9},{9,8},{10,11... | collective-permute-start | bytes 589832 | tf_op jit(solution)/shard_map/ppermute | solution.py:318
  103.3 9.7 %collective-permute-start.41 = (bf16[24,4096]{1,0:T(8,128)(2,1)S(1)}, bf16[24,4096]{1,0:T(8,128)(2,1)S(1)}, u32[]{:S(2)}, u32[]{:S(2)}) collective-permute-start(bf16[24,4096]{1,0:T(8,128)(2,1)S(1)} %collective-permute-done.40.refs_7_), channel_id=1, source_target_pairs={{0,2},{1,3},{2,6},{3,7},{6,10},{7,11},{10,14},{11,15},{14,12},{15,... | collective-permute-start | bytes 589832 | tf_op jit(solution)/shard_map/ppermute | solution.py:318
  103.9 9.2 %collective-permute-start.45 = (bf16[24,4096]{1,0:T(8,128)(2,1)S(1)}, bf16[24,4096]{1,0:T(8,128)(2,1)S(1)}, u32[]{:S(2)}, u32[]{:S(2)}) collective-permute-start(bf16[24,4096]{1,0:T(8,128)(2,1)S(1)} %collective-permute-done.37.refs_1_), channel_id=1, source_target_pairs={{0,1},{1,0},{2,3},{3,2},{4,5},{5,4},{6,7},{7,6},{8,9},{9,8},{10,11... | collective-permute-start | bytes 589832 | tf_op jit(solution)/shard_map/ppermute | solution.py:318
  109.0 6.0 %collective-permute-start.38 = (bf16[24,4096]{1,0:T(8,128)(2,1)S(1)}, bf16[24,4096]{1,0:T(8,128)(2,1)S(1)}, u32[]{:S(2)}, u32[]{:S(2)}) collective-permute-start(bf16[24,4096]{1,0:T(8,128)(2,1)S(1)} %collective-permute-done.37.refs_1_), channel_id=1, source_target_pairs={{0,4},{1,5},{2,0},{3,1},{6,2},{7,3},{10,6},{11,7},{14,10},{15,11},... | collective-permute-start | bytes 589832 | tf_op jit(solution)/shard_map/ppermute | solution.py:318
  109.3 6.2 %collective-permute-start.27 = (bf16[24,4096]{1,0:T(8,128)(2,1)S(1)}, bf16[24,4096]{1,0:T(8,128)(2,1)S(1)}, u32[]{:S(2)}, u32[]{:S(2)}) collective-permute-start(bf16[24,4096]{1,0:T(8,128)(2,1)S(1)} %collective-permute-done.17.refs_7_), channel_id=1, source_target_pairs={{0,1},{1,0},{2,3},{3,2},{4,5},{5,4},{6,7},{7,6},{8,9},{9,8},{10,11... | collective-permute-start | bytes 589832 | tf_op jit(solution)/shard_map/ppermute | solution.py:318
  109.3 8.0 %collective-permute-start.18 = (bf16[24,4096]{1,0:T(8,128)(2,1)S(1)}, bf16[24,4096]{1,0:T(8,128)(2,1)S(1)}, u32[]{:S(2)}, u32[]{:S(2)}) collective-permute-start(bf16[24,4096]{1,0:T(8,128)(2,1)S(1)} %collective-permute-done.17.refs_7_), channel_id=1, source_target_pairs={{0,2},{1,3},{2,6},{3,7},{6,10},{7,11},{10,14},{11,15},{14,12},{15,... | collective-permute-start | bytes 589832 | tf_op jit(solution)/shard_map/ppermute | solution.py:318
  113.0 7.3 %collective-permute-start.14 = (bf16[24,4096]{1,0:T(8,128)(2,1)S(1)}, bf16[24,4096]{1,0:T(8,128)(2,1)S(1)}, u32[]{:S(2)}, u32[]{:S(2)}) collective-permute-start(bf16[24,4096]{1,0:T(8,128)(2,1)S(1)} %collective-permute-done.13.refs_1_), channel_id=1, source_target_pairs={{0,4},{1,5},{2,0},{3,1},{6,2},{7,3},{10,6},{11,7},{14,10},{15,11},... | collective-permute-start | bytes 589832 | tf_op jit(solution)/shard_map/ppermute | solution.py:318
  115.0 6.2 %collective-permute-start.42 = (bf16[24,4096]{1,0:T(8,128)(2,1)S(1)}, bf16[24,4096]{1,0:T(8,128)(2,1)S(1)}, u32[]{:S(2)}, u32[]{:S(2)}) collective-permute-start(bf16[24,4096]{1,0:T(8,128)(2,1)S(1)} %collective-permute-done.41.refs_6_), channel_id=1, source_target_pairs={{0,2},{1,3},{2,6},{3,7},{6,10},{7,11},{10,14},{11,15},{14,12},{15,... | collective-permute-start | bytes 589832 | tf_op jit(solution)/shard_map/ppermute | solution.py:318
  115.5 7.1 %collective-permute-start.50 = (bf16[24,4096]{1,0:T(8,128)(2,1)S(1)}, bf16[24,4096]{1,0:T(8,128)(2,1)S(1)}, u32[]{:S(2)}, u32[]{:S(2)}) collective-permute-start(bf16[24,4096]{1,0:T(8,128)(2,1)S(1)} %collective-permute-done.41.refs_6_), channel_id=1, source_target_pairs={{0,1},{1,0},{2,3},{3,2},{4,5},{5,4},{6,7},{7,6},{8,9},{9,8},{10,11... | collective-permute-start | bytes 589832 | tf_op jit(solution)/shard_map/ppermute | solution.py:318
  117.3 6.0 %collective-permute-start.46 = (bf16[24,4096]{1,0:T(8,128)(2,1)S(1)}, bf16[24,4096]{1,0:T(8,128)(2,1)S(1)}, u32[]{:S(2)}, u32[]{:S(2)}) collective-permute-start(bf16[24,4096]{1,0:T(8,128)(2,1)S(1)} %collective-permute-done.38.refs_2_), channel_id=1, source_target_pairs={{0,1},{1,0},{2,3},{3,2},{4,5},{5,4},{6,7},{7,6},{8,9},{9,8},{10,11... | collective-permute-start | bytes 589832 | tf_op jit(solution)/shard_map/ppermute | solution.py:318
  117.3 7.7 %collective-permute-start.39 = (bf16[24,4096]{1,0:T(8,128)(2,1)S(1)}, bf16[24,4096]{1,0:T(8,128)(2,1)S(1)}, u32[]{:S(2)}, u32[]{:S(2)}) collective-permute-start(bf16[24,4096]{1,0:T(8,128)(2,1)S(1)} %collective-permute-done.38.refs_2_), channel_id=1, source_target_pairs={{0,4},{1,5},{2,0},{3,1},{6,2},{7,3},{10,6},{11,7},{14,10},{15,11},... | collective-permute-start | bytes 589832 | tf_op jit(solution)/shard_map/ppermute | solution.py:318
  120.3 8.5 %collective-permute-start.15 = (bf16[24,4096]{1,0:T(8,128)(2,1)S(1)}, bf16[24,4096]{1,0:T(8,128)(2,1)S(1)}, u32[]{:S(2)}, u32[]{:S(2)}) collective-permute-start(bf16[24,4096]{1,0:T(8,128)(2,1)S(1)} %collective-permute-done.14.refs_2_), channel_id=1, source_target_pairs={{0,4},{1,5},{2,0},{3,1},{6,2},{7,3},{10,6},{11,7},{14,10},{15,11},... | collective-permute-start | bytes 589832 | tf_op jit(solution)/shard_map/ppermute | solution.py:318
  121.2 8.4 %collective-permute-start.43 = (bf16[24,4096]{1,0:T(8,128)(2,1)S(1)}, bf16[24,4096]{1,0:T(8,128)(2,1)S(1)}, u32[]{:S(2)}, u32[]{:S(2)}) collective-permute-start(bf16[24,4096]{1,0:T(8,128)(2,1)S(1)} %collective-permute-done.42.refs_5_), channel_id=1, source_target_pairs={{0,2},{1,3},{2,6},{3,7},{6,10},{7,11},{10,14},{11,15},{14,12},{15,... | collective-permute-start | bytes 589832 | tf_op jit(solution)/shard_map/ppermute | solution.py:318
  122.6 8.7 %collective-permute-start.19 = (bf16[24,4096]{1,0:T(8,128)(2,1)S(1)}, bf16[24,4096]{1,0:T(8,128)(2,1)S(1)}, u32[]{:S(2)}, u32[]{:S(2)}) collective-permute-start(bf16[24,4096]{1,0:T(8,128)(2,1)S(1)} %collective-permute-done.18.refs_6_), channel_id=1, source_target_pairs={{0,2},{1,3},{2,6},{3,7},{6,10},{7,11},{10,14},{11,15},{14,12},{15,... | collective-permute-start | bytes 589832 | tf_op jit(solution)/shard_map/ppermute | solution.py:318
  123.3 7.9 %collective-permute-start.49 = (bf16[24,4096]{1,0:T(8,128)(2,1)S(1)}, bf16[24,4096]{1,0:T(8,128)(2,1)S(1)}, u32[]{:S(2)}, u32[]{:S(2)}) collective-permute-start(bf16[24,4096]{1,0:T(8,128)(2,1)S(1)} %collective-permute-done.42.refs_5_), channel_id=1, source_target_pairs={{0,1},{1,0},{2,3},{3,2},{4,5},{5,4},{6,7},{7,6},{8,9},{9,8},{10,11... | collective-permute-start | bytes 589832 | tf_op jit(solution)/shard_map/ppermute | solution.py:318
  125.0 6.8 %collective-permute-start.47 = (bf16[24,4096]{1,0:T(8,128)(2,1)S(1)}, bf16[24,4096]{1,0:T(8,128)(2,1)S(1)}, u32[]{:S(2)}, u32[]{:S(2)}) collective-permute-start(bf16[24,4096]{1,0:T(8,128)(2,1)S(1)} %collective-permute-done.39.refs_3_), channel_id=1, source_target_pairs={{0,1},{1,0},{2,3},{3,2},{4,5},{5,4},{6,7},{7,6},{8,9},{9,8},{10,11... | collective-permute-start | bytes 589832 | tf_op jit(solution)/shard_map/ppermute | solution.py:318
  128.8 6.5 %collective-permute-start.16 = (bf16[24,4096]{1,0:T(8,128)(2,1)S(1)}, bf16[24,4096]{1,0:T(8,128)(2,1)S(1)}, u32[]{:S(2)}, u32[]{:S(2)}) collective-permute-start(bf16[24,4096]{1,0:T(8,128)(2,1)S(1)} %collective-permute-done.15.refs_3_), channel_id=1, source_target_pairs={{0,4},{1,5},{2,0},{3,1},{6,2},{7,3},{10,6},{11,7},{14,10},{15,11},... | collective-permute-start | bytes 589832 | tf_op jit(solution)/shard_map/ppermute | solution.py:318
  129.6 5.8 %collective-permute-start.48 = (bf16[24,4096]{1,0:T(8,128)(2,1)S(1)}, bf16[24,4096]{1,0:T(8,128)(2,1)S(1)}, u32[]{:S(2)}, u32[]{:S(2)}) collective-permute-start(bf16[24,4096]{1,0:T(8,128)(2,1)S(1)} %collective-permute-done.43.refs_4_), channel_id=1, source_target_pairs={{0,1},{1,0},{2,3},{3,2},{4,5},{5,4},{6,7},{7,6},{8,9},{9,8},{10,11... | collective-permute-start | bytes 589832 | tf_op jit(solution)/shard_map/ppermute | solution.py:318
  131.2 8.5 %collective-permute-start.26 = (bf16[24,4096]{1,0:T(8,128)(2,1)S(1)}, bf16[24,4096]{1,0:T(8,128)(2,1)S(1)}, u32[]{:S(2)}, u32[]{:S(2)}) collective-permute-start(bf16[24,4096]{1,0:T(8,128)(2,1)S(1)} %collective-permute-done.18.refs_6_), channel_id=1, source_target_pairs={{0,1},{1,0},{2,3},{3,2},{4,5},{5,4},{6,7},{7,6},{8,9},{9,8},{10,11... | collective-permute-start | bytes 589832 | tf_op jit(solution)/shard_map/ppermute | solution.py:318
  131.2 8.5 %collective-permute-start.22 = (bf16[24,4096]{1,0:T(8,128)(2,1)S(1)}, bf16[24,4096]{1,0:T(8,128)(2,1)S(1)}, u32[]{:S(2)}, u32[]{:S(2)}) collective-permute-start(bf16[24,4096]{1,0:T(8,128)(2,1)S(1)} %collective-permute-done.14.refs_2_), channel_id=1, source_target_pairs={{0,1},{1,0},{2,3},{3,2},{4,5},{5,4},{6,7},{7,6},{8,9},{9,8},{10,11... | collective-permute-start | bytes 589832 | tf_op jit(solution)/shard_map/ppermute | solution.py:318
  131.8 8.0 %collective-permute-start.23 = (bf16[24,4096]{1,0:T(8,128)(2,1)S(1)}, bf16[24,4096]{1,0:T(8,128)(2,1)S(1)}, u32[]{:S(2)}, u32[]{:S(2)}) collective-permute-start(bf16[24,4096]{1,0:T(8,128)(2,1)S(1)} %collective-permute-done.15.refs_3_), channel_id=1, source_target_pairs={{0,1},{1,0},{2,3},{3,2},{4,5},{5,4},{6,7},{7,6},{8,9},{9,8},{10,11... | collective-permute-start | bytes 589832 | tf_op jit(solution)/shard_map/ppermute | solution.py:318
  135.4 4.4 %collective-permute-start.25 = (bf16[24,4096]{1,0:T(8,128)(2,1)S(1)}, bf16[24,4096]{1,0:T(8,128)(2,1)S(1)}, u32[]{:S(2)}, u32[]{:S(2)}) collective-permute-start(bf16[24,4096]{1,0:T(8,128)(2,1)S(1)} %collective-permute-done.19.refs_5_), channel_id=1, source_target_pairs={{0,1},{1,0},{2,3},{3,2},{4,5},{5,4},{6,7},{7,6},{8,9},{9,8},{10,11... | collective-permute-start | bytes 589832 | tf_op jit(solution)/shard_map/ppermute | solution.py:318
  135.4 4.4 %collective-permute-start.24 = (bf16[24,4096]{1,0:T(8,128)(2,1)S(1)}, bf16[24,4096]{1,0:T(8,128)(2,1)S(1)}, u32[]{:S(2)}, u32[]{:S(2)}) collective-permute-start(bf16[24,4096]{1,0:T(8,128)(2,1)S(1)} %collective-permute-done.16.refs_4_), channel_id=1, source_target_pairs={{0,1},{1,0},{2,3},{3,2},{4,5},{5,4},{6,7},{7,6},{8,9},{9,8},{10,11... | collective-permute-start | bytes 589832 | tf_op jit(solution)/shard_map/ppermute | solution.py:318
  (24 other events, 330.8 us)

commit v2 on v0

v2 whole, which is shorter than its diff:
```python
import functools

import jax
import jax.numpy as jnp
import numpy as np
from jax import lax
from jax.experimental import pallas as pl
from jax.experimental.pallas import tpu as pltpu
from jax.sharding import PartitionSpec as P

D = 8192
HEADS = 64
KVH = 8
HD = 128
GROUP = HEADS // KVH
PARTS = ((0, 4), (4, 4))
MIB = 1 << 20
BF = jnp.bfloat16
F32 = jnp.float32


def chip_cycle(mesh):
    devices = np.moveaxis(mesh.devices, mesh.axis_names.index("gx"), -1)
    devices = devices.reshape(-1, devices.shape[-1])[0][::2]
    count = len(devices)
    places = [getattr(d, "coords", None) for d in devices]
    if any(p is None for p in places):
        return list(range(count))

    def linked(a, b):
        return sum(abs(int(u) - int(v)) for u, v in zip(places[a], places[b])) == 1

    def extend(path):
        if len(path) == count:
            return path if linked(path[-1], path[0]) else None
        for nxt in range(count):
            if nxt not in path and linked(path[-1], nxt):
                found = extend(path + [nxt])
                if found:
                    return found
        return None

    return extend([0]) or list(range(count))


def hops(index, chips):
    far = chips // 2
    near = chips - 1 - far
    return (far, near) if index % 2 == 0 else (near, far)


def sent_slots(index, chips):
    up, down = hops(index, chips)
    first = [up, chips - down]
    ks = first + [k for k in range(chips) if k not in first]
    return [(k, 0) for k in ks] + [(k, 1) for k in ks]


def gathered_slots(chips):
    return [(k, w) for w in (0, 1) for k in range(chips)]


def slot_devices(order, slots):
    chips = len(order)
    me = lax.axis_index("gx")
    chip, core = me // 2, me % 2
    place = sum(jnp.where(chip == c, p, 0) for p, c in enumerate(order))

    def chip_at(distance):
        at = (place + distance) % chips
        return sum(jnp.where(at == p, c, 0) for p, c in enumerate(order))

    at = {m: chip_at(m) for m in sorted({m for m, _ in slots})}
    return [at[m] * 2 + jnp.where(core == w, 0, 1) for m, w in slots]


def picker(order, slots, rows, pad, total):
    row = lax.broadcasted_iota(jnp.int32, (pad, total), 0)
    col = lax.broadcasted_iota(jnp.int32, (pad, total), 1)
    picks = [jnp.where((col == row + dev * rows) & (row < rows), 1.0, 0.0) for dev in slot_devices(order, slots)]
    return jnp.concatenate(picks, axis=0).astype(BF)


def qkv_kernel(order, index, rows, pad, x_ref, gain_ref, w_ref, keep_ref, first_ref, rest_ref, xs_ref, w_buf, in_sem):
    total, depth = x_ref.shape
    begin, heads = PARTS[index]
    piece = heads * HD
    pieces = GROUP + 2
    firsts = [begin * GROUP * HD + j * piece for j in range(GROUP)]
    firsts += [(HEADS + begin) * HD, (HEADS + KVH + begin) * HD]
    slots = sent_slots(index, len(order))
    kept, first = keep_ref.shape[0], first_ref.shape[0]
    ahead = 4

    def load(j):
        return pltpu.make_async_copy(w_ref.at[:, pl.ds(firsts[j], piece)], w_buf.at[j], in_sem.at[j])

    def write(slot, lanes, value):
        if slot < kept:
            keep_ref[slot, :, lanes] = value
        elif slot < kept + first:
            first_ref[slot - kept, :, lanes] = value
        else:
            rest_ref[slot - kept - first, :, lanes] = value

    for j in range(ahead):
        load(j).start()
    features = jnp.dot(picker(order, slots, rows, pad, total), x_ref[...], preferred_element_type=F32)
    xs_ref[...] = (features * gain_ref[...]).astype(BF)
    width = pieces * piece
    extra = keep_ref.shape[2] - width
    if extra:
        me = lax.axis_index("gx")
        square = jnp.sum(features * features, axis=1, keepdims=True)
        lane = lax.broadcasted_iota(jnp.int32, (len(slots) * pad, extra), 1)
        high = square.astype(BF).astype(F32)
        mid = (square - high).astype(BF).astype(F32)
        low = square - high - mid
        held = jnp.where(lane == 3 * me, high, 0.0) + jnp.where(lane == 3 * me + 1, mid, 0.0) + jnp.where(lane == 3 * me + 2, low, 0.0)
        for slot in range(len(slots)):
            write(slot, slice(width, None), held[slot * pad : (slot + 1) * pad].astype(BF))
    for j in range(pieces):
        if j + ahead < pieces:
            load(j + ahead).start()
        load(j).wait()
        out = jnp.dot(xs_ref[...], w_buf[j], preferred_element_type=F32)
        for slot in range(len(slots)):
            write(slot, slice(j * piece, (j + 1) * piece), out[slot * pad : (slot + 1) * pad].astype(BF))


def project(order, index, rows, pad, x, gain, w):
    piece = PARTS[index][1] * HD
    pieces = GROUP + 2
    depth = x.shape[1]
    chips = len(order)
    extra = -(-6 * chips // 128) * 128 if index == 0 else 0
    width = pieces * piece + extra
    vmem = pl.BlockSpec(memory_space=pltpu.VMEM)
    return pl.pallas_call(
        functools.partial(qkv_kernel, order, index, rows, pad),
        in_specs=[vmem, vmem, pl.BlockSpec(memory_space=pltpu.HBM)],
        out_specs=[vmem] * 3,
        scratch_shapes=[
            pltpu.VMEM((2 * chips * pad, depth), BF),
            pltpu.VMEM((pieces, depth, piece), BF),
            pltpu.SemaphoreType.DMA((pieces,)),
        ],
        out_shape=[jax.ShapeDtypeStruct((n, pad, width), BF) for n in (chips, 2, chips - 2)],
        compiler_params=pltpu.CompilerParams(vmem_limit_bytes=(56 if index == 0 else 46) * MIB),
        cost_estimate=pl.CostEstimate(flops=1, bytes_accessed=1, transcendentals=0),
        name="qkv_part",
    )(x, gain, w)


def attend_kernel(part, rows, pad, own_ref, core_ref, left_ref, right_ref, inv_ref, cos_ref, sin_ref, len_ref, k_ref, v_ref, out_ref, s_ref, m_ref):
    begin, heads = part
    live = rows * GROUP
    full = pad * GROUP
    slots = k_ref.shape[1]
    scale = 1.0 / HD**0.5
    inv = inv_ref[...]
    cos = cos_ref[...]
    sin = sin_ref[...]

    def tile(t):
        lanes = slice(t * HD, (t + 1) * HD)
        got = own_ref[0, :, lanes].astype(F32) + core_ref[0, :, lanes].astype(F32)
        return (got + (left_ref[0, :, lanes].astype(F32) + right_ref[0, :, lanes].astype(F32))) * inv

    def turned(t):
        a = tile(t)
        return (a * cos + pltpu.roll(a, HD // 2, 1) * sin).astype(BF)

    r = lax.broadcasted_iota(jnp.int32, (full, full), 0)
    c = lax.broadcasted_iota(jnp.int32, (full, full), 1)
    by_seq = jnp.where(c == (r % GROUP) * pad + r // GROUP, 1.0, 0.0).astype(BF)
    by_head = jnp.where(r == (c % GROUP) * pad + c // GROUP, 1.0, 0.0).astype(BF)
    r2 = lax.broadcasted_iota(jnp.int32, (full, pad), 0)
    c2 = lax.broadcasted_iota(jnp.int32, (full, pad), 1)
    spread = jnp.where(c2 == r2 // GROUP, 1.0, 0.0).astype(BF)
    valid = lax.broadcasted_iota(jnp.int32, (live, slots), 1) < len_ref[...]

    queries, owns, values_new = [], [], []
    for kk in range(heads):
        q = jnp.concatenate([turned(kk * GROUP + g).astype(F32) for g in range(GROUP)], axis=0).astype(BF)
        q = jnp.dot(by_seq, q, preferred_element_type=F32)
        k_new = jnp.dot(spread, turned(heads * GROUP + kk), preferred_element_type=F32)
        values_new.append(jnp.dot(spread, tile(heads * GROUP + heads + kk).astype(BF), preferred_element_type=F32)[:live])
        owns.append((jnp.sum(q * k_new, axis=1, keepdims=True) * scale)[:live])
        queries.append(q)
    for kk in range(heads):
        lanes = slice((begin + kk) * HD, (begin + kk + 1) * HD)
        for s in range(rows):
            s_ref[kk, s * GROUP : (s + 1) * GROUP] = lax.dot_general(
                queries[kk][s * GROUP : (s + 1) * GROUP].astype(BF),
                k_ref[s, :, lanes],
                (((1,), (1,)), ((), ())),
                preferred_element_type=F32,
            )
    own_weights = []
    for kk in range(heads):
        scores = jnp.where(valid, s_ref[kk] * scale, -1e30)
        top = jnp.maximum(jnp.max(scores, axis=1, keepdims=True), owns[kk])
        expo = jnp.where(valid, jnp.exp(scores - top), 0.0)
        own_expo = jnp.exp(owns[kk] - top)
        total = jnp.sum(expo, axis=1, keepdims=True) + own_expo
        s_ref[kk] = expo / total
        own_weights.append((own_expo / total).astype(BF).astype(F32))
    for kk in range(heads):
        lanes = slice((begin + kk) * HD, (begin + kk + 1) * HD)
        for s in range(rows):
            m_ref[kk, s * GROUP : (s + 1) * GROUP] = jnp.dot(
                s_ref[kk, s * GROUP : (s + 1) * GROUP].astype(BF), v_ref[s, :, lanes], preferred_element_type=F32
            )
    for kk in range(heads):
        mixed = m_ref[kk] + own_weights[kk] * values_new[kk]
        mixed = jnp.concatenate([mixed, jnp.zeros((full - live, HD), F32)], axis=0).astype(BF)
        mixed = jnp.dot(by_head, mixed, preferred_element_type=F32)
        for g in range(GROUP):
            out_ref[0, :, (kk * GROUP + g) * HD : (kk * GROUP + g + 1) * HD] = mixed[g * pad : (g + 1) * pad].astype(BF)


def load(name, limit, arrays, begin=0, count=None):
    count = arrays[0].shape[0] if count is None else count

    def kernel(*refs):
        sems = refs[-1]
        copies = [
            pltpu.make_async_copy(refs[i].at[pl.ds(begin, count)], refs[len(arrays) + i], sems.at[i]) for i in range(len(arrays))
        ]
        for copy in copies:
            copy.start()
        for copy in copies:
            copy.wait()

    return pl.pallas_call(
        kernel,
        in_specs=[pl.BlockSpec(memory_space=pltpu.HBM)] * len(arrays),
        out_specs=[pl.BlockSpec(memory_space=pltpu.VMEM)] * len(arrays),
        out_shape=[jax.ShapeDtypeStruct((count,) + a.shape[1:], BF) for a in arrays],
        scratch_shapes=[pltpu.SemaphoreType.DMA((len(arrays),))],
        compiler_params=pltpu.CompilerParams(vmem_limit_bytes=limit * MIB),
        cost_estimate=pl.CostEstimate(flops=1, bytes_accessed=1, transcendentals=0),
        name=name,
    )(*arrays)


def attend(part, rows, pad, own, from_core, from_left, from_right, inv, cos, sin, lens, keys, values):
    slots = keys.shape[1]
    heads = part[1]
    vmem = pl.BlockSpec(memory_space=pltpu.VMEM)
    return pl.pallas_call(
        functools.partial(attend_kernel, part, rows, pad),
        in_specs=[vmem] * 10,
        out_specs=vmem,
        out_shape=jax.ShapeDtypeStruct((1, pad, heads * GROUP * HD), BF),
        scratch_shapes=[
            pltpu.VMEM((heads, rows * GROUP, slots), F32),
            pltpu.VMEM((heads, rows * GROUP, HD), F32),
        ],
        compiler_params=pltpu.CompilerParams(vmem_limit_bytes=12 * MIB),
        cost_estimate=pl.CostEstimate(flops=1, bytes_accessed=1, transcendentals=0),
        name="attend_part",
    )(own, from_core, from_left, from_right, inv, cos, sin, lens, keys, values)


def out_kernel(has_prior, *refs):
    outs, a_ref = refs[-3:-1], refs[-1]
    priors = refs[-5:-3] if has_prior else (None, None)
    blocks = refs[: -7 if has_prior else -5]
    weights = refs[len(blocks) : len(blocks) + 2]
    pad = blocks[0].shape[1]
    for b, block in enumerate(blocks):
        a_ref[b * pad : (b + 1) * pad] = block[0].astype(F32)
    left = a_ref[...].astype(BF)
    for w_ref, prior_ref, out_ref in zip(weights, priors, outs):
        prod = jnp.dot(left, w_ref[...], preferred_element_type=F32)
        out_ref[...] = prod + prior_ref[...] if has_prior else prod


def project_out(pad, blocks, weights, prior):
    count = len(blocks)
    depth, cols = weights[0].shape
    vmem = pl.BlockSpec(memory_space=pltpu.VMEM)
    args = [*blocks, *weights] + ([] if prior is None else list(prior))
    return pl.pallas_call(
        functools.partial(out_kernel, prior is not None),
        in_specs=[vmem] * len(args),
        out_specs=[vmem] * 2,
        scratch_shapes=[pltpu.VMEM((count * pad, depth), F32)],
        out_shape=[jax.ShapeDtypeStruct((count * pad, cols), F32)] * 2,
        compiler_params=pltpu.CompilerParams(vmem_limit_bytes=12 * MIB),
        cost_estimate=pl.CostEstimate(flops=1, bytes_accessed=1, transcendentals=0),
        name="out_part",
    )(*args)


def finish_kernel(order, rows, pad, x_ref, mine_ref, other_ref, out_ref):
    pick = picker(order, gathered_slots(len(order)), rows, pad, x_ref.shape[0])
    features = jnp.dot(pick, x_ref[...], preferred_element_type=F32)
    result = (features + jnp.concatenate([mine_ref[...], other_ref[...]], axis=0)).astype(BF)
    out_ref[...] = lax.dot_general(pick, result, (((0,), (0,)), ((), ())), preferred_element_type=F32).astype(BF)


def finish(order, rows, pad, x, mine, other):
    vmem = pl.BlockSpec(memory_space=pltpu.VMEM)
    return pl.pallas_call(
        functools.partial(finish_kernel, order, rows, pad),
        in_specs=[vmem] * 3,
        out_specs=vmem,
        out_shape=jax.ShapeDtypeStruct(x.shape, BF),
        compiler_params=pltpu.CompilerParams(vmem_limit_bytes=16 * MIB),
        cost_estimate=pl.CostEstimate(flops=1, bytes_accessed=1, transcendentals=0),
        name="finish",
    )(x, mine, other)


def wide(a):
    return a.astype(F32)


def issue_order(steps):
    names = ["P0", "P1"] + ["R0", "R1"] * steps
    names += ["T0", "G0", "T1", "G1"] + ["G0", "G1"] * (steps - 2) + ["G0", "L0", "G1", "O0", "L1", "O1"]
    return names


def per_device(order, hidden_in, norm_gain, w_qkv, w_out, cache_keys, cache_values, lengths):
    rows = cache_keys.shape[0]
    pad = -(-rows // 8) * 8
    chips = len(order)
    up_pairs = [(order[p] * 2 + c, order[(p + 1) % chips] * 2 + c) for p in range(chips) for c in range(2)]
    down_pairs = [(b, a) for a, b in up_pairs]
    sibling = [(i, i ^ 1) for i in range(2 * chips)]
    before = [None]

    def after(a, *others):
        return lax.optimization_barrier((a,) + others)[0]

    def ring(sent):
        before[0] = tuple(sent.values())
        return {way: lax.ppermute(a, "gx", up_pairs if way == "up" else down_pairs) for way, a in sent.items()}

    def tied(a):
        return after(a, before[0])

    def cross(a):
        return lax.ppermute(a, "gx", sibling)

    angles = HD // 2
    inverse = 500000.0 ** (-(jnp.arange(angles, dtype=F32) * 2.0 / HD))
    angle = jnp.pad(lengths, (0, pad - rows)).astype(F32)[:, None] * inverse[None, :]
    cos = jnp.cos(angle)
    sin = jnp.sin(angle)
    cos = jnp.concatenate([cos, cos], axis=1)
    sin = jnp.concatenate([-sin, sin], axis=1)
    lens = jnp.repeat(lengths, GROUP)[:, None]

    gain = norm_gain[None, :]
    inv, w_other, caches, sums = [None], [None], [None], [None]

    def part_steps(index):
        part = PARTS[index]
        ways = dict(zip(("up", "down"), hops(index, chips)))
        steps = max(ways.values())
        sign = {"up": 1, "down": -1}
        ks = [k for k, w in sent_slots(index, chips) if w == 0]
        x = hidden_in if index == 0 else tied(hidden_in)
        keep, first, rest = project(order, index, rows, pad, x, gain, w_qkv)
        before[0] = keep
        got_first = cross(first)
        got_rest = cross(rest)
        yield

        def piece(k):
            at = ks.index(k % chips)
            return keep[at : at + 1], got_first[at : at + 1] if at < 2 else got_rest[at - 2 : at - 1]

        moved = {}
        for step in range(steps):
            sent = {}
            for way, far in ways.items():
                if step < far:
                    here, there = piece(sign[way] * (far - step))
                    total = wide(here) + wide(there)
                    sent[way] = (total + wide(tied(moved[way])) if step else wide(tied(here)) + wide(there)).astype(BF)
            moved = {**moved, **ring(sent)}
            if index == len(PARTS) - 1 and step == 0:
                w_other[0] = cross(tied(w_out))
            if index == len(PARTS) - 1 and step == 1:
                caches[0] = load("load_caches", 40, tied((cache_keys, cache_values)))
                before[0] = caches[0]
            yield
        own, from_core = piece(0)
        if index == 0:
            lanes = slice((GROUP + 2) * part[1] * HD, None)
            parts = [own, from_core, moved["up"], moved["down"]]
            square = jnp.sum(sum(wide(a[0, :, lanes]) for a in parts), axis=1)
            inv[0] = jnp.broadcast_to(lax.rsqrt(square / D + 1e-05)[:, None], (pad, HD))
        own = tied(own)
        if index == len(PARTS) - 1:
            own = after(own, w_other[0])
        attended = attend(part, rows, pad, own, from_core, moved["up"], moved["down"], inv[0], cos, sin, lens, *caches[0])
        before[0] = attended
        yield
        blocks = {0: attended}
        for step in range(steps):
            sent = {way: tied(blocks[-sign[way] * step % chips]) for way, far in ways.items() if step < far}
            for way, a in ring(sent).items():
                blocks[-sign[way] * (step + 1) % chips] = a
            yield
        weights = load("load_weights", 40, (tied(w_out), w_other[0]), part[0] * GROUP * HD, part[1] * GROUP * HD)
        yield
        sums[0] = project_out(pad, [blocks[k] for k in range(chips)], weights, sums[0])
        if index < len(PARTS) - 1:
            before[0] = sums[0]
        yield

    running = [part_steps(i) for i in range(len(PARTS))]
    for name in issue_order(chips // 2):
        next(running[int(name[-1])])
    mine, theirs = sums[0]
    return finish(order, rows, pad, hidden_in, mine, cross(theirs))


def solution(mesh):
    in_specs = (
        P("groups", "gx"),
        P("gx"),
        P("gx", None),
        P(None, "gx"),
        P(("groups", "gx"), None, None),
        P(("groups", "gx"), None, None),
        P(("groups", "gx")),
    )
    out_specs = P("groups", "gx")
    return jax.shard_map(
        functools.partial(per_device, chip_cycle(mesh)), mesh=mesh, in_specs=in_specs, out_specs=out_specs, check_vma=False
    )
```

time: 240 us -> 115 us (0.48)
  blocking collectives: 119 us -> 0 us
  Pallas kernels: 0 us -> 36.3 us
  waiting for transfers between devices: 59.3 us -> 25.8 us
  starting transfers between devices: 6.55 us -> 35.3 us
  matrix products: 25.2 us -> 0 us
  between operations: 14.3 us -> 0.24 us
  other arithmetic: 1.73 us -> 11.8 us
  local copies, waits for them, and re-layouts: 13.8 us -> 5.41 us
    unnamed x1 -> x0, blocking collectives: 88.3 us -> none
    all_gather x1 -> x0, waiting for transfers between devices: 59.2 us -> none  [per_device(): lax.all_gather(attended, 'gx', axis=0, tiled=True)]
    pallas_call x0 -> x10, Pallas kernels: none -> 36.3 us  [the longest x2 14.2 us: project(): pl.pallas_call(functools.partial(qkv_kernel, order, index, rows, pad), in...]
    ppermute x0 -> x34, starting transfers between devices: none -> 35.3 us  [the longest x28 33.5 us: ring(): lax.ppermute(a, 'gx', up_pairs if way == 'up' else down_pairs)]
    psum x1 -> x0, blocking collectives: 30.3 us -> none  [per_device(): square_all = lax.psum(square_part, 'gx')]
    ppermute x0 -> x34, waiting for transfers between devices: none -> 25.8 us  [the longest x28 24.1 us: ring(): lax.ppermute(a, 'gx', up_pairs if way == 'up' else down_pairs)]
    dot_general x5 -> x0, matrix products: 25.2 us -> none  [the longest x1 11 us: per_device(): jnp.dot(scaled, w_qkv, preferred_element_type=jnp.float32)]
    unnamed x24 -> x8, local copies, waits for them, and re-layouts: 13.7 us -> 0.37 us
  transfers between devices with their start and end apart: 3 -> 34, of which waited for: 1 -> 11; matrix products, arithmetic and copies ran while one was open for 0% -> 15% of each run, Pallas kernels for 0% -> 22%
where the time goes in v2:
time: 115 us
  Pallas kernels  36.3 us (32%)
  starting transfers between devices  35.3 us (31%)
  waiting for transfers between devices  25.8 us (22%)
  other arithmetic  11.8 us (10%)
  local copies, waits for them, and re-layouts  5.41 us (5%)
    ppermute x28, starting transfers between devices, ring(): lax.ppermute(a, 'gx', up_pairs if way == 'up' else down_pairs)  33.5 us
    ppermute x28, waiting for transfers between devices, ring(): lax.ppermute(a, 'gx', up_pairs if way == 'up' else down_pairs)  24.1 us
    pallas_call x2, Pallas kernels, project(): pl.pallas_call(functools.partial(qkv_kernel, order, index, rows, pad), in...  14.2 us
    pallas_call x3, Pallas kernels, load(): pl.pallas_call(kernel, in_specs=[pl.BlockSpec(memory_space=pltpu.HBM)] *...  11.3 us
    convert_element_type x8, other arithmetic, part_steps(): (total + wide(tied(moved[way])) if step else wide(tied(here)) + wide(ther...  10.7 us
    pallas_call x2, Pallas kernels, attend(): pl.pallas_call(functools.partial(attend_kernel, part, rows, pad), in_spec...  5.82 us
    pallas_call x2, Pallas kernels, project_out(): pl.pallas_call(functools.partial(out_kernel, prior is not None), in_specs...  3.59 us
    slice x2, local copies, waits for them, and re-layouts, piece(): keep[at:at + 1]  2.88 us
  transfers between devices with their start and end apart: 34, of which 11 were waited for; matrix products, arithmetic and copies ran while one was open for 15% of the time, Pallas kernels for 22%

profile of v2, /device:TPU:0, one launch (start us, length us, event | category | flops | bytes accessed | tf_op | source)
XLA Modules:
  0.0 114.8 jit_solution(5995794828039451165)
XLA Ops:
  0.0 8.0 %qkv_part.2 = (bf16[8,24,5248]{2,1,0:T(8,128)(2,1)}, bf16[2,24,5248]{2,1,0:T(8,128)(2,1)}, bf16[6,24,5248]{2,1,0:T(8,128)(2,1)}) custom-call(bf16[352,512]{1,0:T(8,128)(2,1)} %x_ref.4, f32[1,512]{1,0:T(1,128)} %bitcast.1, bf16[512,10240]{1,0:T(8,128)(2,1)} %w_ref.3), custom_call_target="tpu_custom_call" | custom-call | flops 1 | bytes 1 | tf_op jit(solution)/shard_map/qkv_part/pallas_call | solution.py:139
  8.5 6.2 %qkv_part.3 = (bf16[8,24,5120]{2,1,0:T(8,128)(2,1)S(1)}, bf16[2,24,5120]{2,1,0:T(8,128)(2,1)S(1)}, bf16[6,24,5120]{2,1,0:T(8,128)(2,1)}) custom-call(bf16[352,512]{1,0:T(8,128)(2,1)S(1)} %copy-done, f32[1,512]{1,0:T(1,128)S(1)} %bitcast.2, bf16[512,10240]{1,0:T(8,128)(2,1)} %w_ref.3), custom_call_target="tpu_custom_call" | custom-call | flops 1 | bytes 1 | tf_op jit(solution)/shard_map/qkv_part/pallas_call | solution.py:139
  15.4 2.0 %fusion.1 = (bf16[1,24,5248]{2,1,0:T(8,128)(2,1)}, bf16[1,24,5248]{2,1,0:T(8,128)(2,1)}, bf16[1,24,5248]{2,1,0:T(8,128)(2,1)S(1)}) fusion(bf16[8,24,5248]{2,1,0:T(8,128)(2,1)} %get-tuple-element.56), kind=kLoop, calls=%fused_computation.23 | loop fusion | bytes 1511424 | tf_op jit(solution)/shard_map/slice | solution.py:377
  17.4 0.9 fusion.2
  18.5 1.4 %add_convert_fusion.5 = (bf16[1,24,5248]{2,1,0:T(8,128)(2,1)S(1)}, bf16[1,24,5248]{2,1,0:T(8,128)(2,1)S(1)}) fusion(bf16[1,24,5248]{2,1,0:T(8,128)(2,1)} %get-tuple-element.62, bf16[2,24,5248]{2,1,0:T(8,128)(2,1)} %collective-permute-done.1, bf16[1,24,5248]{2,1,0:T(8,128)(2,1)} %get-tuple-element.60), kind=kLoop, calls=%fused_computation.5 | loop fusion | flops 1007616 | bytes 1511424 | tf_op jit(solution)/shard_map/convert_element_type | solution.py:386
  19.9 1.4 %add_convert_fusion.12 = (bf16[1,24,5120]{2,1,0:T(8,128)(2,1)S(1)}, bf16[1,24,5120]{2,1,0:T(8,128)(2,1)S(1)}) fusion(bf16[1,24,5120]{2,1,0:T(8,128)(2,1)} %get-tuple-element.66, bf16[2,24,5120]{2,1,0:T(8,128)(2,1)} %collective-permute-done.2, bf16[1,24,5120]{2,1,0:T(8,128)(2,1)} %get-tuple-element.63), kind=kLoop, calls=%fused_computation.12 | loop fusion | flops 983040 | bytes 1474560 | tf_op jit(solution)/shard_map/convert_element_type | solution.py:386
  21.9 2.7 %collective-permute-start.6 = (bf16[1,24,5248]{2,1,0:T(8,128)(2,1)S(1)}, bf16[1,24,5248]{2,1,0:T(8,128)(2,1)S(1)}, u32[]{:S(2)}, u32[]{:S(2)}) collective-permute-start(bf16[1,24,5248]{2,1,0:T(8,128)(2,1)S(1)} %get-tuple-element.121), channel_id=1, source_target_pairs={{2,0},{3,1},{6,2},{7,3},{10,6},{11,7},{14,10},{15,11},{12,14},{13,... | collective-permute-start | bytes 755720 | tf_op jit(solution)/shard_map/ppermute | solution.py:342
  24.7 6.4 %collective-permute-done.6 = bf16[1,24,5248]{2,1,0:T(8,128)(2,1)S(1)} collective-permute-done((bf16[1,24,5248]{2,1,0:T(8,128)(2,1)S(1)}, bf16[1,24,5248]{2,1,0:T(8,128)(2,1)S(1)}, u32[]{:S(2)}, u32[]{:S(2)}) %collective-permute-start.6) | collective-permute-done | bytes 251936 | tf_op jit(solution)/shard_map/ppermute | solution.py:342
  31.1 1.8 %collective-permute-start.9 = (bf16[1,24,5120]{2,1,0:T(8,128)(2,1)S(1)}, bf16[1,24,5120]{2,1,0:T(8,128)(2,1)S(1)}, u32[]{:S(2)}, u32[]{:S(2)}) collective-permute-start(bf16[1,24,5120]{2,1,0:T(8,128)(2,1)S(1)} %get-tuple-element.123), channel_id=1, source_target_pairs={{0,2},{1,3},{2,6},{3,7},{6,10},{7,11},{10,14},{11,15},{14,12},{15,... | collective-permute-start | bytes 737288 | tf_op jit(solution)/shard_map/ppermute | solution.py:342
  32.9 1.3 %collective-permute-start.3 = (bf16[1,24,5120]{2,1,0:T(8,128)(2,1)S(1)}, bf16[1,24,5120]{2,1,0:T(8,128)(2,1)S(1)}, u32[]{:S(2)}, u32[]{:S(2)}) collective-permute-start(bf16[1,24,5120]{2,1,0:T(8,128)(2,1)S(1)} %get-tuple-element.124), channel_id=1, source_target_pairs={{2,0},{3,1},{6,2},{7,3},{10,6},{11,7},{14,10},{15,11},{12,14},{13,... | collective-permute-start | bytes 737288 | tf_op jit(solution)/shard_map/ppermute | solution.py:342
  34.2 1.0 slice.164.core_ref
  35.2 1.5 %add_convert_fusion.3 = (bf16[1,24,5248]{2,1,0:T(8,128)(2,1)S(1)}, bf16[1,24,5248]{2,1,0:T(8,128)(2,1)S(1)}) fusion(bf16[1,24,5248]{2,1,0:T(8,128)(2,1)S(1)} %collective-permute-done.6, bf16[6,24,5248]{2,1,0:T(8,128)(2,1)} %collective-permute-done.4, bf16[8,24,5248]{2,1,0:T(8,128)(2,1)} %get-tuple-element.56, bf16[1,24,5248]{2,1,0:T(8,128)(2,1)S(1)} %collective-permute-done.5), kind=kLoop, calls=%fused_computation.3 | loop fusion | flops 1511424 | bytes 2015232 | tf_op jit(solution)/shard_map/convert_element_type | solution.py:386
  36.7 1.6 %collective-permute-start.10 = (bf16[1,24,5248]{2,1,0:T(8,128)(2,1)S(1)}, bf16[1,24,5248]{2,1,0:T(8,128)(2,1)S(1)}, u32[]{:S(2)}, u32[]{:S(2)}) collective-permute-start(bf16[1,24,5248]{2,1,0:T(8,128)(2,1)S(1)} %get-tuple-element.109), channel_id=1, source_target_pairs={{2,0},{3,1},{6,2},{7,3},{10,6},{11,7},{14,10},{15,11},{12,14},{13,... | collective-permute-start | bytes 755720 | tf_op jit(solution)/shard_map/ppermute | solution.py:342
  38.8 2.9 %collective-permute-done.3 = bf16[1,24,5120]{2,1,0:T(8,128)(2,1)S(1)} collective-permute-done((bf16[1,24,5120]{2,1,0:T(8,128)(2,1)S(1)}, bf16[1,24,5120]{2,1,0:T(8,128)(2,1)S(1)}, u32[]{:S(2)}, u32[]{:S(2)}) %collective-permute-start.3) | collective-permute-done | bytes 245792 | tf_op jit(solution)/shard_map/ppermute | solution.py:342
  41.8 1.2 %add_convert_fusion.10 = (bf16[1,24,5120]{2,1,0:T(8,128)(2,1)S(1)}, bf16[1,24,5120]{2,1,0:T(8,128)(2,1)S(1)}) fusion(bf16[1,24,5120]{2,1,0:T(8,128)(2,1)S(1)} %collective-permute-done.9, bf16[6,24,5120]{2,1,0:T(8,128)(2,1)} %collective-permute-done, bf16[8,24,5120]{2,1,0:T(8,128)(2,1)S(1)} %get-tuple-element.58, ...), kind=kLoop, calls=%fused_computation.10 | loop fusion | flops 1474560 | bytes 1966080 | tf_op jit(solution)/shard_map/convert_element_type | solution.py:386
  43.0 1.6 %collective-permute-start.13 = (bf16[1,24,5120]{2,1,0:T(8,128)(2,1)S(1)}, bf16[1,24,5120]{2,1,0:T(8,128)(2,1)S(1)}, u32[]{:S(2)}, u32[]{:S(2)}) collective-permute-start(bf16[1,24,5120]{2,1,0:T(8,128)(2,1)S(1)} %get-tuple-element.113), channel_id=1, source_target_pairs={{0,2},{1,3},{2,6},{3,7},{6,10},{7,11},{10,14},{11,15},{14,12},{15,... | collective-permute-start | bytes 737288 | tf_op jit(solution)/shard_map/ppermute | solution.py:342
  45.1 4.3 %load_caches.1 = (bf16[22,128,1024]{2,1,0:T(8,128)(2,1)S(1)}, bf16[22,128,1024]{2,1,0:T(8,128)(2,1)S(1)}) custom-call(bf16[22,128,1024]{2,1,0:T(8,128)(2,1)} %refs_0_, bf16[22,128,1024]{2,1,0:T(8,128)(2,1)} %refs_1_), custom_call_target="tpu_custom_call" | custom-call | flops 1 | bytes 1 | tf_op jit(solution)/shard_map/load_caches/pallas_call | solution.py:236
  49.5 1.0 slice.160.core_ref
  50.4 1.5 %add_convert_fusion.1 = (bf16[1,24,5248]{2,1,0:T(8,128)(2,1)S(1)}, bf16[1,24,5248]{2,1,0:T(8,128)(2,1)S(1)}) fusion(bf16[1,24,5248]{2,1,0:T(8,128)(2,1)S(1)} %collective-permute-done.10, bf16[6,24,5248]{2,1,0:T(8,128)(2,1)} %collective-permute-done.4, bf16[8,24,5248]{2,1,0:T(8,128)(2,1)} %get-tuple-element.56, bf16[1,24,5248]{2,1,0:T(8,128)(2,1)S(1)} %collective-permute-done.8), kind=kLoop, calls=%fused_computation.1 | loop fusion | flops 1511424 | bytes 2015232 | tf_op jit(solution)/shard_map/convert_element_type | solution.py:386
  52.0 1.6 %collective-permute-start.12 = (bf16[1,24,5248]{2,1,0:T(8,128)(2,1)S(1)}, bf16[1,24,5248]{2,1,0:T(8,128)(2,1)S(1)}, u32[]{:S(2)}, u32[]{:S(2)}) collective-permute-start(bf16[1,24,5248]{2,1,0:T(8,128)(2,1)S(1)} %get-tuple-element.108), channel_id=1, source_target_pairs={{0,2},{1,3},{2,6},{3,7},{6,10},{7,11},{10,14},{11,15},{14,12},{15,... | collective-permute-start | bytes 755720 | tf_op jit(solution)/shard_map/ppermute | solution.py:342
  54.1 1.4 %add_convert_fusion.8 = (bf16[1,24,5120]{2,1,0:T(8,128)(2,1)S(1)}, bf16[1,24,5120]{2,1,0:T(8,128)(2,1)S(1)}) fusion(bf16[1,24,5120]{2,1,0:T(8,128)(2,1)S(1)} %collective-permute-done.13, bf16[6,24,5120]{2,1,0:T(8,128)(2,1)} %collective-permute-done, bf16[8,24,5120]{2,1,0:T(8,128)(2,1)S(1)} %get-tuple-element.58, bf16[1,24,5120]{2,1,0:T(8,128)(2,1)} %collective-permute-done.7), kind=kLoop, calls=%fused_computation.8 | loop fusion | flops 1474560 | bytes 1966080 | tf_op jit(solution)/shard_map/convert_element_type | solution.py:386
  55.4 1.1 collective-permute-start.11
  56.5 1.0 collective-permute-start.17
  57.5 3.5 %collective-permute-done.12 = bf16[1,24,5248]{2,1,0:T(8,128)(2,1)S(1)} collective-permute-done((bf16[1,24,5248]{2,1,0:T(8,128)(2,1)S(1)}, bf16[1,24,5248]{2,1,0:T(8,128)(2,1)S(1)}, u32[]{:S(2)}, u32[]{:S(2)}) %collective-permute-start.12) | collective-permute-done | bytes 251936 | tf_op jit(solution)/shard_map/ppermute | solution.py:342
  61.0 1.2 %add_convert_fusion = bf16[1,24,5248]{2,1,0:T(8,128)(2,1)S(1)} fusion(bf16[1,24,5248]{2,1,0:T(8,128)(2,1)S(1)} %collective-permute-done.12, bf16[6,24,5248]{2,1,0:T(8,128)(2,1)} %collective-permute-done.4, bf16[8,24,5248]{2,1,0:T(8,128)(2,1)} %get-tuple-element.56), kind=kLoop, calls=%fused_computation | loop fusion | flops 755712 | bytes 1007616 | tf_op jit(solution)/shard_map/convert_element_type | solution.py:386
  62.1 1.7 %collective-permute-start.14 = (bf16[1,24,5248]{2,1,0:T(8,128)(2,1)S(1)}, bf16[1,24,5248]{2,1,0:T(8,128)(2,1)S(1)}, u32[]{:S(2)}, u32[]{:S(2)}) collective-permute-start(bf16[1,24,5248]{2,1,0:T(8,128)(2,1)S(1)} %add_convert_fusion), channel_id=1, source_target_pairs={{0,2},{1,3},{2,6},{3,7},{6,10},{7,11},{10,14},{11,15},{14,12},{15,... | collective-permute-start | bytes 755720 | tf_op jit(solution)/shard_map/ppermute | solution.py:342
  64.0 1.0 add_convert_fusion.7
  65.6 2.9 %collective-permute-done.14.left_ref = bf16[1,24,5248]{2,1,0:T(8,128)(2,1)S(1)} collective-permute-done((bf16[1,24,5248]{2,1,0:T(8,128)(2,1)S(1)}, bf16[1,24,5248]{2,1,0:T(8,128)(2,1)S(1)}, u32[]{:S(2)}, u32[]{:S(2)}) %collective-permute-start.14) | collective-permute-done | bytes 251936 | tf_op jit(solution)/shard_map/ppermute | solution.py:342
  69.4 2.9 %attend_part.2.refs_0_ = bf16[1,24,4096]{2,1,0:T(8,128)(2,1)S(1)} custom-call(bf16[1,24,5248]{2,1,0:T(8,128)(2,1)S(1)} %get-tuple-element.81.own_ref, bf16[1,24,5248]{2,1,0:T(8,128)(2,1)S(1)} %slice.160.core_ref, bf16[1,24,5248]{2,1,0:T(8,128)(2,1)S(1)} %collective-permute-done.14.left_ref, bf16[1,24,5248]{2,1,0:T(8,128)(2,1)S(1)} %collective-permute-done.15.right_ref, ...), custom_call_target="tpu_custom_call" | custom-call | flops 1 | bytes 1 | tf_op jit(solution)/shard_map/attend_part/pallas_call | solution.py:252
  72.3 1.7 %collective-permute-start.20 = (bf16[1,24,4096]{2,1,0:T(8,128)(2,1)S(1)}, bf16[1,24,4096]{2,1,0:T(8,128)(2,1)S(1)}, u32[]{:S(2)}, u32[]{:S(2)}) collective-permute-start(bf16[1,24,4096]{2,1,0:T(8,128)(2,1)S(1)} %attend_part.2.refs_0_), channel_id=1, source_target_pairs={{0,2},{1,3},{2,6},{3,7},{6,10},{7,11},{10,14},{11,15},{14,12},{15,... | collective-permute-start | bytes 589832 | tf_op jit(solution)/shard_map/ppermute | solution.py:342
  74.4 2.9 %attend_part.3.refs_0_ = bf16[1,24,4096]{2,1,0:T(8,128)(2,1)S(1)} custom-call(bf16[1,24,5120]{2,1,0:T(8,128)(2,1)S(1)} %get-tuple-element.85.own_ref, bf16[1,24,5120]{2,1,0:T(8,128)(2,1)S(1)} %slice.164.core_ref, bf16[1,24,5120]{2,1,0:T(8,128)(2,1)S(1)} %collective-permute-done.17.left_ref, bf16[1,24,5120]{2,1,0:T(8,128)(2,1)S(1)} %collective-permute-done.18.right_ref, ...), custom_call_target="tpu_custom_call" | custom-call | flops 1 | bytes 1 | tf_op jit(solution)/shard_map/attend_part/pallas_call | solution.py:252
  77.6 1.2 %collective-permute-start.19 = (bf16[1,24,4096]{2,1,0:T(8,128)(2,1)S(1)}, bf16[1,24,4096]{2,1,0:T(8,128)(2,1)S(1)}, u32[]{:S(2)}, u32[]{:S(2)}) collective-permute-start(bf16[1,24,4096]{2,1,0:T(8,128)(2,1)S(1)} %attend_part.3.refs_0_), channel_id=1, source_target_pairs={{2,0},{3,1},{6,2},{7,3},{10,6},{11,7},{14,10},{15,11},{12,14},{13,... | collective-permute-start | bytes 589832 | tf_op jit(solution)/shard_map/ppermute | solution.py:342
  79.7 1.7 %collective-permute-start.23 = (bf16[1,24,4096]{2,1,0:T(8,128)(2,1)S(1)}, bf16[1,24,4096]{2,1,0:T(8,128)(2,1)S(1)}, u32[]{:S(2)}, u32[]{:S(2)}) collective-permute-start(bf16[1,24,4096]{2,1,0:T(8,128)(2,1)S(1)} %collective-permute-done.20.refs_7_), channel_id=1, source_target_pairs={{0,2},{1,3},{2,6},{3,7},{6,10},{7,11},{10,14},{11,15},{14,12},{15,... | collective-permute-start | bytes 589832 | tf_op jit(solution)/shard_map/ppermute | solution.py:342
  82.0 4.0 %collective-permute-done.19.refs_1_ = bf16[1,24,4096]{2,1,0:T(8,128)(2,1)S(1)} collective-permute-done((bf16[1,24,4096]{2,1,0:T(8,128)(2,1)S(1)}, bf16[1,24,4096]{2,1,0:T(8,128)(2,1)S(1)}, u32[]{:S(2)}, u32[]{:S(2)}) %collective-permute-start.19) | collective-permute-done | bytes 196640 | tf_op jit(solution)/shard_map/ppermute | solution.py:342
  86.7 1.3 %collective-permute-start.28 = (bf16[1,24,4096]{2,1,0:T(8,128)(2,1)S(1)}, bf16[1,24,4096]{2,1,0:T(8,128)(2,1)S(1)}, u32[]{:S(2)}, u32[]{:S(2)}) collective-permute-start(bf16[1,24,4096]{2,1,0:T(8,128)(2,1)S(1)} %collective-permute-done.24.refs_7_), channel_id=1, source_target_pairs={{0,2},{1,3},{2,6},{3,7},{6,10},{7,11},{10,14},{11,15},{14,12},{15,... | collective-permute-start | bytes 589832 | tf_op jit(solution)/shard_map/ppermute | solution.py:342
  88.0 0.9 collective-permute-done.23.refs_6_
  88.9 2.5 %collective-permute-start.27 = (bf16[1,24,4096]{2,1,0:T(8,128)(2,1)S(1)}, bf16[1,24,4096]{2,1,0:T(8,128)(2,1)S(1)}, u32[]{:S(2)}, u32[]{:S(2)}) collective-permute-start(bf16[1,24,4096]{2,1,0:T(8,128)(2,1)S(1)} %collective-permute-done.23.refs_6_), channel_id=1, source_target_pairs={{0,2},{1,3},{2,6},{3,7},{6,10},{7,11},{10,14},{11,15},{14,12},{15,... | collective-permute-start | bytes 589832 | tf_op jit(solution)/shard_map/ppermute | solution.py:342
  91.4 1.0 collective-permute-done.22.refs_2_
  92.7 1.4 %collective-permute-start.31 = (bf16[1,24,4096]{2,1,0:T(8,128)(2,1)S(1)}, bf16[1,24,4096]{2,1,0:T(8,128)(2,1)S(1)}, u32[]{:S(2)}, u32[]{:S(2)}) collective-permute-start(bf16[1,24,4096]{2,1,0:T(8,128)(2,1)S(1)} %collective-permute-done.25.refs_2_), channel_id=1, source_target_pairs={{2,0},{3,1},{6,2},{7,3},{10,6},{11,7},{14,10},{15,11},{12,14},{13,... | collective-permute-start | bytes 589832 | tf_op jit(solution)/shard_map/ppermute | solution.py:342
  94.1 1.9 %collective-permute-done.27.refs_5_ = bf16[1,24,4096]{2,1,0:T(8,128)(2,1)S(1)} collective-permute-done((bf16[1,24,4096]{2,1,0:T(8,128)(2,1)S(1)}, bf16[1,24,4096]{2,1,0:T(8,128)(2,1)S(1)}, u32[]{:S(2)}, u32[]{:S(2)}) %collective-permute-start.27) | collective-permute-done | bytes 196640 | tf_op jit(solution)/shard_map/ppermute | solution.py:342
  96.0 2.5 %collective-permute-start.32 = (bf16[1,24,4096]{2,1,0:T(8,128)(2,1)S(1)}, bf16[1,24,4096]{2,1,0:T(8,128)(2,1)S(1)}, u32[]{:S(2)}, u32[]{:S(2)}) collective-permute-start(bf16[1,24,4096]{2,1,0:T(8,128)(2,1)S(1)} %collective-permute-done.27.refs_5_), channel_id=1, source_target_pairs={{0,2},{1,3},{2,6},{3,7},{6,10},{7,11},{10,14},{11,15},{14,12},{15,... | collective-permute-start | bytes 589832 | tf_op jit(solution)/shard_map/ppermute | solution.py:342
  98.5 2.5 %collective-permute-start.30 = (bf16[1,24,4096]{2,1,0:T(8,128)(2,1)S(1)}, bf16[1,24,4096]{2,1,0:T(8,128)(2,1)S(1)}, u32[]{:S(2)}, u32[]{:S(2)}) collective-permute-start(bf16[1,24,4096]{2,1,0:T(8,128)(2,1)S(1)} %collective-permute-done.28.refs_6_), channel_id=1, source_target_pairs={{0,2},{1,3},{2,6},{3,7},{6,10},{7,11},{10,14},{11,15},{14,12},{15,... | collective-permute-start | bytes 589832 | tf_op jit(solution)/shard_map/ppermute | solution.py:342
  101.0 3.5 %load_weights.2 = (bf16[4096,512]{1,0:T(8,128)(2,1)S(1)}, bf16[4096,512]{1,0:T(8,128)(2,1)S(1)}) custom-call(bf16[8192,512]{1,0:T(8,128)(2,1)} %refs_0_.2, bf16[8192,512]{1,0:T(8,128)(2,1)} %copy-done.2), custom_call_target="tpu_custom_call" | custom-call | flops 1 | bytes 1 | tf_op jit(solution)/shard_map/load_weights/pallas_call | solution.py:236
  104.5 1.8 %out_part.2 = (f32[192,512]{1,0:T(8,128)S(1)}, f32[192,512]{1,0:T(8,128)S(1)}) custom-call(bf16[1,24,4096]{2,1,0:T(8,128)(2,1)S(1)} %attend_part.2.refs_0_, bf16[1,24,4096]{2,1,0:T(8,128)(2,1)S(1)} %collective-permute-done.21.refs_1_, bf16[1,24,4096]{2,1,0:T(8,128)(2,1)S(1)} %collective-permute-done.25.refs_2_, ...), custom_call_target="tpu_custom_call" | custom-call | flops 1 | bytes 1 | tf_op jit(solution)/shard_map/out_part/pallas_call | solution.py:286
  106.3 3.5 %load_weights.3 = (bf16[4096,512]{1,0:T(8,128)(2,1)S(1)}, bf16[4096,512]{1,0:T(8,128)(2,1)S(1)}) custom-call(bf16[8192,512]{1,0:T(8,128)(2,1)} %refs_0_.2, bf16[8192,512]{1,0:T(8,128)(2,1)} %copy-done.2), custom_call_target="tpu_custom_call" | custom-call | flops 1 | bytes 1 | tf_op jit(solution)/shard_map/load_weights/pallas_call | solution.py:236
  109.8 1.8 %out_part.3 = (f32[192,512]{1,0:T(8,128)S(1)}, f32[192,512]{1,0:T(8,128)S(1)}) custom-call(bf16[1,24,4096]{2,1,0:T(8,128)(2,1)S(1)} %attend_part.3.refs_0_, bf16[1,24,4096]{2,1,0:T(8,128)(2,1)S(1)} %collective-permute-done.19.refs_1_, bf16[1,24,4096]{2,1,0:T(8,128)(2,1)S(1)} %collective-permute-done.22.refs_2_, ...), custom_call_target="tpu_custom_call" | custom-call | flops 1 | bytes 1 | tf_op jit(solution)/shard_map/out_part/pallas_call | solution.py:286
  111.7 1.7 %collective-permute-done.33.other_ref = f32[192,512]{1,0:T(8,128)S(1)} collective-permute-done((f32[192,512]{1,0:T(8,128)S(1)}, f32[192,512]{1,0:T(8,128)S(1)}, u32[]{:S(2)}, u32[]{:S(2)}) %collective-permute-start.33) | collective-permute-done | bytes 393248 | tf_op jit(solution)/shard_map/ppermute | solution.py:348
  113.4 1.4 %finish.1 = bf16[352,512]{1,0:T(8,128)(2,1)} custom-call(bf16[352,512]{1,0:T(8,128)(2,1)S(1)} %copy-done, f32[192,512]{1,0:T(8,128)S(1)} %get-tuple-element.105.mine_ref, f32[192,512]{1,0:T(8,128)S(1)} %collective-permute-done.33.other_ref), custom_call_target="tpu_custom_call" | custom-call | flops 1 | bytes 1 | tf_op jit(solution)/shard_map/finish/pallas_call | solution.py:307
  (59 shorter events, 8.3 us)
Async XLA Ops:
  0.0 8.5 %copy-start = (bf16[352,512]{1,0:T(8,128)(2,1)S(1)}, bf16[352,512]{1,0:T(8,128)(2,1)}, u32[]{:S(2)}) copy-start(bf16[352,512]{1,0:T(8,128)(2,1)} %x_ref.4) | copy-start | bytes 1081348
  0.0 8.5 %copy-start.1 = (f32[512]{0:T(512)S(1)}, f32[512]{0:T(512)}, u32[]{:S(2)}) copy-start(f32[512]{0:T(512)} %param.8) | copy-start | bytes 6148
  8.0 10.5 %collective-permute-start.1 = (bf16[2,24,5248]{2,1,0:T(8,128)(2,1)}, bf16[2,24,5248]{2,1,0:T(8,128)(2,1)}, u32[]{:S(2)}, u32[]{:S(2)}) collective-permute-start(bf16[2,24,5248]{2,1,0:T(8,128)(2,1)} %get-tuple-element.61), channel_id=1, source_target_pairs={{0,1},{1,0},{2,3},{3,2},{4,5},{5,4},{6,7},{7,6},{8,9},{9,8},{10,11... | collective-permute-start | bytes 1511432 | tf_op jit(solution)/shard_map/ppermute | solution.py:348
  14.7 3.6 %copy-start.3 = (s32[22]{0:T(128)S(1)}, s32[22]{0:T(128)}, u32[]{:S(2)}) copy-start(s32[22]{0:T(128)} %param.13) | copy-start | bytes 268
  14.7 5.2 %collective-permute-start.2 = (bf16[2,24,5120]{2,1,0:T(8,128)(2,1)S(1)}, bf16[2,24,5120]{2,1,0:T(8,128)(2,1)}, u32[]{:S(2)}, u32[]{:S(2)}) collective-permute-start(bf16[2,24,5120]{2,1,0:T(8,128)(2,1)S(1)} %get-tuple-element.64), channel_id=1, source_target_pairs={{0,1},{1,0},{2,3},{3,2},{4,5},{5,4},{6,7},{7,6},{8,9},{9,8},{10,11... | collective-permute-start | bytes 1474568 | tf_op jit(solution)/shard_map/ppermute | solution.py:348
  14.9 20.3 %collective-permute-start.4 = (bf16[6,24,5248]{2,1,0:T(8,128)(2,1)}, bf16[6,24,5248]{2,1,0:T(8,128)(2,1)}, u32[]{:S(2)}, u32[]{:S(2)}) collective-permute-start(bf16[6,24,5248]{2,1,0:T(8,128)(2,1)} %get-tuple-element.65), channel_id=1, source_target_pairs={{0,1},{1,0},{2,3},{3,2},{4,5},{5,4},{6,7},{7,6},{8,9},{9,8},{10,11... | collective-permute-start | bytes 4534280 | tf_op jit(solution)/shard_map/ppermute | solution.py:348
  15.3 18.9 %collective-permute-start = (bf16[6,24,5120]{2,1,0:T(8,128)(2,1)}, bf16[6,24,5120]{2,1,0:T(8,128)(2,1)}, u32[]{:S(2)}, u32[]{:S(2)}) collective-permute-start(bf16[6,24,5120]{2,1,0:T(8,128)(2,1)} %get-tuple-element.59), channel_id=1, source_target_pairs={{0,1},{1,0},{2,3},{3,2},{4,5},{5,4},{6,7},{7,6},{8,9},{9,8},{10,11... | collective-permute-start | bytes 4423688 | tf_op jit(solution)/shard_map/ppermute | solution.py:348
  21.4 53.0 %collective-permute-start.16 = (bf16[8192,512]{1,0:T(8,128)(2,1)}, bf16[8192,512]{1,0:T(8,128)(2,1)S(1)}, u32[]{:S(2)}, u32[]{:S(2)}) collective-permute-start(bf16[8192,512]{1,0:T(8,128)(2,1)} %refs_0_.2), channel_id=1, source_target_pairs={{0,1},{1,0},{2,3},{3,2},{4,5},{5,4},{6,7},{7,6},{8,9},{9,8},{10,11... | collective-permute-start | bytes 25165832 | tf_op jit(solution)/shard_map/ppermute | solution.py:348
  21.9 9.3 %collective-permute-start.6 = (bf16[1,24,5248]{2,1,0:T(8,128)(2,1)S(1)}, bf16[1,24,5248]{2,1,0:T(8,128)(2,1)S(1)}, u32[]{:S(2)}, u32[]{:S(2)}) collective-permute-start(bf16[1,24,5248]{2,1,0:T(8,128)(2,1)S(1)} %get-tuple-element.121), channel_id=1, source_target_pairs={{2,0},{3,1},{6,2},{7,3},{10,6},{11,7},{14,10},{15,11},{12,14},{13,... | collective-permute-start | bytes 755720 | tf_op jit(solution)/shard_map/ppermute | solution.py:342
  24.5 8.4 %collective-permute-start.5 = (bf16[1,24,5248]{2,1,0:T(8,128)(2,1)S(1)}, bf16[1,24,5248]{2,1,0:T(8,128)(2,1)S(1)}, u32[]{:S(2)}, u32[]{:S(2)}) collective-permute-start(bf16[1,24,5248]{2,1,0:T(8,128)(2,1)S(1)} %get-tuple-element.122), channel_id=1, source_target_pairs={{0,2},{1,3},{2,6},{3,7},{6,10},{7,11},{10,14},{11,15},{14,12},{15,... | collective-permute-start | bytes 755720 | tf_op jit(solution)/shard_map/ppermute | solution.py:342
  31.1 7.7 %collective-permute-start.9 = (bf16[1,24,5120]{2,1,0:T(8,128)(2,1)S(1)}, bf16[1,24,5120]{2,1,0:T(8,128)(2,1)S(1)}, u32[]{:S(2)}, u32[]{:S(2)}) collective-permute-start(bf16[1,24,5120]{2,1,0:T(8,128)(2,1)S(1)} %get-tuple-element.123), channel_id=1, source_target_pairs={{0,2},{1,3},{2,6},{3,7},{6,10},{7,11},{10,14},{11,15},{14,12},{15,... | collective-permute-start | bytes 737288 | tf_op jit(solution)/shard_map/ppermute | solution.py:342
  32.9 8.9 %collective-permute-start.3 = (bf16[1,24,5120]{2,1,0:T(8,128)(2,1)S(1)}, bf16[1,24,5120]{2,1,0:T(8,128)(2,1)S(1)}, u32[]{:S(2)}, u32[]{:S(2)}) collective-permute-start(bf16[1,24,5120]{2,1,0:T(8,128)(2,1)S(1)} %get-tuple-element.124), channel_id=1, source_target_pairs={{2,0},{3,1},{6,2},{7,3},{10,6},{11,7},{14,10},{15,11},{12,14},{13,... | collective-permute-start | bytes 737288 | tf_op jit(solution)/shard_map/ppermute | solution.py:342
  36.7 13.7 %collective-permute-start.10 = (bf16[1,24,5248]{2,1,0:T(8,128)(2,1)S(1)}, bf16[1,24,5248]{2,1,0:T(8,128)(2,1)S(1)}, u32[]{:S(2)}, u32[]{:S(2)}) collective-permute-start(bf16[1,24,5248]{2,1,0:T(8,128)(2,1)S(1)} %get-tuple-element.109), channel_id=1, source_target_pairs={{2,0},{3,1},{6,2},{7,3},{10,6},{11,7},{14,10},{15,11},{12,14},{13,... | collective-permute-start | bytes 755720 | tf_op jit(solution)/shard_map/ppermute | solution.py:342
  38.3 12.1 %collective-permute-start.8 = (bf16[1,24,5248]{2,1,0:T(8,128)(2,1)S(1)}, bf16[1,24,5248]{2,1,0:T(8,128)(2,1)S(1)}, u32[]{:S(2)}, u32[]{:S(2)}) collective-permute-start(bf16[1,24,5248]{2,1,0:T(8,128)(2,1)S(1)} %get-tuple-element.110), channel_id=1, source_target_pairs={{0,2},{1,3},{2,6},{3,7},{6,10},{7,11},{10,14},{11,15},{14,12},{15,... | collective-permute-start | bytes 755720 | tf_op jit(solution)/shard_map/ppermute | solution.py:342
  43.0 11.0 %collective-permute-start.13 = (bf16[1,24,5120]{2,1,0:T(8,128)(2,1)S(1)}, bf16[1,24,5120]{2,1,0:T(8,128)(2,1)S(1)}, u32[]{:S(2)}, u32[]{:S(2)}) collective-permute-start(bf16[1,24,5120]{2,1,0:T(8,128)(2,1)S(1)} %get-tuple-element.113), channel_id=1, source_target_pairs={{0,2},{1,3},{2,6},{3,7},{6,10},{7,11},{10,14},{11,15},{14,12},{15,... | collective-permute-start | bytes 737288 | tf_op jit(solution)/shard_map/ppermute | solution.py:342
  44.7 9.4 %collective-permute-start.7 = (bf16[1,24,5120]{2,1,0:T(8,128)(2,1)S(1)}, bf16[1,24,5120]{2,1,0:T(8,128)(2,1)}, u32[]{:S(2)}, u32[]{:S(2)}) collective-permute-start(bf16[1,24,5120]{2,1,0:T(8,128)(2,1)S(1)} %get-tuple-element.114), channel_id=1, source_target_pairs={{2,0},{3,1},{6,2},{7,3},{10,6},{11,7},{14,10},{15,11},{12,14},{13,... | collective-permute-start | bytes 737288 | tf_op jit(solution)/shard_map/ppermute | solution.py:342
  52.0 9.0 %collective-permute-start.12 = (bf16[1,24,5248]{2,1,0:T(8,128)(2,1)S(1)}, bf16[1,24,5248]{2,1,0:T(8,128)(2,1)S(1)}, u32[]{:S(2)}, u32[]{:S(2)}) collective-permute-start(bf16[1,24,5248]{2,1,0:T(8,128)(2,1)S(1)} %get-tuple-element.108), channel_id=1, source_target_pairs={{0,2},{1,3},{2,6},{3,7},{6,10},{7,11},{10,14},{11,15},{14,12},{15,... | collective-permute-start | bytes 755720 | tf_op jit(solution)/shard_map/ppermute | solution.py:342
  53.6 12.0 %collective-permute-start.15 = (bf16[1,24,5248]{2,1,0:T(8,128)(2,1)S(1)}, bf16[1,24,5248]{2,1,0:T(8,128)(2,1)S(1)}, u32[]{:S(2)}, u32[]{:S(2)}) collective-permute-start(bf16[1,24,5248]{2,1,0:T(8,128)(2,1)S(1)} %get-tuple-element.107), channel_id=1, source_target_pairs={{2,0},{3,1},{6,2},{7,3},{10,6},{11,7},{14,10},{15,11},{12,14},{13,... | collective-permute-start | bytes 755720 | tf_op jit(solution)/shard_map/ppermute | solution.py:342
  55.4 8.6 %collective-permute-start.11 = (bf16[1,24,5120]{2,1,0:T(8,128)(2,1)S(1)}, bf16[1,24,5120]{2,1,0:T(8,128)(2,1)S(1)}, u32[]{:S(2)}, u32[]{:S(2)}) collective-permute-start(bf16[1,24,5120]{2,1,0:T(8,128)(2,1)S(1)} %get-tuple-element.112), channel_id=1, source_target_pairs={{2,0},{3,1},{6,2},{7,3},{10,6},{11,7},{14,10},{15,11},{12,14},{13,... | collective-permute-start | bytes 737288 | tf_op jit(solution)/shard_map/ppermute | solution.py:342
  56.5 17.9 %collective-permute-start.17 = (bf16[1,24,5120]{2,1,0:T(8,128)(2,1)S(1)}, bf16[1,24,5120]{2,1,0:T(8,128)(2,1)S(1)}, u32[]{:S(2)}, u32[]{:S(2)}) collective-permute-start(bf16[1,24,5120]{2,1,0:T(8,128)(2,1)S(1)} %get-tuple-element.111), channel_id=1, source_target_pairs={{0,2},{1,3},{2,6},{3,7},{6,10},{7,11},{10,14},{11,15},{14,12},{15,... | collective-permute-start | bytes 737288 | tf_op jit(solution)/shard_map/ppermute | solution.py:342
  62.1 6.3 %collective-permute-start.14 = (bf16[1,24,5248]{2,1,0:T(8,128)(2,1)S(1)}, bf16[1,24,5248]{2,1,0:T(8,128)(2,1)S(1)}, u32[]{:S(2)}, u32[]{:S(2)}) collective-permute-start(bf16[1,24,5248]{2,1,0:T(8,128)(2,1)S(1)} %add_convert_fusion), channel_id=1, source_target_pairs={{0,2},{1,3},{2,6},{3,7},{6,10},{7,11},{10,14},{11,15},{14,12},{15,... | collective-permute-start | bytes 755720 | tf_op jit(solution)/shard_map/ppermute | solution.py:342
  65.1 9.3 %collective-permute-start.18 = (bf16[1,24,5120]{2,1,0:T(8,128)(2,1)S(1)}, bf16[1,24,5120]{2,1,0:T(8,128)(2,1)S(1)}, u32[]{:S(2)}, u32[]{:S(2)}) collective-permute-start(bf16[1,24,5120]{2,1,0:T(8,128)(2,1)S(1)} %add_convert_fusion.7), channel_id=1, source_target_pairs={{2,0},{3,1},{6,2},{7,3},{10,6},{11,7},{14,10},{15,11},{12,14},{13,... | collective-permute-start | bytes 737288 | tf_op jit(solution)/shard_map/ppermute | solution.py:342
  72.3 7.4 %collective-permute-start.20 = (bf16[1,24,4096]{2,1,0:T(8,128)(2,1)S(1)}, bf16[1,24,4096]{2,1,0:T(8,128)(2,1)S(1)}, u32[]{:S(2)}, u32[]{:S(2)}) collective-permute-start(bf16[1,24,4096]{2,1,0:T(8,128)(2,1)S(1)} %attend_part.2.refs_0_), channel_id=1, source_target_pairs={{0,2},{1,3},{2,6},{3,7},{6,10},{7,11},{10,14},{11,15},{14,12},{15,... | collective-permute-start | bytes 589832 | tf_op jit(solution)/shard_map/ppermute | solution.py:342
  74.0 7.8 %collective-permute-start.21 = (bf16[1,24,4096]{2,1,0:T(8,128)(2,1)S(1)}, bf16[1,24,4096]{2,1,0:T(8,128)(2,1)S(1)}, u32[]{:S(2)}, u32[]{:S(2)}) collective-permute-start(bf16[1,24,4096]{2,1,0:T(8,128)(2,1)S(1)} %attend_part.2.refs_0_), channel_id=1, source_target_pairs={{2,0},{3,1},{6,2},{7,3},{10,6},{11,7},{14,10},{15,11},{12,14},{13,... | collective-permute-start | bytes 589832 | tf_op jit(solution)/shard_map/ppermute | solution.py:342
  74.3 3.3 %copy-start.2 = (bf16[8192,512]{1,0:T(8,128)(2,1)}, bf16[8192,512]{1,0:T(8,128)(2,1)S(1)}, u32[]{:S(2)}) copy-start(bf16[8192,512]{1,0:T(8,128)(2,1)S(1)} %collective-permute-done.16.refs_1_) | copy-start | bytes 25165828
  77.6 8.3 %collective-permute-start.19 = (bf16[1,24,4096]{2,1,0:T(8,128)(2,1)S(1)}, bf16[1,24,4096]{2,1,0:T(8,128)(2,1)S(1)}, u32[]{:S(2)}, u32[]{:S(2)}) collective-permute-start(bf16[1,24,4096]{2,1,0:T(8,128)(2,1)S(1)} %attend_part.3.refs_0_), channel_id=1, source_target_pairs={{2,0},{3,1},{6,2},{7,3},{10,6},{11,7},{14,10},{15,11},{12,14},{13,... | collective-permute-start | bytes 589832 | tf_op jit(solution)/shard_map/ppermute | solution.py:342
  78.9 7.8 %collective-permute-start.24 = (bf16[1,24,4096]{2,1,0:T(8,128)(2,1)S(1)}, bf16[1,24,4096]{2,1,0:T(8,128)(2,1)S(1)}, u32[]{:S(2)}, u32[]{:S(2)}) collective-permute-start(bf16[1,24,4096]{2,1,0:T(8,128)(2,1)S(1)} %attend_part.3.refs_0_), channel_id=1, source_target_pairs={{0,2},{1,3},{2,6},{3,7},{6,10},{7,11},{10,14},{11,15},{14,12},{15,... | collective-permute-start | bytes 589832 | tf_op jit(solution)/shard_map/ppermute | solution.py:342
  79.7 9.2 %collective-permute-start.23 = (bf16[1,24,4096]{2,1,0:T(8,128)(2,1)S(1)}, bf16[1,24,4096]{2,1,0:T(8,128)(2,1)S(1)}, u32[]{:S(2)}, u32[]{:S(2)}) collective-permute-start(bf16[1,24,4096]{2,1,0:T(8,128)(2,1)S(1)} %collective-permute-done.20.refs_7_), channel_id=1, source_target_pairs={{0,2},{1,3},{2,6},{3,7},{6,10},{7,11},{10,14},{11,15},{14,12},{15,... | collective-permute-start | bytes 589832 | tf_op jit(solution)/shard_map/ppermute | solution.py:342
  81.8 9.6 %collective-permute-start.25 = (bf16[1,24,4096]{2,1,0:T(8,128)(2,1)S(1)}, bf16[1,24,4096]{2,1,0:T(8,128)(2,1)S(1)}, u32[]{:S(2)}, u32[]{:S(2)}) collective-permute-start(bf16[1,24,4096]{2,1,0:T(8,128)(2,1)S(1)} %collective-permute-done.21.refs_1_), channel_id=1, source_target_pairs={{2,0},{3,1},{6,2},{7,3},{10,6},{11,7},{14,10},{15,11},{12,14},{13,... | collective-permute-start | bytes 589832 | tf_op jit(solution)/shard_map/ppermute | solution.py:342
  86.0 6.4 %collective-permute-start.22 = (bf16[1,24,4096]{2,1,0:T(8,128)(2,1)S(1)}, bf16[1,24,4096]{2,1,0:T(8,128)(2,1)S(1)}, u32[]{:S(2)}, u32[]{:S(2)}) collective-permute-start(bf16[1,24,4096]{2,1,0:T(8,128)(2,1)S(1)} %collective-permute-done.19.refs_1_), channel_id=1, source_target_pairs={{2,0},{3,1},{6,2},{7,3},{10,6},{11,7},{14,10},{15,11},{12,14},{13,... | collective-permute-start | bytes 589832 | tf_op jit(solution)/shard_map/ppermute | solution.py:342
  86.7 7.4 %collective-permute-start.28 = (bf16[1,24,4096]{2,1,0:T(8,128)(2,1)S(1)}, bf16[1,24,4096]{2,1,0:T(8,128)(2,1)S(1)}, u32[]{:S(2)}, u32[]{:S(2)}) collective-permute-start(bf16[1,24,4096]{2,1,0:T(8,128)(2,1)S(1)} %collective-permute-done.24.refs_7_), channel_id=1, source_target_pairs={{0,2},{1,3},{2,6},{3,7},{6,10},{7,11},{10,14},{11,15},{14,12},{15,... | collective-permute-start | bytes 589832 | tf_op jit(solution)/shard_map/ppermute | solution.py:342
  88.9 7.1 %collective-permute-start.27 = (bf16[1,24,4096]{2,1,0:T(8,128)(2,1)S(1)}, bf16[1,24,4096]{2,1,0:T(8,128)(2,1)S(1)}, u32[]{:S(2)}, u32[]{:S(2)}) collective-permute-start(bf16[1,24,4096]{2,1,0:T(8,128)(2,1)S(1)} %collective-permute-done.23.refs_6_), channel_id=1, source_target_pairs={{0,2},{1,3},{2,6},{3,7},{6,10},{7,11},{10,14},{11,15},{14,12},{15,... | collective-permute-start | bytes 589832 | tf_op jit(solution)/shard_map/ppermute | solution.py:342
  92.4 8.6 %collective-permute-start.26 = (bf16[1,24,4096]{2,1,0:T(8,128)(2,1)S(1)}, bf16[1,24,4096]{2,1,0:T(8,128)(2,1)S(1)}, u32[]{:S(2)}, u32[]{:S(2)}) collective-permute-start(bf16[1,24,4096]{2,1,0:T(8,128)(2,1)S(1)} %collective-permute-done.22.refs_2_), channel_id=1, source_target_pairs={{2,0},{3,1},{6,2},{7,3},{10,6},{11,7},{14,10},{15,11},{12,14},{13,... | collective-permute-start | bytes 589832 | tf_op jit(solution)/shard_map/ppermute | solution.py:342
  92.7 11.8 %collective-permute-start.31 = (bf16[1,24,4096]{2,1,0:T(8,128)(2,1)S(1)}, bf16[1,24,4096]{2,1,0:T(8,128)(2,1)S(1)}, u32[]{:S(2)}, u32[]{:S(2)}) collective-permute-start(bf16[1,24,4096]{2,1,0:T(8,128)(2,1)S(1)} %collective-permute-done.25.refs_2_), channel_id=1, source_target_pairs={{2,0},{3,1},{6,2},{7,3},{10,6},{11,7},{14,10},{15,11},{12,14},{13,... | collective-permute-start | bytes 589832 | tf_op jit(solution)/shard_map/ppermute | solution.py:342
  96.0 8.5 %collective-permute-start.32 = (bf16[1,24,4096]{2,1,0:T(8,128)(2,1)S(1)}, bf16[1,24,4096]{2,1,0:T(8,128)(2,1)S(1)}, u32[]{:S(2)}, u32[]{:S(2)}) collective-permute-start(bf16[1,24,4096]{2,1,0:T(8,128)(2,1)S(1)} %collective-permute-done.27.refs_5_), channel_id=1, source_target_pairs={{0,2},{1,3},{2,6},{3,7},{6,10},{7,11},{10,14},{11,15},{14,12},{15,... | collective-permute-start | bytes 589832 | tf_op jit(solution)/shard_map/ppermute | solution.py:342
  98.5 11.3 %collective-permute-start.30 = (bf16[1,24,4096]{2,1,0:T(8,128)(2,1)S(1)}, bf16[1,24,4096]{2,1,0:T(8,128)(2,1)S(1)}, u32[]{:S(2)}, u32[]{:S(2)}) collective-permute-start(bf16[1,24,4096]{2,1,0:T(8,128)(2,1)S(1)} %collective-permute-done.28.refs_6_), channel_id=1, source_target_pairs={{0,2},{1,3},{2,6},{3,7},{6,10},{7,11},{10,14},{11,15},{14,12},{15,... | collective-permute-start | bytes 589832 | tf_op jit(solution)/shard_map/ppermute | solution.py:342
  101.0 8.8 %collective-permute-start.29 = (bf16[1,24,4096]{2,1,0:T(8,128)(2,1)S(1)}, bf16[1,24,4096]{2,1,0:T(8,128)(2,1)S(1)}, u32[]{:S(2)}, u32[]{:S(2)}) collective-permute-start(bf16[1,24,4096]{2,1,0:T(8,128)(2,1)S(1)} %collective-permute-done.26.refs_3_), channel_id=1, source_target_pairs={{2,0},{3,1},{6,2},{7,3},{10,6},{11,7},{14,10},{15,11},{12,14},{13,... | collective-permute-start | bytes 589832 | tf_op jit(solution)/shard_map/ppermute | solution.py:342
  111.6 1.8 %collective-permute-start.33 = (f32[192,512]{1,0:T(8,128)S(1)}, f32[192,512]{1,0:T(8,128)S(1)}, u32[]{:S(2)}, u32[]{:S(2)}) collective-permute-start(f32[192,512]{1,0:T(8,128)S(1)} %get-tuple-element.106), channel_id=1, source_target_pairs={{0,1},{1,0},{2,3},{3,2},{4,5},{5,4},{6,7},{7,6},{8,9},{9,8},{10,11... | collective-permute-start | bytes 1179656 | tf_op jit(solution)/shard_map/ppermute | solution.py:348

commit v3 on v2

--- a/solution.py
+++ b/solution.py
@@ -14,9 +14,13 @@
 HD = 128
 GROUP = HEADS // KVH
 PARTS = ((0, 4), (4, 4))
+LOADS_AHEAD = 6
+PIECE_GROUPS = (1, 2, 3, 4)
+CUTS = 2
 MIB = 1 << 20
 BF = jnp.bfloat16
 F32 = jnp.float32
+TOKEN = jax.ShapeDtypeStruct((8, 128), jnp.float32)
 
 
 def chip_cycle(mesh):
@@ -81,7 +85,9 @@
     return jnp.concatenate(picks, axis=0).astype(BF)
 
 
-def qkv_kernel(order, index, rows, pad, x_ref, gain_ref, w_ref, keep_ref, first_ref, rest_ref, xs_ref, w_buf, in_sem):
+def qkv_kernel(order, index, rows, pad, x_ref, gain_ref, w_ref, *refs):
+    out_refs, (token, xs_ref, w_buf, in_sem) = refs[:4], refs[4:]
+    token[...] = jnp.zeros_like(token)
     total, depth = x_ref.shape
     begin, heads = PARTS[index]
     piece = heads * HD
@@ -89,26 +95,22 @@
     firsts = [begin * GROUP * HD + j * piece for j in range(GROUP)]
     firsts += [(HEADS + begin) * HD, (HEADS + KVH + begin) * HD]
     slots = sent_slots(index, len(order))
-    kept, first = keep_ref.shape[0], first_ref.shape[0]
-    ahead = 4
-
     def load(j):
-        return pltpu.make_async_copy(w_ref.at[:, pl.ds(firsts[j], piece)], w_buf.at[j], in_sem.at[j])
+        lanes = pl.ds(j * piece, piece)
+        return pltpu.make_async_copy(w_ref.at[:, pl.ds(firsts[j], piece)], w_buf.at[:, lanes], in_sem.at[j])
+
+    where = [(ref, at) for ref in out_refs for at in range(ref.shape[0])]
 
     def write(slot, lanes, value):
-        if slot < kept:
-            keep_ref[slot, :, lanes] = value
-        elif slot < kept + first:
-            first_ref[slot - kept, :, lanes] = value
-        else:
-            rest_ref[slot - kept - first, :, lanes] = value
-
-    for j in range(ahead):
+        ref, at = where[slot]
+        ref[at, :, lanes] = value
+
+    for j in range(LOADS_AHEAD):
         load(j).start()
     features = jnp.dot(picker(order, slots, rows, pad, total), x_ref[...], preferred_element_type=F32)
     xs_ref[...] = (features * gain_ref[...]).astype(BF)
     width = pieces * piece
-    extra = keep_ref.shape[2] - width
+    extra = out_refs[0].shape[2] - width
     if extra:
         me = lax.axis_index("gx")
         square = jnp.sum(features * features, axis=1, keepdims=True)
@@ -119,13 +121,17 @@
         held = jnp.where(lane == 3 * me, high, 0.0) + jnp.where(lane == 3 * me + 1, mid, 0.0) + jnp.where(lane == 3 * me + 2, low, 0.0)
         for slot in range(len(slots)):
             write(slot, slice(width, None), held[slot * pad : (slot + 1) * pad].astype(BF))
-    for j in range(pieces):
-        if j + ahead < pieces:
-            load(j + ahead).start()
-        load(j).wait()
-        out = jnp.dot(xs_ref[...], w_buf[j], preferred_element_type=F32)
+    done = 0
+    for group in PIECE_GROUPS:
+        for j in range(done, done + group):
+            if j + LOADS_AHEAD < pieces:
+                load(j + LOADS_AHEAD).start()
+            load(j).wait()
+        lanes = slice(done * piece, (done + group) * piece)
+        out = jnp.dot(xs_ref[...], w_buf[:, lanes], preferred_element_type=F32)
         for slot in range(len(slots)):
-            write(slot, slice(j * piece, (j + 1) * piece), out[slot * pad : (slot + 1) * pad].astype(BF))
+            write(slot, lanes, out[slot * pad : (slot + 1) * pad].astype(BF))
+        done += group
 
 
 def project(order, index, rows, pad, x, gain, w):
@@ -139,32 +145,43 @@
     return pl.pallas_call(
         functools.partial(qkv_kernel, order, index, rows, pad),
         in_specs=[vmem, vmem, pl.BlockSpec(memory_space=pltpu.HBM)],
-        out_specs=[vmem] * 3,
+        out_specs=[vmem] * 5,
         scratch_shapes=[
             pltpu.VMEM((2 * chips * pad, depth), BF),
-            pltpu.VMEM((pieces, depth, piece), BF),
+            pltpu.VMEM((depth, pieces * piece), BF),
             pltpu.SemaphoreType.DMA((pieces,)),
         ],
-        out_shape=[jax.ShapeDtypeStruct((n, pad, width), BF) for n in (chips, 2, chips - 2)],
-        compiler_params=pltpu.CompilerParams(vmem_limit_bytes=(56 if index == 0 else 46) * MIB),
+        out_shape=[jax.ShapeDtypeStruct((n, pad, width), BF) for n in (2, chips - 2, 2, chips - 2)] + [TOKEN],
+        compiler_params=pltpu.CompilerParams(vmem_limit_bytes=51 * MIB),
         cost_estimate=pl.CostEstimate(flops=1, bytes_accessed=1, transcendentals=0),
         name="qkv_part",
     )(x, gain, w)
 
 
-def attend_kernel(part, rows, pad, own_ref, core_ref, left_ref, right_ref, inv_ref, cos_ref, sin_ref, len_ref, k_ref, v_ref, out_ref, s_ref, m_ref):
+def attend_kernel(part, rows, pad, own_ref, left_ref, right_ref, inv_ref, cos_ref, sin_ref, len_ref, k_ref, v_ref, out_ref, s_ref, m_ref, k_buf, v_buf, sems):
     begin, heads = part
     live = rows * GROUP
     full = pad * GROUP
     slots = k_ref.shape[1]
     scale = 1.0 / HD**0.5
+    cuts = [rows * i // CUTS for i in range(CUTS + 1)]
+
+    def load(i, which):
+        source, target = ((k_ref, k_buf), (v_ref, v_buf))[which]
+        seqs = pl.ds(cuts[i], cuts[i + 1] - cuts[i])
+        lanes = pl.ds(begin * HD, heads * HD)
+        return pltpu.make_async_copy(source.at[seqs, :, lanes], target.at[seqs], sems.at[2 * i + which])
+
+    for which in range(2):
+        for i in range(CUTS):
+            load(i, which).start()
     inv = inv_ref[...]
     cos = cos_ref[...]
     sin = sin_ref[...]
 
     def tile(t):
         lanes = slice(t * HD, (t + 1) * HD)
-        got = own_ref[0, :, lanes].astype(F32) + core_ref[0, :, lanes].astype(F32)
+        got = own_ref[0, :, lanes].astype(F32)
         return (got + (left_ref[0, :, lanes].astype(F32) + right_ref[0, :, lanes].astype(F32))) * inv
 
     def turned(t):
@@ -188,15 +205,16 @@
         values_new.append(jnp.dot(spread, tile(heads * GROUP + heads + kk).astype(BF), preferred_element_type=F32)[:live])
         owns.append((jnp.sum(q * k_new, axis=1, keepdims=True) * scale)[:live])
         queries.append(q)
-    for kk in range(heads):
-        lanes = slice((begin + kk) * HD, (begin + kk + 1) * HD)
-        for s in range(rows):
-            s_ref[kk, s * GROUP : (s + 1) * GROUP] = lax.dot_general(
-                queries[kk][s * GROUP : (s + 1) * GROUP].astype(BF),
-                k_ref[s, :, lanes],
-                (((1,), (1,)), ((), ())),
-                preferred_element_type=F32,
-            )
+    for i in range(CUTS):
+        load(i, 0).wait()
+        for kk in range(heads):
+            for s in range(cuts[i], cuts[i + 1]):
+                s_ref[kk, s * GROUP : (s + 1) * GROUP] = lax.dot_general(
+                    queries[kk][s * GROUP : (s + 1) * GROUP].astype(BF),
+                    k_buf[s, :, kk * HD : (kk + 1) * HD],
+                    (((1,), (1,)), ((), ())),
+                    preferred_element_type=F32,
+                )
     own_weights = []
     for kk in range(heads):
         scores = jnp.where(valid, s_ref[kk] * scale, -1e30)
@@ -206,12 +224,15 @@
         total = jnp.sum(expo, axis=1, keepdims=True) + own_expo
         s_ref[kk] = expo / total
         own_weights.append((own_expo / total).astype(BF).astype(F32))
-    for kk in range(heads):
-        lanes = slice((begin + kk) * HD, (begin + kk + 1) * HD)
-        for s in range(rows):
-            m_ref[kk, s * GROUP : (s + 1) * GROUP] = jnp.dot(
-                s_ref[kk, s * GROUP : (s + 1) * GROUP].astype(BF), v_ref[s, :, lanes], preferred_element_type=F32
-            )
+    for i in range(CUTS):
+        load(i, 1).wait()
+        for kk in range(heads):
+            for s in range(cuts[i], cuts[i + 1]):
+                m_ref[kk, s * GROUP : (s + 1) * GROUP] = jnp.dot(
+                    s_ref[kk, s * GROUP : (s + 1) * GROUP].astype(BF),
+                    v_buf[s, :, kk * HD : (kk + 1) * HD],
+                    preferred_element_type=F32,
+                )
     for kk in range(heads):
         mixed = m_ref[kk] + own_weights[kk] * values_new[kk]
         mixed = jnp.concatenate([mixed, jnp.zeros((full - live, HD), F32)], axis=0).astype(BF)
@@ -224,7 +245,7 @@
     count = arrays[0].shape[0] if count is None else count
 
     def kernel(*refs):
-        sems = refs[-1]
+        token, sems = refs[-2:]
         copies = [
             pltpu.make_async_copy(refs[i].at[pl.ds(begin, count)], refs[len(arrays) + i], sems.at[i]) for i in range(len(arrays))
         ]
@@ -232,36 +253,41 @@
             copy.start()
         for copy in copies:
             copy.wait()
-
-    return pl.pallas_call(
+        token[...] = jnp.zeros_like(token)
+
+    *held, token = pl.pallas_call(
         kernel,
         in_specs=[pl.BlockSpec(memory_space=pltpu.HBM)] * len(arrays),
-        out_specs=[pl.BlockSpec(memory_space=pltpu.VMEM)] * len(arrays),
-        out_shape=[jax.ShapeDtypeStruct((count,) + a.shape[1:], BF) for a in arrays],
+        out_specs=[pl.BlockSpec(memory_space=pltpu.VMEM)] * (len(arrays) + 1),
+        out_shape=[jax.ShapeDtypeStruct((count,) + a.shape[1:], BF) for a in arrays] + [TOKEN],
         scratch_shapes=[pltpu.SemaphoreType.DMA((len(arrays),))],
         compiler_params=pltpu.CompilerParams(vmem_limit_bytes=limit * MIB),
         cost_estimate=pl.CostEstimate(flops=1, bytes_accessed=1, transcendentals=0),
         name=name,
     )(*arrays)
-
-
-def attend(part, rows, pad, own, from_core, from_left, from_right, inv, cos, sin, lens, keys, values):
+    return held, token
+
+
+def attend(part, rows, pad, own, from_left, from_right, inv, cos, sin, lens, keys, values):
     slots = keys.shape[1]
     heads = part[1]
     vmem = pl.BlockSpec(memory_space=pltpu.VMEM)
     return pl.pallas_call(
         functools.partial(attend_kernel, part, rows, pad),
-        in_specs=[vmem] * 10,
+        in_specs=[vmem] * 7 + [pl.BlockSpec(memory_space=pltpu.HBM)] * 2,
         out_specs=vmem,
         out_shape=jax.ShapeDtypeStruct((1, pad, heads * GROUP * HD), BF),
         scratch_shapes=[
             pltpu.VMEM((heads, rows * GROUP, slots), F32),
             pltpu.VMEM((heads, rows * GROUP, HD), F32),
+            pltpu.VMEM((rows, slots, heads * HD), BF),
+            pltpu.VMEM((rows, slots, heads * HD), BF),
+            pltpu.SemaphoreType.DMA((2 * CUTS,)),
         ],
-        compiler_params=pltpu.CompilerParams(vmem_limit_bytes=12 * MIB),
+        compiler_params=pltpu.CompilerParams(vmem_limit_bytes=51 * MIB),
         cost_estimate=pl.CostEstimate(flops=1, bytes_accessed=1, transcendentals=0),
         name="attend_part",
-    )(own, from_core, from_left, from_right, inv, cos, sin, lens, keys, values)
+    )(own, from_left, from_right, inv, cos, sin, lens, keys, values)
 
 
 def out_kernel(has_prior, *refs):
@@ -320,8 +346,8 @@
 
 
 def issue_order(steps):
-    names = ["P0", "P1"] + ["R0", "R1"] * steps
-    names += ["T0", "G0", "T1", "G1"] + ["G0", "G1"] * (steps - 2) + ["G0", "L0", "G1", "O0", "L1", "O1"]
+    names = ["P0", "R0", "P1", "R0", "R1"] + ["R0", "R1"] * (steps - 2) + ["R1"]
+    names += ["T0", "G0", "T1", "G1", "L0", "G0", "G1", "L1"] + ["G0", "G1"] * (steps - 2) + ["O0", "O1"]
     return names
 
 
@@ -347,17 +373,16 @@
     def cross(a):
         return lax.ppermute(a, "gx", sibling)
 
-    angles = HD // 2
-    inverse = 500000.0 ** (-(jnp.arange(angles, dtype=F32) * 2.0 / HD))
-    angle = jnp.pad(lengths, (0, pad - rows)).astype(F32)[:, None] * inverse[None, :]
-    cos = jnp.cos(angle)
-    sin = jnp.sin(angle)
-    cos = jnp.concatenate([cos, cos], axis=1)
-    sin = jnp.concatenate([-sin, sin], axis=1)
-    lens = jnp.repeat(lengths, GROUP)[:, None]
+    def positions(lengths):
+        angles = HD // 2
+        inverse = 500000.0 ** (-(jnp.arange(angles, dtype=F32) * 2.0 / HD))
+        angle = jnp.pad(lengths, (0, pad - rows)).astype(F32)[:, None] * inverse[None, :]
+        cos = jnp.cos(angle)
+        sin = jnp.sin(angle)
+        return jnp.concatenate([cos, cos], axis=1), jnp.concatenate([-sin, sin], axis=1), jnp.repeat(lengths, GROUP)[:, None]
 
     gain = norm_gain[None, :]
-    inv, w_other, caches, sums = [None], [None], [None], [None]
+    inv, w_other, places, sums = [None], [None], [None], [None]
 
     def part_steps(index):
         part = PARTS[index]
@@ -366,41 +391,46 @@
         sign = {"up": 1, "down": -1}
         ks = [k for k, w in sent_slots(index, chips) if w == 0]
         x = hidden_in if index == 0 else tied(hidden_in)
-        keep, first, rest = project(order, index, rows, pad, x, gain, w_qkv)
-        before[0] = keep
+        keep_first, keep_rest, first, rest, before[0] = project(order, index, rows, pad, x, gain, w_qkv)
         got_first = cross(first)
         got_rest = cross(rest)
         yield
 
+        front = (wide(tied(keep_first)) + wide(got_first)).astype(BF)
+        back = []
+
         def piece(k):
             at = ks.index(k % chips)
-            return keep[at : at + 1], got_first[at : at + 1] if at < 2 else got_rest[at - 2 : at - 1]
+            if at < 2:
+                return front[at : at + 1]
+            if not back:
+                back.append((wide(keep_rest) + wide(got_rest)).astype(BF))
+            return back[0][at - 2 : at - 1]
 
         moved = {}
         for step in range(steps):
             sent = {}
             for way, far in ways.items():
                 if step < far:
-                    here, there = piece(sign[way] * (far - step))
-                    total = wide(here) + wide(there)
-                    sent[way] = (total + wide(tied(moved[way])) if step else wide(tied(here)) + wide(there)).astype(BF)
+                    sent[way] = piece(sign[way] * (far - step))
+                    if step:
+                        sent[way] = (wide(sent[way]) + wide(tied(moved[way]))).astype(BF)
             moved = {**moved, **ring(sent)}
-            if index == len(PARTS) - 1 and step == 0:
+            if index == 1 and step == 0:
                 w_other[0] = cross(tied(w_out))
-            if index == len(PARTS) - 1 and step == 1:
-                caches[0] = load("load_caches", 40, tied((cache_keys, cache_values)))
-                before[0] = caches[0]
+            if index == 1 and step == 1:
+                places[0] = positions(tied(lengths))
             yield
-        own, from_core = piece(0)
+        own = piece(0)
         if index == 0:
             lanes = slice((GROUP + 2) * part[1] * HD, None)
-            parts = [own, from_core, moved["up"], moved["down"]]
+            parts = [own, moved["up"], moved["down"]]
             square = jnp.sum(sum(wide(a[0, :, lanes]) for a in parts), axis=1)
             inv[0] = jnp.broadcast_to(lax.rsqrt(square / D + 1e-05)[:, None], (pad, HD))
         own = tied(own)
-        if index == len(PARTS) - 1:
+        if index == 1:
             own = after(own, w_other[0])
-        attended = attend(part, rows, pad, own, from_core, moved["up"], moved["down"], inv[0], cos, sin, lens, *caches[0])
+        attended = attend(part, rows, pad, own, moved["up"], moved["down"], inv[0], *places[0], cache_keys, cache_values)
         before[0] = attended
         yield
         blocks = {0: attended}
@@ -409,8 +439,10 @@
             for way, a in ring(sent).items():
                 blocks[-sign[way] * (step + 1) % chips] = a
             yield
-        weights = load("load_weights", 40, (tied(w_out), w_other[0]), part[0] * GROUP * HD, part[1] * GROUP * HD)
-        yield
+            if step == index:
+                held = (tied(w_out), w_other[0])
+                weights, before[0] = load("load_weights", 40, held, part[0] * GROUP * HD, part[1] * GROUP * HD)
+                yield
         sums[0] = project_out(pad, [blocks[k] for k in range(chips)], weights, sums[0])
         if index < len(PARTS) - 1:
             before[0] = sums[0]

time: 115 us -> 103 us (0.90)
  other arithmetic: 11.8 us -> 4.99 us
  waiting for transfers between devices: 25.8 us -> 31.8 us
  starting transfers between devices: 35.3 us -> 30.7 us
  local copies, waits for them, and re-layouts: 5.41 us -> 2.02 us
  Pallas kernels: 36.3 us -> 33.2 us
    convert_element_type x9 -> x11, other arithmetic: 10.7 us -> 4.65 us  [the longest x6 3.71 us: part_steps(): sent[way] = (wide(sent[way]) + wide(tied(moved[way]))).astype(BF)]
    slice x4, local copies, waits for them, and re-layouts: 4.81 us -> 0.11 us  [the longest x2 0.07 us: piece(): return front[at:at + 1]]
    ppermute x28, waiting for transfers between devices: 24.1 us -> 28.7 us  [ring(): lax.ppermute(a, 'gx', up_pairs if way == 'up' else down_pairs)]
    ppermute x28, starting transfers between devices: 33.5 us -> 29.4 us  [ring(): lax.ppermute(a, 'gx', up_pairs if way == 'up' else down_pairs)]
    pallas_call x2, Pallas kernels: 5.82 us -> 9.61 us  [attend(): pl.pallas_call(functools.partial(attend_kernel, part, rows, pad), in_spec...]
    pallas_call x2, Pallas kernels: 14.2 us -> 10.4 us  [project(): pl.pallas_call(functools.partial(qkv_kernel, order, index, rows, pad), in...]
    pallas_call x3 -> x2, Pallas kernels: 11.3 us -> 8.15 us  [load(): pl.pallas_call(kernel, in_specs=[pl.BlockSpec(memory_space=pltpu.HBM)] *...]
    ppermute x6, waiting for transfers between devices: 1.72 us -> 3.15 us  [cross(): return lax.ppermute(a, 'gx', sibling)]
  transfers between devices with their start and end apart: 34 -> 34, of which waited for: 11 -> 17; matrix products, arithmetic and copies ran while one was open for 15% -> 5% of each run, Pallas kernels for 22% -> 24%
where the time goes in v3:
time: 103 us
  Pallas kernels  33.2 us (32%)
  waiting for transfers between devices  31.8 us (31%)
  starting transfers between devices  30.7 us (30%)
  other arithmetic  4.99 us (5%)
  local copies, waits for them, and re-layouts  2.02 us (2%)
    ppermute x28, starting transfers between devices, ring(): lax.ppermute(a, 'gx', up_pairs if way == 'up' else down_pairs)  29.4 us
    ppermute x28, waiting for transfers between devices, ring(): lax.ppermute(a, 'gx', up_pairs if way == 'up' else down_pairs)  28.7 us
    pallas_call x2, Pallas kernels, project(): pl.pallas_call(functools.partial(qkv_kernel, order, index, rows, pad), in...  10.4 us
    pallas_call x2, Pallas kernels, attend(): pl.pallas_call(functools.partial(attend_kernel, part, rows, pad), in_spec...  9.61 us
    pallas_call x2, Pallas kernels, load(): pl.pallas_call(kernel, in_specs=[pl.BlockSpec(memory_space=pltpu.HBM)] *...  8.15 us
    convert_element_type x6, other arithmetic, part_steps(): sent[way] = (wide(sent[way]) + wide(tied(moved[way]))).astype(BF)  3.71 us
    pallas_call x2, Pallas kernels, project_out(): pl.pallas_call(functools.partial(out_kernel, prior is not None), in_specs...  3.6 us
    ppermute x6, waiting for transfers between devices, cross(): return lax.ppermute(a, 'gx', sibling)  3.15 us
  transfers between devices with their start and end apart: 34, of which 17 were waited for; matrix products, arithmetic and copies ran while one was open for 5% of the time, Pallas kernels for 24%

profile of v3, /device:TPU:0, one launch (start us, length us, event | category | flops | bytes accessed | tf_op | source)
XLA Modules:
  0.0 103.0 jit_solution(14390214722027481189)
XLA Ops:
  0.0 1.0 copy-done
  1.0 0.7 copy-done.2
  1.7 5.2 %qkv_part.2 = (bf16[2,24,5248]{2,1,0:T(8,128)(2,1)S(1)}, bf16[6,24,5248]{2,1,0:T(8,128)(2,1)S(1)}, bf16[2,24,5248]{2,1,0:T(8,128)(2,1)S(1)}, bf16[6,24,5248]{2,1,0:T(8,128)(2,1)}, f32[8,128]{1,0:T(8,128)}) custom-call(bf16[352,512]{1,0:T(8,128)(2,1)S(1)} %copy-done, f32[1,512]{1,0:T(1,128)S(1)} %bitcast.1, bf16[512,10240]{1,0:T(8,128)(2,1)} %w_ref.3), custom_call_target="tpu_custom_call" | custom-call | flops 1 | bytes 1 | tf_op jit(solution)/shard_map/qkv_part/pallas_call | solution.py:145
  7.5 1.4 %collective-permute-done = bf16[2,24,5248]{2,1,0:T(8,128)(2,1)S(1)} collective-permute-done((bf16[2,24,5248]{2,1,0:T(8,128)(2,1)S(1)}, bf16[2,24,5248]{2,1,0:T(8,128)(2,1)S(1)}, u32[]{:S(2)}, u32[]{:S(2)}) %collective-permute-start) | collective-permute-done | bytes 503840 | tf_op jit(solution)/shard_map/ppermute | solution.py:374
  9.1 3.0 %collective-permute-start.4 = (bf16[1,24,5248]{2,1,0:T(8,128)(2,1)S(1)}, bf16[1,24,5248]{2,1,0:T(8,128)(2,1)S(1)}, u32[]{:S(2)}, u32[]{:S(2)}) collective-permute-start(bf16[1,24,5248]{2,1,0:T(8,128)(2,1)S(1)} %get-tuple-element.113), channel_id=1, source_target_pairs={{2,0},{3,1},{6,2},{7,3},{10,6},{11,7},{14,10},{15,11},{12,14},{13,... | collective-permute-start | bytes 755720 | tf_op jit(solution)/shard_map/ppermute | solution.py:368
  12.1 5.2 %qkv_part.3 = (bf16[2,24,5120]{2,1,0:T(8,128)(2,1)S(1)}, bf16[6,24,5120]{2,1,0:T(8,128)(2,1)S(1)}, bf16[2,24,5120]{2,1,0:T(8,128)(2,1)S(1)}, bf16[6,24,5120]{2,1,0:T(8,128)(2,1)}, f32[8,128]{1,0:T(8,128)}) custom-call(bf16[352,512]{1,0:T(8,128)(2,1)S(1)} %copy-done, f32[1,512]{1,0:T(1,128)S(1)} %bitcast.2, bf16[512,10240]{1,0:T(8,128)(2,1)} %w_ref.3), custom_call_target="tpu_custom_call" | custom-call | flops 1 | bytes 1 | tf_op jit(solution)/shard_map/qkv_part/pallas_call | solution.py:145
  17.4 1.0 %collective-permute-done.4 = bf16[1,24,5248]{2,1,0:T(8,128)(2,1)S(1)} collective-permute-done((bf16[1,24,5248]{2,1,0:T(8,128)(2,1)S(1)}, bf16[1,24,5248]{2,1,0:T(8,128)(2,1)S(1)}, u32[]{:S(2)}, u32[]{:S(2)}) %collective-permute-start.4) | collective-permute-done | bytes 251936 | tf_op jit(solution)/shard_map/ppermute | solution.py:368
  18.4 1.5 %collective-permute-done.3 = bf16[1,24,5248]{2,1,0:T(8,128)(2,1)S(1)} collective-permute-done((bf16[1,24,5248]{2,1,0:T(8,128)(2,1)S(1)}, bf16[1,24,5248]{2,1,0:T(8,128)(2,1)S(1)}, u32[]{:S(2)}, u32[]{:S(2)}) %collective-permute-start.3) | collective-permute-done | bytes 251936 | tf_op jit(solution)/shard_map/ppermute | solution.py:368
  20.5 1.6 %collective-permute-start.8 = (bf16[1,24,5248]{2,1,0:T(8,128)(2,1)S(1)}, bf16[1,24,5248]{2,1,0:T(8,128)(2,1)S(1)}, u32[]{:S(2)}, u32[]{:S(2)}) collective-permute-start(bf16[1,24,5248]{2,1,0:T(8,128)(2,1)S(1)} %get-tuple-element.107), channel_id=1, source_target_pairs={{2,0},{3,1},{6,2},{7,3},{10,6},{11,7},{14,10},{15,11},{12,14},{13,... | collective-permute-start | bytes 755720 | tf_op jit(solution)/shard_map/ppermute | solution.py:368
  23.7 3.8 %collective-permute-done.8 = bf16[1,24,5248]{2,1,0:T(8,128)(2,1)S(1)} collective-permute-done((bf16[1,24,5248]{2,1,0:T(8,128)(2,1)S(1)}, bf16[1,24,5248]{2,1,0:T(8,128)(2,1)S(1)}, u32[]{:S(2)}, u32[]{:S(2)}) %collective-permute-start.8) | collective-permute-done | bytes 251936 | tf_op jit(solution)/shard_map/ppermute | solution.py:368
  27.5 1.6 %collective-permute-start.6 = (bf16[1,24,5120]{2,1,0:T(8,128)(2,1)S(1)}, bf16[1,24,5120]{2,1,0:T(8,128)(2,1)S(1)}, u32[]{:S(2)}, u32[]{:S(2)}) collective-permute-start(bf16[1,24,5120]{2,1,0:T(8,128)(2,1)S(1)} %get-tuple-element.116), channel_id=1, source_target_pairs={{2,0},{3,1},{6,2},{7,3},{10,6},{11,7},{14,10},{15,11},{12,14},{13,... | collective-permute-start | bytes 737288 | tf_op jit(solution)/shard_map/ppermute | solution.py:368
  29.1 2.0 %collective-permute-done.7 = bf16[1,24,5248]{2,1,0:T(8,128)(2,1)S(1)} collective-permute-done((bf16[1,24,5248]{2,1,0:T(8,128)(2,1)S(1)}, bf16[1,24,5248]{2,1,0:T(8,128)(2,1)S(1)}, u32[]{:S(2)}, u32[]{:S(2)}) %collective-permute-start.7) | collective-permute-done | bytes 251936 | tf_op jit(solution)/shard_map/ppermute | solution.py:368
  31.3 1.6 %collective-permute-start.15 = (bf16[1,24,5248]{2,1,0:T(8,128)(2,1)S(1)}, bf16[1,24,5248]{2,1,0:T(8,128)(2,1)S(1)}, u32[]{:S(2)}, u32[]{:S(2)}) collective-permute-start(bf16[1,24,5248]{2,1,0:T(8,128)(2,1)S(1)} %get-tuple-element.105), channel_id=1, source_target_pairs={{2,0},{3,1},{6,2},{7,3},{10,6},{11,7},{14,10},{15,11},{12,14},{13,... | collective-permute-start | bytes 755720 | tf_op jit(solution)/shard_map/ppermute | solution.py:368
  32.9 1.2 %collective-permute-done.11 = bf16[1,24,5120]{2,1,0:T(8,128)(2,1)S(1)} collective-permute-done((bf16[1,24,5120]{2,1,0:T(8,128)(2,1)S(1)}, bf16[1,24,5120]{2,1,0:T(8,128)(2,1)S(1)}, u32[]{:S(2)}, u32[]{:S(2)}) %collective-permute-start.11) | collective-permute-done | bytes 245792 | tf_op jit(solution)/shard_map/ppermute | solution.py:368
  34.5 1.6 %collective-permute-done.6 = bf16[1,24,5120]{2,1,0:T(8,128)(2,1)S(1)} collective-permute-done((bf16[1,24,5120]{2,1,0:T(8,128)(2,1)S(1)}, bf16[1,24,5120]{2,1,0:T(8,128)(2,1)S(1)}, u32[]{:S(2)}, u32[]{:S(2)}) %collective-permute-start.6) | collective-permute-done | bytes 245792 | tf_op jit(solution)/shard_map/ppermute | solution.py:368
  36.5 1.0 add_convert_fusion.12
  37.5 1.2 %collective-permute-start.13 = (bf16[1,24,5120]{2,1,0:T(8,128)(2,1)}, bf16[1,24,5120]{2,1,0:T(8,128)(2,1)}, u32[]{:S(2)}, u32[]{:S(2)}) collective-permute-start(bf16[1,24,5120]{2,1,0:T(8,128)(2,1)} %get-tuple-element.111), channel_id=1, source_target_pairs={{0,2},{1,3},{2,6},{3,7},{6,10},{7,11},{10,14},{11,15},{14,12},{15,... | collective-permute-start | bytes 737288 | tf_op jit(solution)/shard_map/ppermute | solution.py:368
  38.7 0.8 collective-permute-start.9
  39.7 3.0 %collective-permute-done.10 = bf16[1,24,5248]{2,1,0:T(8,128)(2,1)S(1)} collective-permute-done((bf16[1,24,5248]{2,1,0:T(8,128)(2,1)S(1)}, bf16[1,24,5248]{2,1,0:T(8,128)(2,1)S(1)}, u32[]{:S(2)}, u32[]{:S(2)}) %collective-permute-start.10) | collective-permute-done | bytes 251936 | tf_op jit(solution)/shard_map/ppermute | solution.py:368
  42.8 2.7 %collective-permute-done.13 = bf16[1,24,5120]{2,1,0:T(8,128)(2,1)} collective-permute-done((bf16[1,24,5120]{2,1,0:T(8,128)(2,1)}, bf16[1,24,5120]{2,1,0:T(8,128)(2,1)}, u32[]{:S(2)}, u32[]{:S(2)}) %collective-permute-start.13) | collective-permute-done | bytes 245792 | tf_op jit(solution)/shard_map/ppermute | solution.py:368
  45.5 1.4 %add_convert_fusion.10 = (bf16[1,24,5120]{2,1,0:T(8,128)(2,1)S(1)}, bf16[1,24,5120]{2,1,0:T(8,128)(2,1)S(1)}) fusion(bf16[1,24,5120]{2,1,0:T(8,128)(2,1)} %collective-permute-done.13, bf16[6,24,5120]{2,1,0:T(8,128)(2,1)} %copy-done.3, bf16[1,24,5120]{2,1,0:T(8,128)(2,1)} %collective-permute-done.9), kind=kLoop, calls=%fused_computation.10 | loop fusion | flops 983040 | bytes 1474560 | tf_op jit(solution)/shard_map/convert_element_type | solution.py:417
  46.9 1.6 %collective-permute-start.12 = (bf16[1,24,5120]{2,1,0:T(8,128)(2,1)S(1)}, bf16[1,24,5120]{2,1,0:T(8,128)(2,1)S(1)}, u32[]{:S(2)}, u32[]{:S(2)}) collective-permute-start(bf16[1,24,5120]{2,1,0:T(8,128)(2,1)S(1)} %get-tuple-element.110), channel_id=1, source_target_pairs={{2,0},{3,1},{6,2},{7,3},{10,6},{11,7},{14,10},{15,11},{12,14},{13,... | collective-permute-start | bytes 737288 | tf_op jit(solution)/shard_map/ppermute | solution.py:368
  49.2 1.1 %collective-permute-start.17 = (bf16[1,24,5120]{2,1,0:T(8,128)(2,1)S(1)}, bf16[1,24,5120]{2,1,0:T(8,128)(2,1)S(1)}, u32[]{:S(2)}, u32[]{:S(2)}) collective-permute-start(bf16[1,24,5120]{2,1,0:T(8,128)(2,1)S(1)} %get-tuple-element.109), channel_id=1, source_target_pairs={{0,2},{1,3},{2,6},{3,7},{6,10},{7,11},{10,14},{11,15},{14,12},{15,... | collective-permute-start | bytes 737288 | tf_op jit(solution)/shard_map/ppermute | solution.py:368
  50.3 3.1 %collective-permute-done.12 = bf16[1,24,5120]{2,1,0:T(8,128)(2,1)S(1)} collective-permute-done((bf16[1,24,5120]{2,1,0:T(8,128)(2,1)S(1)}, bf16[1,24,5120]{2,1,0:T(8,128)(2,1)S(1)}, u32[]{:S(2)}, u32[]{:S(2)}) %collective-permute-start.12) | collective-permute-done | bytes 245792 | tf_op jit(solution)/shard_map/ppermute | solution.py:368
  53.4 1.0 add_convert_fusion.9
  54.4 1.6 %collective-permute-start.18 = (bf16[1,24,5120]{2,1,0:T(8,128)(2,1)S(1)}, bf16[1,24,5120]{2,1,0:T(8,128)(2,1)S(1)}, u32[]{:S(2)}, u32[]{:S(2)}) collective-permute-start(bf16[1,24,5120]{2,1,0:T(8,128)(2,1)S(1)} %add_convert_fusion.9), channel_id=1, source_target_pairs={{2,0},{3,1},{6,2},{7,3},{10,6},{11,7},{14,10},{15,11},{12,14},{13,... | collective-permute-start | bytes 737288 | tf_op jit(solution)/shard_map/ppermute | solution.py:368
  56.5 4.8 %attend_part.2.refs_0_ = bf16[1,24,4096]{2,1,0:T(8,128)(2,1)S(1)} custom-call(bf16[1,24,5248]{2,1,0:T(8,128)(2,1)S(1)} %slice.80.own_ref, bf16[1,24,5248]{2,1,0:T(8,128)(2,1)S(1)} %collective-permute-done.14.left_ref, bf16[1,24,5248]{2,1,0:T(8,128)(2,1)S(1)} %collective-permute-done.15.right_ref, f32[24,128]{1,0:T(8,128)S(1)} %broadcast_in_dim.7.inv_ref, ...), custom_call_target="tpu_custom_call" | custom-call | flops 1 | bytes 1 | tf_op jit(solution)/shard_map/attend_part/pallas_call | solution.py:275
  61.3 1.7 %collective-permute-start.21 = (bf16[1,24,4096]{2,1,0:T(8,128)(2,1)S(1)}, bf16[1,24,4096]{2,1,0:T(8,128)(2,1)S(1)}, u32[]{:S(2)}, u32[]{:S(2)}) collective-permute-start(bf16[1,24,4096]{2,1,0:T(8,128)(2,1)S(1)} %attend_part.2.refs_0_), channel_id=1, source_target_pairs={{2,0},{3,1},{6,2},{7,3},{10,6},{11,7},{14,10},{15,11},{12,14},{13,... | collective-permute-start | bytes 589832 | tf_op jit(solution)/shard_map/ppermute | solution.py:368
  63.4 4.8 %attend_part.3.refs_0_ = bf16[1,24,4096]{2,1,0:T(8,128)(2,1)S(1)} custom-call(bf16[1,24,5120]{2,1,0:T(8,128)(2,1)S(1)} %slice.79.own_ref, bf16[1,24,5120]{2,1,0:T(8,128)(2,1)S(1)} %collective-permute-done.17.left_ref, bf16[1,24,5120]{2,1,0:T(8,128)(2,1)S(1)} %collective-permute-done.18.right_ref, f32[24,128]{1,0:T(8,128)S(1)} %broadcast_in_dim.7.inv_ref, ...), custom_call_target="tpu_custom_call" | custom-call | flops 1 | bytes 1 | tf_op jit(solution)/shard_map/attend_part/pallas_call | solution.py:275
  68.2 1.7 %collective-permute-start.19 = (bf16[1,24,4096]{2,1,0:T(8,128)(2,1)S(1)}, bf16[1,24,4096]{2,1,0:T(8,128)(2,1)S(1)}, u32[]{:S(2)}, u32[]{:S(2)}) collective-permute-start(bf16[1,24,4096]{2,1,0:T(8,128)(2,1)S(1)} %attend_part.3.refs_0_), channel_id=1, source_target_pairs={{2,0},{3,1},{6,2},{7,3},{10,6},{11,7},{14,10},{15,11},{12,14},{13,... | collective-permute-start | bytes 589832 | tf_op jit(solution)/shard_map/ppermute | solution.py:368
  70.3 4.1 %load_weights.2 = (bf16[4096,512]{1,0:T(8,128)(2,1)S(1)}, bf16[4096,512]{1,0:T(8,128)(2,1)S(1)}, f32[8,128]{1,0:T(8,128)}) custom-call(bf16[8192,512]{1,0:T(8,128)(2,1)} %refs_0_.1, bf16[8192,512]{1,0:T(8,128)(2,1)} %collective-permute-done.16.refs_1_), custom_call_target="tpu_custom_call" | custom-call | flops 1 | bytes 1 | tf_op jit(solution)/shard_map/load_weights/pallas_call | solution.py:258
  74.4 1.1 %collective-permute-start.23 = (bf16[1,24,4096]{2,1,0:T(8,128)(2,1)S(1)}, bf16[1,24,4096]{2,1,0:T(8,128)(2,1)S(1)}, u32[]{:S(2)}, u32[]{:S(2)}) collective-permute-start(bf16[1,24,4096]{2,1,0:T(8,128)(2,1)S(1)} %collective-permute-done.20.refs_7_), channel_id=1, source_target_pairs={{0,2},{1,3},{2,6},{3,7},{6,10},{7,11},{10,14},{11,15},{14,12},{15,... | collective-permute-start | bytes 589832 | tf_op jit(solution)/shard_map/ppermute | solution.py:368
  75.5 1.0 collective-permute-start.25
  76.5 1.6 %collective-permute-start.22 = (bf16[1,24,4096]{2,1,0:T(8,128)(2,1)S(1)}, bf16[1,24,4096]{2,1,0:T(8,128)(2,1)S(1)}, u32[]{:S(2)}, u32[]{:S(2)}) collective-permute-start(bf16[1,24,4096]{2,1,0:T(8,128)(2,1)S(1)} %collective-permute-done.19.refs_1_), channel_id=1, source_target_pairs={{2,0},{3,1},{6,2},{7,3},{10,6},{11,7},{14,10},{15,11},{12,14},{13,... | collective-permute-start | bytes 589832 | tf_op jit(solution)/shard_map/ppermute | solution.py:368
  78.5 4.1 %load_weights.3 = (bf16[4096,512]{1,0:T(8,128)(2,1)S(1)}, bf16[4096,512]{1,0:T(8,128)(2,1)S(1)}, f32[8,128]{1,0:T(8,128)}) custom-call(bf16[8192,512]{1,0:T(8,128)(2,1)} %refs_0_.1, bf16[8192,512]{1,0:T(8,128)(2,1)} %collective-permute-done.16.refs_1_), custom_call_target="tpu_custom_call" | custom-call | flops 1 | bytes 1 | tf_op jit(solution)/shard_map/load_weights/pallas_call | solution.py:258
  82.6 1.1 %collective-permute-start.27 = (bf16[1,24,4096]{2,1,0:T(8,128)(2,1)S(1)}, bf16[1,24,4096]{2,1,0:T(8,128)(2,1)S(1)}, u32[]{:S(2)}, u32[]{:S(2)}) collective-permute-start(bf16[1,24,4096]{2,1,0:T(8,128)(2,1)S(1)} %collective-permute-done.23.refs_6_), channel_id=1, source_target_pairs={{0,2},{1,3},{2,6},{3,7},{6,10},{7,11},{10,14},{11,15},{14,12},{15,... | collective-permute-start | bytes 589832 | tf_op jit(solution)/shard_map/ppermute | solution.py:368
  83.7 2.7 %collective-permute-done.22.refs_2_ = bf16[1,24,4096]{2,1,0:T(8,128)(2,1)S(1)} collective-permute-done((bf16[1,24,4096]{2,1,0:T(8,128)(2,1)S(1)}, bf16[1,24,4096]{2,1,0:T(8,128)(2,1)S(1)}, u32[]{:S(2)}, u32[]{:S(2)}) %collective-permute-start.22) | collective-permute-done | bytes 196640 | tf_op jit(solution)/shard_map/ppermute | solution.py:368
  86.8 1.6 %collective-permute-start.31 = (bf16[1,24,4096]{2,1,0:T(8,128)(2,1)S(1)}, bf16[1,24,4096]{2,1,0:T(8,128)(2,1)S(1)}, u32[]{:S(2)}, u32[]{:S(2)}) collective-permute-start(bf16[1,24,4096]{2,1,0:T(8,128)(2,1)S(1)} %collective-permute-done.25.refs_2_), channel_id=1, source_target_pairs={{2,0},{3,1},{6,2},{7,3},{10,6},{11,7},{14,10},{15,11},{12,14},{13,... | collective-permute-start | bytes 589832 | tf_op jit(solution)/shard_map/ppermute | solution.py:368
  88.8 1.7 %collective-permute-done.27.refs_5_ = bf16[1,24,4096]{2,1,0:T(8,128)(2,1)S(1)} collective-permute-done((bf16[1,24,4096]{2,1,0:T(8,128)(2,1)S(1)}, bf16[1,24,4096]{2,1,0:T(8,128)(2,1)S(1)}, u32[]{:S(2)}, u32[]{:S(2)}) %collective-permute-start.27) | collective-permute-done | bytes 196640 | tf_op jit(solution)/shard_map/ppermute | solution.py:368
  90.5 0.9 collective-permute-start.32
  91.4 0.7 collective-permute-done.26.refs_3_
  92.0 0.8 collective-permute-start.29
  92.9 1.3 %collective-permute-done.31.refs_3_ = bf16[1,24,4096]{2,1,0:T(8,128)(2,1)S(1)} collective-permute-done((bf16[1,24,4096]{2,1,0:T(8,128)(2,1)S(1)}, bf16[1,24,4096]{2,1,0:T(8,128)(2,1)S(1)}, u32[]{:S(2)}, u32[]{:S(2)}) %collective-permute-start.31) | collective-permute-done | bytes 196640 | tf_op jit(solution)/shard_map/ppermute | solution.py:368
  94.1 2.0 %collective-permute-done.32.refs_4_ = bf16[1,24,4096]{2,1,0:T(8,128)(2,1)S(1)} collective-permute-done((bf16[1,24,4096]{2,1,0:T(8,128)(2,1)S(1)}, bf16[1,24,4096]{2,1,0:T(8,128)(2,1)S(1)}, u32[]{:S(2)}, u32[]{:S(2)}) %collective-permute-start.32) | collective-permute-done | bytes 196640 | tf_op jit(solution)/shard_map/ppermute | solution.py:368
  96.2 1.8 %out_part.2 = (f32[192,512]{1,0:T(8,128)S(1)}, f32[192,512]{1,0:T(8,128)S(1)}) custom-call(bf16[1,24,4096]{2,1,0:T(8,128)(2,1)S(1)} %attend_part.2.refs_0_, bf16[1,24,4096]{2,1,0:T(8,128)(2,1)S(1)} %collective-permute-done.21.refs_1_, bf16[1,24,4096]{2,1,0:T(8,128)(2,1)S(1)} %collective-permute-done.25.refs_2_, ...), custom_call_target="tpu_custom_call" | custom-call | flops 1 | bytes 1 | tf_op jit(solution)/shard_map/out_part/pallas_call | solution.py:312
  98.0 1.8 %out_part.3 = (f32[192,512]{1,0:T(8,128)S(1)}, f32[192,512]{1,0:T(8,128)S(1)}) custom-call(bf16[1,24,4096]{2,1,0:T(8,128)(2,1)S(1)} %attend_part.3.refs_0_, bf16[1,24,4096]{2,1,0:T(8,128)(2,1)S(1)} %collective-permute-done.19.refs_1_, bf16[1,24,4096]{2,1,0:T(8,128)(2,1)S(1)} %collective-permute-done.22.refs_2_, ...), custom_call_target="tpu_custom_call" | custom-call | flops 1 | bytes 1 | tf_op jit(solution)/shard_map/out_part/pallas_call | solution.py:312
  99.9 1.7 %collective-permute-done.33.other_ref = f32[192,512]{1,0:T(8,128)S(1)} collective-permute-done((f32[192,512]{1,0:T(8,128)S(1)}, f32[192,512]{1,0:T(8,128)S(1)}, u32[]{:S(2)}, u32[]{:S(2)}) %collective-permute-start.33) | collective-permute-done | bytes 393248 | tf_op jit(solution)/shard_map/ppermute | solution.py:374
  101.6 1.4 %finish.1 = bf16[352,512]{1,0:T(8,128)(2,1)} custom-call(bf16[352,512]{1,0:T(8,128)(2,1)S(1)} %copy-done.1, f32[192,512]{1,0:T(8,128)S(1)} %get-tuple-element.103.mine_ref, f32[192,512]{1,0:T(8,128)S(1)} %collective-permute-done.33.other_ref), custom_call_target="tpu_custom_call" | custom-call | flops 1 | bytes 1 | tf_op jit(solution)/shard_map/finish/pallas_call | solution.py:333
  (64 shorter events, 7.2 us)
Async XLA Ops:
  0.0 1.0 copy-start
  1.0 0.7 copy-start.2
  6.9 2.0 %collective-permute-start = (bf16[2,24,5248]{2,1,0:T(8,128)(2,1)S(1)}, bf16[2,24,5248]{2,1,0:T(8,128)(2,1)S(1)}, u32[]{:S(2)}, u32[]{:S(2)}) collective-permute-start(bf16[2,24,5248]{2,1,0:T(8,128)(2,1)S(1)} %get-tuple-element.56), channel_id=1, source_target_pairs={{0,1},{1,0},{2,3},{3,2},{4,5},{5,4},{6,7},{7,6},{8,9},{9,8},{10,11... | collective-permute-start | bytes 1511432 | tf_op jit(solution)/shard_map/ppermute | solution.py:374
  7.4 12.5 %collective-permute-start.2 = (bf16[6,24,5248]{2,1,0:T(8,128)(2,1)}, bf16[6,24,5248]{2,1,0:T(8,128)(2,1)S(1)}, u32[]{:S(2)}, u32[]{:S(2)}) collective-permute-start(bf16[6,24,5248]{2,1,0:T(8,128)(2,1)} %get-tuple-element.61), channel_id=1, source_target_pairs={{0,1},{1,0},{2,3},{3,2},{4,5},{5,4},{6,7},{7,6},{8,9},{9,8},{10,11... | collective-permute-start | bytes 4534280 | tf_op jit(solution)/shard_map/ppermute | solution.py:374
  9.1 9.3 %collective-permute-start.4 = (bf16[1,24,5248]{2,1,0:T(8,128)(2,1)S(1)}, bf16[1,24,5248]{2,1,0:T(8,128)(2,1)S(1)}, u32[]{:S(2)}, u32[]{:S(2)}) collective-permute-start(bf16[1,24,5248]{2,1,0:T(8,128)(2,1)S(1)} %get-tuple-element.113), channel_id=1, source_target_pairs={{2,0},{3,1},{6,2},{7,3},{10,6},{11,7},{14,10},{15,11},{12,14},{13,... | collective-permute-start | bytes 755720 | tf_op jit(solution)/shard_map/ppermute | solution.py:368
  12.1 7.8 %collective-permute-start.3 = (bf16[1,24,5248]{2,1,0:T(8,128)(2,1)S(1)}, bf16[1,24,5248]{2,1,0:T(8,128)(2,1)S(1)}, u32[]{:S(2)}, u32[]{:S(2)}) collective-permute-start(bf16[1,24,5248]{2,1,0:T(8,128)(2,1)S(1)} %get-tuple-element.114), channel_id=1, source_target_pairs={{0,2},{1,3},{2,6},{3,7},{6,10},{7,11},{10,14},{11,15},{14,12},{15,... | collective-permute-start | bytes 755720 | tf_op jit(solution)/shard_map/ppermute | solution.py:368
  17.3 5.2 %collective-permute-start.5 = (bf16[2,24,5120]{2,1,0:T(8,128)(2,1)S(1)}, bf16[2,24,5120]{2,1,0:T(8,128)(2,1)S(1)}, u32[]{:S(2)}, u32[]{:S(2)}) collective-permute-start(bf16[2,24,5120]{2,1,0:T(8,128)(2,1)S(1)} %get-tuple-element.67), channel_id=1, source_target_pairs={{0,1},{1,0},{2,3},{3,2},{4,5},{5,4},{6,7},{7,6},{8,9},{9,8},{10,11... | collective-permute-start | bytes 1474568 | tf_op jit(solution)/shard_map/ppermute | solution.py:374
  20.5 2.3 %copy-start.5 = (bf16[6,24,5120]{2,1,0:T(8,128)(2,1)S(1)}, bf16[6,24,5120]{2,1,0:T(8,128)(2,1)}, u32[]{:S(2)}) copy-start(bf16[6,24,5120]{2,1,0:T(8,128)(2,1)} %get-tuple-element.59) | copy-start | bytes 4423684
  20.5 7.0 %collective-permute-start.8 = (bf16[1,24,5248]{2,1,0:T(8,128)(2,1)S(1)}, bf16[1,24,5248]{2,1,0:T(8,128)(2,1)S(1)}, u32[]{:S(2)}, u32[]{:S(2)}) collective-permute-start(bf16[1,24,5248]{2,1,0:T(8,128)(2,1)S(1)} %get-tuple-element.107), channel_id=1, source_target_pairs={{2,0},{3,1},{6,2},{7,3},{10,6},{11,7},{14,10},{15,11},{12,14},{13,... | collective-permute-start | bytes 755720 | tf_op jit(solution)/shard_map/ppermute | solution.py:368
  22.1 9.0 %collective-permute-start.7 = (bf16[1,24,5248]{2,1,0:T(8,128)(2,1)S(1)}, bf16[1,24,5248]{2,1,0:T(8,128)(2,1)S(1)}, u32[]{:S(2)}, u32[]{:S(2)}) collective-permute-start(bf16[1,24,5248]{2,1,0:T(8,128)(2,1)S(1)} %get-tuple-element.108), channel_id=1, source_target_pairs={{0,2},{1,3},{2,6},{3,7},{6,10},{7,11},{10,14},{11,15},{14,12},{15,... | collective-permute-start | bytes 755720 | tf_op jit(solution)/shard_map/ppermute | solution.py:368
  22.7 40.7 %collective-permute-start.16 = (bf16[8192,512]{1,0:T(8,128)(2,1)}, bf16[8192,512]{1,0:T(8,128)(2,1)}, u32[]{:S(2)}, u32[]{:S(2)}) collective-permute-start(bf16[8192,512]{1,0:T(8,128)(2,1)} %refs_0_.1), channel_id=1, source_target_pairs={{0,1},{1,0},{2,3},{3,2},{4,5},{5,4},{6,7},{7,6},{8,9},{9,8},{10,11... | collective-permute-start | bytes 25165832 | tf_op jit(solution)/shard_map/ppermute | solution.py:374
  22.8 13.3 %collective-permute-start.1 = (bf16[6,24,5120]{2,1,0:T(8,128)(2,1)S(1)}, bf16[6,24,5120]{2,1,0:T(8,128)(2,1)S(1)}, u32[]{:S(2)}, u32[]{:S(2)}) collective-permute-start(bf16[6,24,5120]{2,1,0:T(8,128)(2,1)S(1)} %copy-done.5), channel_id=1, source_target_pairs={{0,1},{1,0},{2,3},{3,2},{4,5},{5,4},{6,7},{7,6},{8,9},{9,8},{10,11... | collective-permute-start | bytes 4423688 | tf_op jit(solution)/shard_map/ppermute | solution.py:374
  23.3 10.7 %collective-permute-start.11 = (bf16[1,24,5120]{2,1,0:T(8,128)(2,1)S(1)}, bf16[1,24,5120]{2,1,0:T(8,128)(2,1)S(1)}, u32[]{:S(2)}, u32[]{:S(2)}) collective-permute-start(bf16[1,24,5120]{2,1,0:T(8,128)(2,1)S(1)} %get-tuple-element.115), channel_id=1, source_target_pairs={{0,2},{1,3},{2,6},{3,7},{6,10},{7,11},{10,14},{11,15},{14,12},{15,... | collective-permute-start | bytes 737288 | tf_op jit(solution)/shard_map/ppermute | solution.py:368
  27.5 8.6 %collective-permute-start.6 = (bf16[1,24,5120]{2,1,0:T(8,128)(2,1)S(1)}, bf16[1,24,5120]{2,1,0:T(8,128)(2,1)S(1)}, u32[]{:S(2)}, u32[]{:S(2)}) collective-permute-start(bf16[1,24,5120]{2,1,0:T(8,128)(2,1)S(1)} %get-tuple-element.116), channel_id=1, source_target_pairs={{2,0},{3,1},{6,2},{7,3},{10,6},{11,7},{14,10},{15,11},{12,14},{13,... | collective-permute-start | bytes 737288 | tf_op jit(solution)/shard_map/ppermute | solution.py:368
  31.3 24.8 %collective-permute-start.15 = (bf16[1,24,5248]{2,1,0:T(8,128)(2,1)S(1)}, bf16[1,24,5248]{2,1,0:T(8,128)(2,1)S(1)}, u32[]{:S(2)}, u32[]{:S(2)}) collective-permute-start(bf16[1,24,5248]{2,1,0:T(8,128)(2,1)S(1)} %get-tuple-element.105), channel_id=1, source_target_pairs={{2,0},{3,1},{6,2},{7,3},{10,6},{11,7},{14,10},{15,11},{12,14},{13,... | collective-permute-start | bytes 755720 | tf_op jit(solution)/shard_map/ppermute | solution.py:368
  34.1 8.7 %collective-permute-start.10 = (bf16[1,24,5248]{2,1,0:T(8,128)(2,1)S(1)}, bf16[1,24,5248]{2,1,0:T(8,128)(2,1)S(1)}, u32[]{:S(2)}, u32[]{:S(2)}) collective-permute-start(bf16[1,24,5248]{2,1,0:T(8,128)(2,1)S(1)} %get-tuple-element.106), channel_id=1, source_target_pairs={{0,2},{1,3},{2,6},{3,7},{6,10},{7,11},{10,14},{11,15},{14,12},{15,... | collective-permute-start | bytes 755720 | tf_op jit(solution)/shard_map/ppermute | solution.py:368
  36.5 3.1 %copy-start.3 = (bf16[6,24,5120]{2,1,0:T(8,128)(2,1)}, bf16[6,24,5120]{2,1,0:T(8,128)(2,1)S(1)}, u32[]{:S(2)}) copy-start(bf16[6,24,5120]{2,1,0:T(8,128)(2,1)S(1)} %add_convert_fusion.1) | copy-start | bytes 4423684
  36.5 3.1 %copy-start.4 = (s32[22]{0:T(128)S(1)}, s32[22]{0:T(128)}, u32[]{:S(2)}) copy-start(s32[22]{0:T(128)} %param.13) | copy-start | bytes 268
  37.5 8.0 %collective-permute-start.13 = (bf16[1,24,5120]{2,1,0:T(8,128)(2,1)}, bf16[1,24,5120]{2,1,0:T(8,128)(2,1)}, u32[]{:S(2)}, u32[]{:S(2)}) collective-permute-start(bf16[1,24,5120]{2,1,0:T(8,128)(2,1)} %get-tuple-element.111), channel_id=1, source_target_pairs={{0,2},{1,3},{2,6},{3,7},{6,10},{7,11},{10,14},{11,15},{14,12},{15,... | collective-permute-start | bytes 737288 | tf_op jit(solution)/shard_map/ppermute | solution.py:368
  38.7 6.8 %collective-permute-start.9 = (bf16[1,24,5120]{2,1,0:T(8,128)(2,1)S(1)}, bf16[1,24,5120]{2,1,0:T(8,128)(2,1)}, u32[]{:S(2)}, u32[]{:S(2)}) collective-permute-start(bf16[1,24,5120]{2,1,0:T(8,128)(2,1)S(1)} %get-tuple-element.112), channel_id=1, source_target_pairs={{2,0},{3,1},{6,2},{7,3},{10,6},{11,7},{14,10},{15,11},{12,14},{13,... | collective-permute-start | bytes 737288 | tf_op jit(solution)/shard_map/ppermute | solution.py:368
  46.9 6.5 %collective-permute-start.12 = (bf16[1,24,5120]{2,1,0:T(8,128)(2,1)S(1)}, bf16[1,24,5120]{2,1,0:T(8,128)(2,1)S(1)}, u32[]{:S(2)}, u32[]{:S(2)}) collective-permute-start(bf16[1,24,5120]{2,1,0:T(8,128)(2,1)S(1)} %get-tuple-element.110), channel_id=1, source_target_pairs={{2,0},{3,1},{6,2},{7,3},{10,6},{11,7},{14,10},{15,11},{12,14},{13,... | collective-permute-start | bytes 737288 | tf_op jit(solution)/shard_map/ppermute | solution.py:368
  48.8 7.6 %collective-permute-start.14 = (bf16[1,24,5248]{2,1,0:T(8,128)(2,1)S(1)}, bf16[1,24,5248]{2,1,0:T(8,128)(2,1)S(1)}, u32[]{:S(2)}, u32[]{:S(2)}) collective-permute-start(bf16[1,24,5248]{2,1,0:T(8,128)(2,1)S(1)} %add_convert_fusion.4), channel_id=1, source_target_pairs={{0,2},{1,3},{2,6},{3,7},{6,10},{7,11},{10,14},{11,15},{14,12},{15,... | collective-permute-start | bytes 755720 | tf_op jit(solution)/shard_map/ppermute | solution.py:368
  49.2 14.2 %collective-permute-start.17 = (bf16[1,24,5120]{2,1,0:T(8,128)(2,1)S(1)}, bf16[1,24,5120]{2,1,0:T(8,128)(2,1)S(1)}, u32[]{:S(2)}, u32[]{:S(2)}) collective-permute-start(bf16[1,24,5120]{2,1,0:T(8,128)(2,1)S(1)} %get-tuple-element.109), channel_id=1, source_target_pairs={{0,2},{1,3},{2,6},{3,7},{6,10},{7,11},{10,14},{11,15},{14,12},{15,... | collective-permute-start | bytes 737288 | tf_op jit(solution)/shard_map/ppermute | solution.py:368
  54.4 9.0 %collective-permute-start.18 = (bf16[1,24,5120]{2,1,0:T(8,128)(2,1)S(1)}, bf16[1,24,5120]{2,1,0:T(8,128)(2,1)S(1)}, u32[]{:S(2)}, u32[]{:S(2)}) collective-permute-start(bf16[1,24,5120]{2,1,0:T(8,128)(2,1)S(1)} %add_convert_fusion.9), channel_id=1, source_target_pairs={{2,0},{3,1},{6,2},{7,3},{10,6},{11,7},{14,10},{15,11},{12,14},{13,... | collective-permute-start | bytes 737288 | tf_op jit(solution)/shard_map/ppermute | solution.py:368
  61.3 14.1 %collective-permute-start.21 = (bf16[1,24,4096]{2,1,0:T(8,128)(2,1)S(1)}, bf16[1,24,4096]{2,1,0:T(8,128)(2,1)S(1)}, u32[]{:S(2)}, u32[]{:S(2)}) collective-permute-start(bf16[1,24,4096]{2,1,0:T(8,128)(2,1)S(1)} %attend_part.2.refs_0_), channel_id=1, source_target_pairs={{2,0},{3,1},{6,2},{7,3},{10,6},{11,7},{14,10},{15,11},{12,14},{13,... | collective-permute-start | bytes 589832 | tf_op jit(solution)/shard_map/ppermute | solution.py:368
  63.0 11.4 %collective-permute-start.20 = (bf16[1,24,4096]{2,1,0:T(8,128)(2,1)S(1)}, bf16[1,24,4096]{2,1,0:T(8,128)(2,1)S(1)}, u32[]{:S(2)}, u32[]{:S(2)}) collective-permute-start(bf16[1,24,4096]{2,1,0:T(8,128)(2,1)S(1)} %attend_part.2.refs_0_), channel_id=1, source_target_pairs={{0,2},{1,3},{2,6},{3,7},{6,10},{7,11},{10,14},{11,15},{14,12},{15,... | collective-permute-start | bytes 589832 | tf_op jit(solution)/shard_map/ppermute | solution.py:368
  68.2 8.3 %collective-permute-start.19 = (bf16[1,24,4096]{2,1,0:T(8,128)(2,1)S(1)}, bf16[1,24,4096]{2,1,0:T(8,128)(2,1)S(1)}, u32[]{:S(2)}, u32[]{:S(2)}) collective-permute-start(bf16[1,24,4096]{2,1,0:T(8,128)(2,1)S(1)} %attend_part.3.refs_0_), channel_id=1, source_target_pairs={{2,0},{3,1},{6,2},{7,3},{10,6},{11,7},{14,10},{15,11},{12,14},{13,... | collective-permute-start | bytes 589832 | tf_op jit(solution)/shard_map/ppermute | solution.py:368
  69.9 8.2 %collective-permute-start.24 = (bf16[1,24,4096]{2,1,0:T(8,128)(2,1)S(1)}, bf16[1,24,4096]{2,1,0:T(8,128)(2,1)S(1)}, u32[]{:S(2)}, u32[]{:S(2)}) collective-permute-start(bf16[1,24,4096]{2,1,0:T(8,128)(2,1)S(1)} %attend_part.3.refs_0_), channel_id=1, source_target_pairs={{0,2},{1,3},{2,6},{3,7},{6,10},{7,11},{10,14},{11,15},{14,12},{15,... | collective-permute-start | bytes 589832 | tf_op jit(solution)/shard_map/ppermute | solution.py:368
  74.4 8.2 %collective-permute-start.23 = (bf16[1,24,4096]{2,1,0:T(8,128)(2,1)S(1)}, bf16[1,24,4096]{2,1,0:T(8,128)(2,1)S(1)}, u32[]{:S(2)}, u32[]{:S(2)}) collective-permute-start(bf16[1,24,4096]{2,1,0:T(8,128)(2,1)S(1)} %collective-permute-done.20.refs_7_), channel_id=1, source_target_pairs={{0,2},{1,3},{2,6},{3,7},{6,10},{7,11},{10,14},{11,15},{14,12},{15,... | collective-permute-start | bytes 589832 | tf_op jit(solution)/shard_map/ppermute | solution.py:368
  75.5 8.2 %collective-permute-start.25 = (bf16[1,24,4096]{2,1,0:T(8,128)(2,1)S(1)}, bf16[1,24,4096]{2,1,0:T(8,128)(2,1)S(1)}, u32[]{:S(2)}, u32[]{:S(2)}) collective-permute-start(bf16[1,24,4096]{2,1,0:T(8,128)(2,1)S(1)} %collective-permute-done.21.refs_1_), channel_id=1, source_target_pairs={{2,0},{3,1},{6,2},{7,3},{10,6},{11,7},{14,10},{15,11},{12,14},{13,... | collective-permute-start | bytes 589832 | tf_op jit(solution)/shard_map/ppermute | solution.py:368
  76.5 9.9 %collective-permute-start.22 = (bf16[1,24,4096]{2,1,0:T(8,128)(2,1)S(1)}, bf16[1,24,4096]{2,1,0:T(8,128)(2,1)S(1)}, u32[]{:S(2)}, u32[]{:S(2)}) collective-permute-start(bf16[1,24,4096]{2,1,0:T(8,128)(2,1)S(1)} %collective-permute-done.19.refs_1_), channel_id=1, source_target_pairs={{2,0},{3,1},{6,2},{7,3},{10,6},{11,7},{14,10},{15,11},{12,14},{13,... | collective-permute-start | bytes 589832 | tf_op jit(solution)/shard_map/ppermute | solution.py:368
  78.1 10.3 %collective-permute-start.28 = (bf16[1,24,4096]{2,1,0:T(8,128)(2,1)S(1)}, bf16[1,24,4096]{2,1,0:T(8,128)(2,1)S(1)}, u32[]{:S(2)}, u32[]{:S(2)}) collective-permute-start(bf16[1,24,4096]{2,1,0:T(8,128)(2,1)S(1)} %collective-permute-done.24.refs_7_), channel_id=1, source_target_pairs={{0,2},{1,3},{2,6},{3,7},{6,10},{7,11},{10,14},{11,15},{14,12},{15,... | collective-permute-start | bytes 589832 | tf_op jit(solution)/shard_map/ppermute | solution.py:368
  82.6 7.9 %collective-permute-start.27 = (bf16[1,24,4096]{2,1,0:T(8,128)(2,1)S(1)}, bf16[1,24,4096]{2,1,0:T(8,128)(2,1)S(1)}, u32[]{:S(2)}, u32[]{:S(2)}) collective-permute-start(bf16[1,24,4096]{2,1,0:T(8,128)(2,1)S(1)} %collective-permute-done.23.refs_6_), channel_id=1, source_target_pairs={{0,2},{1,3},{2,6},{3,7},{6,10},{7,11},{10,14},{11,15},{14,12},{15,... | collective-permute-start | bytes 589832 | tf_op jit(solution)/shard_map/ppermute | solution.py:368
  86.4 5.7 %collective-permute-start.26 = (bf16[1,24,4096]{2,1,0:T(8,128)(2,1)S(1)}, bf16[1,24,4096]{2,1,0:T(8,128)(2,1)S(1)}, u32[]{:S(2)}, u32[]{:S(2)}) collective-permute-start(bf16[1,24,4096]{2,1,0:T(8,128)(2,1)S(1)} %collective-permute-done.22.refs_2_), channel_id=1, source_target_pairs={{2,0},{3,1},{6,2},{7,3},{10,6},{11,7},{14,10},{15,11},{12,14},{13,... | collective-permute-start | bytes 589832 | tf_op jit(solution)/shard_map/ppermute | solution.py:368
  86.8 7.4 %collective-permute-start.31 = (bf16[1,24,4096]{2,1,0:T(8,128)(2,1)S(1)}, bf16[1,24,4096]{2,1,0:T(8,128)(2,1)S(1)}, u32[]{:S(2)}, u32[]{:S(2)}) collective-permute-start(bf16[1,24,4096]{2,1,0:T(8,128)(2,1)S(1)} %collective-permute-done.25.refs_2_), channel_id=1, source_target_pairs={{2,0},{3,1},{6,2},{7,3},{10,6},{11,7},{14,10},{15,11},{12,14},{13,... | collective-permute-start | bytes 589832 | tf_op jit(solution)/shard_map/ppermute | solution.py:368
  88.4 9.6 %collective-permute-start.30 = (bf16[1,24,4096]{2,1,0:T(8,128)(2,1)S(1)}, bf16[1,24,4096]{2,1,0:T(8,128)(2,1)S(1)}, u32[]{:S(2)}, u32[]{:S(2)}) collective-permute-start(bf16[1,24,4096]{2,1,0:T(8,128)(2,1)S(1)} %collective-permute-done.28.refs_6_), channel_id=1, source_target_pairs={{0,2},{1,3},{2,6},{3,7},{6,10},{7,11},{10,14},{11,15},{14,12},{15,... | collective-permute-start | bytes 589832 | tf_op jit(solution)/shard_map/ppermute | solution.py:368
  90.5 5.7 %collective-permute-start.32 = (bf16[1,24,4096]{2,1,0:T(8,128)(2,1)S(1)}, bf16[1,24,4096]{2,1,0:T(8,128)(2,1)S(1)}, u32[]{:S(2)}, u32[]{:S(2)}) collective-permute-start(bf16[1,24,4096]{2,1,0:T(8,128)(2,1)S(1)} %collective-permute-done.27.refs_5_), channel_id=1, source_target_pairs={{0,2},{1,3},{2,6},{3,7},{6,10},{7,11},{10,14},{11,15},{14,12},{15,... | collective-permute-start | bytes 589832 | tf_op jit(solution)/shard_map/ppermute | solution.py:368
  92.0 6.0 %collective-permute-start.29 = (bf16[1,24,4096]{2,1,0:T(8,128)(2,1)S(1)}, bf16[1,24,4096]{2,1,0:T(8,128)(2,1)S(1)}, u32[]{:S(2)}, u32[]{:S(2)}) collective-permute-start(bf16[1,24,4096]{2,1,0:T(8,128)(2,1)S(1)} %collective-permute-done.26.refs_3_), channel_id=1, source_target_pairs={{2,0},{3,1},{6,2},{7,3},{10,6},{11,7},{14,10},{15,11},{12,14},{13,... | collective-permute-start | bytes 589832 | tf_op jit(solution)/shard_map/ppermute | solution.py:368
  98.0 3.6 %copy-start.1 = (bf16[352,512]{1,0:T(8,128)(2,1)S(1)}, bf16[352,512]{1,0:T(8,128)(2,1)}, u32[]{:S(2)}) copy-start(bf16[352,512]{1,0:T(8,128)(2,1)} %x_ref.4) | copy-start | bytes 1081348
  99.8 1.8 %collective-permute-start.33 = (f32[192,512]{1,0:T(8,128)S(1)}, f32[192,512]{1,0:T(8,128)S(1)}, u32[]{:S(2)}, u32[]{:S(2)}) collective-permute-start(f32[192,512]{1,0:T(8,128)S(1)} %get-tuple-element.104), channel_id=1, source_target_pairs={{0,1},{1,0},{2,3},{3,2},{4,5},{5,4},{6,7},{7,6},{8,9},{9,8},{10,11... | collective-permute-start | bytes 1179656 | tf_op jit(solution)/shard_map/ppermute | solution.py:374

commit v4 on v3

--- a/solution.py
+++ b/solution.py
@@ -64,6 +64,49 @@
     return [(k, w) for w in (0, 1) for k in range(chips)]
 
 
+def split_rows(rows):
+    assert rows % 8 == 6
+    return rows // 8
+
+
+def packed_width(rows, width):
+    return split_rows(rows) * width + 3 * width // 4
+
+
+def pack_rest(a):
+    row = lax.broadcasted_iota(jnp.int32, (8, HD), 0)
+    b, c, d = pltpu.roll(a[1], 6, 0), pltpu.roll(a[2], 4, 0), pltpu.roll(a[3], 2, 0)
+    return a[0] + jnp.where(row >= 6, b, 0.0), jnp.where(row < 4, b, c), jnp.where(row < 2, c, d)
+
+
+def unpack_rest(tiles, q):
+    row = lax.broadcasted_iota(jnp.int32, (8, HD), 0)
+    first, second, third = tiles
+    if q == 0:
+        return jnp.where(row < 6, first, 0.0)
+    if q == 1:
+        return pltpu.roll(jnp.where(row >= 6, first, jnp.where(row < 4, second, 0.0)), 2, 0)
+    if q == 2:
+        return pltpu.roll(jnp.where(row >= 4, second, jnp.where(row < 2, third, 0.0)), 4, 0)
+    return pltpu.roll(jnp.where(row >= 2, third, 0.0), 6, 0)
+
+
+def pack_tiles(rows, width, lane, tiles, write):
+    full = split_rows(rows)
+    for i in range(full):
+        for q in range(4):
+            write(i * width + lane + q * HD, tiles[q][i * 8 : (i + 1) * 8])
+    for i, rest in enumerate(pack_rest([a[full * 8 : full * 8 + 8] for a in tiles])):
+        write(full * width + lane * 3 // 4 + i * HD, rest)
+
+
+def unpack_tile(rows, width, lane, read):
+    full = split_rows(rows)
+    group, q = lane // (4 * HD) * 4 * HD, lane // HD % 4
+    rest = [read(full * width + group * 3 // 4 + i * HD) for i in range(3)]
+    return jnp.concatenate([read(i * width + lane) for i in range(full)] + [unpack_rest(rest, q)], axis=0)
+
+
 def slot_devices(order, slots):
     chips = len(order)
     me = lax.axis_index("gx")
@@ -86,7 +129,7 @@
 
 
 def qkv_kernel(order, index, rows, pad, x_ref, gain_ref, w_ref, *refs):
-    out_refs, (token, xs_ref, w_buf, in_sem) = refs[:4], refs[4:]
+    out_refs, (token, xs_ref, x_buf, gain_buf, w_buf, in_sem) = refs[:4], refs[4:]
     token[...] = jnp.zeros_like(token)
     total, depth = x_ref.shape
     begin, heads = PARTS[index]
@@ -101,16 +144,26 @@
 
     where = [(ref, at) for ref in out_refs for at in range(ref.shape[0])]
 
-    def write(slot, lanes, value):
+    def write(slot, lane, value):
         ref, at = where[slot]
-        ref[at, :, lanes] = value
-
+        ref[at, :, lane : lane + HD] = value.astype(BF)
+
+    small = [
+        pltpu.make_async_copy(x_ref, x_buf, in_sem.at[pieces]),
+        pltpu.make_async_copy(gain_ref, gain_buf, in_sem.at[pieces + 1]),
+    ]
+    for copy in small:
+        copy.start()
     for j in range(LOADS_AHEAD):
         load(j).start()
-    features = jnp.dot(picker(order, slots, rows, pad, total), x_ref[...], preferred_element_type=F32)
-    xs_ref[...] = (features * gain_ref[...]).astype(BF)
+    pick = picker(order, slots, rows, pad, total)
+    for copy in small:
+        copy.wait()
+    features = jnp.dot(pick, x_buf[...], preferred_element_type=F32)
+    xs_ref[...] = (features * gain_buf[...]).astype(BF)
     width = pieces * piece
-    extra = out_refs[0].shape[2] - width
+    packed = packed_width(rows, width)
+    extra = (out_refs[0].shape[2] - packed) // 3
     if extra:
         me = lax.axis_index("gx")
         square = jnp.sum(features * features, axis=1, keepdims=True)
@@ -120,7 +173,8 @@
         low = square - high - mid
         held = jnp.where(lane == 3 * me, high, 0.0) + jnp.where(lane == 3 * me + 1, mid, 0.0) + jnp.where(lane == 3 * me + 2, low, 0.0)
         for slot in range(len(slots)):
-            write(slot, slice(width, None), held[slot * pad : (slot + 1) * pad].astype(BF))
+            for i in range(3):
+                write(slot, packed + i * extra, held[slot * pad + i * 8 : slot * pad + i * 8 + 8])
     done = 0
     for group in PIECE_GROUPS:
         for j in range(done, done + group):
@@ -130,7 +184,10 @@
         lanes = slice(done * piece, (done + group) * piece)
         out = jnp.dot(xs_ref[...], w_buf[:, lanes], preferred_element_type=F32)
         for slot in range(len(slots)):
-            write(slot, lanes, out[slot * pad : (slot + 1) * pad].astype(BF))
+            block = out[slot * pad : (slot + 1) * pad]
+            for lane in range(0, group * piece, 4 * HD):
+                tiles = [block[:, lane + q * HD : lane + (q + 1) * HD] for q in range(4)]
+                pack_tiles(rows, width, done * piece + lane, tiles, functools.partial(write, slot))
         done += group
 
 
@@ -140,18 +197,20 @@
     depth = x.shape[1]
     chips = len(order)
     extra = -(-6 * chips // 128) * 128 if index == 0 else 0
-    width = pieces * piece + extra
+    width = packed_width(rows, pieces * piece) + 3 * extra
     vmem = pl.BlockSpec(memory_space=pltpu.VMEM)
     return pl.pallas_call(
         functools.partial(qkv_kernel, order, index, rows, pad),
-        in_specs=[vmem, vmem, pl.BlockSpec(memory_space=pltpu.HBM)],
+        in_specs=[pl.BlockSpec(memory_space=pltpu.HBM)] * 3,
         out_specs=[vmem] * 5,
         scratch_shapes=[
             pltpu.VMEM((2 * chips * pad, depth), BF),
+            pltpu.VMEM(x.shape, BF),
+            pltpu.VMEM(gain.shape, F32),
             pltpu.VMEM((depth, pieces * piece), BF),
-            pltpu.SemaphoreType.DMA((pieces,)),
+            pltpu.SemaphoreType.DMA((pieces + 2,)),
         ],
-        out_shape=[jax.ShapeDtypeStruct((n, pad, width), BF) for n in (2, chips - 2, 2, chips - 2)] + [TOKEN],
+        out_shape=[jax.ShapeDtypeStruct((n, 8, width), BF) for n in (2, chips - 2, 2, chips - 2)] + [TOKEN],
         compiler_params=pltpu.CompilerParams(vmem_limit_bytes=51 * MIB),
         cost_estimate=pl.CostEstimate(flops=1, bytes_accessed=1, transcendentals=0),
         name="qkv_part",
@@ -179,10 +238,13 @@
     cos = cos_ref[...]
     sin = sin_ref[...]
 
+    def summed(lane):
+        lanes = slice(lane, lane + HD)
+        got = own_ref[0, :, lanes].astype(F32)
+        return got + (left_ref[0, :, lanes].astype(F32) + right_ref[0, :, lanes].astype(F32))
+
     def tile(t):
-        lanes = slice(t * HD, (t + 1) * HD)
-        got = own_ref[0, :, lanes].astype(F32)
-        return (got + (left_ref[0, :, lanes].astype(F32) + right_ref[0, :, lanes].astype(F32))) * inv
+        return unpack_tile(rows, (GROUP + 2) * heads * HD, t * HD, summed) * inv
 
     def turned(t):
         a = tile(t)
@@ -196,6 +258,9 @@
     c2 = lax.broadcasted_iota(jnp.int32, (full, pad), 1)
     spread = jnp.where(c2 == r2 // GROUP, 1.0, 0.0).astype(BF)
     valid = lax.broadcasted_iota(jnp.int32, (live, slots), 1) < len_ref[...]
+
+    def write(lane, value):
+        out_ref[0, :, lane : lane + HD] = value.astype(BF)
 
     queries, owns, values_new = [], [], []
     for kk in range(heads):
@@ -237,8 +302,9 @@
         mixed = m_ref[kk] + own_weights[kk] * values_new[kk]
         mixed = jnp.concatenate([mixed, jnp.zeros((full - live, HD), F32)], axis=0).astype(BF)
         mixed = jnp.dot(by_head, mixed, preferred_element_type=F32)
-        for g in range(GROUP):
-            out_ref[0, :, (kk * GROUP + g) * HD : (kk * GROUP + g + 1) * HD] = mixed[g * pad : (g + 1) * pad].astype(BF)
+        tiles = [mixed[g * pad : (g + 1) * pad] for g in range(GROUP)]
+        for g in range(0, GROUP, 4):
+            pack_tiles(rows, heads * GROUP * HD, (kk * GROUP + g) * HD, tiles[g : g + 4], write)
 
 
 def load(name, limit, arrays, begin=0, count=None):
@@ -276,7 +342,7 @@
         functools.partial(attend_kernel, part, rows, pad),
         in_specs=[vmem] * 7 + [pl.BlockSpec(memory_space=pltpu.HBM)] * 2,
         out_specs=vmem,
-        out_shape=jax.ShapeDtypeStruct((1, pad, heads * GROUP * HD), BF),
+        out_shape=jax.ShapeDtypeStruct((1, 8, packed_width(rows, heads * GROUP * HD)), BF),
         scratch_shapes=[
             pltpu.VMEM((heads, rows * GROUP, slots), F32),
             pltpu.VMEM((heads, rows * GROUP, HD), F32),
@@ -290,55 +356,77 @@
     )(own, from_left, from_right, inv, cos, sin, lens, keys, values)
 
 
-def out_kernel(has_prior, *refs):
+def features_kernel(order, rows, pad, x_ref, x_other_ref, mine_ref, theirs_ref):
+    slots = gathered_slots(len(order))
+    pick = picker(order, slots[: len(order)], rows, pad, x_ref.shape[0])
+    mine_ref[...] = jnp.dot(pick, x_ref[...], preferred_element_type=F32)
+    theirs_ref[...] = jnp.dot(pick, x_other_ref[...], preferred_element_type=F32)
+
+
+def features_of(order, rows, pad, x, x_other):
+    vmem = pl.BlockSpec(memory_space=pltpu.VMEM)
+    return pl.pallas_call(
+        functools.partial(features_kernel, order, rows, pad),
+        in_specs=[vmem] * 2,
+        out_specs=[vmem] * 2,
+        out_shape=[jax.ShapeDtypeStruct((len(order) * pad, x.shape[1]), F32)] * 2,
+        compiler_params=pltpu.CompilerParams(vmem_limit_bytes=8 * MIB),
+        cost_estimate=pl.CostEstimate(flops=1, bytes_accessed=1, transcendentals=0),
+        name="features",
+    )(x, x_other)
+
+
+def out_kernel(rows, pad, *refs):
     outs, a_ref = refs[-3:-1], refs[-1]
-    priors = refs[-5:-3] if has_prior else (None, None)
-    blocks = refs[: -7 if has_prior else -5]
-    weights = refs[len(blocks) : len(blocks) + 2]
-    pad = blocks[0].shape[1]
+    priors, weights, blocks = refs[-5:-3], refs[-7:-5], refs[:-7]
+    width = weights[0].shape[0]
     for b, block in enumerate(blocks):
-        a_ref[b * pad : (b + 1) * pad] = block[0].astype(F32)
+        for lane in range(0, width, HD):
+            tile = unpack_tile(rows, width, lane, lambda at: block[0, :, at : at + HD].astype(F32))
+            a_ref[b * pad : (b + 1) * pad, lane : lane + HD] = tile
     left = a_ref[...].astype(BF)
     for w_ref, prior_ref, out_ref in zip(weights, priors, outs):
-        prod = jnp.dot(left, w_ref[...], preferred_element_type=F32)
-        out_ref[...] = prod + prior_ref[...] if has_prior else prod
-
-
-def project_out(pad, blocks, weights, prior):
+        out_ref[...] = (prior_ref[...] + jnp.dot(left, w_ref[...], preferred_element_type=F32)).astype(out_ref.dtype)
+
+
+def project_out(rows, pad, blocks, weights, prior, dtype):
     count = len(blocks)
     depth, cols = weights[0].shape
     vmem = pl.BlockSpec(memory_space=pltpu.VMEM)
-    args = [*blocks, *weights] + ([] if prior is None else list(prior))
+    args = [*blocks, *weights, *prior]
     return pl.pallas_call(
-        functools.partial(out_kernel, prior is not None),
+        functools.partial(out_kernel, rows, pad),
         in_specs=[vmem] * len(args),
         out_specs=[vmem] * 2,
         scratch_shapes=[pltpu.VMEM((count * pad, depth), F32)],
-        out_shape=[jax.ShapeDtypeStruct((count * pad, cols), F32)] * 2,
+        out_shape=[jax.ShapeDtypeStruct((count * pad, cols), dtype)] * 2,
         compiler_params=pltpu.CompilerParams(vmem_limit_bytes=12 * MIB),
         cost_estimate=pl.CostEstimate(flops=1, bytes_accessed=1, transcendentals=0),
         name="out_part",
     )(*args)
 
 
-def finish_kernel(order, rows, pad, x_ref, mine_ref, other_ref, out_ref):
-    pick = picker(order, gathered_slots(len(order)), rows, pad, x_ref.shape[0])
-    features = jnp.dot(pick, x_ref[...], preferred_element_type=F32)
-    result = (features + jnp.concatenate([mine_ref[...], other_ref[...]], axis=0)).astype(BF)
-    out_ref[...] = lax.dot_general(pick, result, (((0,), (0,)), ((), ())), preferred_element_type=F32).astype(BF)
-
-
-def finish(order, rows, pad, x, mine, other):
+def place_kernel(order, rows, pad, which, rows_ref, *refs):
+    out_ref = refs[-1]
+    chips = len(order)
+    pick = picker(order, gathered_slots(chips)[which * chips : (which + 1) * chips], rows, pad, out_ref.shape[0])
+    placed = lax.dot_general(pick, rows_ref[...], (((0,), (0,)), ((), ())), preferred_element_type=F32)
+    if len(refs) > 1:
+        placed = placed + refs[0][...].astype(F32)
+    out_ref[...] = placed.astype(BF)
+
+
+def place(order, rows, pad, which, result, *other):
     vmem = pl.BlockSpec(memory_space=pltpu.VMEM)
     return pl.pallas_call(
-        functools.partial(finish_kernel, order, rows, pad),
-        in_specs=[vmem] * 3,
+        functools.partial(place_kernel, order, rows, pad, which),
+        in_specs=[vmem] * (1 + len(other)),
         out_specs=vmem,
-        out_shape=jax.ShapeDtypeStruct(x.shape, BF),
-        compiler_params=pltpu.CompilerParams(vmem_limit_bytes=16 * MIB),
+        out_shape=jax.ShapeDtypeStruct((2 * len(order) * rows, result.shape[1]), BF),
+        compiler_params=pltpu.CompilerParams(vmem_limit_bytes=8 * MIB),
         cost_estimate=pl.CostEstimate(flops=1, bytes_accessed=1, transcendentals=0),
-        name="finish",
-    )(x, mine, other)
+        name="place",
+    )(result, *other)
 
 
 def wide(a):
@@ -347,8 +435,7 @@
 
 def issue_order(steps):
     names = ["P0", "R0", "P1", "R0", "R1"] + ["R0", "R1"] * (steps - 2) + ["R1"]
-    names += ["T0", "G0", "T1", "G1", "L0", "G0", "G1", "L1"] + ["G0", "G1"] * (steps - 2) + ["O0", "O1"]
-    return names
+    return names + ["T0", "G0", "T1", "G1", "G0", "W0", "G1", "G0", "W1", "G1"] + ["G0", "G1"] * (steps - 3) + ["O0", "O1"]
 
 
 def per_device(order, hidden_in, norm_gain, w_qkv, w_out, cache_keys, cache_values, lengths):
@@ -382,7 +469,7 @@
         return jnp.concatenate([cos, cos], axis=1), jnp.concatenate([-sin, sin], axis=1), jnp.repeat(lengths, GROUP)[:, None]
 
     gain = norm_gain[None, :]
-    inv, w_other, places, sums = [None], [None], [None], [None]
+    inv, w_other, x_other, places, sums, weights = [None], [None], [None], [None], [None], {}
 
     def part_steps(index):
         part = PARTS[index]
@@ -418,17 +505,21 @@
             moved = {**moved, **ring(sent)}
             if index == 1 and step == 0:
                 w_other[0] = cross(tied(w_out))
+                x_other[0] = cross(tied(hidden_in))
             if index == 1 and step == 1:
                 places[0] = positions(tied(lengths))
+                sums[0] = features_of(order, rows, pad, hidden_in, x_other[0])
             yield
         own = piece(0)
         if index == 0:
-            lanes = slice((GROUP + 2) * part[1] * HD, None)
-            parts = [own, moved["up"], moved["down"]]
-            square = jnp.sum(sum(wide(a[0, :, lanes]) for a in parts), axis=1)
+            first = packed_width(rows, (GROUP + 2) * part[1] * HD)
+            terms = sum(wide(a[0, :, first:]) for a in (own, moved["up"], moved["down"]))
+            square = jnp.sum(terms.reshape(8, 3, -1), axis=2).T.reshape(pad)
             inv[0] = jnp.broadcast_to(lax.rsqrt(square / D + 1e-05)[:, None], (pad, HD))
         own = tied(own)
-        if index == 1:
+        if index == 0:
+            own = after(own, x_other[0])
+        if index == 1 and 1 not in weights:
             own = after(own, w_other[0])
         attended = attend(part, rows, pad, own, moved["up"], moved["down"], inv[0], *places[0], cache_keys, cache_values)
         before[0] = attended
@@ -439,20 +530,22 @@
             for way, a in ring(sent).items():
                 blocks[-sign[way] * (step + 1) % chips] = a
             yield
-            if step == index:
-                held = (tied(w_out), w_other[0])
-                weights, before[0] = load("load_weights", 40, held, part[0] * GROUP * HD, part[1] * GROUP * HD)
-                yield
-        sums[0] = project_out(pad, [blocks[k] for k in range(chips)], weights, sums[0])
-        if index < len(PARTS) - 1:
-            before[0] = sums[0]
+        last = index == len(PARTS) - 1
+        sums[0] = project_out(rows, pad, [blocks[k] for k in range(chips)], weights[index], sums[0], BF if last else F32)
         yield
 
     running = [part_steps(i) for i in range(len(PARTS))]
     for name in issue_order(chips // 2):
-        next(running[int(name[-1])])
+        index = int(name[-1])
+        if name[0] == "W":
+            begin, heads = PARTS[index]
+            held = (tied(w_out), w_other[0])
+            weights[index], before[0] = load("load_weights", 40, held, begin * GROUP * HD, heads * GROUP * HD)
+        else:
+            next(running[index])
     mine, theirs = sums[0]
-    return finish(order, rows, pad, hidden_in, mine, cross(theirs))
+    other = cross(theirs)
+    return place(order, rows, pad, 1, other, place(order, rows, pad, 0, mine))
 
 
 def solution(mesh):

time: 103 us -> 99.2 us (0.963)
  waiting for transfers between devices: 31.8 us -> 26.2 us
  Pallas kernels: 33.2 us -> 35 us
    ppermute x28, waiting for transfers between devices: 28.7 us -> 23.8 us  [ring(): lax.ppermute(a, 'gx', up_pairs if way == 'up' else down_pairs)]
    pallas_call x3 -> x5, Pallas kernels: 5 us -> 6.44 us  [the longest x2 3.61 us: project_out(): pl.pallas_call(functools.partial(out_kernel, rows, pad), in_specs=[vmem]...]
    ppermute x28, starting transfers between devices: 29.4 us -> 30.5 us  [ring(): lax.ppermute(a, 'gx', up_pairs if way == 'up' else down_pairs)]
    ppermute x6 -> x7, waiting for transfers between devices: 3.15 us -> 2.43 us  [cross(): return lax.ppermute(a, 'gx', sibling)]
  transfers between devices with their start and end apart: 34 -> 35, of which waited for: 17 -> 16; matrix products, arithmetic and copies ran while one was open for 5% -> 5% of each run, Pallas kernels for 24% -> 27%
where the time goes in v4:
time: 99.2 us; the launch traced here: 98.9 us
  Pallas kernels  35 us (35%)
  starting transfers between devices  31.7 us (32%)
  waiting for transfers between devices  26.2 us (26%)
  other arithmetic  4.61 us (5%)
  local copies, waits for them, and re-layouts  1.1 us (1%)
    ppermute x28, starting transfers between devices, ring(): lax.ppermute(a, 'gx', up_pairs if way == 'up' else down_pairs)  30.5 us
    ppermute x28, waiting for transfers between devices, ring(): lax.ppermute(a, 'gx', up_pairs if way == 'up' else down_pairs)  23.8 us
    pallas_call x2, Pallas kernels, project(): pl.pallas_call(functools.partial(qkv_kernel, order, index, rows, pad), in...  10.9 us
    pallas_call x2, Pallas kernels, attend(): pl.pallas_call(functools.partial(attend_kernel, part, rows, pad), in_spec...  9.59 us
    pallas_call x2, Pallas kernels, load(): pl.pallas_call(kernel, in_specs=[pl.BlockSpec(memory_space=pltpu.HBM)] *...  8.15 us
    pallas_call x2, Pallas kernels, project_out(): pl.pallas_call(functools.partial(out_kernel, rows, pad), in_specs=[vmem]...  3.61 us
    convert_element_type x6, other arithmetic, part_steps(): sent[way] = (wide(sent[way]) + wide(tied(moved[way]))).astype(BF)  3.44 us
    ppermute x7, waiting for transfers between devices, cross(): return lax.ppermute(a, 'gx', sibling)  2.43 us
  transfers between devices with their start and end apart: 35, of which 16 were waited for; matrix products, arithmetic and copies ran while one was open for 5% of the time, Pallas kernels for 27%

profile of v4, /device:TPU:0, one launch (start us, length us, event | category | flops | bytes accessed | tf_op | source)
XLA Modules:
  0.0 98.9 jit_solution(16484634256122789311)
XLA Ops:
  0.0 0.7 copy-done
  0.7 5.5 %qkv_part.2 = (bf16[2,8,14464]{2,1,0:T(8,128)(2,1)S(1)}, bf16[6,8,14464]{2,1,0:T(8,128)(2,1)S(1)}, bf16[2,8,14464]{2,1,0:T(8,128)(2,1)S(1)}, bf16[6,8,14464]{2,1,0:T(8,128)(2,1)}, f32[8,128]{1,0:T(8,128)}) custom-call(bf16[352,512]{1,0:T(8,128)(2,1)} %x_ref.4, f32[1,512]{1,0:T(1,128)S(1)} %bitcast.5, bf16[512,10240]{1,0:T(8,128)(2,1)} %w_ref.3), custom_call_target="tpu_custom_call" | custom-call | flops 1 | bytes 1 | tf_op jit(solution)/shard_map/qkv_part/pallas_call | solution.py:202
  6.2 0.5 collective-permute-start
  6.8 1.4 %collective-permute-done = bf16[2,8,14464]{2,1,0:T(8,128)(2,1)S(1)} collective-permute-done((bf16[2,8,14464]{2,1,0:T(8,128)(2,1)S(1)}, bf16[2,8,14464]{2,1,0:T(8,128)(2,1)S(1)}, u32[]{:S(2)}, u32[]{:S(2)}) %collective-permute-start) | collective-permute-done | bytes 462880 | tf_op jit(solution)/shard_map/ppermute | solution.py:461
  8.3 2.9 %collective-permute-start.3 = (bf16[1,8,14464]{2,1,0:T(8,128)(2,1)S(1)}, bf16[1,8,14464]{2,1,0:T(8,128)(2,1)S(1)}, u32[]{:S(2)}, u32[]{:S(2)}) collective-permute-start(bf16[1,8,14464]{2,1,0:T(8,128)(2,1)S(1)} %get-tuple-element.122), channel_id=1, source_target_pairs={{0,2},{1,3},{2,6},{3,7},{6,10},{7,11},{10,14},{11,15},{14,12},{15,... | collective-permute-start | bytes 694280 | tf_op jit(solution)/shard_map/ppermute | solution.py:455
  11.4 5.3 %qkv_part.3 = (bf16[2,8,14080]{2,1,0:T(8,128)(2,1)S(1)}, bf16[6,8,14080]{2,1,0:T(8,128)(2,1)S(1)}, bf16[2,8,14080]{2,1,0:T(8,128)(2,1)S(1)}, bf16[6,8,14080]{2,1,0:T(8,128)(2,1)}, f32[8,128]{1,0:T(8,128)}) custom-call(bf16[352,512]{1,0:T(8,128)(2,1)} %x_ref.4, f32[1,512]{1,0:T(1,128)S(1)} %bitcast.6, bf16[512,10240]{1,0:T(8,128)(2,1)} %w_ref.3), custom_call_target="tpu_custom_call" | custom-call | flops 1 | bytes 1 | tf_op jit(solution)/shard_map/qkv_part/pallas_call | solution.py:202
  16.8 0.5 collective-permute-start.1
  17.3 1.3 %collective-permute-done.4 = bf16[1,8,14464]{2,1,0:T(8,128)(2,1)S(1)} collective-permute-done((bf16[1,8,14464]{2,1,0:T(8,128)(2,1)S(1)}, bf16[1,8,14464]{2,1,0:T(8,128)(2,1)S(1)}, u32[]{:S(2)}, u32[]{:S(2)}) %collective-permute-start.4) | collective-permute-done | bytes 231456 | tf_op jit(solution)/shard_map/ppermute | solution.py:455
  19.1 1.6 %collective-permute-start.7 = (bf16[1,8,14464]{2,1,0:T(8,128)(2,1)S(1)}, bf16[1,8,14464]{2,1,0:T(8,128)(2,1)S(1)}, u32[]{:S(2)}, u32[]{:S(2)}) collective-permute-start(bf16[1,8,14464]{2,1,0:T(8,128)(2,1)S(1)} %get-tuple-element.116), channel_id=1, source_target_pairs={{0,2},{1,3},{2,6},{3,7},{6,10},{7,11},{10,14},{11,15},{14,12},{15,... | collective-permute-start | bytes 694280 | tf_op jit(solution)/shard_map/ppermute | solution.py:455
  21.4 0.7 collective-permute-start.6
  22.0 1.4 %collective-permute-start.11 = (bf16[1,8,14080]{2,1,0:T(8,128)(2,1)S(1)}, bf16[1,8,14080]{2,1,0:T(8,128)(2,1)S(1)}, u32[]{:S(2)}, u32[]{:S(2)}) collective-permute-start(bf16[1,8,14080]{2,1,0:T(8,128)(2,1)S(1)} %get-tuple-element.123), channel_id=1, source_target_pairs={{0,2},{1,3},{2,6},{3,7},{6,10},{7,11},{10,14},{11,15},{14,12},{15,... | collective-permute-start | bytes 675848 | tf_op jit(solution)/shard_map/ppermute | solution.py:455
  23.5 4.1 %collective-permute-done.7 = bf16[1,8,14464]{2,1,0:T(8,128)(2,1)S(1)} collective-permute-done((bf16[1,8,14464]{2,1,0:T(8,128)(2,1)S(1)}, bf16[1,8,14464]{2,1,0:T(8,128)(2,1)S(1)}, u32[]{:S(2)}, u32[]{:S(2)}) %collective-permute-start.7) | collective-permute-done | bytes 231456 | tf_op jit(solution)/shard_map/ppermute | solution.py:455
  27.6 1.8 %collective-permute-done.8 = bf16[1,8,14464]{2,1,0:T(8,128)(2,1)S(1)} collective-permute-done((bf16[1,8,14464]{2,1,0:T(8,128)(2,1)S(1)}, bf16[1,8,14464]{2,1,0:T(8,128)(2,1)S(1)}, u32[]{:S(2)}, u32[]{:S(2)}) %collective-permute-start.8) | collective-permute-done | bytes 231456 | tf_op jit(solution)/shard_map/ppermute | solution.py:455
  29.5 2.5 %collective-permute-done.6 = bf16[1,8,14080]{2,1,0:T(8,128)(2,1)S(1)} collective-permute-done((bf16[1,8,14080]{2,1,0:T(8,128)(2,1)S(1)}, bf16[1,8,14080]{2,1,0:T(8,128)(2,1)S(1)}, u32[]{:S(2)}, u32[]{:S(2)}) %collective-permute-start.6) | collective-permute-done | bytes 225312 | tf_op jit(solution)/shard_map/ppermute | solution.py:455
  31.9 1.6 %collective-permute-start.10 = (bf16[1,8,14464]{2,1,0:T(8,128)(2,1)S(1)}, bf16[1,8,14464]{2,1,0:T(8,128)(2,1)S(1)}, u32[]{:S(2)}, u32[]{:S(2)}) collective-permute-start(bf16[1,8,14464]{2,1,0:T(8,128)(2,1)S(1)} %get-tuple-element.114), channel_id=1, source_target_pairs={{0,2},{1,3},{2,6},{3,7},{6,10},{7,11},{10,14},{11,15},{14,12},{15,... | collective-permute-start | bytes 694280 | tf_op jit(solution)/shard_map/ppermute | solution.py:455
  34.3 1.0 %add_convert_fusion.12 = (bf16[1,8,14080]{2,1,0:T(8,128)(2,1)}, bf16[1,8,14080]{2,1,0:T(8,128)(2,1)}) fusion(bf16[1,8,14080]{2,1,0:T(8,128)(2,1)S(1)} %collective-permute-done.11, bf16[6,8,14080]{2,1,0:T(8,128)(2,1)S(1)} %add_convert_fusion.1, bf16[1,8,14080]{2,1,0:T(8,128)(2,1)S(1)} %collective-permute-done.6), kind=kLoop, calls=%fused_computation.12 | loop fusion | flops 901120 | bytes 1351680 | tf_op jit(solution)/shard_map/convert_element_type | solution.py:504
  36.0 2.1 %collective-permute-done.10 = bf16[1,8,14464]{2,1,0:T(8,128)(2,1)S(1)} collective-permute-done((bf16[1,8,14464]{2,1,0:T(8,128)(2,1)S(1)}, bf16[1,8,14464]{2,1,0:T(8,128)(2,1)S(1)}, u32[]{:S(2)}, u32[]{:S(2)}) %collective-permute-start.10) | collective-permute-done | bytes 231456 | tf_op jit(solution)/shard_map/ppermute | solution.py:455
  38.1 1.6 %collective-permute-start.13 = (bf16[1,8,14080]{2,1,0:T(8,128)(2,1)}, bf16[1,8,14080]{2,1,0:T(8,128)(2,1)S(1)}, u32[]{:S(2)}, u32[]{:S(2)}) collective-permute-start(bf16[1,8,14080]{2,1,0:T(8,128)(2,1)} %get-tuple-element.119), channel_id=1, source_target_pairs={{0,2},{1,3},{2,6},{3,7},{6,10},{7,11},{10,14},{11,15},{14,12},{15,... | collective-permute-start | bytes 675848 | tf_op jit(solution)/shard_map/ppermute | solution.py:455
  39.8 3.9 %collective-permute-done.9 = bf16[1,8,14080]{2,1,0:T(8,128)(2,1)S(1)} collective-permute-done((bf16[1,8,14080]{2,1,0:T(8,128)(2,1)}, bf16[1,8,14080]{2,1,0:T(8,128)(2,1)S(1)}, u32[]{:S(2)}, u32[]{:S(2)}) %collective-permute-start.9) | collective-permute-done | bytes 225312 | tf_op jit(solution)/shard_map/ppermute | solution.py:455
  43.7 2.2 %collective-permute-start.15 = (bf16[1,8,14464]{2,1,0:T(8,128)(2,1)S(1)}, bf16[1,8,14464]{2,1,0:T(8,128)(2,1)S(1)}, u32[]{:S(2)}, u32[]{:S(2)}) collective-permute-start(bf16[1,8,14464]{2,1,0:T(8,128)(2,1)S(1)} %add_convert_fusion.4), channel_id=1, source_target_pairs={{0,2},{1,3},{2,6},{3,7},{6,10},{7,11},{10,14},{11,15},{14,12},{15,... | collective-permute-start | bytes 694280 | tf_op jit(solution)/shard_map/ppermute | solution.py:455
  45.9 1.2 %add_convert_fusion.10 = (bf16[1,8,14080]{2,1,0:T(8,128)(2,1)S(1)}, bf16[1,8,14080]{2,1,0:T(8,128)(2,1)S(1)}) fusion(bf16[1,8,14080]{2,1,0:T(8,128)(2,1)S(1)} %collective-permute-done.13, bf16[6,8,14080]{2,1,0:T(8,128)(2,1)} %copy-done.1, bf16[1,8,14080]{2,1,0:T(8,128)(2,1)S(1)} %collective-permute-done.9), kind=kLoop, calls=%fused_computation.10 | loop fusion | flops 901120 | bytes 1351680 | tf_op jit(solution)/shard_map/convert_element_type | solution.py:504
  47.2 2.0 %collective-permute-start.18 = (bf16[1,8,14080]{2,1,0:T(8,128)(2,1)S(1)}, bf16[1,8,14080]{2,1,0:T(8,128)(2,1)S(1)}, u32[]{:S(2)}, u32[]{:S(2)}) collective-permute-start(bf16[1,8,14080]{2,1,0:T(8,128)(2,1)S(1)} %get-tuple-element.117), channel_id=1, source_target_pairs={{0,2},{1,3},{2,6},{3,7},{6,10},{7,11},{10,14},{11,15},{14,12},{15,... | collective-permute-start | bytes 675848 | tf_op jit(solution)/shard_map/ppermute | solution.py:455
  49.3 2.8 %collective-permute-done.15.left_ref = bf16[1,8,14464]{2,1,0:T(8,128)(2,1)S(1)} collective-permute-done((bf16[1,8,14464]{2,1,0:T(8,128)(2,1)S(1)}, bf16[1,8,14464]{2,1,0:T(8,128)(2,1)S(1)}, u32[]{:S(2)}, u32[]{:S(2)}) %collective-permute-start.15) | collective-permute-done | bytes 231456 | tf_op jit(solution)/shard_map/ppermute | solution.py:455
  52.1 1.0 %collective-permute-done.12 = bf16[1,8,14080]{2,1,0:T(8,128)(2,1)S(1)} collective-permute-done((bf16[1,8,14080]{2,1,0:T(8,128)(2,1)S(1)}, bf16[1,8,14080]{2,1,0:T(8,128)(2,1)S(1)}, u32[]{:S(2)}, u32[]{:S(2)}) %collective-permute-start.12) | collective-permute-done | bytes 225312 | tf_op jit(solution)/shard_map/ppermute | solution.py:455
  53.1 1.0 %add_convert_fusion.9 = bf16[1,8,14080]{2,1,0:T(8,128)(2,1)S(1)} fusion(bf16[1,8,14080]{2,1,0:T(8,128)(2,1)S(1)} %collective-permute-done.12, bf16[6,8,14080]{2,1,0:T(8,128)(2,1)} %copy-done.1), kind=kLoop, calls=%fused_computation.9 | loop fusion | flops 450560 | bytes 675840 | tf_op jit(solution)/shard_map/convert_element_type | solution.py:504
  54.4 4.8 %attend_part.2.refs_0_ = bf16[1,8,11264]{2,1,0:T(8,128)(2,1)S(1)} custom-call(bf16[1,8,14464]{2,1,0:T(8,128)(2,1)S(1)} %slice.80.own_ref, bf16[1,8,14464]{2,1,0:T(8,128)(2,1)S(1)} %collective-permute-done.15.left_ref, bf16[1,8,14464]{2,1,0:T(8,128)(2,1)S(1)} %collective-permute-done.16.right_ref, f32[24,128]{1,0:T(8,128)S(1)} %broadcast_in_dim.7.inv_ref, ...), custom_call_target="tpu_custom_call" | custom-call | flops 1 | bytes 1 | tf_op jit(solution)/shard_map/attend_part/pallas_call | solution.py:341
  59.2 1.9 %collective-permute-start.22 = (bf16[1,8,11264]{2,1,0:T(8,128)(2,1)S(1)}, bf16[1,8,11264]{2,1,0:T(8,128)(2,1)S(1)}, u32[]{:S(2)}, u32[]{:S(2)}) collective-permute-start(bf16[1,8,11264]{2,1,0:T(8,128)(2,1)S(1)} %attend_part.2.refs_0_), channel_id=1, source_target_pairs={{2,0},{3,1},{6,2},{7,3},{10,6},{11,7},{14,10},{15,11},{12,14},{13,... | collective-permute-start | bytes 540680 | tf_op jit(solution)/shard_map/ppermute | solution.py:455
  62.0 4.8 %attend_part.3.refs_0_ = bf16[1,8,11264]{2,1,0:T(8,128)(2,1)S(1)} custom-call(bf16[1,8,14080]{2,1,0:T(8,128)(2,1)S(1)} %slice.79.own_ref, bf16[1,8,14080]{2,1,0:T(8,128)(2,1)S(1)} %collective-permute-done.18.left_ref, bf16[1,8,14080]{2,1,0:T(8,128)(2,1)S(1)} %collective-permute-done.19.right_ref, f32[24,128]{1,0:T(8,128)S(1)} %broadcast_in_dim.7.inv_ref, ...), custom_call_target="tpu_custom_call" | custom-call | flops 1 | bytes 1 | tf_op jit(solution)/shard_map/attend_part/pallas_call | solution.py:341
  66.8 1.2 %collective-permute-start.20 = (bf16[1,8,11264]{2,1,0:T(8,128)(2,1)S(1)}, bf16[1,8,11264]{2,1,0:T(8,128)(2,1)S(1)}, u32[]{:S(2)}, u32[]{:S(2)}) collective-permute-start(bf16[1,8,11264]{2,1,0:T(8,128)(2,1)S(1)} %attend_part.3.refs_0_), channel_id=1, source_target_pairs={{2,0},{3,1},{6,2},{7,3},{10,6},{11,7},{14,10},{15,11},{12,14},{13,... | collective-permute-start | bytes 540680 | tf_op jit(solution)/shard_map/ppermute | solution.py:455
  67.9 0.9 collective-permute-start.25
  68.8 1.1 %collective-permute-start.26 = (bf16[1,8,11264]{2,1,0:T(8,128)(2,1)S(1)}, bf16[1,8,11264]{2,1,0:T(8,128)(2,1)S(1)}, u32[]{:S(2)}, u32[]{:S(2)}) collective-permute-start(bf16[1,8,11264]{2,1,0:T(8,128)(2,1)S(1)} %collective-permute-done.22.refs_1_), channel_id=1, source_target_pairs={{2,0},{3,1},{6,2},{7,3},{10,6},{11,7},{14,10},{15,11},{12,14},{13,... | collective-permute-start | bytes 540680 | tf_op jit(solution)/shard_map/ppermute | solution.py:455
  70.0 0.9 collective-permute-start.24
  70.9 4.1 %load_weights.2 = (bf16[4096,512]{1,0:T(8,128)(2,1)S(1)}, bf16[4096,512]{1,0:T(8,128)(2,1)S(1)}, f32[8,128]{1,0:T(8,128)}) custom-call(bf16[8192,512]{1,0:T(8,128)(2,1)} %refs_0_.1, bf16[8192,512]{1,0:T(8,128)(2,1)} %collective-permute-done.17.refs_1_), custom_call_target="tpu_custom_call" | custom-call | flops 1 | bytes 1 | tf_op jit(solution)/shard_map/load_weights/pallas_call | solution.py:324
  75.0 1.2 %collective-permute-start.23 = (bf16[1,8,11264]{2,1,0:T(8,128)(2,1)S(1)}, bf16[1,8,11264]{2,1,0:T(8,128)(2,1)S(1)}, u32[]{:S(2)}, u32[]{:S(2)}) collective-permute-start(bf16[1,8,11264]{2,1,0:T(8,128)(2,1)S(1)} %collective-permute-done.20.refs_1_), channel_id=1, source_target_pairs={{2,0},{3,1},{6,2},{7,3},{10,6},{11,7},{14,10},{15,11},{12,14},{13,... | collective-permute-start | bytes 540680 | tf_op jit(solution)/shard_map/ppermute | solution.py:455
  76.2 0.9 collective-permute-start.29
  77.0 1.5 %collective-permute-done.24.refs_6_ = bf16[1,8,11264]{2,1,0:T(8,128)(2,1)S(1)} collective-permute-done((bf16[1,8,11264]{2,1,0:T(8,128)(2,1)S(1)}, bf16[1,8,11264]{2,1,0:T(8,128)(2,1)S(1)}, u32[]{:S(2)}, u32[]{:S(2)}) %collective-permute-start.24) | collective-permute-done | bytes 180256 | tf_op jit(solution)/shard_map/ppermute | solution.py:455
  78.8 4.1 %load_weights.3 = (bf16[4096,512]{1,0:T(8,128)(2,1)S(1)}, bf16[4096,512]{1,0:T(8,128)(2,1)S(1)}, f32[8,128]{1,0:T(8,128)}) custom-call(bf16[8192,512]{1,0:T(8,128)(2,1)} %refs_0_.1, bf16[8192,512]{1,0:T(8,128)(2,1)} %collective-permute-done.17.refs_1_), custom_call_target="tpu_custom_call" | custom-call | flops 1 | bytes 1 | tf_op jit(solution)/shard_map/load_weights/pallas_call | solution.py:324
  82.9 1.9 %collective-permute-start.27 = (bf16[1,8,11264]{2,1,0:T(8,128)(2,1)S(1)}, bf16[1,8,11264]{2,1,0:T(8,128)(2,1)S(1)}, u32[]{:S(2)}, u32[]{:S(2)}) collective-permute-start(bf16[1,8,11264]{2,1,0:T(8,128)(2,1)S(1)} %collective-permute-done.23.refs_2_), channel_id=1, source_target_pairs={{2,0},{3,1},{6,2},{7,3},{10,6},{11,7},{14,10},{15,11},{12,14},{13,... | collective-permute-start | bytes 540680 | tf_op jit(solution)/shard_map/ppermute | solution.py:455
  84.8 2.0 %collective-permute-start.32 = (bf16[1,8,11264]{2,1,0:T(8,128)(2,1)S(1)}, bf16[1,8,11264]{2,1,0:T(8,128)(2,1)S(1)}, u32[]{:S(2)}, u32[]{:S(2)}) collective-permute-start(bf16[1,8,11264]{2,1,0:T(8,128)(2,1)S(1)} %collective-permute-done.26.refs_2_), channel_id=1, source_target_pairs={{2,0},{3,1},{6,2},{7,3},{10,6},{11,7},{14,10},{15,11},{12,14},{13,... | collective-permute-start | bytes 540680 | tf_op jit(solution)/shard_map/ppermute | solution.py:455
  86.9 0.9 collective-permute-start.31
  87.8 1.2 %collective-permute-done.27.refs_3_ = bf16[1,8,11264]{2,1,0:T(8,128)(2,1)S(1)} collective-permute-done((bf16[1,8,11264]{2,1,0:T(8,128)(2,1)S(1)}, bf16[1,8,11264]{2,1,0:T(8,128)(2,1)S(1)}, u32[]{:S(2)}, u32[]{:S(2)}) %collective-permute-start.27) | collective-permute-done | bytes 180256 | tf_op jit(solution)/shard_map/ppermute | solution.py:455
  89.0 1.3 %collective-permute-start.30 = (bf16[1,8,11264]{2,1,0:T(8,128)(2,1)S(1)}, bf16[1,8,11264]{2,1,0:T(8,128)(2,1)S(1)}, u32[]{:S(2)}, u32[]{:S(2)}) collective-permute-start(bf16[1,8,11264]{2,1,0:T(8,128)(2,1)S(1)} %collective-permute-done.27.refs_3_), channel_id=1, source_target_pairs={{2,0},{3,1},{6,2},{7,3},{10,6},{11,7},{14,10},{15,11},{12,14},{13,... | collective-permute-start | bytes 540680 | tf_op jit(solution)/shard_map/ppermute | solution.py:455
  90.3 1.4 %features.1 = (f32[192,512]{1,0:T(8,128)S(1)}, f32[192,512]{1,0:T(8,128)S(1)}) custom-call(bf16[352,512]{1,0:T(8,128)(2,1)} %x_ref.4, bf16[352,512]{1,0:T(8,128)(2,1)S(1)} %collective-permute-done.14.x_other_ref), custom_call_target="tpu_custom_call" | custom-call | flops 1 | bytes 1 | tf_op jit(solution)/shard_map/features/pallas_call | solution.py:368
  91.7 0.7 collective-permute-done.33.refs_4_
  92.4 1.8 %out_part.2 = (f32[192,512]{1,0:T(8,128)S(1)}, f32[192,512]{1,0:T(8,128)S(1)}) custom-call(bf16[1,8,11264]{2,1,0:T(8,128)(2,1)S(1)} %attend_part.2.refs_0_, bf16[1,8,11264]{2,1,0:T(8,128)(2,1)S(1)} %collective-permute-done.22.refs_1_, bf16[1,8,11264]{2,1,0:T(8,128)(2,1)S(1)} %collective-permute-done.26.refs_2_, ...), custom_call_target="tpu_custom_call" | custom-call | flops 1 | bytes 1 | tf_op jit(solution)/shard_map/out_part/pallas_call | solution.py:397
  94.5 1.8 %out_part.3 = (bf16[192,512]{1,0:T(8,128)(2,1)S(1)}, bf16[192,512]{1,0:T(8,128)(2,1)S(1)}) custom-call(bf16[1,8,11264]{2,1,0:T(8,128)(2,1)S(1)} %attend_part.3.refs_0_, bf16[1,8,11264]{2,1,0:T(8,128)(2,1)S(1)} %collective-permute-done.20.refs_1_, bf16[1,8,11264]{2,1,0:T(8,128)(2,1)S(1)} %collective-permute-done.23.refs_2_, ...), custom_call_target="tpu_custom_call" | custom-call | flops 1 | bytes 1 | tf_op jit(solution)/shard_map/out_part/pallas_call | solution.py:397
  96.8 1.1 %collective-permute-done.34.rows_ref = bf16[192,512]{1,0:T(8,128)(2,1)S(1)} collective-permute-done((bf16[192,512]{1,0:T(8,128)(2,1)S(1)}, bf16[192,512]{1,0:T(8,128)(2,1)S(1)}, u32[]{:S(2)}, u32[]{:S(2)}) %collective-permute-start.34) | collective-permute-done | bytes 196640 | tf_op jit(solution)/shard_map/ppermute | solution.py:461
  97.8 1.1 %place.3 = bf16[352,512]{1,0:T(8,128)(2,1)} custom-call(bf16[192,512]{1,0:T(8,128)(2,1)S(1)} %collective-permute-done.34.rows_ref, bf16[352,512]{1,0:T(8,128)(2,1)S(1)} %place.2.refs_0_), custom_call_target="tpu_custom_call" | custom-call | flops 1 | bytes 1 | tf_op jit(solution)/shard_map/place/pallas_call | solution.py:421
  (63 shorter events, 5.5 us)
Async XLA Ops:
  0.0 0.7 copy-start
  6.2 2.0 %collective-permute-start = (bf16[2,8,14464]{2,1,0:T(8,128)(2,1)S(1)}, bf16[2,8,14464]{2,1,0:T(8,128)(2,1)S(1)}, u32[]{:S(2)}, u32[]{:S(2)}) collective-permute-start(bf16[2,8,14464]{2,1,0:T(8,128)(2,1)S(1)} %get-tuple-element.60), channel_id=1, source_target_pairs={{0,1},{1,0},{2,3},{3,2},{4,5},{5,4},{6,7},{7,6},{8,9},{9,8},{10,11... | collective-permute-start | bytes 1388552 | tf_op jit(solution)/shard_map/ppermute | solution.py:461
  6.7 12.0 %collective-permute-start.2 = (bf16[6,8,14464]{2,1,0:T(8,128)(2,1)}, bf16[6,8,14464]{2,1,0:T(8,128)(2,1)S(1)}, u32[]{:S(2)}, u32[]{:S(2)}) collective-permute-start(bf16[6,8,14464]{2,1,0:T(8,128)(2,1)} %get-tuple-element.65), channel_id=1, source_target_pairs={{0,1},{1,0},{2,3},{3,2},{4,5},{5,4},{6,7},{7,6},{8,9},{9,8},{10,11... | collective-permute-start | bytes 4165640 | tf_op jit(solution)/shard_map/ppermute | solution.py:461
  8.3 9.0 %collective-permute-start.3 = (bf16[1,8,14464]{2,1,0:T(8,128)(2,1)S(1)}, bf16[1,8,14464]{2,1,0:T(8,128)(2,1)S(1)}, u32[]{:S(2)}, u32[]{:S(2)}) collective-permute-start(bf16[1,8,14464]{2,1,0:T(8,128)(2,1)S(1)} %get-tuple-element.122), channel_id=1, source_target_pairs={{0,2},{1,3},{2,6},{3,7},{6,10},{7,11},{10,14},{11,15},{14,12},{15,... | collective-permute-start | bytes 694280 | tf_op jit(solution)/shard_map/ppermute | solution.py:455
  11.3 7.4 %collective-permute-start.4 = (bf16[1,8,14464]{2,1,0:T(8,128)(2,1)S(1)}, bf16[1,8,14464]{2,1,0:T(8,128)(2,1)S(1)}, u32[]{:S(2)}, u32[]{:S(2)}) collective-permute-start(bf16[1,8,14464]{2,1,0:T(8,128)(2,1)S(1)} %get-tuple-element.121), channel_id=1, source_target_pairs={{2,0},{3,1},{6,2},{7,3},{10,6},{11,7},{14,10},{15,11},{12,14},{13,... | collective-permute-start | bytes 694280 | tf_op jit(solution)/shard_map/ppermute | solution.py:455
  16.7 4.5 %collective-permute-start.5 = (bf16[2,8,14080]{2,1,0:T(8,128)(2,1)S(1)}, bf16[2,8,14080]{2,1,0:T(8,128)(2,1)S(1)}, u32[]{:S(2)}, u32[]{:S(2)}) collective-permute-start(bf16[2,8,14080]{2,1,0:T(8,128)(2,1)S(1)} %get-tuple-element.71), channel_id=1, source_target_pairs={{0,1},{1,0},{2,3},{3,2},{4,5},{5,4},{6,7},{7,6},{8,9},{9,8},{10,11... | collective-permute-start | bytes 1351688 | tf_op jit(solution)/shard_map/ppermute | solution.py:461
  16.8 17.1 %collective-permute-start.1 = (bf16[6,8,14080]{2,1,0:T(8,128)(2,1)}, bf16[6,8,14080]{2,1,0:T(8,128)(2,1)S(1)}, u32[]{:S(2)}, u32[]{:S(2)}) collective-permute-start(bf16[6,8,14080]{2,1,0:T(8,128)(2,1)} %get-tuple-element.63), channel_id=1, source_target_pairs={{0,1},{1,0},{2,3},{3,2},{4,5},{5,4},{6,7},{7,6},{8,9},{9,8},{10,11... | collective-permute-start | bytes 4055048 | tf_op jit(solution)/shard_map/ppermute | solution.py:461
  19.1 8.4 %collective-permute-start.7 = (bf16[1,8,14464]{2,1,0:T(8,128)(2,1)S(1)}, bf16[1,8,14464]{2,1,0:T(8,128)(2,1)S(1)}, u32[]{:S(2)}, u32[]{:S(2)}) collective-permute-start(bf16[1,8,14464]{2,1,0:T(8,128)(2,1)S(1)} %get-tuple-element.116), channel_id=1, source_target_pairs={{0,2},{1,3},{2,6},{3,7},{6,10},{7,11},{10,14},{11,15},{14,12},{15,... | collective-permute-start | bytes 694280 | tf_op jit(solution)/shard_map/ppermute | solution.py:455
  20.8 8.6 %collective-permute-start.8 = (bf16[1,8,14464]{2,1,0:T(8,128)(2,1)S(1)}, bf16[1,8,14464]{2,1,0:T(8,128)(2,1)S(1)}, u32[]{:S(2)}, u32[]{:S(2)}) collective-permute-start(bf16[1,8,14464]{2,1,0:T(8,128)(2,1)S(1)} %get-tuple-element.115), channel_id=1, source_target_pairs={{2,0},{3,1},{6,2},{7,3},{10,6},{11,7},{14,10},{15,11},{12,14},{13,... | collective-permute-start | bytes 694280 | tf_op jit(solution)/shard_map/ppermute | solution.py:455
  21.4 10.6 %collective-permute-start.6 = (bf16[1,8,14080]{2,1,0:T(8,128)(2,1)S(1)}, bf16[1,8,14080]{2,1,0:T(8,128)(2,1)S(1)}, u32[]{:S(2)}, u32[]{:S(2)}) collective-permute-start(bf16[1,8,14080]{2,1,0:T(8,128)(2,1)S(1)} %get-tuple-element.124), channel_id=1, source_target_pairs={{2,0},{3,1},{6,2},{7,3},{10,6},{11,7},{14,10},{15,11},{12,14},{13,... | collective-permute-start | bytes 675848 | tf_op jit(solution)/shard_map/ppermute | solution.py:455
  22.0 11.5 %collective-permute-start.11 = (bf16[1,8,14080]{2,1,0:T(8,128)(2,1)S(1)}, bf16[1,8,14080]{2,1,0:T(8,128)(2,1)S(1)}, u32[]{:S(2)}, u32[]{:S(2)}) collective-permute-start(bf16[1,8,14080]{2,1,0:T(8,128)(2,1)S(1)} %get-tuple-element.123), channel_id=1, source_target_pairs={{0,2},{1,3},{2,6},{3,7},{6,10},{7,11},{10,14},{11,15},{14,12},{15,... | collective-permute-start | bytes 675848 | tf_op jit(solution)/shard_map/ppermute | solution.py:455
  27.6 33.9 %collective-permute-start.17 = (bf16[8192,512]{1,0:T(8,128)(2,1)}, bf16[8192,512]{1,0:T(8,128)(2,1)}, u32[]{:S(2)}, u32[]{:S(2)}) collective-permute-start(bf16[8192,512]{1,0:T(8,128)(2,1)} %refs_0_.1), channel_id=1, source_target_pairs={{0,1},{1,0},{2,3},{3,2},{4,5},{5,4},{6,7},{7,6},{8,9},{9,8},{10,11... | collective-permute-start | bytes 25165832 | tf_op jit(solution)/shard_map/ppermute | solution.py:461
  29.3 24.9 %collective-permute-start.14 = (bf16[352,512]{1,0:T(8,128)(2,1)}, bf16[352,512]{1,0:T(8,128)(2,1)S(1)}, u32[]{:S(2)}, u32[]{:S(2)}) collective-permute-start(bf16[352,512]{1,0:T(8,128)(2,1)} %x_ref.4), channel_id=1, source_target_pairs={{0,1},{1,0},{2,3},{3,2},{4,5},{5,4},{6,7},{7,6},{8,9},{9,8},{10,11... | collective-permute-start | bytes 1081352 | tf_op jit(solution)/shard_map/ppermute | solution.py:461
  31.9 6.2 %collective-permute-start.10 = (bf16[1,8,14464]{2,1,0:T(8,128)(2,1)S(1)}, bf16[1,8,14464]{2,1,0:T(8,128)(2,1)S(1)}, u32[]{:S(2)}, u32[]{:S(2)}) collective-permute-start(bf16[1,8,14464]{2,1,0:T(8,128)(2,1)S(1)} %get-tuple-element.114), channel_id=1, source_target_pairs={{0,2},{1,3},{2,6},{3,7},{6,10},{7,11},{10,14},{11,15},{14,12},{15,... | collective-permute-start | bytes 694280 | tf_op jit(solution)/shard_map/ppermute | solution.py:455
  33.5 13.7 %collective-permute-start.16 = (bf16[1,8,14464]{2,1,0:T(8,128)(2,1)S(1)}, bf16[1,8,14464]{2,1,0:T(8,128)(2,1)S(1)}, u32[]{:S(2)}, u32[]{:S(2)}) collective-permute-start(bf16[1,8,14464]{2,1,0:T(8,128)(2,1)S(1)} %get-tuple-element.113), channel_id=1, source_target_pairs={{2,0},{3,1},{6,2},{7,3},{10,6},{11,7},{14,10},{15,11},{12,14},{13,... | collective-permute-start | bytes 694280 | tf_op jit(solution)/shard_map/ppermute | solution.py:455
  34.0 1.8 %copy-start.2 = (s32[22]{0:T(128)S(1)}, s32[22]{0:T(128)}, u32[]{:S(2)}) copy-start(s32[22]{0:T(128)} %param.13) | copy-start | bytes 268
  34.3 1.5 %copy-start.1 = (bf16[6,8,14080]{2,1,0:T(8,128)(2,1)}, bf16[6,8,14080]{2,1,0:T(8,128)(2,1)S(1)}, u32[]{:S(2)}) copy-start(bf16[6,8,14080]{2,1,0:T(8,128)(2,1)S(1)} %add_convert_fusion.1) | copy-start | bytes 4055044
  35.3 8.4 %collective-permute-start.9 = (bf16[1,8,14080]{2,1,0:T(8,128)(2,1)}, bf16[1,8,14080]{2,1,0:T(8,128)(2,1)S(1)}, u32[]{:S(2)}, u32[]{:S(2)}) collective-permute-start(bf16[1,8,14080]{2,1,0:T(8,128)(2,1)} %get-tuple-element.120), channel_id=1, source_target_pairs={{2,0},{3,1},{6,2},{7,3},{10,6},{11,7},{14,10},{15,11},{12,14},{13,... | collective-permute-start | bytes 675848 | tf_op jit(solution)/shard_map/ppermute | solution.py:455
  38.1 7.8 %collective-permute-start.13 = (bf16[1,8,14080]{2,1,0:T(8,128)(2,1)}, bf16[1,8,14080]{2,1,0:T(8,128)(2,1)S(1)}, u32[]{:S(2)}, u32[]{:S(2)}) collective-permute-start(bf16[1,8,14080]{2,1,0:T(8,128)(2,1)} %get-tuple-element.119), channel_id=1, source_target_pairs={{0,2},{1,3},{2,6},{3,7},{6,10},{7,11},{10,14},{11,15},{14,12},{15,... | collective-permute-start | bytes 675848 | tf_op jit(solution)/shard_map/ppermute | solution.py:455
  43.7 8.3 %collective-permute-start.15 = (bf16[1,8,14464]{2,1,0:T(8,128)(2,1)S(1)}, bf16[1,8,14464]{2,1,0:T(8,128)(2,1)S(1)}, u32[]{:S(2)}, u32[]{:S(2)}) collective-permute-start(bf16[1,8,14464]{2,1,0:T(8,128)(2,1)S(1)} %add_convert_fusion.4), channel_id=1, source_target_pairs={{0,2},{1,3},{2,6},{3,7},{6,10},{7,11},{10,14},{11,15},{14,12},{15,... | collective-permute-start | bytes 694280 | tf_op jit(solution)/shard_map/ppermute | solution.py:455
  47.1 6.0 %collective-permute-start.12 = (bf16[1,8,14080]{2,1,0:T(8,128)(2,1)S(1)}, bf16[1,8,14080]{2,1,0:T(8,128)(2,1)S(1)}, u32[]{:S(2)}, u32[]{:S(2)}) collective-permute-start(bf16[1,8,14080]{2,1,0:T(8,128)(2,1)S(1)} %get-tuple-element.118), channel_id=1, source_target_pairs={{2,0},{3,1},{6,2},{7,3},{10,6},{11,7},{14,10},{15,11},{12,14},{13,... | collective-permute-start | bytes 675848 | tf_op jit(solution)/shard_map/ppermute | solution.py:455
  47.2 14.2 %collective-permute-start.18 = (bf16[1,8,14080]{2,1,0:T(8,128)(2,1)S(1)}, bf16[1,8,14080]{2,1,0:T(8,128)(2,1)S(1)}, u32[]{:S(2)}, u32[]{:S(2)}) collective-permute-start(bf16[1,8,14080]{2,1,0:T(8,128)(2,1)S(1)} %get-tuple-element.117), channel_id=1, source_target_pairs={{0,2},{1,3},{2,6},{3,7},{6,10},{7,11},{10,14},{11,15},{14,12},{15,... | collective-permute-start | bytes 675848 | tf_op jit(solution)/shard_map/ppermute | solution.py:455
  54.1 7.8 %collective-permute-start.19 = (bf16[1,8,14080]{2,1,0:T(8,128)(2,1)S(1)}, bf16[1,8,14080]{2,1,0:T(8,128)(2,1)S(1)}, u32[]{:S(2)}, u32[]{:S(2)}) collective-permute-start(bf16[1,8,14080]{2,1,0:T(8,128)(2,1)S(1)} %add_convert_fusion.9), channel_id=1, source_target_pairs={{2,0},{3,1},{6,2},{7,3},{10,6},{11,7},{14,10},{15,11},{12,14},{13,... | collective-permute-start | bytes 675848 | tf_op jit(solution)/shard_map/ppermute | solution.py:455
  59.2 9.7 %collective-permute-start.22 = (bf16[1,8,11264]{2,1,0:T(8,128)(2,1)S(1)}, bf16[1,8,11264]{2,1,0:T(8,128)(2,1)S(1)}, u32[]{:S(2)}, u32[]{:S(2)}) collective-permute-start(bf16[1,8,11264]{2,1,0:T(8,128)(2,1)S(1)} %attend_part.2.refs_0_), channel_id=1, source_target_pairs={{2,0},{3,1},{6,2},{7,3},{10,6},{11,7},{14,10},{15,11},{12,14},{13,... | collective-permute-start | bytes 540680 | tf_op jit(solution)/shard_map/ppermute | solution.py:455
  61.0 8.9 %collective-permute-start.21 = (bf16[1,8,11264]{2,1,0:T(8,128)(2,1)S(1)}, bf16[1,8,11264]{2,1,0:T(8,128)(2,1)S(1)}, u32[]{:S(2)}, u32[]{:S(2)}) collective-permute-start(bf16[1,8,11264]{2,1,0:T(8,128)(2,1)S(1)} %attend_part.2.refs_0_), channel_id=1, source_target_pairs={{0,2},{1,3},{2,6},{3,7},{6,10},{7,11},{10,14},{11,15},{14,12},{15,... | collective-permute-start | bytes 540680 | tf_op jit(solution)/shard_map/ppermute | solution.py:455
  66.8 8.2 %collective-permute-start.20 = (bf16[1,8,11264]{2,1,0:T(8,128)(2,1)S(1)}, bf16[1,8,11264]{2,1,0:T(8,128)(2,1)S(1)}, u32[]{:S(2)}, u32[]{:S(2)}) collective-permute-start(bf16[1,8,11264]{2,1,0:T(8,128)(2,1)S(1)} %attend_part.3.refs_0_), channel_id=1, source_target_pairs={{2,0},{3,1},{6,2},{7,3},{10,6},{11,7},{14,10},{15,11},{12,14},{13,... | collective-permute-start | bytes 540680 | tf_op jit(solution)/shard_map/ppermute | solution.py:455
  67.9 8.2 %collective-permute-start.25 = (bf16[1,8,11264]{2,1,0:T(8,128)(2,1)S(1)}, bf16[1,8,11264]{2,1,0:T(8,128)(2,1)S(1)}, u32[]{:S(2)}, u32[]{:S(2)}) collective-permute-start(bf16[1,8,11264]{2,1,0:T(8,128)(2,1)S(1)} %attend_part.3.refs_0_), channel_id=1, source_target_pairs={{0,2},{1,3},{2,6},{3,7},{6,10},{7,11},{10,14},{11,15},{14,12},{15,... | collective-permute-start | bytes 540680 | tf_op jit(solution)/shard_map/ppermute | solution.py:455
  68.8 8.2 %collective-permute-start.26 = (bf16[1,8,11264]{2,1,0:T(8,128)(2,1)S(1)}, bf16[1,8,11264]{2,1,0:T(8,128)(2,1)S(1)}, u32[]{:S(2)}, u32[]{:S(2)}) collective-permute-start(bf16[1,8,11264]{2,1,0:T(8,128)(2,1)S(1)} %collective-permute-done.22.refs_1_), channel_id=1, source_target_pairs={{2,0},{3,1},{6,2},{7,3},{10,6},{11,7},{14,10},{15,11},{12,14},{13,... | collective-permute-start | bytes 540680 | tf_op jit(solution)/shard_map/ppermute | solution.py:455
  70.0 8.6 %collective-permute-start.24 = (bf16[1,8,11264]{2,1,0:T(8,128)(2,1)S(1)}, bf16[1,8,11264]{2,1,0:T(8,128)(2,1)S(1)}, u32[]{:S(2)}, u32[]{:S(2)}) collective-permute-start(bf16[1,8,11264]{2,1,0:T(8,128)(2,1)S(1)} %collective-permute-done.21.refs_7_), channel_id=1, source_target_pairs={{0,2},{1,3},{2,6},{3,7},{6,10},{7,11},{10,14},{11,15},{14,12},{15,... | collective-permute-start | bytes 540680 | tf_op jit(solution)/shard_map/ppermute | solution.py:455
  75.0 7.9 %collective-permute-start.23 = (bf16[1,8,11264]{2,1,0:T(8,128)(2,1)S(1)}, bf16[1,8,11264]{2,1,0:T(8,128)(2,1)S(1)}, u32[]{:S(2)}, u32[]{:S(2)}) collective-permute-start(bf16[1,8,11264]{2,1,0:T(8,128)(2,1)S(1)} %collective-permute-done.20.refs_1_), channel_id=1, source_target_pairs={{2,0},{3,1},{6,2},{7,3},{10,6},{11,7},{14,10},{15,11},{12,14},{13,... | collective-permute-start | bytes 540680 | tf_op jit(solution)/shard_map/ppermute | solution.py:455
  76.2 10.7 %collective-permute-start.29 = (bf16[1,8,11264]{2,1,0:T(8,128)(2,1)S(1)}, bf16[1,8,11264]{2,1,0:T(8,128)(2,1)S(1)}, u32[]{:S(2)}, u32[]{:S(2)}) collective-permute-start(bf16[1,8,11264]{2,1,0:T(8,128)(2,1)S(1)} %collective-permute-done.25.refs_7_), channel_id=1, source_target_pairs={{0,2},{1,3},{2,6},{3,7},{6,10},{7,11},{10,14},{11,15},{14,12},{15,... | collective-permute-start | bytes 540680 | tf_op jit(solution)/shard_map/ppermute | solution.py:455
  78.6 8.3 %collective-permute-start.28 = (bf16[1,8,11264]{2,1,0:T(8,128)(2,1)S(1)}, bf16[1,8,11264]{2,1,0:T(8,128)(2,1)S(1)}, u32[]{:S(2)}, u32[]{:S(2)}) collective-permute-start(bf16[1,8,11264]{2,1,0:T(8,128)(2,1)S(1)} %collective-permute-done.24.refs_6_), channel_id=1, source_target_pairs={{0,2},{1,3},{2,6},{3,7},{6,10},{7,11},{10,14},{11,15},{14,12},{15,... | collective-permute-start | bytes 540680 | tf_op jit(solution)/shard_map/ppermute | solution.py:455
  82.9 6.1 %collective-permute-start.27 = (bf16[1,8,11264]{2,1,0:T(8,128)(2,1)S(1)}, bf16[1,8,11264]{2,1,0:T(8,128)(2,1)S(1)}, u32[]{:S(2)}, u32[]{:S(2)}) collective-permute-start(bf16[1,8,11264]{2,1,0:T(8,128)(2,1)S(1)} %collective-permute-done.23.refs_2_), channel_id=1, source_target_pairs={{2,0},{3,1},{6,2},{7,3},{10,6},{11,7},{14,10},{15,11},{12,14},{13,... | collective-permute-start | bytes 540680 | tf_op jit(solution)/shard_map/ppermute | solution.py:455
  84.8 6.9 %collective-permute-start.32 = (bf16[1,8,11264]{2,1,0:T(8,128)(2,1)S(1)}, bf16[1,8,11264]{2,1,0:T(8,128)(2,1)S(1)}, u32[]{:S(2)}, u32[]{:S(2)}) collective-permute-start(bf16[1,8,11264]{2,1,0:T(8,128)(2,1)S(1)} %collective-permute-done.26.refs_2_), channel_id=1, source_target_pairs={{2,0},{3,1},{6,2},{7,3},{10,6},{11,7},{14,10},{15,11},{12,14},{13,... | collective-permute-start | bytes 540680 | tf_op jit(solution)/shard_map/ppermute | solution.py:455
  86.9 5.5 %collective-permute-start.33 = (bf16[1,8,11264]{2,1,0:T(8,128)(2,1)S(1)}, bf16[1,8,11264]{2,1,0:T(8,128)(2,1)S(1)}, u32[]{:S(2)}, u32[]{:S(2)}) collective-permute-start(bf16[1,8,11264]{2,1,0:T(8,128)(2,1)S(1)} %collective-permute-done.28.refs_5_), channel_id=1, source_target_pairs={{0,2},{1,3},{2,6},{3,7},{6,10},{7,11},{10,14},{11,15},{14,12},{15,... | collective-permute-start | bytes 540680 | tf_op jit(solution)/shard_map/ppermute | solution.py:455
  86.9 7.4 %collective-permute-start.31 = (bf16[1,8,11264]{2,1,0:T(8,128)(2,1)S(1)}, bf16[1,8,11264]{2,1,0:T(8,128)(2,1)S(1)}, u32[]{:S(2)}, u32[]{:S(2)}) collective-permute-start(bf16[1,8,11264]{2,1,0:T(8,128)(2,1)S(1)} %collective-permute-done.29.refs_6_), channel_id=1, source_target_pairs={{0,2},{1,3},{2,6},{3,7},{6,10},{7,11},{10,14},{11,15},{14,12},{15,... | collective-permute-start | bytes 540680 | tf_op jit(solution)/shard_map/ppermute | solution.py:455
  89.0 5.5 %collective-permute-start.30 = (bf16[1,8,11264]{2,1,0:T(8,128)(2,1)S(1)}, bf16[1,8,11264]{2,1,0:T(8,128)(2,1)S(1)}, u32[]{:S(2)}, u32[]{:S(2)}) collective-permute-start(bf16[1,8,11264]{2,1,0:T(8,128)(2,1)S(1)} %collective-permute-done.27.refs_3_), channel_id=1, source_target_pairs={{2,0},{3,1},{6,2},{7,3},{10,6},{11,7},{14,10},{15,11},{12,14},{13,... | collective-permute-start | bytes 540680 | tf_op jit(solution)/shard_map/ppermute | solution.py:455
  96.3 1.5 %collective-permute-start.34 = (bf16[192,512]{1,0:T(8,128)(2,1)S(1)}, bf16[192,512]{1,0:T(8,128)(2,1)S(1)}, u32[]{:S(2)}, u32[]{:S(2)}) collective-permute-start(bf16[192,512]{1,0:T(8,128)(2,1)S(1)} %get-tuple-element.111), channel_id=1, source_target_pairs={{0,1},{1,0},{2,3},{3,2},{4,5},{5,4},{6,7},{7,6},{8,9},{9,8},{10,11... | collective-permute-start | bytes 589832 | tf_op jit(solution)/shard_map/ppermute | solution.py:461

commit v5 on v4

--- a/solution.py
+++ b/solution.py
@@ -50,7 +50,7 @@
 def hops(index, chips):
     far = chips // 2
     near = chips - 1 - far
-    return (far, near) if index % 2 == 0 else (near, far)
+    return (near, far) if index % 2 == 0 else (far, near)
 
 
 def sent_slots(index, chips):
@@ -503,10 +503,10 @@
                     if step:
                         sent[way] = (wide(sent[way]) + wide(tied(moved[way]))).astype(BF)
             moved = {**moved, **ring(sent)}
-            if index == 1 and step == 0:
+            if index == 1 and step == 1:
                 w_other[0] = cross(tied(w_out))
                 x_other[0] = cross(tied(hidden_in))
-            if index == 1 and step == 1:
+            if index == 1 and step == 2:
                 places[0] = positions(tied(lengths))
                 sums[0] = features_of(order, rows, pad, hidden_in, x_other[0])
             yield

time: 99.2 us -> 96.4 us (0.972)
  waiting for transfers between devices: 26.2 us -> 23.7 us
  other arithmetic: 4.61 us -> 3.45 us
    ppermute x28, waiting for transfers between devices: 23.8 us -> 21.2 us  [ring(): lax.ppermute(a, 'gx', up_pairs if way == 'up' else down_pairs)]
    convert_element_type x6, other arithmetic: 3.44 us -> 2.27 us  [part_steps(): sent[way] = (wide(sent[way]) + wide(tied(moved[way]))).astype(BF)]
  transfers between devices with their start and end apart: 35 -> 35, of which waited for: 16 -> 13; matrix products, arithmetic and copies ran while one was open for 5% -> 4% of each run, Pallas kernels for 27% -> 28%
where the time goes in v5:
time: 96.4 us; the launch traced here: 96.2 us
  Pallas kernels  35.1 us (36%)
  starting transfers between devices  32.6 us (34%)
  waiting for transfers between devices  23.7 us (25%)
  other arithmetic  3.45 us (4%)
  local copies, waits for them, and re-layouts  1.1 us (1%)
    ppermute x28, starting transfers between devices, ring(): lax.ppermute(a, 'gx', up_pairs if way == 'up' else down_pairs)  31.3 us
    ppermute x28, waiting for transfers between devices, ring(): lax.ppermute(a, 'gx', up_pairs if way == 'up' else down_pairs)  21.2 us
    pallas_call x2, Pallas kernels, project(): pl.pallas_call(functools.partial(qkv_kernel, order, index, rows, pad), in...  10.9 us
    pallas_call x2, Pallas kernels, attend(): pl.pallas_call(functools.partial(attend_kernel, part, rows, pad), in_spec...  9.61 us
    pallas_call x2, Pallas kernels, load(): pl.pallas_call(kernel, in_specs=[pl.BlockSpec(memory_space=pltpu.HBM)] *...  8.15 us
    pallas_call x2, Pallas kernels, project_out(): pl.pallas_call(functools.partial(out_kernel, rows, pad), in_specs=[vmem]...  3.6 us
    ppermute x7, waiting for transfers between devices, cross(): return lax.ppermute(a, 'gx', sibling)  2.43 us
    convert_element_type x6, other arithmetic, part_steps(): sent[way] = (wide(sent[way]) + wide(tied(moved[way]))).astype(BF)  2.27 us
  transfers between devices with their start and end apart: 35, of which 13 were waited for; matrix products, arithmetic and copies ran while one was open for 4% of the time, Pallas kernels for 28%

profile of v5, /device:TPU:0, one launch (start us, length us, event | category | flops | bytes accessed | tf_op | source)
XLA Modules:
  0.0 96.2 jit_solution(12215754688510841776)
XLA Ops:
  0.0 0.7 copy-done
  0.7 5.5 %qkv_part.2 = (bf16[2,8,14464]{2,1,0:T(8,128)(2,1)S(1)}, bf16[6,8,14464]{2,1,0:T(8,128)(2,1)S(1)}, bf16[2,8,14464]{2,1,0:T(8,128)(2,1)S(1)}, bf16[6,8,14464]{2,1,0:T(8,128)(2,1)}, f32[8,128]{1,0:T(8,128)}) custom-call(bf16[352,512]{1,0:T(8,128)(2,1)} %x_ref.4, f32[1,512]{1,0:T(1,128)S(1)} %bitcast.5, bf16[512,10240]{1,0:T(8,128)(2,1)} %w_ref.3), custom_call_target="tpu_custom_call" | custom-call | flops 1 | bytes 1 | tf_op jit(solution)/shard_map/qkv_part/pallas_call | solution.py:202
  6.2 0.5 collective-permute-start
  6.8 1.4 %collective-permute-done = bf16[2,8,14464]{2,1,0:T(8,128)(2,1)S(1)} collective-permute-done((bf16[2,8,14464]{2,1,0:T(8,128)(2,1)S(1)}, bf16[2,8,14464]{2,1,0:T(8,128)(2,1)S(1)}, u32[]{:S(2)}, u32[]{:S(2)}) %collective-permute-start) | collective-permute-done | bytes 462880 | tf_op jit(solution)/shard_map/ppermute | solution.py:461
  8.3 2.9 %collective-permute-start.3 = (bf16[1,8,14464]{2,1,0:T(8,128)(2,1)S(1)}, bf16[1,8,14464]{2,1,0:T(8,128)(2,1)S(1)}, u32[]{:S(2)}, u32[]{:S(2)}) collective-permute-start(bf16[1,8,14464]{2,1,0:T(8,128)(2,1)S(1)} %get-tuple-element.122), channel_id=1, source_target_pairs={{0,2},{1,3},{2,6},{3,7},{6,10},{7,11},{10,14},{11,15},{14,12},{15,... | collective-permute-start | bytes 694280 | tf_op jit(solution)/shard_map/ppermute | solution.py:455
  11.4 5.4 %qkv_part.3 = (bf16[2,8,14080]{2,1,0:T(8,128)(2,1)S(1)}, bf16[6,8,14080]{2,1,0:T(8,128)(2,1)S(1)}, bf16[2,8,14080]{2,1,0:T(8,128)(2,1)S(1)}, bf16[6,8,14080]{2,1,0:T(8,128)(2,1)}, f32[8,128]{1,0:T(8,128)}) custom-call(bf16[352,512]{1,0:T(8,128)(2,1)} %x_ref.4, f32[1,512]{1,0:T(1,128)S(1)} %bitcast.6, bf16[512,10240]{1,0:T(8,128)(2,1)} %w_ref.3), custom_call_target="tpu_custom_call" | custom-call | flops 1 | bytes 1 | tf_op jit(solution)/shard_map/qkv_part/pallas_call | solution.py:202
  16.8 0.5 collective-permute-start.1
  17.3 1.3 %collective-permute-done.4 = bf16[1,8,14464]{2,1,0:T(8,128)(2,1)S(1)} collective-permute-done((bf16[1,8,14464]{2,1,0:T(8,128)(2,1)S(1)}, bf16[1,8,14464]{2,1,0:T(8,128)(2,1)S(1)}, u32[]{:S(2)}, u32[]{:S(2)}) %collective-permute-start.4) | collective-permute-done | bytes 231456 | tf_op jit(solution)/shard_map/ppermute | solution.py:455
  19.1 1.6 %collective-permute-start.7 = (bf16[1,8,14464]{2,1,0:T(8,128)(2,1)S(1)}, bf16[1,8,14464]{2,1,0:T(8,128)(2,1)S(1)}, u32[]{:S(2)}, u32[]{:S(2)}) collective-permute-start(bf16[1,8,14464]{2,1,0:T(8,128)(2,1)S(1)} %get-tuple-element.116), channel_id=1, source_target_pairs={{0,2},{1,3},{2,6},{3,7},{6,10},{7,11},{10,14},{11,15},{14,12},{15,... | collective-permute-start | bytes 694280 | tf_op jit(solution)/shard_map/ppermute | solution.py:455
  20.8 0.4 collective-permute-start.8
  21.4 1.6 %collective-permute-start.6 = (bf16[1,8,14080]{2,1,0:T(8,128)(2,1)S(1)}, bf16[1,8,14080]{2,1,0:T(8,128)(2,1)S(1)}, u32[]{:S(2)}, u32[]{:S(2)}) collective-permute-start(bf16[1,8,14080]{2,1,0:T(8,128)(2,1)S(1)} %get-tuple-element.124), channel_id=1, source_target_pairs={{0,2},{1,3},{2,6},{3,7},{6,10},{7,11},{10,14},{11,15},{14,12},{15,... | collective-permute-start | bytes 675848 | tf_op jit(solution)/shard_map/ppermute | solution.py:455
  23.0 0.4 collective-permute-start.11
  23.5 4.3 %collective-permute-done.7 = bf16[1,8,14464]{2,1,0:T(8,128)(2,1)S(1)} collective-permute-done((bf16[1,8,14464]{2,1,0:T(8,128)(2,1)S(1)}, bf16[1,8,14464]{2,1,0:T(8,128)(2,1)S(1)}, u32[]{:S(2)}, u32[]{:S(2)}) %collective-permute-start.7) | collective-permute-done | bytes 231456 | tf_op jit(solution)/shard_map/ppermute | solution.py:455
  27.8 1.6 %collective-permute-done.8 = bf16[1,8,14464]{2,1,0:T(8,128)(2,1)S(1)} collective-permute-done((bf16[1,8,14464]{2,1,0:T(8,128)(2,1)S(1)}, bf16[1,8,14464]{2,1,0:T(8,128)(2,1)S(1)}, u32[]{:S(2)}, u32[]{:S(2)}) %collective-permute-start.8) | collective-permute-done | bytes 231456 | tf_op jit(solution)/shard_map/ppermute | solution.py:455
  29.5 0.5 collective-permute-start.10
  30.0 1.6 %collective-permute-start.15 = (bf16[1,8,14464]{2,1,0:T(8,128)(2,1)S(1)}, bf16[1,8,14464]{2,1,0:T(8,128)(2,1)S(1)}, u32[]{:S(2)}, u32[]{:S(2)}) collective-permute-start(bf16[1,8,14464]{2,1,0:T(8,128)(2,1)S(1)} %get-tuple-element.114), channel_id=1, source_target_pairs={{0,2},{1,3},{2,6},{3,7},{6,10},{7,11},{10,14},{11,15},{14,12},{15,... | collective-permute-start | bytes 694280 | tf_op jit(solution)/shard_map/ppermute | solution.py:455
  31.9 2.3 %collective-permute-done.11 = bf16[1,8,14080]{2,1,0:T(8,128)(2,1)S(1)} collective-permute-done((bf16[1,8,14080]{2,1,0:T(8,128)(2,1)S(1)}, bf16[1,8,14080]{2,1,0:T(8,128)(2,1)S(1)}, u32[]{:S(2)}, u32[]{:S(2)}) %collective-permute-start.11) | collective-permute-done | bytes 225312 | tf_op jit(solution)/shard_map/ppermute | solution.py:455
  34.6 1.6 %collective-permute-start.9 = (bf16[1,8,14080]{2,1,0:T(8,128)(2,1)S(1)}, bf16[1,8,14080]{2,1,0:T(8,128)(2,1)S(1)}, u32[]{:S(2)}, u32[]{:S(2)}) collective-permute-start(bf16[1,8,14080]{2,1,0:T(8,128)(2,1)S(1)} %get-tuple-element.120), channel_id=1, source_target_pairs={{0,2},{1,3},{2,6},{3,7},{6,10},{7,11},{10,14},{11,15},{14,12},{15,... | collective-permute-start | bytes 675848 | tf_op jit(solution)/shard_map/ppermute | solution.py:455
  36.8 2.3 %collective-permute-done.10 = bf16[1,8,14464]{2,1,0:T(8,128)(2,1)S(1)} collective-permute-done((bf16[1,8,14464]{2,1,0:T(8,128)(2,1)S(1)}, bf16[1,8,14464]{2,1,0:T(8,128)(2,1)S(1)}, u32[]{:S(2)}, u32[]{:S(2)}) %collective-permute-start.10) | collective-permute-done | bytes 231456 | tf_op jit(solution)/shard_map/ppermute | solution.py:455
  39.2 1.5 %collective-permute-done.9 = bf16[1,8,14080]{2,1,0:T(8,128)(2,1)S(1)} collective-permute-done((bf16[1,8,14080]{2,1,0:T(8,128)(2,1)S(1)}, bf16[1,8,14080]{2,1,0:T(8,128)(2,1)S(1)}, u32[]{:S(2)}, u32[]{:S(2)}) %collective-permute-start.9) | collective-permute-done | bytes 225312 | tf_op jit(solution)/shard_map/ppermute | solution.py:455
  40.7 1.4 %collective-permute-start.16 = (bf16[1,8,14464]{2,1,0:T(8,128)(2,1)S(1)}, bf16[1,8,14464]{2,1,0:T(8,128)(2,1)S(1)}, u32[]{:S(2)}, u32[]{:S(2)}) collective-permute-start(bf16[1,8,14464]{2,1,0:T(8,128)(2,1)S(1)} %add_convert_fusion.4), channel_id=1, source_target_pairs={{2,0},{3,1},{6,2},{7,3},{10,6},{11,7},{14,10},{15,11},{12,14},{13,... | collective-permute-start | bytes 694280 | tf_op jit(solution)/shard_map/ppermute | solution.py:455
  42.2 0.9 add_convert_fusion.10
  43.1 1.9 %collective-permute-start.12 = (bf16[1,8,14080]{2,1,0:T(8,128)(2,1)}, bf16[1,8,14080]{2,1,0:T(8,128)(2,1)S(1)}, u32[]{:S(2)}, u32[]{:S(2)}) collective-permute-start(bf16[1,8,14080]{2,1,0:T(8,128)(2,1)} %get-tuple-element.118), channel_id=1, source_target_pairs={{0,2},{1,3},{2,6},{3,7},{6,10},{7,11},{10,14},{11,15},{14,12},{15,... | collective-permute-start | bytes 675848 | tf_op jit(solution)/shard_map/ppermute | solution.py:455
  45.6 3.7 %collective-permute-done.16.right_ref = bf16[1,8,14464]{2,1,0:T(8,128)(2,1)S(1)} collective-permute-done((bf16[1,8,14464]{2,1,0:T(8,128)(2,1)S(1)}, bf16[1,8,14464]{2,1,0:T(8,128)(2,1)S(1)}, u32[]{:S(2)}, u32[]{:S(2)}) %collective-permute-start.16) | collective-permute-done | bytes 231456 | tf_op jit(solution)/shard_map/ppermute | solution.py:455
  49.3 1.0 %add_convert_fusion.9 = bf16[1,8,14080]{2,1,0:T(8,128)(2,1)S(1)} fusion(bf16[1,8,14080]{2,1,0:T(8,128)(2,1)S(1)} %collective-permute-done.12, bf16[6,8,14080]{2,1,0:T(8,128)(2,1)} %copy-done.1), kind=kLoop, calls=%fused_computation.9 | loop fusion | flops 450560 | bytes 675840 | tf_op jit(solution)/shard_map/convert_element_type | solution.py:504
  50.3 1.9 %collective-permute-start.18 = (bf16[1,8,14080]{2,1,0:T(8,128)(2,1)S(1)}, bf16[1,8,14080]{2,1,0:T(8,128)(2,1)S(1)}, u32[]{:S(2)}, u32[]{:S(2)}) collective-permute-start(bf16[1,8,14080]{2,1,0:T(8,128)(2,1)S(1)} %add_convert_fusion.9), channel_id=1, source_target_pairs={{0,2},{1,3},{2,6},{3,7},{6,10},{7,11},{10,14},{11,15},{14,12},{15,... | collective-permute-start | bytes 675848 | tf_op jit(solution)/shard_map/ppermute | solution.py:455
  52.4 4.8 %attend_part.2.refs_0_ = bf16[1,8,11264]{2,1,0:T(8,128)(2,1)S(1)} custom-call(bf16[1,8,14464]{2,1,0:T(8,128)(2,1)S(1)} %slice.80.own_ref, bf16[1,8,14464]{2,1,0:T(8,128)(2,1)S(1)} %collective-permute-done.15.left_ref, bf16[1,8,14464]{2,1,0:T(8,128)(2,1)S(1)} %collective-permute-done.16.right_ref, f32[24,128]{1,0:T(8,128)S(1)} %broadcast_in_dim.7.inv_ref, ...), custom_call_target="tpu_custom_call" | custom-call | flops 1 | bytes 1 | tf_op jit(solution)/shard_map/attend_part/pallas_call | solution.py:341
  57.5 1.9 %collective-permute-start.21 = (bf16[1,8,11264]{2,1,0:T(8,128)(2,1)S(1)}, bf16[1,8,11264]{2,1,0:T(8,128)(2,1)S(1)}, u32[]{:S(2)}, u32[]{:S(2)}) collective-permute-start(bf16[1,8,11264]{2,1,0:T(8,128)(2,1)S(1)} %attend_part.2.refs_0_), channel_id=1, source_target_pairs={{0,2},{1,3},{2,6},{3,7},{6,10},{7,11},{10,14},{11,15},{14,12},{15,... | collective-permute-start | bytes 540680 | tf_op jit(solution)/shard_map/ppermute | solution.py:455
  59.3 4.8 %attend_part.3.refs_0_ = bf16[1,8,11264]{2,1,0:T(8,128)(2,1)S(1)} custom-call(bf16[1,8,14080]{2,1,0:T(8,128)(2,1)S(1)} %slice.79.own_ref, bf16[1,8,14080]{2,1,0:T(8,128)(2,1)S(1)} %collective-permute-done.18.left_ref, bf16[1,8,14080]{2,1,0:T(8,128)(2,1)S(1)} %collective-permute-done.19.right_ref, f32[24,128]{1,0:T(8,128)S(1)} %broadcast_in_dim.7.inv_ref, ...), custom_call_target="tpu_custom_call" | custom-call | flops 1 | bytes 1 | tf_op jit(solution)/shard_map/attend_part/pallas_call | solution.py:341
  64.1 1.0 collective-permute-start.25
  65.1 1.1 %collective-permute-start.20 = (bf16[1,8,11264]{2,1,0:T(8,128)(2,1)S(1)}, bf16[1,8,11264]{2,1,0:T(8,128)(2,1)S(1)}, u32[]{:S(2)}, u32[]{:S(2)}) collective-permute-start(bf16[1,8,11264]{2,1,0:T(8,128)(2,1)S(1)} %attend_part.3.refs_0_), channel_id=1, source_target_pairs={{2,0},{3,1},{6,2},{7,3},{10,6},{11,7},{14,10},{15,11},{12,14},{13,... | collective-permute-start | bytes 540680 | tf_op jit(solution)/shard_map/ppermute | solution.py:455
  66.5 1.8 %collective-permute-start.24 = (bf16[1,8,11264]{2,1,0:T(8,128)(2,1)S(1)}, bf16[1,8,11264]{2,1,0:T(8,128)(2,1)S(1)}, u32[]{:S(2)}, u32[]{:S(2)}) collective-permute-start(bf16[1,8,11264]{2,1,0:T(8,128)(2,1)S(1)} %collective-permute-done.21.refs_7_), channel_id=1, source_target_pairs={{0,2},{1,3},{2,6},{3,7},{6,10},{7,11},{10,14},{11,15},{14,12},{15,... | collective-permute-start | bytes 540680 | tf_op jit(solution)/shard_map/ppermute | solution.py:455
  68.3 4.1 %load_weights.2 = (bf16[4096,512]{1,0:T(8,128)(2,1)S(1)}, bf16[4096,512]{1,0:T(8,128)(2,1)S(1)}, f32[8,128]{1,0:T(8,128)}) custom-call(bf16[8192,512]{1,0:T(8,128)(2,1)} %refs_0_.1, bf16[8192,512]{1,0:T(8,128)(2,1)} %collective-permute-done.17.refs_1_), custom_call_target="tpu_custom_call" | custom-call | flops 1 | bytes 1 | tf_op jit(solution)/shard_map/load_weights/pallas_call | solution.py:324
  72.4 1.0 collective-permute-start.28
  73.3 1.1 %collective-permute-start.23 = (bf16[1,8,11264]{2,1,0:T(8,128)(2,1)S(1)}, bf16[1,8,11264]{2,1,0:T(8,128)(2,1)S(1)}, u32[]{:S(2)}, u32[]{:S(2)}) collective-permute-start(bf16[1,8,11264]{2,1,0:T(8,128)(2,1)S(1)} %collective-permute-done.20.refs_1_), channel_id=1, source_target_pairs={{2,0},{3,1},{6,2},{7,3},{10,6},{11,7},{14,10},{15,11},{12,14},{13,... | collective-permute-start | bytes 540680 | tf_op jit(solution)/shard_map/ppermute | solution.py:455
  74.8 4.1 %load_weights.3 = (bf16[4096,512]{1,0:T(8,128)(2,1)S(1)}, bf16[4096,512]{1,0:T(8,128)(2,1)S(1)}, f32[8,128]{1,0:T(8,128)}) custom-call(bf16[8192,512]{1,0:T(8,128)(2,1)} %refs_0_.1, bf16[8192,512]{1,0:T(8,128)(2,1)} %collective-permute-done.17.refs_1_), custom_call_target="tpu_custom_call" | custom-call | flops 1 | bytes 1 | tf_op jit(solution)/shard_map/load_weights/pallas_call | solution.py:324
  78.9 1.7 %collective-permute-start.29 = (bf16[1,8,11264]{2,1,0:T(8,128)(2,1)S(1)}, bf16[1,8,11264]{2,1,0:T(8,128)(2,1)S(1)}, u32[]{:S(2)}, u32[]{:S(2)}) collective-permute-start(bf16[1,8,11264]{2,1,0:T(8,128)(2,1)S(1)} %collective-permute-done.28.refs_6_), channel_id=1, source_target_pairs={{0,2},{1,3},{2,6},{3,7},{6,10},{7,11},{10,14},{11,15},{14,12},{15,... | collective-permute-start | bytes 540680 | tf_op jit(solution)/shard_map/ppermute | solution.py:455
  80.6 1.4 %collective-permute-start.33 = (bf16[1,8,11264]{2,1,0:T(8,128)(2,1)S(1)}, bf16[1,8,11264]{2,1,0:T(8,128)(2,1)S(1)}, u32[]{:S(2)}, u32[]{:S(2)}) collective-permute-start(bf16[1,8,11264]{2,1,0:T(8,128)(2,1)S(1)} %collective-permute-done.24.refs_6_), channel_id=1, source_target_pairs={{0,2},{1,3},{2,6},{3,7},{6,10},{7,11},{10,14},{11,15},{14,12},{15,... | collective-permute-start | bytes 540680 | tf_op jit(solution)/shard_map/ppermute | solution.py:455
  82.0 0.6 collective-permute-start.32
  82.6 0.6 collective-permute-start.27
  83.3 3.0 %collective-permute-done.29.refs_5_ = bf16[1,8,11264]{2,1,0:T(8,128)(2,1)S(1)} collective-permute-done((bf16[1,8,11264]{2,1,0:T(8,128)(2,1)S(1)}, bf16[1,8,11264]{2,1,0:T(8,128)(2,1)S(1)}, u32[]{:S(2)}, u32[]{:S(2)}) %collective-permute-start.29) | collective-permute-done | bytes 180256 | tf_op jit(solution)/shard_map/ppermute | solution.py:455
  86.3 1.6 %collective-permute-start.31 = (bf16[1,8,11264]{2,1,0:T(8,128)(2,1)S(1)}, bf16[1,8,11264]{2,1,0:T(8,128)(2,1)S(1)}, u32[]{:S(2)}, u32[]{:S(2)}) collective-permute-start(bf16[1,8,11264]{2,1,0:T(8,128)(2,1)S(1)} %collective-permute-done.29.refs_5_), channel_id=1, source_target_pairs={{0,2},{1,3},{2,6},{3,7},{6,10},{7,11},{10,14},{11,15},{14,12},{15,... | collective-permute-start | bytes 540680 | tf_op jit(solution)/shard_map/ppermute | solution.py:455
  87.9 1.4 %features.1 = (f32[192,512]{1,0:T(8,128)S(1)}, f32[192,512]{1,0:T(8,128)S(1)}) custom-call(bf16[352,512]{1,0:T(8,128)(2,1)} %x_ref.4, bf16[352,512]{1,0:T(8,128)(2,1)S(1)} %collective-permute-done.14.x_other_ref), custom_call_target="tpu_custom_call" | custom-call | flops 1 | bytes 1 | tf_op jit(solution)/shard_map/features/pallas_call | solution.py:368
  89.2 1.8 %out_part.2 = (f32[192,512]{1,0:T(8,128)S(1)}, f32[192,512]{1,0:T(8,128)S(1)}) custom-call(bf16[1,8,11264]{2,1,0:T(8,128)(2,1)S(1)} %attend_part.2.refs_0_, bf16[1,8,11264]{2,1,0:T(8,128)(2,1)S(1)} %collective-permute-done.22.refs_1_, bf16[1,8,11264]{2,1,0:T(8,128)(2,1)S(1)} %collective-permute-done.26.refs_2_, ...), custom_call_target="tpu_custom_call" | custom-call | flops 1 | bytes 1 | tf_op jit(solution)/shard_map/out_part/pallas_call | solution.py:397
  91.1 0.7 collective-permute-done.31.refs_4_
  91.8 1.8 %out_part.3 = (bf16[192,512]{1,0:T(8,128)(2,1)S(1)}, bf16[192,512]{1,0:T(8,128)(2,1)S(1)}) custom-call(bf16[1,8,11264]{2,1,0:T(8,128)(2,1)S(1)} %attend_part.3.refs_0_, bf16[1,8,11264]{2,1,0:T(8,128)(2,1)S(1)} %collective-permute-done.20.refs_1_, bf16[1,8,11264]{2,1,0:T(8,128)(2,1)S(1)} %collective-permute-done.23.refs_2_, ...), custom_call_target="tpu_custom_call" | custom-call | flops 1 | bytes 1 | tf_op jit(solution)/shard_map/out_part/pallas_call | solution.py:397
  94.0 1.1 %collective-permute-done.34.rows_ref = bf16[192,512]{1,0:T(8,128)(2,1)S(1)} collective-permute-done((bf16[192,512]{1,0:T(8,128)(2,1)S(1)}, bf16[192,512]{1,0:T(8,128)(2,1)S(1)}, u32[]{:S(2)}, u32[]{:S(2)}) %collective-permute-start.34) | collective-permute-done | bytes 196640 | tf_op jit(solution)/shard_map/ppermute | solution.py:461
  95.1 1.1 %place.3 = bf16[352,512]{1,0:T(8,128)(2,1)} custom-call(bf16[192,512]{1,0:T(8,128)(2,1)S(1)} %collective-permute-done.34.rows_ref, bf16[352,512]{1,0:T(8,128)(2,1)S(1)} %place.2.refs_0_), custom_call_target="tpu_custom_call" | custom-call | flops 1 | bytes 1 | tf_op jit(solution)/shard_map/place/pallas_call | solution.py:421
  (63 shorter events, 4.7 us)
Async XLA Ops:
  0.0 0.7 copy-start
  6.2 2.0 %collective-permute-start = (bf16[2,8,14464]{2,1,0:T(8,128)(2,1)S(1)}, bf16[2,8,14464]{2,1,0:T(8,128)(2,1)S(1)}, u32[]{:S(2)}, u32[]{:S(2)}) collective-permute-start(bf16[2,8,14464]{2,1,0:T(8,128)(2,1)S(1)} %get-tuple-element.60), channel_id=1, source_target_pairs={{0,1},{1,0},{2,3},{3,2},{4,5},{5,4},{6,7},{7,6},{8,9},{9,8},{10,11... | collective-permute-start | bytes 1388552 | tf_op jit(solution)/shard_map/ppermute | solution.py:461
  6.7 12.0 %collective-permute-start.2 = (bf16[6,8,14464]{2,1,0:T(8,128)(2,1)}, bf16[6,8,14464]{2,1,0:T(8,128)(2,1)S(1)}, u32[]{:S(2)}, u32[]{:S(2)}) collective-permute-start(bf16[6,8,14464]{2,1,0:T(8,128)(2,1)} %get-tuple-element.65), channel_id=1, source_target_pairs={{0,1},{1,0},{2,3},{3,2},{4,5},{5,4},{6,7},{7,6},{8,9},{9,8},{10,11... | collective-permute-start | bytes 4165640 | tf_op jit(solution)/shard_map/ppermute | solution.py:461
  8.3 9.0 %collective-permute-start.3 = (bf16[1,8,14464]{2,1,0:T(8,128)(2,1)S(1)}, bf16[1,8,14464]{2,1,0:T(8,128)(2,1)S(1)}, u32[]{:S(2)}, u32[]{:S(2)}) collective-permute-start(bf16[1,8,14464]{2,1,0:T(8,128)(2,1)S(1)} %get-tuple-element.122), channel_id=1, source_target_pairs={{0,2},{1,3},{2,6},{3,7},{6,10},{7,11},{10,14},{11,15},{14,12},{15,... | collective-permute-start | bytes 694280 | tf_op jit(solution)/shard_map/ppermute | solution.py:455
  11.3 7.4 %collective-permute-start.4 = (bf16[1,8,14464]{2,1,0:T(8,128)(2,1)S(1)}, bf16[1,8,14464]{2,1,0:T(8,128)(2,1)S(1)}, u32[]{:S(2)}, u32[]{:S(2)}) collective-permute-start(bf16[1,8,14464]{2,1,0:T(8,128)(2,1)S(1)} %get-tuple-element.121), channel_id=1, source_target_pairs={{2,0},{3,1},{6,2},{7,3},{10,6},{11,7},{14,10},{15,11},{12,14},{13,... | collective-permute-start | bytes 694280 | tf_op jit(solution)/shard_map/ppermute | solution.py:455
  16.8 4.5 %collective-permute-start.5 = (bf16[2,8,14080]{2,1,0:T(8,128)(2,1)S(1)}, bf16[2,8,14080]{2,1,0:T(8,128)(2,1)S(1)}, u32[]{:S(2)}, u32[]{:S(2)}) collective-permute-start(bf16[2,8,14080]{2,1,0:T(8,128)(2,1)S(1)} %get-tuple-element.71), channel_id=1, source_target_pairs={{0,1},{1,0},{2,3},{3,2},{4,5},{5,4},{6,7},{7,6},{8,9},{9,8},{10,11... | collective-permute-start | bytes 1351688 | tf_op jit(solution)/shard_map/ppermute | solution.py:461
  16.8 17.3 %collective-permute-start.1 = (bf16[6,8,14080]{2,1,0:T(8,128)(2,1)}, bf16[6,8,14080]{2,1,0:T(8,128)(2,1)S(1)}, u32[]{:S(2)}, u32[]{:S(2)}) collective-permute-start(bf16[6,8,14080]{2,1,0:T(8,128)(2,1)} %get-tuple-element.63), channel_id=1, source_target_pairs={{0,1},{1,0},{2,3},{3,2},{4,5},{5,4},{6,7},{7,6},{8,9},{9,8},{10,11... | collective-permute-start | bytes 4055048 | tf_op jit(solution)/shard_map/ppermute | solution.py:461
  19.1 8.6 %collective-permute-start.7 = (bf16[1,8,14464]{2,1,0:T(8,128)(2,1)S(1)}, bf16[1,8,14464]{2,1,0:T(8,128)(2,1)S(1)}, u32[]{:S(2)}, u32[]{:S(2)}) collective-permute-start(bf16[1,8,14464]{2,1,0:T(8,128)(2,1)S(1)} %get-tuple-element.116), channel_id=1, source_target_pairs={{0,2},{1,3},{2,6},{3,7},{6,10},{7,11},{10,14},{11,15},{14,12},{15,... | collective-permute-start | bytes 694280 | tf_op jit(solution)/shard_map/ppermute | solution.py:455
  20.8 8.6 %collective-permute-start.8 = (bf16[1,8,14464]{2,1,0:T(8,128)(2,1)S(1)}, bf16[1,8,14464]{2,1,0:T(8,128)(2,1)S(1)}, u32[]{:S(2)}, u32[]{:S(2)}) collective-permute-start(bf16[1,8,14464]{2,1,0:T(8,128)(2,1)S(1)} %get-tuple-element.115), channel_id=1, source_target_pairs={{2,0},{3,1},{6,2},{7,3},{10,6},{11,7},{14,10},{15,11},{12,14},{13,... | collective-permute-start | bytes 694280 | tf_op jit(solution)/shard_map/ppermute | solution.py:455
  21.4 10.5 %collective-permute-start.6 = (bf16[1,8,14080]{2,1,0:T(8,128)(2,1)S(1)}, bf16[1,8,14080]{2,1,0:T(8,128)(2,1)S(1)}, u32[]{:S(2)}, u32[]{:S(2)}) collective-permute-start(bf16[1,8,14080]{2,1,0:T(8,128)(2,1)S(1)} %get-tuple-element.124), channel_id=1, source_target_pairs={{0,2},{1,3},{2,6},{3,7},{6,10},{7,11},{10,14},{11,15},{14,12},{15,... | collective-permute-start | bytes 675848 | tf_op jit(solution)/shard_map/ppermute | solution.py:455
  23.0 11.2 %collective-permute-start.11 = (bf16[1,8,14080]{2,1,0:T(8,128)(2,1)S(1)}, bf16[1,8,14080]{2,1,0:T(8,128)(2,1)S(1)}, u32[]{:S(2)}, u32[]{:S(2)}) collective-permute-start(bf16[1,8,14080]{2,1,0:T(8,128)(2,1)S(1)} %get-tuple-element.123), channel_id=1, source_target_pairs={{2,0},{3,1},{6,2},{7,3},{10,6},{11,7},{14,10},{15,11},{12,14},{13,... | collective-permute-start | bytes 675848 | tf_op jit(solution)/shard_map/ppermute | solution.py:455
  29.5 9.7 %collective-permute-start.10 = (bf16[1,8,14464]{2,1,0:T(8,128)(2,1)S(1)}, bf16[1,8,14464]{2,1,0:T(8,128)(2,1)S(1)}, u32[]{:S(2)}, u32[]{:S(2)}) collective-permute-start(bf16[1,8,14464]{2,1,0:T(8,128)(2,1)S(1)} %get-tuple-element.113), channel_id=1, source_target_pairs={{2,0},{3,1},{6,2},{7,3},{10,6},{11,7},{14,10},{15,11},{12,14},{13,... | collective-permute-start | bytes 694280 | tf_op jit(solution)/shard_map/ppermute | solution.py:455
  30.0 15.5 %collective-permute-start.15 = (bf16[1,8,14464]{2,1,0:T(8,128)(2,1)S(1)}, bf16[1,8,14464]{2,1,0:T(8,128)(2,1)S(1)}, u32[]{:S(2)}, u32[]{:S(2)}) collective-permute-start(bf16[1,8,14464]{2,1,0:T(8,128)(2,1)S(1)} %get-tuple-element.114), channel_id=1, source_target_pairs={{0,2},{1,3},{2,6},{3,7},{6,10},{7,11},{10,14},{11,15},{14,12},{15,... | collective-permute-start | bytes 694280 | tf_op jit(solution)/shard_map/ppermute | solution.py:455
  34.5 8.6 %copy-start.1 = (bf16[6,8,14080]{2,1,0:T(8,128)(2,1)}, bf16[6,8,14080]{2,1,0:T(8,128)(2,1)S(1)}, u32[]{:S(2)}) copy-start(bf16[6,8,14080]{2,1,0:T(8,128)(2,1)S(1)} %add_convert_fusion.1) | copy-start | bytes 4055044
  34.6 10.4 %copy-start.2 = (s32[22]{0:T(128)S(1)}, s32[22]{0:T(128)}, u32[]{:S(2)}) copy-start(s32[22]{0:T(128)} %param.13) | copy-start | bytes 268
  34.6 6.0 %collective-permute-start.9 = (bf16[1,8,14080]{2,1,0:T(8,128)(2,1)S(1)}, bf16[1,8,14080]{2,1,0:T(8,128)(2,1)S(1)}, u32[]{:S(2)}, u32[]{:S(2)}) collective-permute-start(bf16[1,8,14080]{2,1,0:T(8,128)(2,1)S(1)} %get-tuple-element.120), channel_id=1, source_target_pairs={{0,2},{1,3},{2,6},{3,7},{6,10},{7,11},{10,14},{11,15},{14,12},{15,... | collective-permute-start | bytes 675848 | tf_op jit(solution)/shard_map/ppermute | solution.py:455
  36.3 6.0 %collective-permute-start.13 = (bf16[1,8,14080]{2,1,0:T(8,128)(2,1)S(1)}, bf16[1,8,14080]{2,1,0:T(8,128)(2,1)S(1)}, u32[]{:S(2)}, u32[]{:S(2)}) collective-permute-start(bf16[1,8,14080]{2,1,0:T(8,128)(2,1)S(1)} %get-tuple-element.119), channel_id=1, source_target_pairs={{2,0},{3,1},{6,2},{7,3},{10,6},{11,7},{14,10},{15,11},{12,14},{13,... | collective-permute-start | bytes 675848 | tf_op jit(solution)/shard_map/ppermute | solution.py:455
  36.7 22.6 %collective-permute-start.17 = (bf16[8192,512]{1,0:T(8,128)(2,1)}, bf16[8192,512]{1,0:T(8,128)(2,1)}, u32[]{:S(2)}, u32[]{:S(2)}) collective-permute-start(bf16[8192,512]{1,0:T(8,128)(2,1)} %refs_0_.1), channel_id=1, source_target_pairs={{0,1},{1,0},{2,3},{3,2},{4,5},{5,4},{6,7},{7,6},{8,9},{9,8},{10,11... | collective-permute-start | bytes 25165832 | tf_op jit(solution)/shard_map/ppermute | solution.py:461
  39.1 13.2 %collective-permute-start.14 = (bf16[352,512]{1,0:T(8,128)(2,1)}, bf16[352,512]{1,0:T(8,128)(2,1)S(1)}, u32[]{:S(2)}, u32[]{:S(2)}) collective-permute-start(bf16[352,512]{1,0:T(8,128)(2,1)} %x_ref.4), channel_id=1, source_target_pairs={{0,1},{1,0},{2,3},{3,2},{4,5},{5,4},{6,7},{7,6},{8,9},{9,8},{10,11... | collective-permute-start | bytes 1081352 | tf_op jit(solution)/shard_map/ppermute | solution.py:461
  40.7 8.6 %collective-permute-start.16 = (bf16[1,8,14464]{2,1,0:T(8,128)(2,1)S(1)}, bf16[1,8,14464]{2,1,0:T(8,128)(2,1)S(1)}, u32[]{:S(2)}, u32[]{:S(2)}) collective-permute-start(bf16[1,8,14464]{2,1,0:T(8,128)(2,1)S(1)} %add_convert_fusion.4), channel_id=1, source_target_pairs={{2,0},{3,1},{6,2},{7,3},{10,6},{11,7},{14,10},{15,11},{12,14},{13,... | collective-permute-start | bytes 694280 | tf_op jit(solution)/shard_map/ppermute | solution.py:455
  43.1 6.2 %collective-permute-start.12 = (bf16[1,8,14080]{2,1,0:T(8,128)(2,1)}, bf16[1,8,14080]{2,1,0:T(8,128)(2,1)S(1)}, u32[]{:S(2)}, u32[]{:S(2)}) collective-permute-start(bf16[1,8,14080]{2,1,0:T(8,128)(2,1)} %get-tuple-element.118), channel_id=1, source_target_pairs={{0,2},{1,3},{2,6},{3,7},{6,10},{7,11},{10,14},{11,15},{14,12},{15,... | collective-permute-start | bytes 675848 | tf_op jit(solution)/shard_map/ppermute | solution.py:455
  45.4 13.9 %collective-permute-start.19 = (bf16[1,8,14080]{2,1,0:T(8,128)(2,1)}, bf16[1,8,14080]{2,1,0:T(8,128)(2,1)S(1)}, u32[]{:S(2)}, u32[]{:S(2)}) collective-permute-start(bf16[1,8,14080]{2,1,0:T(8,128)(2,1)} %get-tuple-element.117), channel_id=1, source_target_pairs={{2,0},{3,1},{6,2},{7,3},{10,6},{11,7},{14,10},{15,11},{12,14},{13,... | collective-permute-start | bytes 675848 | tf_op jit(solution)/shard_map/ppermute | solution.py:455
  50.3 9.0 %collective-permute-start.18 = (bf16[1,8,14080]{2,1,0:T(8,128)(2,1)S(1)}, bf16[1,8,14080]{2,1,0:T(8,128)(2,1)S(1)}, u32[]{:S(2)}, u32[]{:S(2)}) collective-permute-start(bf16[1,8,14080]{2,1,0:T(8,128)(2,1)S(1)} %add_convert_fusion.9), channel_id=1, source_target_pairs={{0,2},{1,3},{2,6},{3,7},{6,10},{7,11},{10,14},{11,15},{14,12},{15,... | collective-permute-start | bytes 675848 | tf_op jit(solution)/shard_map/ppermute | solution.py:455
  57.2 9.0 %collective-permute-start.22 = (bf16[1,8,11264]{2,1,0:T(8,128)(2,1)S(1)}, bf16[1,8,11264]{2,1,0:T(8,128)(2,1)S(1)}, u32[]{:S(2)}, u32[]{:S(2)}) collective-permute-start(bf16[1,8,11264]{2,1,0:T(8,128)(2,1)S(1)} %attend_part.2.refs_0_), channel_id=1, source_target_pairs={{2,0},{3,1},{6,2},{7,3},{10,6},{11,7},{14,10},{15,11},{12,14},{13,... | collective-permute-start | bytes 540680 | tf_op jit(solution)/shard_map/ppermute | solution.py:455
  57.5 9.0 %collective-permute-start.21 = (bf16[1,8,11264]{2,1,0:T(8,128)(2,1)S(1)}, bf16[1,8,11264]{2,1,0:T(8,128)(2,1)S(1)}, u32[]{:S(2)}, u32[]{:S(2)}) collective-permute-start(bf16[1,8,11264]{2,1,0:T(8,128)(2,1)S(1)} %attend_part.2.refs_0_), channel_id=1, source_target_pairs={{0,2},{1,3},{2,6},{3,7},{6,10},{7,11},{10,14},{11,15},{14,12},{15,... | collective-permute-start | bytes 540680 | tf_op jit(solution)/shard_map/ppermute | solution.py:455
  64.1 8.2 %collective-permute-start.25 = (bf16[1,8,11264]{2,1,0:T(8,128)(2,1)S(1)}, bf16[1,8,11264]{2,1,0:T(8,128)(2,1)S(1)}, u32[]{:S(2)}, u32[]{:S(2)}) collective-permute-start(bf16[1,8,11264]{2,1,0:T(8,128)(2,1)S(1)} %attend_part.3.refs_0_), channel_id=1, source_target_pairs={{0,2},{1,3},{2,6},{3,7},{6,10},{7,11},{10,14},{11,15},{14,12},{15,... | collective-permute-start | bytes 540680 | tf_op jit(solution)/shard_map/ppermute | solution.py:455
  65.1 8.2 %collective-permute-start.20 = (bf16[1,8,11264]{2,1,0:T(8,128)(2,1)S(1)}, bf16[1,8,11264]{2,1,0:T(8,128)(2,1)S(1)}, u32[]{:S(2)}, u32[]{:S(2)}) collective-permute-start(bf16[1,8,11264]{2,1,0:T(8,128)(2,1)S(1)} %attend_part.3.refs_0_), channel_id=1, source_target_pairs={{2,0},{3,1},{6,2},{7,3},{10,6},{11,7},{14,10},{15,11},{12,14},{13,... | collective-permute-start | bytes 540680 | tf_op jit(solution)/shard_map/ppermute | solution.py:455
  66.2 8.2 %collective-permute-start.26 = (bf16[1,8,11264]{2,1,0:T(8,128)(2,1)S(1)}, bf16[1,8,11264]{2,1,0:T(8,128)(2,1)S(1)}, u32[]{:S(2)}, u32[]{:S(2)}) collective-permute-start(bf16[1,8,11264]{2,1,0:T(8,128)(2,1)S(1)} %collective-permute-done.22.refs_1_), channel_id=1, source_target_pairs={{2,0},{3,1},{6,2},{7,3},{10,6},{11,7},{14,10},{15,11},{12,14},{13,... | collective-permute-start | bytes 540680 | tf_op jit(solution)/shard_map/ppermute | solution.py:455
  66.5 8.0 %collective-permute-start.24 = (bf16[1,8,11264]{2,1,0:T(8,128)(2,1)S(1)}, bf16[1,8,11264]{2,1,0:T(8,128)(2,1)S(1)}, u32[]{:S(2)}, u32[]{:S(2)}) collective-permute-start(bf16[1,8,11264]{2,1,0:T(8,128)(2,1)S(1)} %collective-permute-done.21.refs_7_), channel_id=1, source_target_pairs={{0,2},{1,3},{2,6},{3,7},{6,10},{7,11},{10,14},{11,15},{14,12},{15,... | collective-permute-start | bytes 540680 | tf_op jit(solution)/shard_map/ppermute | solution.py:455
  72.4 6.5 %collective-permute-start.28 = (bf16[1,8,11264]{2,1,0:T(8,128)(2,1)S(1)}, bf16[1,8,11264]{2,1,0:T(8,128)(2,1)S(1)}, u32[]{:S(2)}, u32[]{:S(2)}) collective-permute-start(bf16[1,8,11264]{2,1,0:T(8,128)(2,1)S(1)} %collective-permute-done.25.refs_7_), channel_id=1, source_target_pairs={{0,2},{1,3},{2,6},{3,7},{6,10},{7,11},{10,14},{11,15},{14,12},{15,... | collective-permute-start | bytes 540680 | tf_op jit(solution)/shard_map/ppermute | solution.py:455
  73.3 8.7 %collective-permute-start.23 = (bf16[1,8,11264]{2,1,0:T(8,128)(2,1)S(1)}, bf16[1,8,11264]{2,1,0:T(8,128)(2,1)S(1)}, u32[]{:S(2)}, u32[]{:S(2)}) collective-permute-start(bf16[1,8,11264]{2,1,0:T(8,128)(2,1)S(1)} %collective-permute-done.20.refs_1_), channel_id=1, source_target_pairs={{2,0},{3,1},{6,2},{7,3},{10,6},{11,7},{14,10},{15,11},{12,14},{13,... | collective-permute-start | bytes 540680 | tf_op jit(solution)/shard_map/ppermute | solution.py:455
  74.4 7.6 %collective-permute-start.30 = (bf16[1,8,11264]{2,1,0:T(8,128)(2,1)S(1)}, bf16[1,8,11264]{2,1,0:T(8,128)(2,1)S(1)}, u32[]{:S(2)}, u32[]{:S(2)}) collective-permute-start(bf16[1,8,11264]{2,1,0:T(8,128)(2,1)S(1)} %collective-permute-done.26.refs_2_), channel_id=1, source_target_pairs={{2,0},{3,1},{6,2},{7,3},{10,6},{11,7},{14,10},{15,11},{12,14},{13,... | collective-permute-start | bytes 540680 | tf_op jit(solution)/shard_map/ppermute | solution.py:455
  78.9 7.4 %collective-permute-start.29 = (bf16[1,8,11264]{2,1,0:T(8,128)(2,1)S(1)}, bf16[1,8,11264]{2,1,0:T(8,128)(2,1)S(1)}, u32[]{:S(2)}, u32[]{:S(2)}) collective-permute-start(bf16[1,8,11264]{2,1,0:T(8,128)(2,1)S(1)} %collective-permute-done.28.refs_6_), channel_id=1, source_target_pairs={{0,2},{1,3},{2,6},{3,7},{6,10},{7,11},{10,14},{11,15},{14,12},{15,... | collective-permute-start | bytes 540680 | tf_op jit(solution)/shard_map/ppermute | solution.py:455
  80.6 8.6 %collective-permute-start.33 = (bf16[1,8,11264]{2,1,0:T(8,128)(2,1)S(1)}, bf16[1,8,11264]{2,1,0:T(8,128)(2,1)S(1)}, u32[]{:S(2)}, u32[]{:S(2)}) collective-permute-start(bf16[1,8,11264]{2,1,0:T(8,128)(2,1)S(1)} %collective-permute-done.24.refs_6_), channel_id=1, source_target_pairs={{0,2},{1,3},{2,6},{3,7},{6,10},{7,11},{10,14},{11,15},{14,12},{15,... | collective-permute-start | bytes 540680 | tf_op jit(solution)/shard_map/ppermute | solution.py:455
  82.0 7.2 %collective-permute-start.32 = (bf16[1,8,11264]{2,1,0:T(8,128)(2,1)S(1)}, bf16[1,8,11264]{2,1,0:T(8,128)(2,1)S(1)}, u32[]{:S(2)}, u32[]{:S(2)}) collective-permute-start(bf16[1,8,11264]{2,1,0:T(8,128)(2,1)S(1)} %collective-permute-done.30.refs_3_), channel_id=1, source_target_pairs={{2,0},{3,1},{6,2},{7,3},{10,6},{11,7},{14,10},{15,11},{12,14},{13,... | collective-permute-start | bytes 540680 | tf_op jit(solution)/shard_map/ppermute | solution.py:455
  82.6 8.4 %collective-permute-start.27 = (bf16[1,8,11264]{2,1,0:T(8,128)(2,1)S(1)}, bf16[1,8,11264]{2,1,0:T(8,128)(2,1)S(1)}, u32[]{:S(2)}, u32[]{:S(2)}) collective-permute-start(bf16[1,8,11264]{2,1,0:T(8,128)(2,1)S(1)} %collective-permute-done.23.refs_2_), channel_id=1, source_target_pairs={{2,0},{3,1},{6,2},{7,3},{10,6},{11,7},{14,10},{15,11},{12,14},{13,... | collective-permute-start | bytes 540680 | tf_op jit(solution)/shard_map/ppermute | solution.py:455
  86.3 5.5 %collective-permute-start.31 = (bf16[1,8,11264]{2,1,0:T(8,128)(2,1)S(1)}, bf16[1,8,11264]{2,1,0:T(8,128)(2,1)S(1)}, u32[]{:S(2)}, u32[]{:S(2)}) collective-permute-start(bf16[1,8,11264]{2,1,0:T(8,128)(2,1)S(1)} %collective-permute-done.29.refs_5_), channel_id=1, source_target_pairs={{0,2},{1,3},{2,6},{3,7},{6,10},{7,11},{10,14},{11,15},{14,12},{15,... | collective-permute-start | bytes 540680 | tf_op jit(solution)/shard_map/ppermute | solution.py:455
  93.6 1.5 %collective-permute-start.34 = (bf16[192,512]{1,0:T(8,128)(2,1)S(1)}, bf16[192,512]{1,0:T(8,128)(2,1)S(1)}, u32[]{:S(2)}, u32[]{:S(2)}) collective-permute-start(bf16[192,512]{1,0:T(8,128)(2,1)S(1)} %get-tuple-element.111), channel_id=1, source_target_pairs={{0,1},{1,0},{2,3},{3,2},{4,5},{5,4},{6,7},{7,6},{8,9},{9,8},{10,11... | collective-permute-start | bytes 589832 | tf_op jit(solution)/shard_map/ppermute | solution.py:461

commit v6 on v5

--- a/solution.py
+++ b/solution.py
@@ -15,7 +15,7 @@
 GROUP = HEADS // KVH
 PARTS = ((0, 4), (4, 4))
 LOADS_AHEAD = 6
-PIECE_GROUPS = (1, 2, 3, 4)
+PIECE_GROUPS = (2, 3, 3, 2)
 CUTS = 2
 MIB = 1 << 20
 BF = jnp.bfloat16

time: 96.4 us -> 96.2 us (level)
  no operation moved by 1% of the time
where the time goes in v6:
time: 96.2 us; the launch traced here: 96 us
  Pallas kernels  34.9 us (36%)
  starting transfers between devices  32.6 us (34%)
  waiting for transfers between devices  23.7 us (25%)
  other arithmetic  3.45 us (4%)
  local copies, waits for them, and re-layouts  1.1 us (1%)
    ppermute x28, starting transfers between devices, ring(): lax.ppermute(a, 'gx', up_pairs if way == 'up' else down_pairs)  31.3 us
    ppermute x28, waiting for transfers between devices, ring(): lax.ppermute(a, 'gx', up_pairs if way == 'up' else down_pairs)  21.2 us
    pallas_call x2, Pallas kernels, project(): pl.pallas_call(functools.partial(qkv_kernel, order, index, rows, pad), in...  10.7 us
    pallas_call x2, Pallas kernels, attend(): pl.pallas_call(functools.partial(attend_kernel, part, rows, pad), in_spec...  9.61 us
    pallas_call x2, Pallas kernels, load(): pl.pallas_call(kernel, in_specs=[pl.BlockSpec(memory_space=pltpu.HBM)] *...  8.15 us
    pallas_call x2, Pallas kernels, project_out(): pl.pallas_call(functools.partial(out_kernel, rows, pad), in_specs=[vmem]...  3.59 us
    ppermute x7, waiting for transfers between devices, cross(): return lax.ppermute(a, 'gx', sibling)  2.43 us
    convert_element_type x6, other arithmetic, part_steps(): sent[way] = (wide(sent[way]) + wide(tied(moved[way]))).astype(BF)  2.27 us
  transfers between devices with their start and end apart: 35, of which 13 were waited for; matrix products, arithmetic and copies ran while one was open for 4% of the time, Pallas kernels for 28%

profile of v6, /device:TPU:0, one launch (start us, length us, event | category | flops | bytes accessed | tf_op | source)
XLA Modules:
  0.0 96.0 jit_solution(1082429595935061241)
XLA Ops:
  0.0 0.7 copy-done
  0.7 5.4 %qkv_part.2 = (bf16[2,8,14464]{2,1,0:T(8,128)(2,1)S(1)}, bf16[6,8,14464]{2,1,0:T(8,128)(2,1)S(1)}, bf16[2,8,14464]{2,1,0:T(8,128)(2,1)S(1)}, bf16[6,8,14464]{2,1,0:T(8,128)(2,1)}, f32[8,128]{1,0:T(8,128)}) custom-call(bf16[352,512]{1,0:T(8,128)(2,1)} %x_ref.4, f32[1,512]{1,0:T(1,128)S(1)} %bitcast.5, bf16[512,10240]{1,0:T(8,128)(2,1)} %w_ref.3), custom_call_target="tpu_custom_call" | custom-call | flops 1 | bytes 1 | tf_op jit(solution)/shard_map/qkv_part/pallas_call | solution.py:202
  6.1 0.5 collective-permute-start
  6.7 1.4 %collective-permute-done = bf16[2,8,14464]{2,1,0:T(8,128)(2,1)S(1)} collective-permute-done((bf16[2,8,14464]{2,1,0:T(8,128)(2,1)S(1)}, bf16[2,8,14464]{2,1,0:T(8,128)(2,1)S(1)}, u32[]{:S(2)}, u32[]{:S(2)}) %collective-permute-start) | collective-permute-done | bytes 462880 | tf_op jit(solution)/shard_map/ppermute | solution.py:461
  8.2 2.9 %collective-permute-start.3 = (bf16[1,8,14464]{2,1,0:T(8,128)(2,1)S(1)}, bf16[1,8,14464]{2,1,0:T(8,128)(2,1)S(1)}, u32[]{:S(2)}, u32[]{:S(2)}) collective-permute-start(bf16[1,8,14464]{2,1,0:T(8,128)(2,1)S(1)} %get-tuple-element.122), channel_id=1, source_target_pairs={{0,2},{1,3},{2,6},{3,7},{6,10},{7,11},{10,14},{11,15},{14,12},{15,... | collective-permute-start | bytes 694280 | tf_op jit(solution)/shard_map/ppermute | solution.py:455
  11.3 5.3 %qkv_part.3 = (bf16[2,8,14080]{2,1,0:T(8,128)(2,1)S(1)}, bf16[6,8,14080]{2,1,0:T(8,128)(2,1)S(1)}, bf16[2,8,14080]{2,1,0:T(8,128)(2,1)S(1)}, bf16[6,8,14080]{2,1,0:T(8,128)(2,1)}, f32[8,128]{1,0:T(8,128)}) custom-call(bf16[352,512]{1,0:T(8,128)(2,1)} %x_ref.4, f32[1,512]{1,0:T(1,128)S(1)} %bitcast.6, bf16[512,10240]{1,0:T(8,128)(2,1)} %w_ref.3), custom_call_target="tpu_custom_call" | custom-call | flops 1 | bytes 1 | tf_op jit(solution)/shard_map/qkv_part/pallas_call | solution.py:202
  16.7 0.5 collective-permute-start.1
  17.2 1.4 %collective-permute-done.4 = bf16[1,8,14464]{2,1,0:T(8,128)(2,1)S(1)} collective-permute-done((bf16[1,8,14464]{2,1,0:T(8,128)(2,1)S(1)}, bf16[1,8,14464]{2,1,0:T(8,128)(2,1)S(1)}, u32[]{:S(2)}, u32[]{:S(2)}) %collective-permute-start.4) | collective-permute-done | bytes 231456 | tf_op jit(solution)/shard_map/ppermute | solution.py:455
  19.1 1.6 %collective-permute-start.7 = (bf16[1,8,14464]{2,1,0:T(8,128)(2,1)S(1)}, bf16[1,8,14464]{2,1,0:T(8,128)(2,1)S(1)}, u32[]{:S(2)}, u32[]{:S(2)}) collective-permute-start(bf16[1,8,14464]{2,1,0:T(8,128)(2,1)S(1)} %get-tuple-element.116), channel_id=1, source_target_pairs={{0,2},{1,3},{2,6},{3,7},{6,10},{7,11},{10,14},{11,15},{14,12},{15,... | collective-permute-start | bytes 694280 | tf_op jit(solution)/shard_map/ppermute | solution.py:455
  20.7 0.4 collective-permute-start.8
  21.3 1.6 %collective-permute-start.6 = (bf16[1,8,14080]{2,1,0:T(8,128)(2,1)S(1)}, bf16[1,8,14080]{2,1,0:T(8,128)(2,1)S(1)}, u32[]{:S(2)}, u32[]{:S(2)}) collective-permute-start(bf16[1,8,14080]{2,1,0:T(8,128)(2,1)S(1)} %get-tuple-element.124), channel_id=1, source_target_pairs={{0,2},{1,3},{2,6},{3,7},{6,10},{7,11},{10,14},{11,15},{14,12},{15,... | collective-permute-start | bytes 675848 | tf_op jit(solution)/shard_map/ppermute | solution.py:455
  22.9 0.4 collective-permute-start.11
  23.4 4.3 %collective-permute-done.7 = bf16[1,8,14464]{2,1,0:T(8,128)(2,1)S(1)} collective-permute-done((bf16[1,8,14464]{2,1,0:T(8,128)(2,1)S(1)}, bf16[1,8,14464]{2,1,0:T(8,128)(2,1)S(1)}, u32[]{:S(2)}, u32[]{:S(2)}) %collective-permute-start.7) | collective-permute-done | bytes 231456 | tf_op jit(solution)/shard_map/ppermute | solution.py:455
  27.7 1.6 %collective-permute-done.8 = bf16[1,8,14464]{2,1,0:T(8,128)(2,1)S(1)} collective-permute-done((bf16[1,8,14464]{2,1,0:T(8,128)(2,1)S(1)}, bf16[1,8,14464]{2,1,0:T(8,128)(2,1)S(1)}, u32[]{:S(2)}, u32[]{:S(2)}) %collective-permute-start.8) | collective-permute-done | bytes 231456 | tf_op jit(solution)/shard_map/ppermute | solution.py:455
  29.4 0.5 collective-permute-start.10
  29.9 1.6 %collective-permute-start.15 = (bf16[1,8,14464]{2,1,0:T(8,128)(2,1)S(1)}, bf16[1,8,14464]{2,1,0:T(8,128)(2,1)S(1)}, u32[]{:S(2)}, u32[]{:S(2)}) collective-permute-start(bf16[1,8,14464]{2,1,0:T(8,128)(2,1)S(1)} %get-tuple-element.114), channel_id=1, source_target_pairs={{0,2},{1,3},{2,6},{3,7},{6,10},{7,11},{10,14},{11,15},{14,12},{15,... | collective-permute-start | bytes 694280 | tf_op jit(solution)/shard_map/ppermute | solution.py:455
  31.9 2.2 %collective-permute-done.11 = bf16[1,8,14080]{2,1,0:T(8,128)(2,1)S(1)} collective-permute-done((bf16[1,8,14080]{2,1,0:T(8,128)(2,1)S(1)}, bf16[1,8,14080]{2,1,0:T(8,128)(2,1)S(1)}, u32[]{:S(2)}, u32[]{:S(2)}) %collective-permute-start.11) | collective-permute-done | bytes 225312 | tf_op jit(solution)/shard_map/ppermute | solution.py:455
  34.6 1.6 %collective-permute-start.9 = (bf16[1,8,14080]{2,1,0:T(8,128)(2,1)S(1)}, bf16[1,8,14080]{2,1,0:T(8,128)(2,1)S(1)}, u32[]{:S(2)}, u32[]{:S(2)}) collective-permute-start(bf16[1,8,14080]{2,1,0:T(8,128)(2,1)S(1)} %get-tuple-element.120), channel_id=1, source_target_pairs={{0,2},{1,3},{2,6},{3,7},{6,10},{7,11},{10,14},{11,15},{14,12},{15,... | collective-permute-start | bytes 675848 | tf_op jit(solution)/shard_map/ppermute | solution.py:455
  36.7 2.3 %collective-permute-done.10 = bf16[1,8,14464]{2,1,0:T(8,128)(2,1)S(1)} collective-permute-done((bf16[1,8,14464]{2,1,0:T(8,128)(2,1)S(1)}, bf16[1,8,14464]{2,1,0:T(8,128)(2,1)S(1)}, u32[]{:S(2)}, u32[]{:S(2)}) %collective-permute-start.10) | collective-permute-done | bytes 231456 | tf_op jit(solution)/shard_map/ppermute | solution.py:455
  39.1 1.5 %collective-permute-done.9 = bf16[1,8,14080]{2,1,0:T(8,128)(2,1)S(1)} collective-permute-done((bf16[1,8,14080]{2,1,0:T(8,128)(2,1)S(1)}, bf16[1,8,14080]{2,1,0:T(8,128)(2,1)S(1)}, u32[]{:S(2)}, u32[]{:S(2)}) %collective-permute-start.9) | collective-permute-done | bytes 225312 | tf_op jit(solution)/shard_map/ppermute | solution.py:455
  40.6 1.3 %collective-permute-start.16 = (bf16[1,8,14464]{2,1,0:T(8,128)(2,1)S(1)}, bf16[1,8,14464]{2,1,0:T(8,128)(2,1)S(1)}, u32[]{:S(2)}, u32[]{:S(2)}) collective-permute-start(bf16[1,8,14464]{2,1,0:T(8,128)(2,1)S(1)} %add_convert_fusion.4), channel_id=1, source_target_pairs={{2,0},{3,1},{6,2},{7,3},{10,6},{11,7},{14,10},{15,11},{12,14},{13,... | collective-permute-start | bytes 694280 | tf_op jit(solution)/shard_map/ppermute | solution.py:455
  42.2 0.9 add_convert_fusion.10
  43.1 2.0 %collective-permute-start.12 = (bf16[1,8,14080]{2,1,0:T(8,128)(2,1)}, bf16[1,8,14080]{2,1,0:T(8,128)(2,1)S(1)}, u32[]{:S(2)}, u32[]{:S(2)}) collective-permute-start(bf16[1,8,14080]{2,1,0:T(8,128)(2,1)} %get-tuple-element.118), channel_id=1, source_target_pairs={{0,2},{1,3},{2,6},{3,7},{6,10},{7,11},{10,14},{11,15},{14,12},{15,... | collective-permute-start | bytes 675848 | tf_op jit(solution)/shard_map/ppermute | solution.py:455
  45.5 3.7 %collective-permute-done.16.right_ref = bf16[1,8,14464]{2,1,0:T(8,128)(2,1)S(1)} collective-permute-done((bf16[1,8,14464]{2,1,0:T(8,128)(2,1)S(1)}, bf16[1,8,14464]{2,1,0:T(8,128)(2,1)S(1)}, u32[]{:S(2)}, u32[]{:S(2)}) %collective-permute-start.16) | collective-permute-done | bytes 231456 | tf_op jit(solution)/shard_map/ppermute | solution.py:455
  49.3 1.0 %add_convert_fusion.9 = bf16[1,8,14080]{2,1,0:T(8,128)(2,1)S(1)} fusion(bf16[1,8,14080]{2,1,0:T(8,128)(2,1)S(1)} %collective-permute-done.12, bf16[6,8,14080]{2,1,0:T(8,128)(2,1)} %copy-done.1), kind=kLoop, calls=%fused_computation.9 | loop fusion | flops 450560 | bytes 675840 | tf_op jit(solution)/shard_map/convert_element_type | solution.py:504
  50.3 2.0 %collective-permute-start.18 = (bf16[1,8,14080]{2,1,0:T(8,128)(2,1)S(1)}, bf16[1,8,14080]{2,1,0:T(8,128)(2,1)S(1)}, u32[]{:S(2)}, u32[]{:S(2)}) collective-permute-start(bf16[1,8,14080]{2,1,0:T(8,128)(2,1)S(1)} %add_convert_fusion.9), channel_id=1, source_target_pairs={{0,2},{1,3},{2,6},{3,7},{6,10},{7,11},{10,14},{11,15},{14,12},{15,... | collective-permute-start | bytes 675848 | tf_op jit(solution)/shard_map/ppermute | solution.py:455
  52.4 4.8 %attend_part.2.refs_0_ = bf16[1,8,11264]{2,1,0:T(8,128)(2,1)S(1)} custom-call(bf16[1,8,14464]{2,1,0:T(8,128)(2,1)S(1)} %slice.80.own_ref, bf16[1,8,14464]{2,1,0:T(8,128)(2,1)S(1)} %collective-permute-done.15.left_ref, bf16[1,8,14464]{2,1,0:T(8,128)(2,1)S(1)} %collective-permute-done.16.right_ref, f32[24,128]{1,0:T(8,128)S(1)} %broadcast_in_dim.7.inv_ref, ...), custom_call_target="tpu_custom_call" | custom-call | flops 1 | bytes 1 | tf_op jit(solution)/shard_map/attend_part/pallas_call | solution.py:341
  57.4 1.9 %collective-permute-start.21 = (bf16[1,8,11264]{2,1,0:T(8,128)(2,1)S(1)}, bf16[1,8,11264]{2,1,0:T(8,128)(2,1)S(1)}, u32[]{:S(2)}, u32[]{:S(2)}) collective-permute-start(bf16[1,8,11264]{2,1,0:T(8,128)(2,1)S(1)} %attend_part.2.refs_0_), channel_id=1, source_target_pairs={{0,2},{1,3},{2,6},{3,7},{6,10},{7,11},{10,14},{11,15},{14,12},{15,... | collective-permute-start | bytes 540680 | tf_op jit(solution)/shard_map/ppermute | solution.py:455
  59.3 4.8 %attend_part.3.refs_0_ = bf16[1,8,11264]{2,1,0:T(8,128)(2,1)S(1)} custom-call(bf16[1,8,14080]{2,1,0:T(8,128)(2,1)S(1)} %slice.79.own_ref, bf16[1,8,14080]{2,1,0:T(8,128)(2,1)S(1)} %collective-permute-done.18.left_ref, bf16[1,8,14080]{2,1,0:T(8,128)(2,1)S(1)} %collective-permute-done.19.right_ref, f32[24,128]{1,0:T(8,128)S(1)} %broadcast_in_dim.7.inv_ref, ...), custom_call_target="tpu_custom_call" | custom-call | flops 1 | bytes 1 | tf_op jit(solution)/shard_map/attend_part/pallas_call | solution.py:341
  64.1 0.8 collective-permute-start.25
  65.0 1.3 %collective-permute-start.20 = (bf16[1,8,11264]{2,1,0:T(8,128)(2,1)S(1)}, bf16[1,8,11264]{2,1,0:T(8,128)(2,1)S(1)}, u32[]{:S(2)}, u32[]{:S(2)}) collective-permute-start(bf16[1,8,11264]{2,1,0:T(8,128)(2,1)S(1)} %attend_part.3.refs_0_), channel_id=1, source_target_pairs={{2,0},{3,1},{6,2},{7,3},{10,6},{11,7},{14,10},{15,11},{12,14},{13,... | collective-permute-start | bytes 540680 | tf_op jit(solution)/shard_map/ppermute | solution.py:455
  66.5 1.8 %collective-permute-start.24 = (bf16[1,8,11264]{2,1,0:T(8,128)(2,1)S(1)}, bf16[1,8,11264]{2,1,0:T(8,128)(2,1)S(1)}, u32[]{:S(2)}, u32[]{:S(2)}) collective-permute-start(bf16[1,8,11264]{2,1,0:T(8,128)(2,1)S(1)} %collective-permute-done.21.refs_7_), channel_id=1, source_target_pairs={{0,2},{1,3},{2,6},{3,7},{6,10},{7,11},{10,14},{11,15},{14,12},{15,... | collective-permute-start | bytes 540680 | tf_op jit(solution)/shard_map/ppermute | solution.py:455
  68.3 4.1 %load_weights.2 = (bf16[4096,512]{1,0:T(8,128)(2,1)S(1)}, bf16[4096,512]{1,0:T(8,128)(2,1)S(1)}, f32[8,128]{1,0:T(8,128)}) custom-call(bf16[8192,512]{1,0:T(8,128)(2,1)} %refs_0_.1, bf16[8192,512]{1,0:T(8,128)(2,1)} %collective-permute-done.17.refs_1_), custom_call_target="tpu_custom_call" | custom-call | flops 1 | bytes 1 | tf_op jit(solution)/shard_map/load_weights/pallas_call | solution.py:324
  72.3 0.8 collective-permute-start.28
  73.2 1.3 %collective-permute-start.23 = (bf16[1,8,11264]{2,1,0:T(8,128)(2,1)S(1)}, bf16[1,8,11264]{2,1,0:T(8,128)(2,1)S(1)}, u32[]{:S(2)}, u32[]{:S(2)}) collective-permute-start(bf16[1,8,11264]{2,1,0:T(8,128)(2,1)S(1)} %collective-permute-done.20.refs_1_), channel_id=1, source_target_pairs={{2,0},{3,1},{6,2},{7,3},{10,6},{11,7},{14,10},{15,11},{12,14},{13,... | collective-permute-start | bytes 540680 | tf_op jit(solution)/shard_map/ppermute | solution.py:455
  74.7 4.1 %load_weights.3 = (bf16[4096,512]{1,0:T(8,128)(2,1)S(1)}, bf16[4096,512]{1,0:T(8,128)(2,1)S(1)}, f32[8,128]{1,0:T(8,128)}) custom-call(bf16[8192,512]{1,0:T(8,128)(2,1)} %refs_0_.1, bf16[8192,512]{1,0:T(8,128)(2,1)} %collective-permute-done.17.refs_1_), custom_call_target="tpu_custom_call" | custom-call | flops 1 | bytes 1 | tf_op jit(solution)/shard_map/load_weights/pallas_call | solution.py:324
  78.8 1.8 %collective-permute-start.29 = (bf16[1,8,11264]{2,1,0:T(8,128)(2,1)S(1)}, bf16[1,8,11264]{2,1,0:T(8,128)(2,1)S(1)}, u32[]{:S(2)}, u32[]{:S(2)}) collective-permute-start(bf16[1,8,11264]{2,1,0:T(8,128)(2,1)S(1)} %collective-permute-done.28.refs_6_), channel_id=1, source_target_pairs={{0,2},{1,3},{2,6},{3,7},{6,10},{7,11},{10,14},{11,15},{14,12},{15,... | collective-permute-start | bytes 540680 | tf_op jit(solution)/shard_map/ppermute | solution.py:455
  80.6 1.3 %collective-permute-start.33 = (bf16[1,8,11264]{2,1,0:T(8,128)(2,1)S(1)}, bf16[1,8,11264]{2,1,0:T(8,128)(2,1)S(1)}, u32[]{:S(2)}, u32[]{:S(2)}) collective-permute-start(bf16[1,8,11264]{2,1,0:T(8,128)(2,1)S(1)} %collective-permute-done.24.refs_6_), channel_id=1, source_target_pairs={{0,2},{1,3},{2,6},{3,7},{6,10},{7,11},{10,14},{11,15},{14,12},{15,... | collective-permute-start | bytes 540680 | tf_op jit(solution)/shard_map/ppermute | solution.py:455
  81.9 0.7 collective-permute-start.32
  82.6 0.5 collective-permute-start.27
  83.1 3.0 %collective-permute-done.29.refs_5_ = bf16[1,8,11264]{2,1,0:T(8,128)(2,1)S(1)} collective-permute-done((bf16[1,8,11264]{2,1,0:T(8,128)(2,1)S(1)}, bf16[1,8,11264]{2,1,0:T(8,128)(2,1)S(1)}, u32[]{:S(2)}, u32[]{:S(2)}) %collective-permute-start.29) | collective-permute-done | bytes 180256 | tf_op jit(solution)/shard_map/ppermute | solution.py:455
  86.1 1.7 %collective-permute-start.31 = (bf16[1,8,11264]{2,1,0:T(8,128)(2,1)S(1)}, bf16[1,8,11264]{2,1,0:T(8,128)(2,1)S(1)}, u32[]{:S(2)}, u32[]{:S(2)}) collective-permute-start(bf16[1,8,11264]{2,1,0:T(8,128)(2,1)S(1)} %collective-permute-done.29.refs_5_), channel_id=1, source_target_pairs={{0,2},{1,3},{2,6},{3,7},{6,10},{7,11},{10,14},{11,15},{14,12},{15,... | collective-permute-start | bytes 540680 | tf_op jit(solution)/shard_map/ppermute | solution.py:455
  87.9 1.4 %features.1 = (f32[192,512]{1,0:T(8,128)S(1)}, f32[192,512]{1,0:T(8,128)S(1)}) custom-call(bf16[352,512]{1,0:T(8,128)(2,1)} %x_ref.4, bf16[352,512]{1,0:T(8,128)(2,1)S(1)} %collective-permute-done.14.x_other_ref), custom_call_target="tpu_custom_call" | custom-call | flops 1 | bytes 1 | tf_op jit(solution)/shard_map/features/pallas_call | solution.py:368
  89.2 1.8 %out_part.2 = (f32[192,512]{1,0:T(8,128)S(1)}, f32[192,512]{1,0:T(8,128)S(1)}) custom-call(bf16[1,8,11264]{2,1,0:T(8,128)(2,1)S(1)} %attend_part.2.refs_0_, bf16[1,8,11264]{2,1,0:T(8,128)(2,1)S(1)} %collective-permute-done.22.refs_1_, bf16[1,8,11264]{2,1,0:T(8,128)(2,1)S(1)} %collective-permute-done.26.refs_2_, ...), custom_call_target="tpu_custom_call" | custom-call | flops 1 | bytes 1 | tf_op jit(solution)/shard_map/out_part/pallas_call | solution.py:397
  91.1 0.6 collective-permute-done.31.refs_4_
  91.6 1.8 %out_part.3 = (bf16[192,512]{1,0:T(8,128)(2,1)S(1)}, bf16[192,512]{1,0:T(8,128)(2,1)S(1)}) custom-call(bf16[1,8,11264]{2,1,0:T(8,128)(2,1)S(1)} %attend_part.3.refs_0_, bf16[1,8,11264]{2,1,0:T(8,128)(2,1)S(1)} %collective-permute-done.20.refs_1_, bf16[1,8,11264]{2,1,0:T(8,128)(2,1)S(1)} %collective-permute-done.23.refs_2_, ...), custom_call_target="tpu_custom_call" | custom-call | flops 1 | bytes 1 | tf_op jit(solution)/shard_map/out_part/pallas_call | solution.py:397
  93.9 1.1 %collective-permute-done.34.rows_ref = bf16[192,512]{1,0:T(8,128)(2,1)S(1)} collective-permute-done((bf16[192,512]{1,0:T(8,128)(2,1)S(1)}, bf16[192,512]{1,0:T(8,128)(2,1)S(1)}, u32[]{:S(2)}, u32[]{:S(2)}) %collective-permute-start.34) | collective-permute-done | bytes 196640 | tf_op jit(solution)/shard_map/ppermute | solution.py:461
  94.9 1.1 %place.3 = bf16[352,512]{1,0:T(8,128)(2,1)} custom-call(bf16[192,512]{1,0:T(8,128)(2,1)S(1)} %collective-permute-done.34.rows_ref, bf16[352,512]{1,0:T(8,128)(2,1)S(1)} %place.2.refs_0_), custom_call_target="tpu_custom_call" | custom-call | flops 1 | bytes 1 | tf_op jit(solution)/shard_map/place/pallas_call | solution.py:421
  (63 shorter events, 4.7 us)
Async XLA Ops:
  0.0 0.7 copy-start
  6.1 2.0 %collective-permute-start = (bf16[2,8,14464]{2,1,0:T(8,128)(2,1)S(1)}, bf16[2,8,14464]{2,1,0:T(8,128)(2,1)S(1)}, u32[]{:S(2)}, u32[]{:S(2)}) collective-permute-start(bf16[2,8,14464]{2,1,0:T(8,128)(2,1)S(1)} %get-tuple-element.60), channel_id=1, source_target_pairs={{0,1},{1,0},{2,3},{3,2},{4,5},{5,4},{6,7},{7,6},{8,9},{9,8},{10,11... | collective-permute-start | bytes 1388552 | tf_op jit(solution)/shard_map/ppermute | solution.py:461
  6.6 12.0 %collective-permute-start.2 = (bf16[6,8,14464]{2,1,0:T(8,128)(2,1)}, bf16[6,8,14464]{2,1,0:T(8,128)(2,1)S(1)}, u32[]{:S(2)}, u32[]{:S(2)}) collective-permute-start(bf16[6,8,14464]{2,1,0:T(8,128)(2,1)} %get-tuple-element.65), channel_id=1, source_target_pairs={{0,1},{1,0},{2,3},{3,2},{4,5},{5,4},{6,7},{7,6},{8,9},{9,8},{10,11... | collective-permute-start | bytes 4165640 | tf_op jit(solution)/shard_map/ppermute | solution.py:461
  8.2 8.9 %collective-permute-start.3 = (bf16[1,8,14464]{2,1,0:T(8,128)(2,1)S(1)}, bf16[1,8,14464]{2,1,0:T(8,128)(2,1)S(1)}, u32[]{:S(2)}, u32[]{:S(2)}) collective-permute-start(bf16[1,8,14464]{2,1,0:T(8,128)(2,1)S(1)} %get-tuple-element.122), channel_id=1, source_target_pairs={{0,2},{1,3},{2,6},{3,7},{6,10},{7,11},{10,14},{11,15},{14,12},{15,... | collective-permute-start | bytes 694280 | tf_op jit(solution)/shard_map/ppermute | solution.py:455
  11.2 7.4 %collective-permute-start.4 = (bf16[1,8,14464]{2,1,0:T(8,128)(2,1)S(1)}, bf16[1,8,14464]{2,1,0:T(8,128)(2,1)S(1)}, u32[]{:S(2)}, u32[]{:S(2)}) collective-permute-start(bf16[1,8,14464]{2,1,0:T(8,128)(2,1)S(1)} %get-tuple-element.121), channel_id=1, source_target_pairs={{2,0},{3,1},{6,2},{7,3},{10,6},{11,7},{14,10},{15,11},{12,14},{13,... | collective-permute-start | bytes 694280 | tf_op jit(solution)/shard_map/ppermute | solution.py:455
  16.6 4.5 %collective-permute-start.5 = (bf16[2,8,14080]{2,1,0:T(8,128)(2,1)S(1)}, bf16[2,8,14080]{2,1,0:T(8,128)(2,1)S(1)}, u32[]{:S(2)}, u32[]{:S(2)}) collective-permute-start(bf16[2,8,14080]{2,1,0:T(8,128)(2,1)S(1)} %get-tuple-element.71), channel_id=1, source_target_pairs={{0,1},{1,0},{2,3},{3,2},{4,5},{5,4},{6,7},{7,6},{8,9},{9,8},{10,11... | collective-permute-start | bytes 1351688 | tf_op jit(solution)/shard_map/ppermute | solution.py:461
  16.7 17.4 %collective-permute-start.1 = (bf16[6,8,14080]{2,1,0:T(8,128)(2,1)}, bf16[6,8,14080]{2,1,0:T(8,128)(2,1)S(1)}, u32[]{:S(2)}, u32[]{:S(2)}) collective-permute-start(bf16[6,8,14080]{2,1,0:T(8,128)(2,1)} %get-tuple-element.63), channel_id=1, source_target_pairs={{0,1},{1,0},{2,3},{3,2},{4,5},{5,4},{6,7},{7,6},{8,9},{9,8},{10,11... | collective-permute-start | bytes 4055048 | tf_op jit(solution)/shard_map/ppermute | solution.py:461
  19.1 8.6 %collective-permute-start.7 = (bf16[1,8,14464]{2,1,0:T(8,128)(2,1)S(1)}, bf16[1,8,14464]{2,1,0:T(8,128)(2,1)S(1)}, u32[]{:S(2)}, u32[]{:S(2)}) collective-permute-start(bf16[1,8,14464]{2,1,0:T(8,128)(2,1)S(1)} %get-tuple-element.116), channel_id=1, source_target_pairs={{0,2},{1,3},{2,6},{3,7},{6,10},{7,11},{10,14},{11,15},{14,12},{15,... | collective-permute-start | bytes 694280 | tf_op jit(solution)/shard_map/ppermute | solution.py:455
  20.7 8.6 %collective-permute-start.8 = (bf16[1,8,14464]{2,1,0:T(8,128)(2,1)S(1)}, bf16[1,8,14464]{2,1,0:T(8,128)(2,1)S(1)}, u32[]{:S(2)}, u32[]{:S(2)}) collective-permute-start(bf16[1,8,14464]{2,1,0:T(8,128)(2,1)S(1)} %get-tuple-element.115), channel_id=1, source_target_pairs={{2,0},{3,1},{6,2},{7,3},{10,6},{11,7},{14,10},{15,11},{12,14},{13,... | collective-permute-start | bytes 694280 | tf_op jit(solution)/shard_map/ppermute | solution.py:455
  21.3 10.6 %collective-permute-start.6 = (bf16[1,8,14080]{2,1,0:T(8,128)(2,1)S(1)}, bf16[1,8,14080]{2,1,0:T(8,128)(2,1)S(1)}, u32[]{:S(2)}, u32[]{:S(2)}) collective-permute-start(bf16[1,8,14080]{2,1,0:T(8,128)(2,1)S(1)} %get-tuple-element.124), channel_id=1, source_target_pairs={{0,2},{1,3},{2,6},{3,7},{6,10},{7,11},{10,14},{11,15},{14,12},{15,... | collective-permute-start | bytes 675848 | tf_op jit(solution)/shard_map/ppermute | solution.py:455
  22.9 11.2 %collective-permute-start.11 = (bf16[1,8,14080]{2,1,0:T(8,128)(2,1)S(1)}, bf16[1,8,14080]{2,1,0:T(8,128)(2,1)S(1)}, u32[]{:S(2)}, u32[]{:S(2)}) collective-permute-start(bf16[1,8,14080]{2,1,0:T(8,128)(2,1)S(1)} %get-tuple-element.123), channel_id=1, source_target_pairs={{2,0},{3,1},{6,2},{7,3},{10,6},{11,7},{14,10},{15,11},{12,14},{13,... | collective-permute-start | bytes 675848 | tf_op jit(solution)/shard_map/ppermute | solution.py:455
  29.4 9.7 %collective-permute-start.10 = (bf16[1,8,14464]{2,1,0:T(8,128)(2,1)S(1)}, bf16[1,8,14464]{2,1,0:T(8,128)(2,1)S(1)}, u32[]{:S(2)}, u32[]{:S(2)}) collective-permute-start(bf16[1,8,14464]{2,1,0:T(8,128)(2,1)S(1)} %get-tuple-element.113), channel_id=1, source_target_pairs={{2,0},{3,1},{6,2},{7,3},{10,6},{11,7},{14,10},{15,11},{12,14},{13,... | collective-permute-start | bytes 694280 | tf_op jit(solution)/shard_map/ppermute | solution.py:455
  29.9 15.5 %collective-permute-start.15 = (bf16[1,8,14464]{2,1,0:T(8,128)(2,1)S(1)}, bf16[1,8,14464]{2,1,0:T(8,128)(2,1)S(1)}, u32[]{:S(2)}, u32[]{:S(2)}) collective-permute-start(bf16[1,8,14464]{2,1,0:T(8,128)(2,1)S(1)} %get-tuple-element.114), channel_id=1, source_target_pairs={{0,2},{1,3},{2,6},{3,7},{6,10},{7,11},{10,14},{11,15},{14,12},{15,... | collective-permute-start | bytes 694280 | tf_op jit(solution)/shard_map/ppermute | solution.py:455
  34.4 8.6 %copy-start.1 = (bf16[6,8,14080]{2,1,0:T(8,128)(2,1)}, bf16[6,8,14080]{2,1,0:T(8,128)(2,1)S(1)}, u32[]{:S(2)}) copy-start(bf16[6,8,14080]{2,1,0:T(8,128)(2,1)S(1)} %add_convert_fusion.1) | copy-start | bytes 4055044
  34.5 10.5 %copy-start.2 = (s32[22]{0:T(128)S(1)}, s32[22]{0:T(128)}, u32[]{:S(2)}) copy-start(s32[22]{0:T(128)} %param.13) | copy-start | bytes 268
  34.6 6.0 %collective-permute-start.9 = (bf16[1,8,14080]{2,1,0:T(8,128)(2,1)S(1)}, bf16[1,8,14080]{2,1,0:T(8,128)(2,1)S(1)}, u32[]{:S(2)}, u32[]{:S(2)}) collective-permute-start(bf16[1,8,14080]{2,1,0:T(8,128)(2,1)S(1)} %get-tuple-element.120), channel_id=1, source_target_pairs={{0,2},{1,3},{2,6},{3,7},{6,10},{7,11},{10,14},{11,15},{14,12},{15,... | collective-permute-start | bytes 675848 | tf_op jit(solution)/shard_map/ppermute | solution.py:455
  36.2 6.0 %collective-permute-start.13 = (bf16[1,8,14080]{2,1,0:T(8,128)(2,1)S(1)}, bf16[1,8,14080]{2,1,0:T(8,128)(2,1)S(1)}, u32[]{:S(2)}, u32[]{:S(2)}) collective-permute-start(bf16[1,8,14080]{2,1,0:T(8,128)(2,1)S(1)} %get-tuple-element.119), channel_id=1, source_target_pairs={{2,0},{3,1},{6,2},{7,3},{10,6},{11,7},{14,10},{15,11},{12,14},{13,... | collective-permute-start | bytes 675848 | tf_op jit(solution)/shard_map/ppermute | solution.py:455
  36.7 22.7 %collective-permute-start.17 = (bf16[8192,512]{1,0:T(8,128)(2,1)}, bf16[8192,512]{1,0:T(8,128)(2,1)}, u32[]{:S(2)}, u32[]{:S(2)}) collective-permute-start(bf16[8192,512]{1,0:T(8,128)(2,1)} %refs_0_.1), channel_id=1, source_target_pairs={{0,1},{1,0},{2,3},{3,2},{4,5},{5,4},{6,7},{7,6},{8,9},{9,8},{10,11... | collective-permute-start | bytes 25165832 | tf_op jit(solution)/shard_map/ppermute | solution.py:461
  39.1 13.3 %collective-permute-start.14 = (bf16[352,512]{1,0:T(8,128)(2,1)}, bf16[352,512]{1,0:T(8,128)(2,1)S(1)}, u32[]{:S(2)}, u32[]{:S(2)}) collective-permute-start(bf16[352,512]{1,0:T(8,128)(2,1)} %x_ref.4), channel_id=1, source_target_pairs={{0,1},{1,0},{2,3},{3,2},{4,5},{5,4},{6,7},{7,6},{8,9},{9,8},{10,11... | collective-permute-start | bytes 1081352 | tf_op jit(solution)/shard_map/ppermute | solution.py:461
  40.6 8.6 %collective-permute-start.16 = (bf16[1,8,14464]{2,1,0:T(8,128)(2,1)S(1)}, bf16[1,8,14464]{2,1,0:T(8,128)(2,1)S(1)}, u32[]{:S(2)}, u32[]{:S(2)}) collective-permute-start(bf16[1,8,14464]{2,1,0:T(8,128)(2,1)S(1)} %add_convert_fusion.4), channel_id=1, source_target_pairs={{2,0},{3,1},{6,2},{7,3},{10,6},{11,7},{14,10},{15,11},{12,14},{13,... | collective-permute-start | bytes 694280 | tf_op jit(solution)/shard_map/ppermute | solution.py:455
  43.1 6.2 %collective-permute-start.12 = (bf16[1,8,14080]{2,1,0:T(8,128)(2,1)}, bf16[1,8,14080]{2,1,0:T(8,128)(2,1)S(1)}, u32[]{:S(2)}, u32[]{:S(2)}) collective-permute-start(bf16[1,8,14080]{2,1,0:T(8,128)(2,1)} %get-tuple-element.118), channel_id=1, source_target_pairs={{0,2},{1,3},{2,6},{3,7},{6,10},{7,11},{10,14},{11,15},{14,12},{15,... | collective-permute-start | bytes 675848 | tf_op jit(solution)/shard_map/ppermute | solution.py:455
  45.4 13.9 %collective-permute-start.19 = (bf16[1,8,14080]{2,1,0:T(8,128)(2,1)}, bf16[1,8,14080]{2,1,0:T(8,128)(2,1)S(1)}, u32[]{:S(2)}, u32[]{:S(2)}) collective-permute-start(bf16[1,8,14080]{2,1,0:T(8,128)(2,1)} %get-tuple-element.117), channel_id=1, source_target_pairs={{2,0},{3,1},{6,2},{7,3},{10,6},{11,7},{14,10},{15,11},{12,14},{13,... | collective-permute-start | bytes 675848 | tf_op jit(solution)/shard_map/ppermute | solution.py:455
  50.3 9.1 %collective-permute-start.18 = (bf16[1,8,14080]{2,1,0:T(8,128)(2,1)S(1)}, bf16[1,8,14080]{2,1,0:T(8,128)(2,1)S(1)}, u32[]{:S(2)}, u32[]{:S(2)}) collective-permute-start(bf16[1,8,14080]{2,1,0:T(8,128)(2,1)S(1)} %add_convert_fusion.9), channel_id=1, source_target_pairs={{0,2},{1,3},{2,6},{3,7},{6,10},{7,11},{10,14},{11,15},{14,12},{15,... | collective-permute-start | bytes 675848 | tf_op jit(solution)/shard_map/ppermute | solution.py:455
  57.2 9.0 %collective-permute-start.22 = (bf16[1,8,11264]{2,1,0:T(8,128)(2,1)S(1)}, bf16[1,8,11264]{2,1,0:T(8,128)(2,1)S(1)}, u32[]{:S(2)}, u32[]{:S(2)}) collective-permute-start(bf16[1,8,11264]{2,1,0:T(8,128)(2,1)S(1)} %attend_part.2.refs_0_), channel_id=1, source_target_pairs={{2,0},{3,1},{6,2},{7,3},{10,6},{11,7},{14,10},{15,11},{12,14},{13,... | collective-permute-start | bytes 540680 | tf_op jit(solution)/shard_map/ppermute | solution.py:455
  57.4 9.1 %collective-permute-start.21 = (bf16[1,8,11264]{2,1,0:T(8,128)(2,1)S(1)}, bf16[1,8,11264]{2,1,0:T(8,128)(2,1)S(1)}, u32[]{:S(2)}, u32[]{:S(2)}) collective-permute-start(bf16[1,8,11264]{2,1,0:T(8,128)(2,1)S(1)} %attend_part.2.refs_0_), channel_id=1, source_target_pairs={{0,2},{1,3},{2,6},{3,7},{6,10},{7,11},{10,14},{11,15},{14,12},{15,... | collective-permute-start | bytes 540680 | tf_op jit(solution)/shard_map/ppermute | solution.py:455
  64.1 8.2 %collective-permute-start.25 = (bf16[1,8,11264]{2,1,0:T(8,128)(2,1)S(1)}, bf16[1,8,11264]{2,1,0:T(8,128)(2,1)S(1)}, u32[]{:S(2)}, u32[]{:S(2)}) collective-permute-start(bf16[1,8,11264]{2,1,0:T(8,128)(2,1)S(1)} %attend_part.3.refs_0_), channel_id=1, source_target_pairs={{0,2},{1,3},{2,6},{3,7},{6,10},{7,11},{10,14},{11,15},{14,12},{15,... | collective-permute-start | bytes 540680 | tf_op jit(solution)/shard_map/ppermute | solution.py:455
  65.0 8.2 %collective-permute-start.20 = (bf16[1,8,11264]{2,1,0:T(8,128)(2,1)S(1)}, bf16[1,8,11264]{2,1,0:T(8,128)(2,1)S(1)}, u32[]{:S(2)}, u32[]{:S(2)}) collective-permute-start(bf16[1,8,11264]{2,1,0:T(8,128)(2,1)S(1)} %attend_part.3.refs_0_), channel_id=1, source_target_pairs={{2,0},{3,1},{6,2},{7,3},{10,6},{11,7},{14,10},{15,11},{12,14},{13,... | collective-permute-start | bytes 540680 | tf_op jit(solution)/shard_map/ppermute | solution.py:455
  66.2 8.2 %collective-permute-start.26 = (bf16[1,8,11264]{2,1,0:T(8,128)(2,1)S(1)}, bf16[1,8,11264]{2,1,0:T(8,128)(2,1)S(1)}, u32[]{:S(2)}, u32[]{:S(2)}) collective-permute-start(bf16[1,8,11264]{2,1,0:T(8,128)(2,1)S(1)} %collective-permute-done.22.refs_1_), channel_id=1, source_target_pairs={{2,0},{3,1},{6,2},{7,3},{10,6},{11,7},{14,10},{15,11},{12,14},{13,... | collective-permute-start | bytes 540680 | tf_op jit(solution)/shard_map/ppermute | solution.py:455
  66.5 8.0 %collective-permute-start.24 = (bf16[1,8,11264]{2,1,0:T(8,128)(2,1)S(1)}, bf16[1,8,11264]{2,1,0:T(8,128)(2,1)S(1)}, u32[]{:S(2)}, u32[]{:S(2)}) collective-permute-start(bf16[1,8,11264]{2,1,0:T(8,128)(2,1)S(1)} %collective-permute-done.21.refs_7_), channel_id=1, source_target_pairs={{0,2},{1,3},{2,6},{3,7},{6,10},{7,11},{10,14},{11,15},{14,12},{15,... | collective-permute-start | bytes 540680 | tf_op jit(solution)/shard_map/ppermute | solution.py:455
  72.3 6.5 %collective-permute-start.28 = (bf16[1,8,11264]{2,1,0:T(8,128)(2,1)S(1)}, bf16[1,8,11264]{2,1,0:T(8,128)(2,1)S(1)}, u32[]{:S(2)}, u32[]{:S(2)}) collective-permute-start(bf16[1,8,11264]{2,1,0:T(8,128)(2,1)S(1)} %collective-permute-done.25.refs_7_), channel_id=1, source_target_pairs={{0,2},{1,3},{2,6},{3,7},{6,10},{7,11},{10,14},{11,15},{14,12},{15,... | collective-permute-start | bytes 540680 | tf_op jit(solution)/shard_map/ppermute | solution.py:455
  73.2 8.8 %collective-permute-start.23 = (bf16[1,8,11264]{2,1,0:T(8,128)(2,1)S(1)}, bf16[1,8,11264]{2,1,0:T(8,128)(2,1)S(1)}, u32[]{:S(2)}, u32[]{:S(2)}) collective-permute-start(bf16[1,8,11264]{2,1,0:T(8,128)(2,1)S(1)} %collective-permute-done.20.refs_1_), channel_id=1, source_target_pairs={{2,0},{3,1},{6,2},{7,3},{10,6},{11,7},{14,10},{15,11},{12,14},{13,... | collective-permute-start | bytes 540680 | tf_op jit(solution)/shard_map/ppermute | solution.py:455
  74.4 7.5 %collective-permute-start.30 = (bf16[1,8,11264]{2,1,0:T(8,128)(2,1)S(1)}, bf16[1,8,11264]{2,1,0:T(8,128)(2,1)S(1)}, u32[]{:S(2)}, u32[]{:S(2)}) collective-permute-start(bf16[1,8,11264]{2,1,0:T(8,128)(2,1)S(1)} %collective-permute-done.26.refs_2_), channel_id=1, source_target_pairs={{2,0},{3,1},{6,2},{7,3},{10,6},{11,7},{14,10},{15,11},{12,14},{13,... | collective-permute-start | bytes 540680 | tf_op jit(solution)/shard_map/ppermute | solution.py:455
  78.8 7.3 %collective-permute-start.29 = (bf16[1,8,11264]{2,1,0:T(8,128)(2,1)S(1)}, bf16[1,8,11264]{2,1,0:T(8,128)(2,1)S(1)}, u32[]{:S(2)}, u32[]{:S(2)}) collective-permute-start(bf16[1,8,11264]{2,1,0:T(8,128)(2,1)S(1)} %collective-permute-done.28.refs_6_), channel_id=1, source_target_pairs={{0,2},{1,3},{2,6},{3,7},{6,10},{7,11},{10,14},{11,15},{14,12},{15,... | collective-permute-start | bytes 540680 | tf_op jit(solution)/shard_map/ppermute | solution.py:455
  80.6 8.6 %collective-permute-start.33 = (bf16[1,8,11264]{2,1,0:T(8,128)(2,1)S(1)}, bf16[1,8,11264]{2,1,0:T(8,128)(2,1)S(1)}, u32[]{:S(2)}, u32[]{:S(2)}) collective-permute-start(bf16[1,8,11264]{2,1,0:T(8,128)(2,1)S(1)} %collective-permute-done.24.refs_6_), channel_id=1, source_target_pairs={{0,2},{1,3},{2,6},{3,7},{6,10},{7,11},{10,14},{11,15},{14,12},{15,... | collective-permute-start | bytes 540680 | tf_op jit(solution)/shard_map/ppermute | solution.py:455
  81.9 7.3 %collective-permute-start.32 = (bf16[1,8,11264]{2,1,0:T(8,128)(2,1)S(1)}, bf16[1,8,11264]{2,1,0:T(8,128)(2,1)S(1)}, u32[]{:S(2)}, u32[]{:S(2)}) collective-permute-start(bf16[1,8,11264]{2,1,0:T(8,128)(2,1)S(1)} %collective-permute-done.30.refs_3_), channel_id=1, source_target_pairs={{2,0},{3,1},{6,2},{7,3},{10,6},{11,7},{14,10},{15,11},{12,14},{13,... | collective-permute-start | bytes 540680 | tf_op jit(solution)/shard_map/ppermute | solution.py:455
  82.6 8.4 %collective-permute-start.27 = (bf16[1,8,11264]{2,1,0:T(8,128)(2,1)S(1)}, bf16[1,8,11264]{2,1,0:T(8,128)(2,1)S(1)}, u32[]{:S(2)}, u32[]{:S(2)}) collective-permute-start(bf16[1,8,11264]{2,1,0:T(8,128)(2,1)S(1)} %collective-permute-done.23.refs_2_), channel_id=1, source_target_pairs={{2,0},{3,1},{6,2},{7,3},{10,6},{11,7},{14,10},{15,11},{12,14},{13,... | collective-permute-start | bytes 540680 | tf_op jit(solution)/shard_map/ppermute | solution.py:455
  86.1 5.5 %collective-permute-start.31 = (bf16[1,8,11264]{2,1,0:T(8,128)(2,1)S(1)}, bf16[1,8,11264]{2,1,0:T(8,128)(2,1)S(1)}, u32[]{:S(2)}, u32[]{:S(2)}) collective-permute-start(bf16[1,8,11264]{2,1,0:T(8,128)(2,1)S(1)} %collective-permute-done.29.refs_5_), channel_id=1, source_target_pairs={{0,2},{1,3},{2,6},{3,7},{6,10},{7,11},{10,14},{11,15},{14,12},{15,... | collective-permute-start | bytes 540680 | tf_op jit(solution)/shard_map/ppermute | solution.py:455
  93.4 1.5 %collective-permute-start.34 = (bf16[192,512]{1,0:T(8,128)(2,1)S(1)}, bf16[192,512]{1,0:T(8,128)(2,1)S(1)}, u32[]{:S(2)}, u32[]{:S(2)}) collective-permute-start(bf16[192,512]{1,0:T(8,128)(2,1)S(1)} %get-tuple-element.111), channel_id=1, source_target_pairs={{0,1},{1,0},{2,3},{3,2},{4,5},{5,4},{6,7},{7,6},{8,9},{9,8},{10,11... | collective-permute-start | bytes 589832 | tf_op jit(solution)/shard_map/ppermute | solution.py:461
